TPU v7x, 512 devices: a whole 4x8x8 slice. The times are simulated.
512 devices in a mesh: ctx: 64 (over z, y_lo, x), tp: 8 (over y_hi, core).
Axes of the slice: x: 4, y: 8 (y_hi: 4, y_lo: 2; y = y_hi * 2 + y_lo), z: 8, core: 2. Of those that a mesh axis runs over, the one named last changes fastest.
Arguments:
- byte_states: bfloat16 [16384, 1024], P('ctx'), may hold values from -12 to 12, as said below
- patch_of_byte: int32 [16384], P('ctx'), may hold values from 0 to 125, as said below
- patch_first: int32 [64], replicated, may hold values from 0 to 4063, as said below
- moved: int32 [2, 64], replicated, may hold values from 0 to 32, as said below
- w_qkv: bfloat16 [3, 1024, 2048], P(None, None, 'tp'), may hold values from -0.25 to 0.25, as said below
- d_attn: bfloat16 [4096, 2048], P('ctx', 'tp'), may hold values from -6 to 6
Outputs:
- attn_out: bfloat16 [4096, 2048], P('ctx', 'tp')
- byte_grad: bfloat16 [16384, 1024], P('ctx', 'tp')
Inputs may be any that keep to these rules, and one draw needn't show every extreme that they name: `patch_of_byte`: within each byte shard the numbers start at 0 and rise by 0 or 1 from byte to byte; a shard holds at most 126 patches, reached on some shard. `patch_first`: the sum of the patch counts of all earlier byte shards; shard 0 starts at 0. moved[0, 0] = 0 and moved[1, 63] = 0; every other entry is 1 to 32; every patch shard thereby receives exactly 64 patches, and the patch counts agree with patch_first and patch_of_byte. `w_qkv`: independent entries of order 1024 ** -0.5. `byte_states`: entries of order one.
All inputs are finite; a program needn't handle non-finite values.
Results may differ from a plain program's by a relative error of at most 0.011.
Values may be sent and summed in bfloat16 or wider, within the bound.
No kernel may reach another device: no remote copies, remote signals or barrier semaphores. Data moves between devices by JAX's collectives and lax.ppermute only.
A program may use at most 64 MiB of HBM per device.

v0:
```python
import jax
import jax.numpy as jnp
from jax import lax
from jax.sharding import PartitionSpec as P

HD = 128


def extended_2(x, sides, width):
    for axis, dim in sides:
        peers, length = (lax.axis_size(axis), x.shape[dim])
        up = [(i, (i + 1) % peers) for i in range(peers - 1)]
        down = [(j, i) for i, j in up]
        last = lax.slice_in_dim(x, length - width, length, axis=dim)
        first = lax.slice_in_dim(x, 0, width, axis=dim)
        before = lax.ppermute(last, axis, up)
        after = lax.ppermute(first, axis, down)
        x = jnp.concatenate([before, x, after], axis=dim)
    return x


def in_one_piece(arrays, axis, dim, along):
    ends, at = ([], 0)
    for a in arrays[:-1]:
        at += a.shape[along]
        ends.append(at)
    both = jnp.concatenate(arrays, axis=along)
    return tuple(jnp.split(lax.all_gather(both, axis, axis=dim, tiled=True), ends, axis=along))


def cut_along(x, dim, peers):
    shape = x.shape
    pieces = x.reshape(*shape[:dim], peers, shape[dim] // peers, *shape[dim + 1 :])
    return jnp.moveaxis(pieces, dim, 0)


def sent_and_summed(x, axis, dim):
    pieces = cut_along(x, dim, lax.axis_size(axis))
    arrived = lax.all_to_all(pieces, axis, split_axis=0, concat_axis=0, tiled=True)
    return arrived.sum(axis=0)


def pick_own(values, index):
    return lax.dynamic_index_in_dim(values, index, 0, keepdims=False)


def shards(byte_states, patch_of_byte, patch_first, moved, w_qkv, d_attn):
    ctx_index = lax.axis_index("ctx")
    n_ctx = lax.axis_size("ctx")
    rows = d_attn.shape[0]
    feats = d_attn.shape[1]
    heads = feats // HD
    capacity = 2 * rows
    total = rows * n_ctx
    scale = HD ** (-0.5)
    ends = jnp.concatenate([patch_first[1:], jnp.full((1,), total, jnp.int32)])
    counts = ends - patch_first
    lower_moves = moved[0]
    upper_moves = moved[1]
    zero_one = jnp.zeros((1,), jnp.int32)
    below_high = jnp.concatenate([zero_one, upper_moves[:-1]])
    above_low = jnp.concatenate([lower_moves[1:], zero_one])
    prev_first = jnp.concatenate([zero_one, patch_first[:-1]])
    prev_count = jnp.concatenate([zero_one, counts[:-1]])
    ranks = jnp.arange(rows, dtype=jnp.int32)[None, :]
    from_low = ranks < below_high[:, None]
    from_high = ranks >= (rows - above_low)[:, None]
    lower_local = prev_count[:, None] - below_high[:, None] + ranks
    own_local = lower_moves[:, None] + ranks - below_high[:, None]
    upper_local = ranks - (rows - above_low)[:, None]
    ids_all = jnp.where(
        from_low,
        prev_first[:, None] + lower_local,
        jnp.where(from_high, ends[:, None] + upper_local, patch_first[:, None] + own_local),
    )
    source_all = jnp.where(
        from_low,
        lower_local,
        jnp.where(from_high, 2 * capacity + upper_local, capacity + own_local),
    )
    wanted = pick_own(ids_all, ctx_index)
    source_rows = pick_own(source_all, ctx_index)
    key_place = ids_all.reshape(-1)
    slots = jnp.arange(capacity, dtype=jnp.int32)
    member = patch_of_byte[None, :] == slots[:, None]
    lengths = jnp.sum(member.astype(jnp.float32), axis=1)
    onehot = member.astype(jnp.bfloat16)
    pooled_local = (
        jnp.dot(onehot, byte_states, preferred_element_type=jnp.float32)
        / jnp.maximum(lengths, 1.0)[:, None]
    ).astype(jnp.bfloat16)
    extended = extended_2(pooled_local, (("ctx", 0),), capacity)
    picker = (source_rows[:, None] == jnp.arange(3 * capacity, dtype=jnp.int32)[None, :]).astype(
        jnp.bfloat16
    )
    pooled = jnp.dot(picker, extended, preferred_element_type=jnp.float32).astype(jnp.bfloat16)
    query = jnp.dot(pooled, w_qkv[0], preferred_element_type=jnp.float32).astype(jnp.bfloat16)
    keyed = jnp.dot(pooled, w_qkv[1], preferred_element_type=jnp.float32).astype(jnp.bfloat16)
    valued = jnp.dot(pooled, w_qkv[2], preferred_element_type=jnp.float32).astype(jnp.bfloat16)
    keys_all, values_all = in_one_piece((keyed, valued), "ctx", 0, 1)
    query3 = query.reshape(rows, heads, HD)
    keys3 = keys_all.reshape(total, heads, HD)
    values3 = values_all.reshape(total, heads, HD)
    causal = (wanted[:, None] >= key_place[None, :])[None, :, :]
    score = jnp.einsum("qhd,khd->hqk", query3, keys3, preferred_element_type=jnp.float32) * scale
    masked = jnp.where(causal, score, -jnp.inf)
    top = jnp.max(masked, axis=2, keepdims=True)
    lse = top + jnp.log(jnp.sum(jnp.exp(masked - top), axis=2, keepdims=True))
    prob = jnp.exp(jnp.where(causal, score - lse, -jnp.inf))
    probs = prob.astype(jnp.bfloat16)
    output3 = jnp.einsum("hqk,khd->qhd", probs, values3, preferred_element_type=jnp.float32).astype(
        jnp.bfloat16
    )
    attn_out = output3.reshape(rows, feats)
    grad3 = d_attn.reshape(rows, heads, HD)
    delta = jnp.sum(grad3.astype(jnp.float32) * output3.astype(jnp.float32), axis=2)
    dprob = jnp.einsum("qhd,khd->hqk", grad3, values3, preferred_element_type=jnp.float32)
    dscore = (prob * (dprob - jnp.transpose(delta)[:, :, None])).astype(jnp.bfloat16)
    d_query = (
        jnp.einsum("hqk,khd->qhd", dscore, keys3, preferred_element_type=jnp.float32) * scale
    ).astype(jnp.bfloat16)
    key_terms = (
        jnp.einsum("hqk,qhd->khd", dscore, query3, preferred_element_type=jnp.float32) * scale
    )
    value_terms = jnp.einsum("hqk,qhd->khd", probs, grad3, preferred_element_type=jnp.float32)
    key_terms = key_terms.reshape(n_ctx, rows, feats)
    value_terms = value_terms.reshape(n_ctx, rows, feats)
    key_recv, value_recv = (
        lax.all_to_all(key_terms, "ctx", split_axis=0, concat_axis=0, tiled=True),
        lax.all_to_all(value_terms, "ctx", split_axis=0, concat_axis=0, tiled=True),
    )
    d_key = jnp.sum(key_recv, axis=0).astype(jnp.bfloat16)
    d_value = jnp.sum(value_recv, axis=0).astype(jnp.bfloat16)
    d_query = d_query.reshape(rows, feats)
    contract = (((1,), (1,)), ((), ()))
    partial_value = lax.dot_general(d_query, w_qkv[0], contract, preferred_element_type=jnp.float32)
    partial_value = partial_value + lax.dot_general(
        d_key, w_qkv[1], contract, preferred_element_type=jnp.float32
    )
    partial_value = partial_value + lax.dot_general(
        d_value, w_qkv[2], contract, preferred_element_type=jnp.float32
    )
    d_pooled = sent_and_summed(partial_value, "tp", 1).astype(jnp.bfloat16)
    returned = extended_2(d_pooled, (("ctx", 0),), rows)
    my_count = pick_own(counts, ctx_index)
    my_low = pick_own(lower_moves, ctx_index)
    my_high = pick_own(upper_moves, ctx_index)
    my_below = pick_own(below_high, ctx_index)
    target = jnp.where(
        patch_of_byte < my_low,
        rows - my_low + patch_of_byte,
        jnp.where(
            patch_of_byte >= my_count - my_high,
            2 * rows + patch_of_byte - (my_count - my_high),
            rows + my_below + patch_of_byte - my_low,
        ),
    )
    chooser = (target[:, None] == jnp.arange(3 * rows, dtype=jnp.int32)[None, :]).astype(
        jnp.bfloat16
    )
    spread_back = jnp.dot(chooser, returned, preferred_element_type=jnp.float32)
    byte_lengths = jnp.sum(jnp.where(member, lengths[:, None], 0.0), axis=0)
    byte_grad = (spread_back / byte_lengths[:, None]).astype(jnp.bfloat16)
    return (attn_out, byte_grad)


def solution(mesh):
    placed = (P("ctx", None), P("ctx"), P(), P(), P(None, None, "tp"), P("ctx", "tp"))
    return jax.shard_map(
        shards,
        mesh=mesh,
        in_specs=placed,
        out_specs=(P("ctx", "tp"), P("ctx", "tp")),
        check_vma=False,
    )
```

profile of v0, /device:TPU:1, one launch (start us, length us, event | category | flops | bytes accessed | tf_op | source)
XLA Modules:
  0.0 564.5 jit_solution(3717451121622891855)
XLA Ops:
  7.2 0.8 convert_reduce_fusion
  8.2 1.0 fusion.15
  9.3 1.3 collective-permute-start.1
  10.6 4.6 collective-permute-start
  17.8 1.9 select_bitcast_fusion
  22.7 272.5 %all-gather.2.cloned.1.call-done = bf16[4096,512]{1,0:T(8,128)(2,1)} async-done(((bf16[64,512]{1,0:T(8,128)(2,1)}), bf16[4096,512]{1,0:T(8,128)(2,1)}) %all-gather.2.cloned.1.call-update) | async-done | bytes 4194320 | tf_op jit(solution)/shard_map/all_gather | solution.py:28
  295.3 2.9 slice_bitcast_fusion.1
  298.2 1.0 select_reduce_fusion
  300.3 0.8 multiply_reduce_fusion
  301.1 0.9 fusion.3
  302.1 1.0 copy-done.5
  303.0 2.7 fusion
  305.8 7.2 %copy.51 = f32[4096,2,128]{2,1,0:T(2,128)} copy(f32[4096,2,128]{0,2,1:T(8,128)} %fusion) | data formatting | bytes 8388608 | tf_op jit(solution)/shard_map/mul | solution.py:123
  313.0 6.4 %reshape.237 = f32[64,64,256]{2,1,0:T(8,128)} reshape(f32[4096,2,128]{2,1,0:T(2,128)} %copy.51) | data formatting | bytes 8388608 | tf_op jit(solution)/shard_map/reshape | solution.py:126
  319.4 7.5 %all-to-all-start = ((f32[64,64,256]{2,1,0:T(8,128)}), f32[64,64,256]{2,1,0:T(8,128)}, u32[]{:S(2)}, u32[]{:S(2)}) async-start(f32[64,64,256]{2,1,0:T(8,128)} %reshape.237), calls=%async_computation | async-start | bytes 8388608 | tf_op jit(solution)/shard_map/all_to_all | solution.py:129
  327.0 1.1 convolution_bitcast_fusion
  328.0 16.1 %copy.53 = f32[4096,2,128]{2,1,0:T(2,128)} copy(f32[4096,2,128]{2,0,1:T(8,128)S(1)} %convolution_bitcast_fusion) | data formatting | bytes 8388608 | tf_op jit(solution)/shard_map/hqk,qhd->khd/transpose | solution.py:125
  344.2 6.5 %reshape.238 = f32[64,64,256]{2,1,0:T(8,128)} reshape(f32[4096,2,128]{2,1,0:T(2,128)} %copy.53) | data formatting | bytes 8388608 | tf_op jit(solution)/shard_map/reshape | solution.py:127
  350.6 29.2 %all-to-all-done = f32[64,64,256]{2,1,0:T(8,128)} async-done(((f32[64,64,256]{2,1,0:T(8,128)}), f32[64,64,256]{2,1,0:T(8,128)}, u32[]{:S(2)}, u32[]{:S(2)}) %all-to-all-start) | async-done | bytes 4194336 | tf_op jit(solution)/shard_map/all_to_all | solution.py:129
  379.8 36.7 %all-to-all-start.1 = ((f32[64,64,256]{2,1,0:T(8,128)}), f32[64,64,256]{2,1,0:T(8,128)}, u32[]{:S(2)}, u32[]{:S(2)}) async-start(f32[64,64,256]{2,1,0:T(8,128)} %reshape.238), calls=%async_computation.1 | async-start | bytes 8388608 | tf_op jit(solution)/shard_map/all_to_all | solution.py:130
  416.5 1.7 fusion.27
  418.1 1.3 fusion.36
  419.5 2.6 reduce_sum.66
  422.4 51.8 %all-to-all-done.1 = f32[64,64,256]{2,1,0:T(8,128)} async-done(((f32[64,64,256]{2,1,0:T(8,128)}), f32[64,64,256]{2,1,0:T(8,128)}, u32[]{:S(2)}, u32[]{:S(2)}) %all-to-all-start.1) | async-done | bytes 4194336 | tf_op jit(solution)/shard_map/all_to_all | solution.py:130
  474.2 2.4 reduce_sum.67
  476.9 0.7 copy.115
  477.7 62.9 %all-to-all-start.2 = ((f32[8,64,128]{2,1,0:T(8,128)}), f32[8,64,128]{2,1,0:T(8,128)S(1)}, u32[]{:S(2)}, u32[]{:S(2)}) async-start(f32[8,64,128]{2,1,0:T(8,128)} %bitcast.118), calls=%async_computation.2 | async-start | bytes 524288 | tf_op jit(solution)/shard_map/all_to_all | solution.py:39
  541.7 0.7 constant_dynamic-slice_fusion.3
  545.6 5.0 all-to-all-done.2
  550.7 1.3 collective-permute-start.3
  552.0 4.0 collective-permute-start.2
  556.8 0.9 fusion.17
  (73 shorter events, 10.2 us)
Async XLA Ops:
  7.2 1.1 copy-start
  7.2 8.0 %copy-start.8 = (s32[2,64]{1,0:T(2,128)S(1)}, s32[2,64]{1,0:T(2,128)}, u32[]{:S(2)}) copy-start(s32[2,64]{1,0:T(2,128)} %param.9) | copy-start | bytes 1540
  7.2 8.1 %copy-start.7 = (s32[64]{0:T(128)S(1)}, s32[64]{0:T(128)}, u32[]{:S(2)}) copy-start(s32[64]{0:T(128)} %param.8) | copy-start | bytes 772
  7.2 288.1 %all-gather.2.cloned.1.call-start = ((), (), s32[]{:S(2)}) async-start(), calls=%async_computation.3 | async-start | bytes 4259840 | tf_op jit(solution)/shard_map/all_gather | solution.py:28
  8.2 11.8 %copy-start.3 = (bf16[3,1024,256]{2,1,0:T(8,128)(2,1)S(1)}, bf16[3,1024,256]{2,1,0:T(8,128)(2,1)}, u32[]{:S(2)}) copy-start(bf16[3,1024,256]{2,1,0:T(8,128)(2,1)} %param.10) | copy-start | bytes 4718596
  9.3 10.4 %collective-permute-start.1 = (bf16[128,1024]{1,0:T(8,128)(2,1)S(1)}, bf16[128,1024]{1,0:T(8,128)(2,1)S(1)}, u32[]{:S(2)}, u32[]{:S(2)}) collective-permute-start(bf16[128,1024]{1,0:T(8,128)(2,1)S(1)} %fusion.15), channel_id=1, source_target_pairs={{8,0},{16,8},{24,16},{32,24},{40,32},{48,40},{56,48},{64,56},{72,6... | collective-permute-start | bytes 786440 | tf_op jit(solution)/shard_map/ppermute | solution.py:17
  10.6 9.1 %collective-permute-start = (bf16[128,1024]{1,0:T(8,128)(2,1)S(1)}, bf16[128,1024]{1,0:T(8,128)(2,1)S(1)}, u32[]{:S(2)}, u32[]{:S(2)}) collective-permute-start(bf16[128,1024]{1,0:T(8,128)(2,1)S(1)} %fusion.15), channel_id=1, source_target_pairs={{0,8},{8,16},{16,24},{24,32},{32,40},{40,48},{48,56},{56,64},{64,7... | collective-permute-start | bytes 786440 | tf_op jit(solution)/shard_map/ppermute | solution.py:16
  298.2 1.3 copy-start.1
  299.5 0.8 copy-start.6
  302.1 1.0 copy-start.5
  319.4 60.4 %all-to-all-start = ((f32[64,64,256]{2,1,0:T(8,128)}), f32[64,64,256]{2,1,0:T(8,128)}, u32[]{:S(2)}, u32[]{:S(2)}) async-start(f32[64,64,256]{2,1,0:T(8,128)} %reshape.237), calls=%async_computation | async-start | bytes 8388608 | tf_op jit(solution)/shard_map/all_to_all | solution.py:129
  350.6 65.9 %copy-start.2 = (bf16[512,2,8,128]{3,2,1,0:T(8,128)(2,1)S(1)}, bf16[512,2,8,128]{3,2,1,0:T(8,128)(2,1)}, u32[]{:S(2)}) copy-start(bf16[512,2,8,128]{3,2,1,0:T(8,128)(2,1)} %copy-done.1) | copy-start | bytes 6291460
  379.8 94.4 %all-to-all-start.1 = ((f32[64,64,256]{2,1,0:T(8,128)}), f32[64,64,256]{2,1,0:T(8,128)}, u32[]{:S(2)}, u32[]{:S(2)}) async-start(f32[64,64,256]{2,1,0:T(8,128)} %reshape.238), calls=%async_computation.1 | async-start | bytes 8388608 | tf_op jit(solution)/shard_map/all_to_all | solution.py:130
  419.5 2.7 copy-start.4
  476.6 68.3 %copy-start.9 = (s32[256]{0:T(256)S(1)}, s32[256]{0:T(256)}, u32[]{:S(2)}) copy-start(s32[256]{0:T(256)} %param.7) | copy-start | bytes 3076
  477.7 73.0 %all-to-all-start.2 = ((f32[8,64,128]{2,1,0:T(8,128)}), f32[8,64,128]{2,1,0:T(8,128)S(1)}, u32[]{:S(2)}, u32[]{:S(2)}) async-start(f32[8,64,128]{2,1,0:T(8,128)} %bitcast.118), calls=%async_computation.2 | async-start | bytes 524288 | tf_op jit(solution)/shard_map/all_to_all | solution.py:39
  550.7 5.9 %collective-permute-start.3 = (bf16[64,128]{1,0:T(8,128)(2,1)S(1)}, bf16[64,128]{1,0:T(8,128)(2,1)S(1)}, u32[]{:S(2)}, u32[]{:S(2)}) collective-permute-start(bf16[64,128]{1,0:T(8,128)(2,1)S(1)} %reduce_sum.68), channel_id=1, source_target_pairs={{8,0},{16,8},{24,16},{32,24},{40,32},{48,40},{56,48},{64,56},{72,6... | collective-permute-start | bytes 49160 | tf_op jit(solution)/shard_map/ppermute | solution.py:17
  552.0 4.8 collective-permute-start.2
Sparse Core Ops, SparseCore 0:
  21.3 273.9 all-gather.1
where the time goes:
time: 572 us; the launch traced here: 565 us
  waiting for transfers between devices  359 us (63%)
  starting transfers between devices  118 us (21%)
  local copies, waits for them, and re-layouts  47.2 us (8%)
  between operations  16.9 us (3%)
  matrix products  12.9 us (2%)
  other arithmetic  10.5 us (2%)
    all_gather x1, waiting for transfers between devices, in_one_piece(): lax.all_gather(both, axis, axis=dim, tiled=True)  273 us
    all_to_all x1, starting transfers between devices, sent_and_summed(): lax.all_to_all(pieces, axis, split_axis=0, concat_axis=0, tiled=True)  62.9 us
    all_to_all x1, waiting for transfers between devices, shards(): lax.all_to_all(value_terms, 'ctx', split_axis=0, concat_axis=0, tiled=True)  51.8 us
    all_to_all x1, starting transfers between devices, shards(): lax.all_to_all(value_terms, 'ctx', split_axis=0, concat_axis=0, tiled=True)  36.7 us
    all_to_all x1, waiting for transfers between devices, shards(): lax.all_to_all(key_terms, 'ctx', split_axis=0, concat_axis=0, tiled=True)  29.2 us
    transpose x1, local copies, waits for them, and re-layouts, shards(): jnp.einsum('hqk,qhd->khd', probs, grad3, preferred_element_type=jnp.float32)  16.1 us
  transfers between devices with their start and end apart: 8, of which 5 were waited for; matrix products, arithmetic and copies ran while one was open for 7% of the time, Pallas kernels for 0%

commit v1 on v0

v1 whole, which is shorter than its diff:
```python
import jax
import jax.numpy as jnp
from jax import lax
from jax.sharding import Mesh, PartitionSpec as P

HD = 128
SIZES = (4, 2, 2, 4, 4, 2)
NAMES = ("zh", "zl", "yl", "x", "yh", "core")
CTX = ("zh", "zl", "yl", "x")
KEYED = ("zl", "yl", "x")
TP = ("yh", "core")
N_CTX = 64
N_QUERY = 4
N_KEY = 16
BF = jnp.bfloat16
F32 = jnp.float32


def dot(a, b, dims):
    return lax.dot_general(a, b, (dims, ((), ())), preferred_element_type=F32)


def shift(x, axis, n, by):
    return lax.ppermute(x, axis, [(i, (i + by) % n) for i in range(n)])


def swap(x, axis):
    return lax.all_to_all(x, axis, split_axis=0, concat_axis=0, tiled=True)


def shards(byte_states, patch_of_byte, patch_first, moved, w_qkv, d_attn):
    rows, feats = d_attn.shape
    heads = feats // HD
    total = rows * N_CTX
    window = 2 * rows
    half = rows // 2
    scale = HD ** (-0.5)
    c = lax.axis_index(CTX)
    zh = lax.axis_index("zh")

    def entry(values, at):
        return jnp.where((at >= 0) & (at < N_CTX), values[jnp.clip(at, 0, N_CTX - 1)], 0)

    first = patch_first[c]
    low = moved[0, c]
    next_first = jnp.where(c + 1 < N_CTX, entry(patch_first, c + 1), total)
    next_low = entry(moved[0], c + 1)
    prev_high = entry(moved[1], c - 1)
    base = rows * c - half

    places = lax.broadcasted_iota(jnp.int32, (window, 1), 0)
    member = places == (first - base + patch_of_byte)[None, :]
    lengths = jnp.sum(member.astype(F32), axis=1)
    pooled = (
        dot(member.astype(BF), byte_states, ((1,), (0,))) / jnp.maximum(lengths, 1.0)[:, None]
    ).astype(BF)
    rank = jnp.arange(rows, dtype=jnp.int32)
    order = jnp.where(
        rank < prev_high,
        first - prev_high + rank,
        jnp.where(
            rank >= rows - next_low,
            next_first + rank - (rows - next_low),
            first + low + rank - prev_high,
        ),
    )
    slotted = (places == (order - base)[None, :]).astype(BF)
    grads = dot(slotted, d_attn, ((1,), (0,))).astype(BF)
    parts = [dot(pooled, w_qkv[i], ((1,), (0,))).astype(BF) for i in range(3)]
    both = jnp.concatenate([parts[0], grads, parts[1], parts[2]], axis=1)
    mine = both[rows:] + shift(both[:rows], CTX, N_CTX, -1)

    asked = mine[:, : 2 * feats]
    asked = jnp.concatenate(
        [asked] + [shift(asked, "zh", N_QUERY, k) for k in range(1, N_QUERY)], axis=0
    )
    held = swap(jnp.broadcast_to(mine[None, :, 2 * feats :], (N_KEY, rows, 2 * feats)), KEYED)
    held = held.reshape(N_KEY * rows, 2 * feats)
    n_q, n_k = N_QUERY * rows, N_KEY * rows
    row = jnp.arange(n_q, dtype=jnp.int32)
    block = (zh - row // rows) % N_QUERY
    group = c % N_KEY
    query_id = (rows * (block * N_KEY + group) + half + row % rows) % total
    key_id = (n_k * zh + half + jnp.arange(n_k, dtype=jnp.int32)) % total
    causal = query_id[:, None] >= key_id[None, :]

    stats, saved = [], []
    for h in range(heads):
        q = asked[:, h * HD : (h + 1) * HD]
        g = asked[:, feats + h * HD : feats + (h + 1) * HD]
        k = held[:, h * HD : (h + 1) * HD]
        v = held[:, feats + h * HD : feats + (h + 1) * HD]
        score = jnp.where(causal, dot(q, k, ((1,), (1,))) * scale, -1e30)
        top = jnp.max(score, axis=1)
        weight = jnp.where(causal, jnp.exp(score - top[:, None]), 0.0)
        out = dot(weight.astype(BF), v, ((1,), (0,)))
        dprob = dot(g, v, ((1,), (1,)))
        stats += [top, jnp.sum(weight, axis=1), jnp.sum(out * g.astype(F32), axis=1)]
        saved.append((q, g, k, weight, out, dprob))
    stats = jnp.stack(stats + [stats[0]] * (8 - len(stats)), axis=0)
    shared = [stats]
    for k in range(1, N_QUERY):
        shared.append(jnp.roll(shift(stats, "zh", N_QUERY, k), k * rows, axis=1))
    shared = jnp.stack(shared, axis=0)

    query_terms, out_terms, key_terms, value_terms = [], [], [], []
    for h in range(heads):
        q, g, k, weight, out, dprob = saved[h]
        tops, sums, dots = (shared[:, 3 * h + i] for i in range(3))
        peak = jnp.max(tops, axis=0)
        each = jnp.exp(tops - peak[None])
        norm = jnp.sum(each * sums, axis=0)
        delta = jnp.sum(each * dots, axis=0) / norm
        factor = jnp.exp(tops[0] - peak) / norm
        prob = weight * factor[:, None]
        dscore = (prob * (dprob - delta[:, None])).astype(BF)
        query_terms.append(dot(dscore, k, ((1,), (0,))) * scale)
        out_terms.append(out * factor[:, None])
        key_terms.append(dot(dscore, q, ((0,), (0,))) * scale)
        value_terms.append(dot(prob.astype(BF), g, ((0,), (0,))))
    held_terms = jnp.concatenate(key_terms + value_terms, axis=1).astype(BF)
    held_terms = swap(held_terms.reshape(N_KEY, rows, 2 * feats), KEYED)
    held_grads = jnp.sum(held_terms.astype(F32), axis=0).astype(BF)
    asked_terms = jnp.concatenate(query_terms + out_terms, axis=1)
    asked_sum = asked_terms[:rows]
    asked_terms = asked_terms.astype(BF)
    for k in range(1, N_QUERY):
        arrived = shift(asked_terms[k * rows : (k + 1) * rows], "zh", N_QUERY, -k)
        asked_sum = asked_sum + arrived.astype(F32)
    asked_sum = asked_sum.astype(BF)
    d_query, out = asked_sum[:, :feats], asked_sum[:, feats:]

    partial = dot(d_query, w_qkv[0], ((1,), (1,)))
    partial = partial + dot(held_grads[:, :feats], w_qkv[1], ((1,), (1,)))
    partial = partial + dot(held_grads[:, feats:], w_qkv[2], ((1,), (1,)))
    n_tp = 8
    pieces = partial.astype(BF).reshape(rows, n_tp, -1).transpose(1, 0, 2)
    d_pooled = jnp.sum(swap(pieces, TP).astype(F32), axis=0).astype(BF)

    out_window = jnp.concatenate([shift(out, CTX, N_CTX, 1), out], axis=0)
    attn_out = dot(slotted, out_window, ((0,), (0,))).astype(BF)
    grad_window = jnp.concatenate([shift(d_pooled, CTX, N_CTX, 1), d_pooled], axis=0)
    spread = dot(member.astype(BF), grad_window, ((0,), (0,)))
    byte_lengths = jnp.sum(jnp.where(member, lengths[:, None], 0.0), axis=0)
    byte_grad = (spread / byte_lengths[:, None]).astype(BF)
    return attn_out, byte_grad


def solution(mesh):
    fine = Mesh(mesh.devices.reshape(SIZES), NAMES)
    placed = (P(CTX, None), P(CTX), P(), P(), P(None, None, TP), P(CTX, TP))
    return jax.shard_map(
        shards,
        mesh=fine,
        in_specs=placed,
        out_specs=(P(CTX, TP), P(CTX, TP)),
        check_vma=False,
    )
```

time: 572 us -> 140 us (0.24); the launches traced: 565 us -> 139 us
  waiting for transfers between devices: 359 us -> 31.8 us
  starting transfers between devices: 118 us -> 78.4 us
  local copies, waits for them, and re-layouts: 47.2 us -> 7.66 us
  between operations: 16.9 us -> 5.76 us
  other arithmetic: 10.5 us -> 3.46 us
    all_gather x1 -> x0, waiting for transfers between devices: 273 us -> none  [in_one_piece(): lax.all_gather(both, axis, axis=dim, tiled=True)]
    all_to_all x3, starting transfers between devices: 107 us -> 25.7 us  [swap(): return lax.all_to_all(x, axis, split_axis=0, concat_axis=0, tiled=True)]
    all_to_all x3, waiting for transfers between devices: 86 us -> 4.88 us  [swap(): return lax.all_to_all(x, axis, split_axis=0, concat_axis=0, tiled=True)]
    ppermute x4 -> x12, starting transfers between devices: 11.2 us -> 52.7 us  [shift(): return lax.ppermute(x, axis, [(i, (i + by) % n) for i in range(n)])]
    ppermute x4 -> x12, waiting for transfers between devices: 0.24 us -> 27 us  [shift(): return lax.ppermute(x, axis, [(i, (i + by) % n) for i in range(n)])]
    transpose x1 -> x0, local copies, waits for them, and re-layouts: 16.1 us -> none  [shards(): jnp.einsum('hqk,qhd->khd', probs, grad3, preferred_element_type=jnp.float32)]
    reshape x4 -> x1, local copies, waits for them, and re-layouts: 14.2 us -> 0.67 us  [shards(): pieces = partial.astype(BF).reshape(rows, n_tp, -1).transpose(1, 0, 2)]
    mul x1 -> x0, local copies, waits for them, and re-layouts: 7.2 us -> none  [shards(): jnp.einsum('hqk,qhd->khd', dscore, query3, preferred_element_type=jnp.flo...]
  transfers between devices with their start and end apart: 8 -> 15, of which waited for: 5 -> 10; matrix products, arithmetic and copies ran while one was open for 7% -> 2% of each run, Pallas kernels for 0% -> 0%
where the time goes in v1:
time: 140 us; the launch traced here: 139 us
  starting transfers between devices  78.4 us (56%)
  waiting for transfers between devices  31.8 us (23%)
  matrix products  11.7 us (8%)
  local copies, waits for them, and re-layouts  7.66 us (5%)
  between operations  5.76 us (4%)
  other arithmetic  3.46 us (2%)
    ppermute x12, starting transfers between devices, shift(): return lax.ppermute(x, axis, [(i, (i + by) % n) for i in range(n)])  52.7 us
    ppermute x12, waiting for transfers between devices, shift(): return lax.ppermute(x, axis, [(i, (i + by) % n) for i in range(n)])  27 us
    all_to_all x3, starting transfers between devices, swap(): return lax.all_to_all(x, axis, split_axis=0, concat_axis=0, tiled=True)  25.7 us
    dot_general x22, matrix products, dot(): return lax.dot_general(a, b, (dims, ((), ())), preferred_element_type=F32)  11.7 us
    all_to_all x3, waiting for transfers between devices, swap(): return lax.all_to_all(x, axis, split_axis=0, concat_axis=0, tiled=True)  4.88 us
  transfers between devices with their start and end apart: 15, of which 10 were waited for; matrix products, arithmetic and copies ran while one was open for 2% of the time, Pallas kernels for 0%

profile of v1, /device:TPU:1, one launch (start us, length us, event | category | flops | bytes accessed | tf_op | source)
XLA Modules:
  0.0 138.8 jit_solution(11458649838095334979)
XLA Ops:
  1.5 1.3 constant_dynamic-slice_fusion
  2.8 1.3 fusion.103
  11.8 14.7 %collective-permute-start = (bf16[64,1024]{1,0:T(8,128)(2,1)S(1)}, bf16[64,1024]{1,0:T(8,128)(2,1)S(1)}, u32[]{:S(2)}, u32[]{:S(2)}) collective-permute-start(bf16[64,1024]{1,0:T(8,128)(2,1)S(1)} %slice.172), channel_id=1, source_target_pairs={{0,504},{8,0},{16,8},{24,16},{32,24},{40,32},{48,40},{56,48},{64,5... | collective-permute-start | bytes 393224 | tf_op jit(solution)/shard_map/ppermute | solution.py:24
  26.5 2.1 %collective-permute-done = bf16[64,1024]{1,0:T(8,128)(2,1)S(1)} collective-permute-done((bf16[64,1024]{1,0:T(8,128)(2,1)S(1)}, bf16[64,1024]{1,0:T(8,128)(2,1)S(1)}, u32[]{:S(2)}, u32[]{:S(2)}) %collective-permute-start) | collective-permute-done | bytes 131104 | tf_op jit(solution)/shard_map/ppermute | solution.py:24
  28.7 1.1 broadcast_in_dim.19
  29.7 3.7 %all-to-all-start = ((bf16[16,64,512]{2,1,0:T(8,128)(2,1)}), bf16[16,64,512]{2,1,0:T(8,128)(2,1)S(1)}, u32[]{:S(2)}, u32[]{:S(2)}) async-start(bf16[16,64,512]{2,1,0:T(8,128)(2,1)} %broadcast_in_dim.19), calls=%async_computation | async-start | bytes 2097152 | tf_op jit(solution)/shard_map/all_to_all | solution.py:28
  33.4 7.2 %collective-permute-start.3 = (bf16[64,512]{1,0:T(8,128)(2,1)S(1)}, bf16[64,512]{1,0:T(8,128)(2,1)S(1)}, u32[]{:S(2)}, u32[]{:S(2)}) collective-permute-start(bf16[64,512]{1,0:T(8,128)(2,1)S(1)} %get-tuple-element.15), channel_id=1, source_target_pairs={{0,384},{128,0},{256,128},{384,256},{1,385},{129,1},{257,129},{385... | collective-permute-start | bytes 196616 | tf_op jit(solution)/shard_map/ppermute | solution.py:24
  40.7 1.9 %collective-permute-start.2 = (bf16[64,512]{1,0:T(8,128)(2,1)S(1)}, bf16[64,512]{1,0:T(8,128)(2,1)S(1)}, u32[]{:S(2)}, u32[]{:S(2)}) collective-permute-start(bf16[64,512]{1,0:T(8,128)(2,1)S(1)} %get-tuple-element.15), channel_id=1, source_target_pairs={{0,256},{128,384},{256,0},{384,128},{1,257},{129,385},{257,1},{385... | collective-permute-start | bytes 196616 | tf_op jit(solution)/shard_map/ppermute | solution.py:24
  42.6 4.0 %collective-permute-start.1 = (bf16[64,512]{1,0:T(8,128)(2,1)S(1)}, bf16[64,512]{1,0:T(8,128)(2,1)S(1)}, u32[]{:S(2)}, u32[]{:S(2)}) collective-permute-start(bf16[64,512]{1,0:T(8,128)(2,1)S(1)} %get-tuple-element.15), channel_id=1, source_target_pairs={{0,128},{128,256},{256,384},{384,0},{1,129},{129,257},{257,385},{3... | collective-permute-start | bytes 196616 | tf_op jit(solution)/shard_map/ppermute | solution.py:24
  46.7 5.1 %collective-permute-done.2 = bf16[64,512]{1,0:T(8,128)(2,1)S(1)} collective-permute-done((bf16[64,512]{1,0:T(8,128)(2,1)S(1)}, bf16[64,512]{1,0:T(8,128)(2,1)S(1)}, u32[]{:S(2)}, u32[]{:S(2)}) %collective-permute-start.2) | collective-permute-done | bytes 65568 | tf_op jit(solution)/shard_map/ppermute | solution.py:24
  51.7 2.3 %collective-permute-done.1 = bf16[64,512]{1,0:T(8,128)(2,1)S(1)} collective-permute-done((bf16[64,512]{1,0:T(8,128)(2,1)S(1)}, bf16[64,512]{1,0:T(8,128)(2,1)S(1)}, u32[]{:S(2)}, u32[]{:S(2)}) %collective-permute-start.1) | collective-permute-done | bytes 65568 | tf_op jit(solution)/shard_map/ppermute | solution.py:24
  56.7 2.2 %collective-permute-start.6 = (f32[8,256]{1,0:T(8,128)S(1)}, f32[8,256]{1,0:T(8,128)S(1)}, u32[]{:S(2)}, u32[]{:S(2)}) collective-permute-start(f32[8,256]{1,0:T(8,128)S(1)} %stack.44), channel_id=1, source_target_pairs={{0,384},{128,0},{256,128},{384,256},{1,385},{129,1},{257,129},{385... | collective-permute-start | bytes 24584 | tf_op jit(solution)/shard_map/ppermute | solution.py:24
  58.9 5.0 %collective-permute-start.5 = (f32[8,256]{1,0:T(8,128)S(1)}, f32[8,256]{1,0:T(8,128)S(1)}, u32[]{:S(2)}, u32[]{:S(2)}) collective-permute-start(f32[8,256]{1,0:T(8,128)S(1)} %stack.44), channel_id=1, source_target_pairs={{0,256},{128,384},{256,0},{384,128},{1,257},{129,385},{257,1},{385... | collective-permute-start | bytes 24584 | tf_op jit(solution)/shard_map/ppermute | solution.py:24
  64.0 2.5 %collective-permute-start.4 = (f32[8,256]{1,0:T(8,128)S(1)}, f32[8,256]{1,0:T(8,128)S(1)}, u32[]{:S(2)}, u32[]{:S(2)}) collective-permute-start(f32[8,256]{1,0:T(8,128)S(1)} %stack.44), channel_id=1, source_target_pairs={{0,128},{128,256},{256,384},{384,0},{1,129},{129,257},{257,385},{3... | collective-permute-start | bytes 24584 | tf_op jit(solution)/shard_map/ppermute | solution.py:24
  67.3 3.2 %collective-permute-done.4 = f32[8,256]{1,0:T(8,128)S(1)} collective-permute-done((f32[8,256]{1,0:T(8,128)S(1)}, f32[8,256]{1,0:T(8,128)S(1)}, u32[]{:S(2)}, u32[]{:S(2)}) %collective-permute-start.4) | collective-permute-done | bytes 8224 | tf_op jit(solution)/shard_map/ppermute | solution.py:24
  70.8 1.7 %convolution_convert_fusion.1 = bf16[1024,128]{1,0:T(8,128)(2,1)S(1)} fusion(f32[256]{0:T(256)S(1)} %get-tuple-element.22, bf16[256,512]{1,0:T(8,128)(2,1)S(1)} %pad_maximum_fusion.3, f32[256,1024]{1,0:T(8,128)} %copy-done.6, f32[256]{0:T(256)S(1)} %get-tuple-element.31, s32[1024]{0:T(1024)S(1)} %add_select_fusion, s32[256]{0:T(256)S(1)} %and_select_fusion), kind=kOutput, calls=%fused_computation.16 | convolution fusion | flops 68550656 | bytes 1383424 | tf_op jit(solution)/shard_map/dot_general | solution.py:20
  72.6 1.1 fusion.2
  74.6 1.6 %fusion.3 = bf16[256,1024]{1,0:T(8,128)(2,1)S(1)} fusion(f32[256]{0:T(256)S(1)} %get-tuple-element.23, f32[256]{0:T(256)S(1)} %get-tuple-element.24, bf16[1024,512]{1,0:T(8,128)(2,1)S(1)} %bitcast.101, bf16[256,512]{1,0:T(8,128)(2,1)S(1)} %pad_maximum_fusion.3, f32[256,1024]{1,0:T(8,128)} %copy-done.5, f32[256]{0:T(256)S(1)} %get-tuple-element.29, ...), kind=kOutput, calls=%fused_computation.11 | convolution fusion | flops 68943872 | bytes 1908736 | tf_op jit(solution)/shard_map/dot_general | solution.py:20
  76.7 1.1 pad_maximum_fusion
  77.8 10.1 %all-to-all-start.1 = ((bf16[16,64,512]{2,1,0:T(8,128)(2,1)}), bf16[16,64,512]{2,1,0:T(8,128)(2,1)S(1)}, u32[]{:S(2)}, u32[]{:S(2)}) async-start(bf16[16,64,512]{2,1,0:T(8,128)(2,1)} %pad_maximum_fusion), calls=%async_computation.1 | async-start | bytes 2097152 | tf_op jit(solution)/shard_map/all_to_all | solution.py:28
  89.4 2.1 %collective-permute-start.7 = (bf16[64,512]{0,1:T(8,128)(2,1)S(1)}, bf16[64,512]{0,1:T(8,128)(2,1)S(1)}, u32[]{:S(2)}, u32[]{:S(2)}) collective-permute-start(bf16[64,512]{0,1:T(8,128)(2,1)S(1)} %get-tuple-element.12), channel_id=1, source_target_pairs={{0,384},{128,0},{256,128},{384,256},{1,385},{129,1},{257,129},{385... | collective-permute-start | bytes 196616 | tf_op jit(solution)/shard_map/ppermute | solution.py:24
  91.5 4.3 %collective-permute-start.9 = (bf16[64,512]{0,1:T(8,128)(2,1)S(1)}, bf16[64,512]{0,1:T(8,128)(2,1)S(1)}, u32[]{:S(2)}, u32[]{:S(2)}) collective-permute-start(bf16[64,512]{0,1:T(8,128)(2,1)S(1)} %get-tuple-element.13), channel_id=1, source_target_pairs={{0,128},{128,256},{256,384},{384,0},{1,129},{129,257},{257,385},{3... | collective-permute-start | bytes 196616 | tf_op jit(solution)/shard_map/ppermute | solution.py:24
  95.7 2.0 %collective-permute-start.8 = (bf16[64,512]{0,1:T(8,128)(2,1)S(1)}, bf16[64,512]{0,1:T(8,128)(2,1)S(1)}, u32[]{:S(2)}, u32[]{:S(2)}) collective-permute-start(bf16[64,512]{0,1:T(8,128)(2,1)S(1)} %get-tuple-element.14), channel_id=1, source_target_pairs={{0,256},{128,384},{256,0},{384,128},{1,257},{129,385},{257,1},{385... | collective-permute-start | bytes 196616 | tf_op jit(solution)/shard_map/ppermute | solution.py:24
  97.9 7.2 %collective-permute-done.9 = bf16[64,512]{0,1:T(8,128)(2,1)S(1)} collective-permute-done((bf16[64,512]{0,1:T(8,128)(2,1)S(1)}, bf16[64,512]{0,1:T(8,128)(2,1)S(1)}, u32[]{:S(2)}, u32[]{:S(2)}) %collective-permute-start.9) | collective-permute-done | bytes 65568 | tf_op jit(solution)/shard_map/ppermute | solution.py:24
  105.1 1.7 %collective-permute-done.8 = bf16[64,512]{0,1:T(8,128)(2,1)S(1)} collective-permute-done((bf16[64,512]{0,1:T(8,128)(2,1)S(1)}, bf16[64,512]{0,1:T(8,128)(2,1)S(1)}, u32[]{:S(2)}, u32[]{:S(2)}) %collective-permute-start.8) | collective-permute-done | bytes 65568 | tf_op jit(solution)/shard_map/ppermute | solution.py:24
  108.5 12.0 %all-to-all-start.2 = ((bf16[8,64,128]{2,1,0:T(8,128)(2,1)}), bf16[8,64,128]{2,1,0:T(8,128)(2,1)S(1)}, u32[]{:S(2)}, u32[]{:S(2)}) async-start(bf16[8,64,128]{2,1,0:T(8,128)(2,1)} %bitcast.94), calls=%async_computation.2 | async-start | bytes 262144 | tf_op jit(solution)/shard_map/all_to_all | solution.py:28
  120.5 3.7 %collective-permute-start.10 = (bf16[64,256]{0,1:T(8,128)(2,1)S(1)}, bf16[64,256]{0,1:T(8,128)(2,1)S(1)}, u32[]{:S(2)}, u32[]{:S(2)}) collective-permute-start(bf16[64,256]{0,1:T(8,128)(2,1)S(1)} %slice.195), channel_id=1, source_target_pairs={{0,8},{8,16},{16,24},{24,32},{32,40},{40,48},{48,56},{56,64},{64,7... | collective-permute-start | bytes 98312 | tf_op jit(solution)/shard_map/ppermute | solution.py:24
  124.3 4.9 %all-to-all-done.2 = bf16[8,64,128]{2,1,0:T(8,128)(2,1)S(1)} async-done(((bf16[8,64,128]{2,1,0:T(8,128)(2,1)}), bf16[8,64,128]{2,1,0:T(8,128)(2,1)S(1)}, u32[]{:S(2)}, u32[]{:S(2)}) %all-to-all-start.2) | async-done | bytes 131104 | tf_op jit(solution)/shard_map/all_to_all | solution.py:28
  129.2 3.0 %collective-permute-start.11 = (bf16[64,128]{1,0:T(8,128)(2,1)S(1)}, bf16[64,128]{1,0:T(8,128)(2,1)S(1)}, u32[]{:S(2)}, u32[]{:S(2)}) collective-permute-start(bf16[64,128]{1,0:T(8,128)(2,1)S(1)} %reduce_sum.124), channel_id=1, source_target_pairs={{0,8},{8,16},{16,24},{24,32},{32,40},{40,48},{48,56},{56,64},{64,7... | collective-permute-start | bytes 49160 | tf_op jit(solution)/shard_map/ppermute | solution.py:24
  132.3 0.8 convolution_convert_fusion.6
  133.1 4.8 %collective-permute-done.11 = bf16[64,128]{1,0:T(8,128)(2,1)S(1)} collective-permute-done((bf16[64,128]{1,0:T(8,128)(2,1)S(1)}, bf16[64,128]{1,0:T(8,128)(2,1)S(1)}, u32[]{:S(2)}, u32[]{:S(2)}) %collective-permute-start.11) | collective-permute-done | bytes 16416 | tf_op jit(solution)/shard_map/ppermute | solution.py:24
  137.9 0.9 fusion.9
  (108 shorter events, 12.4 us)
Async XLA Ops:
  0.6 5.5 %copy-start = (bf16[256,1024]{1,0:T(8,128)(2,1)S(1)}, bf16[256,1024]{1,0:T(8,128)(2,1)}, u32[]{:S(2)}) copy-start(bf16[256,1024]{1,0:T(8,128)(2,1)} %param.6) | copy-start | bytes 1572868
  0.6 5.7 %copy-start.3 = (bf16[3,1024,256]{2,1,0:T(8,128)(2,1)S(1)}, bf16[3,1024,256]{2,1,0:T(8,128)(2,1)}, u32[]{:S(2)}) copy-start(bf16[3,1024,256]{2,1,0:T(8,128)(2,1)} %param.10) | copy-start | bytes 4718596
  5.4 1.4 %copy-start.15 = (s32[256]{0:T(256)}, s32[256]{0:T(256)S(1)}, u32[]{:S(2)}) copy-start(s32[256]{0:T(256)S(1)} %broadcast_add_fusion) | copy-start | bytes 3076
  6.3 5.2 %copy-start.10 = (bf16[64,256]{1,0:T(8,128)(2,1)S(1)}, bf16[64,256]{1,0:T(8,128)(2,1)}, u32[]{:S(2)}) copy-start(bf16[64,256]{1,0:T(8,128)(2,1)} %param.11) | copy-start | bytes 98308
  11.8 16.9 %collective-permute-start = (bf16[64,1024]{1,0:T(8,128)(2,1)S(1)}, bf16[64,1024]{1,0:T(8,128)(2,1)S(1)}, u32[]{:S(2)}, u32[]{:S(2)}) collective-permute-start(bf16[64,1024]{1,0:T(8,128)(2,1)S(1)} %slice.172), channel_id=1, source_target_pairs={{0,504},{8,0},{16,8},{24,16},{32,24},{40,32},{48,40},{56,48},{64,5... | collective-permute-start | bytes 393224 | tf_op jit(solution)/shard_map/ppermute | solution.py:24
  29.7 24.3 %all-to-all-start = ((bf16[16,64,512]{2,1,0:T(8,128)(2,1)}), bf16[16,64,512]{2,1,0:T(8,128)(2,1)S(1)}, u32[]{:S(2)}, u32[]{:S(2)}) async-start(bf16[16,64,512]{2,1,0:T(8,128)(2,1)} %broadcast_in_dim.19), calls=%async_computation | async-start | bytes 2097152 | tf_op jit(solution)/shard_map/all_to_all | solution.py:28
  33.4 13.2 %collective-permute-start.3 = (bf16[64,512]{1,0:T(8,128)(2,1)S(1)}, bf16[64,512]{1,0:T(8,128)(2,1)S(1)}, u32[]{:S(2)}, u32[]{:S(2)}) collective-permute-start(bf16[64,512]{1,0:T(8,128)(2,1)S(1)} %get-tuple-element.15), channel_id=1, source_target_pairs={{0,384},{128,0},{256,128},{384,256},{1,385},{129,1},{257,129},{385... | collective-permute-start | bytes 196616 | tf_op jit(solution)/shard_map/ppermute | solution.py:24
  40.7 11.1 %collective-permute-start.2 = (bf16[64,512]{1,0:T(8,128)(2,1)S(1)}, bf16[64,512]{1,0:T(8,128)(2,1)S(1)}, u32[]{:S(2)}, u32[]{:S(2)}) collective-permute-start(bf16[64,512]{1,0:T(8,128)(2,1)S(1)} %get-tuple-element.15), channel_id=1, source_target_pairs={{0,256},{128,384},{256,0},{384,128},{1,257},{129,385},{257,1},{385... | collective-permute-start | bytes 196616 | tf_op jit(solution)/shard_map/ppermute | solution.py:24
  42.6 11.4 %collective-permute-start.1 = (bf16[64,512]{1,0:T(8,128)(2,1)S(1)}, bf16[64,512]{1,0:T(8,128)(2,1)S(1)}, u32[]{:S(2)}, u32[]{:S(2)}) collective-permute-start(bf16[64,512]{1,0:T(8,128)(2,1)S(1)} %get-tuple-element.15), channel_id=1, source_target_pairs={{0,128},{128,256},{256,384},{384,0},{1,129},{129,257},{257,385},{3... | collective-permute-start | bytes 196616 | tf_op jit(solution)/shard_map/ppermute | solution.py:24
  46.6 24.1 %copy-start.11 = (s32[256]{0:T(256)}, s32[256]{0:T(256)S(1)}, u32[]{:S(2)}) copy-start(s32[256]{0:T(256)S(1)} %and_select_fusion) | copy-start | bytes 3076
  54.4 19.7 %copy-start.5 = (f32[256,1024]{1,0:T(8,128)}, f32[256,1024]{1,0:T(8,128)S(1)}, u32[]{:S(2)}) copy-start(f32[256,1024]{1,0:T(8,128)S(1)} %get-tuple-element.30) | copy-start | bytes 3145732
  56.3 16.2 %copy-start.8 = (f32[256,128]{0,1:T(8,128)}, f32[256,128]{0,1:T(8,128)S(1)}, u32[]{:S(2)}) copy-start(f32[256,128]{0,1:T(8,128)S(1)} %fusion.21) | copy-start | bytes 393220
  56.7 15.9 %copy-start.7 = (f32[256,1024]{1,0:T(8,128)S(1)}, f32[256,1024]{1,0:T(8,128)}, u32[]{:S(2)}) copy-start(f32[256,1024]{1,0:T(8,128)} %copy-done.6) | copy-start | bytes 3145732
  56.7 9.8 %collective-permute-start.6 = (f32[8,256]{1,0:T(8,128)S(1)}, f32[8,256]{1,0:T(8,128)S(1)}, u32[]{:S(2)}, u32[]{:S(2)}) collective-permute-start(f32[8,256]{1,0:T(8,128)S(1)} %stack.44), channel_id=1, source_target_pairs={{0,384},{128,0},{256,128},{384,256},{1,385},{129,1},{257,129},{385... | collective-permute-start | bytes 24584 | tf_op jit(solution)/shard_map/ppermute | solution.py:24
  58.9 8.3 %collective-permute-start.5 = (f32[8,256]{1,0:T(8,128)S(1)}, f32[8,256]{1,0:T(8,128)S(1)}, u32[]{:S(2)}, u32[]{:S(2)}) collective-permute-start(f32[8,256]{1,0:T(8,128)S(1)} %stack.44), channel_id=1, source_target_pairs={{0,256},{128,384},{256,0},{384,128},{1,257},{129,385},{257,1},{385... | collective-permute-start | bytes 24584 | tf_op jit(solution)/shard_map/ppermute | solution.py:24
  64.0 6.5 %collective-permute-start.4 = (f32[8,256]{1,0:T(8,128)S(1)}, f32[8,256]{1,0:T(8,128)S(1)}, u32[]{:S(2)}, u32[]{:S(2)}) collective-permute-start(f32[8,256]{1,0:T(8,128)S(1)} %stack.44), channel_id=1, source_target_pairs={{0,128},{128,256},{256,384},{384,0},{1,129},{129,257},{257,385},{3... | collective-permute-start | bytes 24584 | tf_op jit(solution)/shard_map/ppermute | solution.py:24
  70.8 3.0 %copy-start.13 = (f32[256]{0:T(256)}, f32[256]{0:T(256)S(1)}, u32[]{:S(2)}) copy-start(f32[256]{0:T(256)S(1)} %get-tuple-element.22) | copy-start | bytes 3076
  72.6 1.6 %copy-start.12 = (s32[256]{0:T(256)S(1)}, s32[256]{0:T(256)}, u32[]{:S(2)}) copy-start(s32[256]{0:T(256)} %copy-done.11) | copy-start | bytes 3076
  76.3 1.5 %copy-start.1 = (bf16[256,1024]{1,0:T(8,128)(2,1)}, bf16[256,1024]{1,0:T(8,128)(2,1)S(1)}, u32[]{:S(2)}) copy-start(bf16[256,1024]{1,0:T(8,128)(2,1)S(1)} %fusion.3) | copy-start | bytes 1572868
  77.8 10.1 %copy-start.9 = (f32[256,128]{0,1:T(8,128)S(1)}, f32[256,128]{0,1:T(8,128)}, u32[]{:S(2)}) copy-start(f32[256,128]{0,1:T(8,128)} %copy-done.8) | copy-start | bytes 393220
  77.8 10.1 %copy-start.14 = (f32[256]{0:T(256)S(1)}, f32[256]{0:T(256)}, u32[]{:S(2)}) copy-start(f32[256]{0:T(256)} %copy-done.13) | copy-start | bytes 3076
  77.8 29.0 %all-to-all-start.1 = ((bf16[16,64,512]{2,1,0:T(8,128)(2,1)}), bf16[16,64,512]{2,1,0:T(8,128)(2,1)S(1)}, u32[]{:S(2)}, u32[]{:S(2)}) async-start(bf16[16,64,512]{2,1,0:T(8,128)(2,1)} %pad_maximum_fusion), calls=%async_computation.1 | async-start | bytes 2097152 | tf_op jit(solution)/shard_map/all_to_all | solution.py:28
  87.9 1.0 copy-start.2
  89.4 17.5 %copy-start.4 = (bf16[3,1024,256]{2,1,0:T(8,128)(2,1)S(1)}, bf16[3,1024,256]{2,1,0:T(8,128)(2,1)}, u32[]{:S(2)}) copy-start(bf16[3,1024,256]{2,1,0:T(8,128)(2,1)} %param.10) | copy-start | bytes 4718596
  89.4 8.4 %collective-permute-start.7 = (bf16[64,512]{0,1:T(8,128)(2,1)S(1)}, bf16[64,512]{0,1:T(8,128)(2,1)S(1)}, u32[]{:S(2)}, u32[]{:S(2)}) collective-permute-start(bf16[64,512]{0,1:T(8,128)(2,1)S(1)} %get-tuple-element.12), channel_id=1, source_target_pairs={{0,384},{128,0},{256,128},{384,256},{1,385},{129,1},{257,129},{385... | collective-permute-start | bytes 196616 | tf_op jit(solution)/shard_map/ppermute | solution.py:24
  91.5 13.6 %collective-permute-start.9 = (bf16[64,512]{0,1:T(8,128)(2,1)S(1)}, bf16[64,512]{0,1:T(8,128)(2,1)S(1)}, u32[]{:S(2)}, u32[]{:S(2)}) collective-permute-start(bf16[64,512]{0,1:T(8,128)(2,1)S(1)} %get-tuple-element.13), channel_id=1, source_target_pairs={{0,128},{128,256},{256,384},{384,0},{1,129},{129,257},{257,385},{3... | collective-permute-start | bytes 196616 | tf_op jit(solution)/shard_map/ppermute | solution.py:24
  95.7 11.0 %collective-permute-start.8 = (bf16[64,512]{0,1:T(8,128)(2,1)S(1)}, bf16[64,512]{0,1:T(8,128)(2,1)S(1)}, u32[]{:S(2)}, u32[]{:S(2)}) collective-permute-start(bf16[64,512]{0,1:T(8,128)(2,1)S(1)} %get-tuple-element.14), channel_id=1, source_target_pairs={{0,256},{128,384},{256,0},{384,128},{1,257},{129,385},{257,1},{385... | collective-permute-start | bytes 196616 | tf_op jit(solution)/shard_map/ppermute | solution.py:24
  106.9 17.2 %copy-start.16 = (s32[256]{0:T(256)S(1)}, s32[256]{0:T(256)}, u32[]{:S(2)}) copy-start(s32[256]{0:T(256)} %copy-done.15) | copy-start | bytes 3076
  107.0 17.2 %copy-start.18 = (f32[128]{0:T(128)S(1)}, f32[128]{0:T(128)}, u32[]{:S(2)}) copy-start(f32[128]{0:T(128)} %copy-done.17) | copy-start | bytes 1540
  108.5 20.7 %all-to-all-start.2 = ((bf16[8,64,128]{2,1,0:T(8,128)(2,1)}), bf16[8,64,128]{2,1,0:T(8,128)(2,1)S(1)}, u32[]{:S(2)}, u32[]{:S(2)}) async-start(bf16[8,64,128]{2,1,0:T(8,128)(2,1)} %bitcast.94), calls=%async_computation.2 | async-start | bytes 262144 | tf_op jit(solution)/shard_map/all_to_all | solution.py:28
  120.5 11.8 %collective-permute-start.10 = (bf16[64,256]{0,1:T(8,128)(2,1)S(1)}, bf16[64,256]{0,1:T(8,128)(2,1)S(1)}, u32[]{:S(2)}, u32[]{:S(2)}) collective-permute-start(bf16[64,256]{0,1:T(8,128)(2,1)S(1)} %slice.195), channel_id=1, source_target_pairs={{0,8},{8,16},{16,24},{24,32},{32,40},{40,48},{48,56},{56,64},{64,7... | collective-permute-start | bytes 98312 | tf_op jit(solution)/shard_map/ppermute | solution.py:24
  129.2 8.7 %collective-permute-start.11 = (bf16[64,128]{1,0:T(8,128)(2,1)S(1)}, bf16[64,128]{1,0:T(8,128)(2,1)S(1)}, u32[]{:S(2)}, u32[]{:S(2)}) collective-permute-start(bf16[64,128]{1,0:T(8,128)(2,1)S(1)} %reduce_sum.124), channel_id=1, source_target_pairs={{0,8},{8,16},{16,24},{24,32},{32,40},{40,48},{48,56},{56,64},{64,7... | collective-permute-start | bytes 49160 | tf_op jit(solution)/shard_map/ppermute | solution.py:24
  (2 other events, 1.6 us)

commit v2 on v1

v2 whole, which is shorter than its diff:
```python
import jax
import jax.numpy as jnp
from jax import lax
from jax.experimental import pallas as pl
from jax.experimental.pallas import tpu as pltpu
from jax.sharding import Mesh, PartitionSpec as P

HD = 128
SIZES = (4, 2, 2, 4, 4, 2)
NAMES = ("zh", "zl", "yl", "x", "yh", "core")
CTX = ("zh", "zl", "yl", "x")
ASK = ("zl", "x")
KEYED = ("zh", "yl")
TP = ("yh", "core")
N_CTX = 64
GROUP = 8
ROWS = 64
HEADS = 2
FEATS = HEADS * HD
TOTAL = N_CTX * ROWS
WINDOW = 2 * ROWS
HALF = ROWS // 2
TILE = GROUP * ROWS
SCALE = HD ** (-0.5)
LOG2E = 1.4426950408889634
NEG = -1e30
FLOOR = -1e29
BF = jnp.bfloat16
F32 = jnp.float32
I32 = jnp.int32


def dot(a, b, dims):
    return lax.dot_general(a, b, (dims, ((), ())), preferred_element_type=F32)


def shift(x, axis, n, by):
    return lax.ppermute(x, axis, [(i, (i + by) % n) for i in range(n)])


def swap(x, axis):
    return lax.all_to_all(x, axis, split_axis=0, concat_axis=0, tiled=True)


def iota(shape, dim):
    return lax.broadcasted_iota(I32, shape, dim)


def call(kernel, ins, outs, flops, scalars=0):
    smem = pl.BlockSpec(memory_space=pltpu.SMEM)
    vmem = pl.BlockSpec(memory_space=pltpu.VMEM)
    size = sum(x.size * x.dtype.itemsize for x in list(ins) + list(outs))
    return pl.pallas_call(
        kernel,
        out_shape=tuple(outs),
        in_specs=[smem] * scalars + [vmem] * (len(ins) - scalars),
        out_specs=tuple([vmem] * len(outs)),
        cost_estimate=pl.CostEstimate(flops=flops, bytes_accessed=size, transcendentals=0),
        compiler_params=pltpu.CompilerParams(vmem_limit_bytes=40 * 1024 * 1024),
    )(*ins)


def shaped(shape, dtype):
    return jax.ShapeDtypeStruct(shape, dtype)


def slot_order(c, first_ref, moved_ref, shape, dim):
    before, after = jnp.maximum(c - 1, 0), jnp.minimum(c + 1, N_CTX - 1)
    first = first_ref[c]
    low = moved_ref[0, c]
    prev_high = jnp.where(c > 0, moved_ref[1, before], 0)
    next_low = jnp.where(c < N_CTX - 1, moved_ref[0, after], 0)
    next_first = jnp.where(c < N_CTX - 1, first_ref[after], TOTAL)
    rank = iota(shape, dim)
    order = jnp.where(
        rank < prev_high,
        first - prev_high + rank,
        jnp.where(
            rank >= ROWS - next_low,
            next_first + rank - (ROWS - next_low),
            first + low + rank - prev_high,
        ),
    )
    return order - (ROWS * c - HALF)


def pool_kernel(c_ref, first_ref, moved_ref, bytes_ref, place_ref, grad_ref, w_ref, sent_ref, own_ref):
    c = c_ref[0]
    offset = first_ref[c] - (ROWS * c - HALF)
    member = iota((WINDOW, bytes_ref.shape[0]), 0) == place_ref[...] + offset
    lengths = jnp.sum(member.astype(F32), axis=1, keepdims=True)
    pooled = dot(member.astype(F32).astype(BF), bytes_ref[...], ((1,), (0,)))
    pooled = (pooled / jnp.maximum(lengths, 1.0)).astype(BF)
    order = slot_order(c, first_ref, moved_ref, (WINDOW, ROWS), 1)
    slotted = (iota((WINDOW, ROWS), 0) == order).astype(F32).astype(BF)
    grads = dot(slotted, grad_ref[...], ((1,), (0,))).astype(BF)
    for at, value in (
        (0, dot(pooled, w_ref[0], ((1,), (0,))).astype(BF)),
        (1, grads),
        (2, dot(pooled, w_ref[1], ((1,), (0,))).astype(BF)),
        (3, dot(pooled, w_ref[2], ((1,), (0,))).astype(BF)),
    ):
        sent_ref[:, at * FEATS : (at + 1) * FEATS] = value[:ROWS]
        own_ref[:, at * FEATS : (at + 1) * FEATS] = value[ROWS:]


def spread_kernel(own_ref, got_ref, ask_ref, held_ref):
    both = own_ref[...] + got_ref[...]
    for i in range(GROUP):
        ask_ref[i] = both[:, : 2 * FEATS]
        held_ref[i] = both[:, 2 * FEATS :]


def tile_ids(at_ref):
    row = iota((1, TILE), 1)
    block, inner = row >> 6, row & 63
    query = at_ref[0] + ROWS * (8 * (block >> 2) + (block & 3)) + inner
    col = iota((TILE, 1), 0)
    block, inner = col >> 6, col & 63
    key = at_ref[1] + ROWS * (16 * (block >> 1) + 4 * (block & 1)) + inner
    return query & (TOTAL - 1), key & (TOTAL - 1)


def columns(ref, at):
    return ref[:, :, at * HD : (at + 1) * HD].reshape(TILE, HD)


def forward_kernel(at_ref, ask_ref, held_ref, stats_ref):
    query_id, key_id = tile_ids(at_ref)
    allowed = query_id >= key_id
    rows = []
    for h in range(HEADS):
        q, g = columns(ask_ref, h), columns(ask_ref, HEADS + h)
        k, v = columns(held_ref, h), columns(held_ref, HEADS + h)
        score = jnp.where(allowed, dot(k, q, ((1,), (1,))) * (SCALE * LOG2E), NEG)
        top = jnp.maximum(jnp.max(score, axis=0, keepdims=True), FLOOR)
        weight = jnp.exp2(score - top)
        dprob = dot(v, g, ((1,), (1,)))
        rows += [
            top,
            jnp.sum(weight, axis=0, keepdims=True),
            jnp.sum(weight * dprob, axis=0, keepdims=True),
        ]
    rows = jnp.concatenate(rows + [rows[0], rows[0]], axis=0)
    for i in range(GROUP):
        stats_ref[i] = rows


def backward_kernel(at_ref, ask_ref, held_ref, stats_ref, key_ref, query_ref):
    query_id, key_id = tile_ids(at_ref)
    allowed = query_id >= key_id
    stats = stats_ref[...]
    for h in range(HEADS):
        tops, sums, dots = (stats[:, 3 * h + i, :] for i in range(3))
        peak = jnp.max(tops, axis=0, keepdims=True)
        each = jnp.exp2(tops - peak)
        norm = jnp.sum(each * sums, axis=0, keepdims=True)
        delta = jnp.sum(each * dots, axis=0, keepdims=True) / norm
        lse = peak + jnp.log(norm) * LOG2E
        q, g = columns(ask_ref, h), columns(ask_ref, HEADS + h)
        k, v = columns(held_ref, h), columns(held_ref, HEADS + h)
        score = jnp.where(allowed, dot(k, q, ((1,), (1,))) * (SCALE * LOG2E), NEG)
        prob = jnp.exp2(score - lse)
        dprob = dot(v, g, ((1,), (1,)))
        dscore = (prob * (dprob - delta)).astype(BF)
        prob = prob.astype(BF)
        d_key = (dot(dscore, q, ((1,), (0,))) * SCALE).astype(BF)
        d_value = dot(prob, g, ((1,), (0,))).astype(BF)
        d_query = (dot(dscore, k, ((0,), (0,))) * SCALE).astype(BF)
        out = dot(prob, v, ((0,), (0,))).astype(BF)
        for ref, at, value in (
            (key_ref, h, d_key),
            (key_ref, HEADS + h, d_value),
            (query_ref, h, d_query),
            (query_ref, HEADS + h, out),
        ):
            ref[:, :, at * HD : (at + 1) * HD] = value.reshape(GROUP, ROWS, HD)


def key_sum_kernel(terms_ref, w_ref, part_ref):
    total = jnp.sum(terms_ref[...].astype(F32), axis=0).astype(BF)
    part_ref[...] = dot(total[:, :FEATS], w_ref[1], ((1,), (1,))) + dot(
        total[:, FEATS:], w_ref[2], ((1,), (1,))
    )


def query_sum_kernel(terms_ref, part_ref, w_ref, piece_ref, out_ref):
    total = jnp.sum(terms_ref[...].astype(F32), axis=0).astype(BF)
    out_ref[...] = total[:, FEATS:]
    part = (part_ref[...] + dot(total[:, :FEATS], w_ref[0], ((1,), (1,)))).astype(BF)
    for i in range(GROUP):
        piece_ref[i] = part[:, i * HD : (i + 1) * HD]


def head_sum_kernel(pieces_ref, sum_ref):
    sum_ref[...] = jnp.sum(pieces_ref[...].astype(F32), axis=0).astype(BF)


def slot_kernel(c_ref, first_ref, moved_ref, before_ref, own_ref, out_ref):
    order = slot_order(c_ref[0], first_ref, moved_ref, (ROWS, WINDOW), 0)
    picker = (iota((ROWS, WINDOW), 1) == order).astype(F32).astype(BF)
    window = jnp.concatenate([before_ref[...], own_ref[...]], axis=0)
    out_ref[...] = dot(picker, window, ((1,), (0,))).astype(BF)


def byte_kernel(c_ref, first_ref, place_ref, before_ref, own_ref, out_ref):
    c = c_ref[0]
    offset = first_ref[c] - (ROWS * c - HALF)
    member = (iota((place_ref.shape[0], WINDOW), 1) == place_ref[...] + offset).astype(F32)
    lengths = jnp.sum(member, axis=0, keepdims=True)
    own_length = jnp.sum(member * lengths, axis=1, keepdims=True)
    window = jnp.concatenate([before_ref[...], own_ref[...]], axis=0)
    out_ref[...] = (dot(member.astype(BF), window, ((1,), (0,))) / own_length).astype(BF)


def shards(byte_states, patch_of_byte, patch_first, moved, w_qkv, d_attn):
    zh, zl, yl, x = (lax.axis_index(name) for name in CTX)
    c = lax.axis_index(CTX).astype(I32)
    c_ref = c.reshape(1)
    at = jnp.stack([ROWS * (16 * zh + 4 * yl) + HALF, ROWS * (8 * zl + x) + HALF]).astype(I32)
    n_bytes = patch_of_byte.shape[0]
    block = shaped((ROWS, 4 * FEATS), BF)
    stack = shaped((GROUP, ROWS, 2 * FEATS), BF)

    sent, own = call(
        pool_kernel,
        (c_ref, patch_first, moved, byte_states, patch_of_byte.reshape(1, n_bytes), d_attn, w_qkv),
        (block, block),
        300_000_000,
        3,
    )
    ask, held = call(spread_kernel, (own, shift(sent, CTX, N_CTX, -1)), (stack, stack), 1_000_000)
    ask = swap(ask, ASK)
    held = swap(held, KEYED)
    (stats,) = call(
        forward_kernel,
        (at, ask, held),
        (shaped((GROUP, 8, TILE), F32),),
        300_000_000,
        1,
    )
    stats = swap(stats, ASK)
    key_terms, query_terms = call(
        backward_kernel, (at, ask, held, stats), (stack, stack), 900_000_000, 1
    )
    key_terms = swap(key_terms, KEYED)
    query_terms = swap(query_terms, ASK)
    (part,) = call(
        key_sum_kernel, (key_terms, w_qkv), (shaped((ROWS, 4 * FEATS), F32),), 70_000_000
    )
    pieces, out = call(
        query_sum_kernel,
        (query_terms, part, w_qkv),
        (shaped((GROUP, ROWS, HD), BF), shaped((ROWS, FEATS), BF)),
        35_000_000,
    )
    (d_pooled,) = call(head_sum_kernel, (swap(pieces, TP),), (shaped((ROWS, HD), BF),), 100_000)
    (attn_out,) = call(
        slot_kernel,
        (c_ref, patch_first, moved, shift(out, CTX, N_CTX, 1), out),
        (shaped((ROWS, FEATS), BF),),
        5_000_000,
        3,
    )
    (byte_grad,) = call(
        byte_kernel,
        (c_ref, patch_first, patch_of_byte.reshape(n_bytes, 1), shift(d_pooled, CTX, N_CTX, 1), d_pooled),
        (shaped((n_bytes, HD), BF),),
        10_000_000,
        2,
    )
    return attn_out, byte_grad


def solution(mesh):
    fine = Mesh(mesh.devices.reshape(SIZES), NAMES)
    placed = (P(CTX, None), P(CTX), P(), P(), P(None, None, TP), P(CTX, TP))
    return jax.shard_map(
        shards,
        mesh=fine,
        in_specs=placed,
        out_specs=(P(CTX, TP), P(CTX, TP)),
        check_vma=False,
    )
```

time: 140 us -> 132 us (0.943)
  starting transfers between devices: 78.4 us -> 39.2 us
  blocking collectives: 0 us -> 38.9 us
  matrix products: 11.7 us -> 0 us
  Pallas kernels: 0 us -> 10.9 us
  between operations: 5.76 us -> 0.79 us
  waiting for transfers between devices: 31.8 us -> 35.6 us
  other arithmetic: 3.46 us -> 0.07 us
  local copies, waits for them, and re-layouts: 7.66 us -> 5.37 us
    all_to_all x0 -> x3, blocking collectives: none -> 38.9 us  [swap(): return lax.all_to_all(x, axis, split_axis=0, concat_axis=0, tiled=True)]
    ppermute x12 -> x3, starting transfers between devices: 52.7 us -> 18.6 us  [shift(): return lax.ppermute(x, axis, [(i, (i + by) % n) for i in range(n)])]
    all_to_all x3, waiting for transfers between devices: 4.88 us -> 28.2 us  [swap(): return lax.all_to_all(x, axis, split_axis=0, concat_axis=0, tiled=True)]
    ppermute x12 -> x3, waiting for transfers between devices: 27 us -> 7.38 us  [shift(): return lax.ppermute(x, axis, [(i, (i + by) % n) for i in range(n)])]
    dot_general x22 -> x0, matrix products: 11.7 us -> none  [dot(): return lax.dot_general(a, b, (dims, ((), ())), preferred_element_type=F32)]
    pallas_call x0 -> x9, Pallas kernels: none -> 10.9 us  [call(): pl.pallas_call(kernel, out_shape=tuple(outs), in_specs=[smem] * scalars +...]
    all_to_all x3, starting transfers between devices: 25.7 us -> 20.5 us  [swap(): return lax.all_to_all(x, axis, split_axis=0, concat_axis=0, tiled=True)]
    unnamed x38 -> x20, local copies, waits for them, and re-layouts: 1.26 us -> 5.24 us
  transfers between devices with their start and end apart: 15 -> 6, of which waited for: 10 -> 5; matrix products, arithmetic and copies ran while one was open for 2% -> 0% of each run, Pallas kernels for 0% -> 1%
where the time goes in v2:
time: 132 us; the launch traced here: 131 us
  starting transfers between devices  39.2 us (30%)
  blocking collectives  38.9 us (29%)
  waiting for transfers between devices  35.6 us (27%)
  Pallas kernels  10.9 us (8%)
  local copies, waits for them, and re-layouts  5.37 us (4%)
    all_to_all x3, blocking collectives, swap(): return lax.all_to_all(x, axis, split_axis=0, concat_axis=0, tiled=True)  38.9 us
    all_to_all x3, waiting for transfers between devices, swap(): return lax.all_to_all(x, axis, split_axis=0, concat_axis=0, tiled=True)  28.2 us
    all_to_all x3, starting transfers between devices, swap(): return lax.all_to_all(x, axis, split_axis=0, concat_axis=0, tiled=True)  20.5 us
    ppermute x3, starting transfers between devices, shift(): return lax.ppermute(x, axis, [(i, (i + by) % n) for i in range(n)])  18.6 us
    pallas_call x9, Pallas kernels, call(): pl.pallas_call(kernel, out_shape=tuple(outs), in_specs=[smem] * scalars +...  10.9 us
    ppermute x3, waiting for transfers between devices, shift(): return lax.ppermute(x, axis, [(i, (i + by) % n) for i in range(n)])  7.38 us
    unnamed x20, local copies, waits for them, and re-layouts  5.24 us
  transfers between devices with their start and end apart: 6, of which 5 were waited for; matrix products, arithmetic and copies ran while one was open for 0% of the time, Pallas kernels for 1%

profile of v2, /device:TPU:1, one launch (start us, length us, event | category | flops | bytes accessed | tf_op | source)
XLA Modules:
  0.0 130.9 jit_solution(12255551614452592585)
XLA Ops:
  0.6 0.0 copy-start
  0.7 1.4 %copy-done = bf16[3,1024,256]{2,1,0:T(8,128)(2,1)S(1)} copy-done((bf16[3,1024,256]{2,1,0:T(8,128)(2,1)S(1)}, bf16[3,1024,256]{2,1,0:T(8,128)(2,1)}, u32[]{:S(2)}) %copy-start) | copy-done | bytes 1572888
  2.1 1.0 copy-done.2
  3.1 0.8 copy-done.3
  3.9 0.7 copy-done.4
  4.5 0.7 copy-done.6
  5.2 0.7 copy-done.8
  5.9 1.1 shard_map.77
  7.0 14.7 %collective-permute-start = (bf16[64,1024]{1,0:T(8,128)(2,1)S(1)}, bf16[64,1024]{1,0:T(8,128)(2,1)S(1)}, u32[]{:S(2)}, u32[]{:S(2)}) collective-permute-start(bf16[64,1024]{1,0:T(8,128)(2,1)S(1)} %get-tuple-element.11), channel_id=1, source_target_pairs={{0,504},{8,0},{16,8},{24,16},{32,24},{40,32},{48,40},{56,48},{64,5... | collective-permute-start | bytes 393224 | tf_op jit(solution)/shard_map/ppermute | solution.py:38
  21.7 2.1 %collective-permute-done.got_ref = bf16[64,1024]{1,0:T(8,128)(2,1)S(1)} collective-permute-done((bf16[64,1024]{1,0:T(8,128)(2,1)S(1)}, bf16[64,1024]{1,0:T(8,128)(2,1)S(1)}, u32[]{:S(2)}, u32[]{:S(2)}) %collective-permute-start) | collective-permute-done | bytes 131104 | tf_op jit(solution)/shard_map/ppermute | solution.py:38
  23.8 0.9 shard_map.78
  24.7 10.3 %all_to_all.30.ask_ref = bf16[8,64,512]{2,1,0:T(8,128)(2,1)S(1)} all-to-all(bf16[8,64,512]{2,1,0:T(8,128)(2,1)S(1)} %get-tuple-element.12), channel_id=1, replica_groups=mesh['zh'=4,'zl'=2,'yl'=2,'x'=4,'yh'=4,'core'=2] {'zl','x'}, dimensions={0} | all-to-all | bytes 1048576 | tf_op jit(solution)/shard_map/all_to_all | solution.py:42
  35.0 7.2 %all-to-all-start.1 = ((bf16[8,64,512]{2,1,0:T(8,128)(2,1)}), bf16[8,64,512]{2,1,0:T(8,128)(2,1)S(1)}, u32[]{:S(2)}, u32[]{:S(2)}) async-start(bf16[8,64,512]{2,1,0:T(8,128)(2,1)} %get-tuple-element.13), calls=%async_computation.1 | async-start | bytes 1048576 | tf_op jit(solution)/shard_map/all_to_all | solution.py:42
  42.2 0.1 pad_add_fusion.at_ref
  42.2 14.9 %all-to-all-done.1.held_ref = bf16[8,64,512]{2,1,0:T(8,128)(2,1)S(1)} async-done(((bf16[8,64,512]{2,1,0:T(8,128)(2,1)}), bf16[8,64,512]{2,1,0:T(8,128)(2,1)S(1)}, u32[]{:S(2)}, u32[]{:S(2)}) %all-to-all-start.1) | async-done | bytes 524320 | tf_op jit(solution)/shard_map/all_to_all | solution.py:42
  57.1 1.5 %shard_map.79 = f32[8,8,512]{2,1,0:T(8,128)S(1)} custom-call(s32[2]{0:T(128)S(1)} %pad_add_fusion.at_ref, bf16[8,64,512]{2,1,0:T(8,128)(2,1)S(1)} %all_to_all.30.ask_ref, bf16[8,64,512]{2,1,0:T(8,128)(2,1)S(1)} %all-to-all-done.1.held_ref), custom_call_target="tpu_custom_call" | custom-call | flops 300000000 | bytes 1179656 | tf_op jit(solution)/shard_map/pallas_call | solution.py:53
  58.6 9.6 %all_to_all.31.stats_ref = f32[8,8,512]{2,1,0:T(8,128)S(1)} all-to-all(f32[8,8,512]{2,1,0:T(8,128)S(1)} %shard_map.79), channel_id=1, replica_groups=mesh['zh'=4,'zl'=2,'yl'=2,'x'=4,'yh'=4,'core'=2] {'zl','x'}, dimensions={0} | all-to-all | bytes 262144 | tf_op jit(solution)/shard_map/all_to_all | solution.py:42
  68.2 3.4 %shard_map.80 = (bf16[8,64,512]{2,1,0:T(8,128)(2,1)S(1)}, bf16[8,64,512]{2,1,0:T(8,128)(2,1)}) custom-call(s32[2]{0:T(128)S(1)} %pad_add_fusion.at_ref, bf16[8,64,512]{2,1,0:T(8,128)(2,1)S(1)} %all_to_all.30.ask_ref, bf16[8,64,512]{2,1,0:T(8,128)(2,1)S(1)} %all-to-all-done.1.held_ref, f32[8,8,512]{2,1,0:T(8,128)S(1)} %all_to_all.31.stats_ref), custom_call_target="tpu_custom_call" | custom-call | flops 900000000 | bytes 2228232 | tf_op jit(solution)/shard_map/pallas_call | solution.py:53
  71.6 19.1 %all_to_all.32.terms_ref = bf16[8,64,512]{2,1,0:T(8,128)(2,1)S(1)} all-to-all(bf16[8,64,512]{2,1,0:T(8,128)(2,1)S(1)} %get-tuple-element.15), channel_id=1, replica_groups=mesh['zh'=4,'zl'=2,'yl'=2,'x'=4,'yh'=4,'core'=2] {'zh','yl'}, dimensions={0} | all-to-all | bytes 1048576 | tf_op jit(solution)/shard_map/all_to_all | solution.py:42
  90.6 3.5 %all-to-all-start.3 = ((bf16[8,64,512]{2,1,0:T(8,128)(2,1)}), bf16[8,64,512]{2,1,0:T(8,128)(2,1)S(1)}, u32[]{:S(2)}, u32[]{:S(2)}) async-start(bf16[8,64,512]{2,1,0:T(8,128)(2,1)} %get-tuple-element.14), calls=%async_computation.3 | async-start | bytes 1048576 | tf_op jit(solution)/shard_map/all_to_all | solution.py:42
  94.1 0.4 shard_map.81.part_ref
  94.6 0.0 copy-start.9
  94.6 6.6 %all-to-all-done.3.terms_ref = bf16[8,64,512]{2,1,0:T(8,128)(2,1)S(1)} async-done(((bf16[8,64,512]{2,1,0:T(8,128)(2,1)}), bf16[8,64,512]{2,1,0:T(8,128)(2,1)S(1)}, u32[]{:S(2)}, u32[]{:S(2)}) %all-to-all-start.3) | async-done | bytes 524320 | tf_op jit(solution)/shard_map/all_to_all | solution.py:42
  101.2 1.0 shard_map.82
  102.2 9.8 %all-to-all-start.5 = ((bf16[8,64,128]{2,1,0:T(8,128)(2,1)}), bf16[8,64,128]{2,1,0:T(8,128)(2,1)S(1)}, u32[]{:S(2)}, u32[]{:S(2)}) async-start(bf16[8,64,128]{2,1,0:T(8,128)(2,1)} %get-tuple-element.17), calls=%async_computation.5 | async-start | bytes 262144 | tf_op jit(solution)/shard_map/all_to_all | solution.py:42
  112.0 2.0 %collective-permute-start.1 = (bf16[64,256]{1,0:T(8,128)(2,1)S(1)}, bf16[64,256]{1,0:T(8,128)(2,1)S(1)}, u32[]{:S(2)}, u32[]{:S(2)}) collective-permute-start(bf16[64,256]{1,0:T(8,128)(2,1)S(1)} %get-tuple-element.16.own_ref), channel_id=1, source_target_pairs={{0,8},{8,16},{16,24},{24,32},{32,40},{40,48},{48,56},{56,64},{64,7... | collective-permute-start | bytes 98312 | tf_op jit(solution)/shard_map/ppermute | solution.py:38
  114.0 6.8 %all-to-all-done.5.pieces_ref = bf16[8,64,128]{2,1,0:T(8,128)(2,1)S(1)} async-done(((bf16[8,64,128]{2,1,0:T(8,128)(2,1)}), bf16[8,64,128]{2,1,0:T(8,128)(2,1)S(1)}, u32[]{:S(2)}, u32[]{:S(2)}) %all-to-all-start.5) | async-done | bytes 131104 | tf_op jit(solution)/shard_map/all_to_all | solution.py:42
  120.8 2.0 %collective-permute-start.2 = (bf16[64,128]{1,0:T(8,128)(2,1)S(1)}, bf16[64,128]{1,0:T(8,128)(2,1)S(1)}, u32[]{:S(2)}, u32[]{:S(2)}) collective-permute-start(bf16[64,128]{1,0:T(8,128)(2,1)S(1)} %shard_map.84.own_ref), channel_id=1, source_target_pairs={{0,8},{8,16},{16,24},{24,32},{32,40},{40,48},{48,56},{56,64},{64,7... | collective-permute-start | bytes 49160 | tf_op jit(solution)/shard_map/ppermute | solution.py:38
  122.7 0.1 copy.8.place_ref
  122.9 1.3 shard_map.83
  124.2 5.2 %collective-permute-done.2.before_ref = bf16[64,128]{1,0:T(8,128)(2,1)S(1)} collective-permute-done((bf16[64,128]{1,0:T(8,128)(2,1)S(1)}, bf16[64,128]{1,0:T(8,128)(2,1)S(1)}, u32[]{:S(2)}, u32[]{:S(2)}) %collective-permute-start.2) | collective-permute-done | bytes 16416 | tf_op jit(solution)/shard_map/ppermute | solution.py:38
  129.5 1.4 %shard_map.85 = bf16[256,128]{1,0:T(8,128)(2,1)} custom-call(s32[1]{0:T(128)} %bitcast.c_ref, s32[64]{0:T(128)S(1)} %copy-done.5, s32[256,1]{1,0:T(8,128)S(1)} %copy.8.place_ref, bf16[64,128]{1,0:T(8,128)(2,1)S(1)} %collective-permute-done.2.before_ref, bf16[64,128]{1,0:T(8,128)(2,1)S(1)} %shard_map.84.own_ref), custom_call_target="tpu_custom_call" | custom-call | flops 10000000 | bytes 99588 | tf_op jit(solution)/shard_map/pallas_call | solution.py:53
  (14 shorter events, 0.1 us)
Async XLA Ops:
  0.6 1.4 %copy-start = (bf16[3,1024,256]{2,1,0:T(8,128)(2,1)S(1)}, bf16[3,1024,256]{2,1,0:T(8,128)(2,1)}, u32[]{:S(2)}) copy-start(bf16[3,1024,256]{2,1,0:T(8,128)(2,1)} %w_ref.5) | copy-start | bytes 4718596
  2.1 1.0 copy-start.2
  3.1 0.8 copy-start.3
  3.9 0.7 copy-start.4
  4.5 0.7 copy-start.6
  5.2 0.7 copy-start.8
  7.0 16.9 %collective-permute-start = (bf16[64,1024]{1,0:T(8,128)(2,1)S(1)}, bf16[64,1024]{1,0:T(8,128)(2,1)S(1)}, u32[]{:S(2)}, u32[]{:S(2)}) collective-permute-start(bf16[64,1024]{1,0:T(8,128)(2,1)S(1)} %get-tuple-element.11), channel_id=1, source_target_pairs={{0,504},{8,0},{16,8},{24,16},{32,24},{40,32},{48,40},{56,48},{64,5... | collective-permute-start | bytes 393224 | tf_op jit(solution)/shard_map/ppermute | solution.py:38
  35.0 22.1 %all-to-all-start.1 = ((bf16[8,64,512]{2,1,0:T(8,128)(2,1)}), bf16[8,64,512]{2,1,0:T(8,128)(2,1)S(1)}, u32[]{:S(2)}, u32[]{:S(2)}) async-start(bf16[8,64,512]{2,1,0:T(8,128)(2,1)} %get-tuple-element.13), calls=%async_computation.1 | async-start | bytes 1048576 | tf_op jit(solution)/shard_map/all_to_all | solution.py:42
  71.6 22.6 %copy-start.1 = (bf16[3,1024,256]{2,1,0:T(8,128)(2,1)S(1)}, bf16[3,1024,256]{2,1,0:T(8,128)(2,1)}, u32[]{:S(2)}) copy-start(bf16[3,1024,256]{2,1,0:T(8,128)(2,1)} %w_ref.5) | copy-start | bytes 4718596
  90.6 10.6 %all-to-all-start.3 = ((bf16[8,64,512]{2,1,0:T(8,128)(2,1)}), bf16[8,64,512]{2,1,0:T(8,128)(2,1)S(1)}, u32[]{:S(2)}, u32[]{:S(2)}) async-start(bf16[8,64,512]{2,1,0:T(8,128)(2,1)} %get-tuple-element.14), calls=%async_computation.3 | async-start | bytes 1048576 | tf_op jit(solution)/shard_map/all_to_all | solution.py:42
  94.6 28.2 %copy-start.7 = (s32[256]{0:T(256)S(1)}, s32[256]{0:T(256)}, u32[]{:S(2)}) copy-start(s32[256]{0:T(256)} %param.7) | copy-start | bytes 3076
  94.6 28.3 %copy-start.5 = (s32[64]{0:T(128)S(1)}, s32[64]{0:T(128)}, u32[]{:S(2)}) copy-start(s32[64]{0:T(128)} %first_ref.5) | copy-start | bytes 772
  94.6 28.3 %copy-start.9 = (s32[2,64]{1,0:T(2,128)S(1)}, s32[2,64]{1,0:T(2,128)}, u32[]{:S(2)}) copy-start(s32[2,64]{1,0:T(2,128)} %moved_ref.3) | copy-start | bytes 1540
  102.2 18.6 %all-to-all-start.5 = ((bf16[8,64,128]{2,1,0:T(8,128)(2,1)}), bf16[8,64,128]{2,1,0:T(8,128)(2,1)S(1)}, u32[]{:S(2)}, u32[]{:S(2)}) async-start(bf16[8,64,128]{2,1,0:T(8,128)(2,1)} %get-tuple-element.17), calls=%async_computation.5 | async-start | bytes 262144 | tf_op jit(solution)/shard_map/all_to_all | solution.py:42
  112.0 10.9 %collective-permute-start.1 = (bf16[64,256]{1,0:T(8,128)(2,1)S(1)}, bf16[64,256]{1,0:T(8,128)(2,1)S(1)}, u32[]{:S(2)}, u32[]{:S(2)}) collective-permute-start(bf16[64,256]{1,0:T(8,128)(2,1)S(1)} %get-tuple-element.16.own_ref), channel_id=1, source_target_pairs={{0,8},{8,16},{16,24},{24,32},{32,40},{40,48},{48,56},{56,64},{64,7... | collective-permute-start | bytes 98312 | tf_op jit(solution)/shard_map/ppermute | solution.py:38
  120.8 8.7 %collective-permute-start.2 = (bf16[64,128]{1,0:T(8,128)(2,1)S(1)}, bf16[64,128]{1,0:T(8,128)(2,1)S(1)}, u32[]{:S(2)}, u32[]{:S(2)}) collective-permute-start(bf16[64,128]{1,0:T(8,128)(2,1)S(1)} %shard_map.84.own_ref), channel_id=1, source_target_pairs={{0,8},{8,16},{16,24},{24,32},{32,40},{40,48},{48,56},{56,64},{64,7... | collective-permute-start | bytes 49160 | tf_op jit(solution)/shard_map/ppermute | solution.py:38

commit v3 on v2

v3 whole, which is shorter than its diff:
```python
import jax
import jax.numpy as jnp
from jax import lax
from jax.experimental import pallas as pl
from jax.experimental.pallas import tpu as pltpu
from jax.sharding import Mesh, PartitionSpec as P

HD = 128
SIZES = (8, 2, 4, 8)
NAMES = ("z", "yl", "x", "tp")
CTX = ("z", "yl", "x")
N_CTX = 64
N_TP = 8
ROWS = 64
HEADS = 2
FEATS = HEADS * HD
TOTAL = N_CTX * ROWS
WINDOW = 2 * ROWS
HALF = ROWS // 2
PARTS_Q = 8
PARTS_K = 4
ROWS_Q = ROWS // PARTS_Q
ROWS_K = ROWS // PARTS_K
TILE_Q = N_CTX * ROWS_Q
TILE_K = N_CTX * ROWS_K
PIECE = 2 * ROWS_Q + 2 * ROWS_K
SCALE = HD ** (-0.5)
LOG2E = 1.4426950408889634
NEG = -1e30
FLOOR = -1e29
BF = jnp.bfloat16
F32 = jnp.float32
I32 = jnp.int32


def dot(a, b, dims):
    return lax.dot_general(a, b, (dims, ((), ())), preferred_element_type=F32)


def shift(x, axis, n, by):
    return lax.ppermute(x, axis, [(i, (i + by) % n) for i in range(n)])


def swap(x, axis):
    return lax.all_to_all(x, axis, split_axis=0, concat_axis=0, tiled=True)


def iota(shape, dim):
    return lax.broadcasted_iota(I32, shape, dim)


def call(kernel, ins, outs, flops, scalars=0):
    smem = pl.BlockSpec(memory_space=pltpu.SMEM)
    vmem = pl.BlockSpec(memory_space=pltpu.VMEM)
    size = sum(x.size * x.dtype.itemsize for x in list(ins) + list(outs))
    return pl.pallas_call(
        kernel,
        out_shape=tuple(outs),
        in_specs=[smem] * scalars + [vmem] * (len(ins) - scalars),
        out_specs=tuple([vmem] * len(outs)),
        cost_estimate=pl.CostEstimate(flops=flops, bytes_accessed=size, transcendentals=0),
        compiler_params=pltpu.CompilerParams(vmem_limit_bytes=40 * 1024 * 1024),
    )(*ins)


def shaped(shape, dtype):
    return jax.ShapeDtypeStruct(shape, dtype)


def slot_order(c, first_ref, moved_ref, shape, dim):
    before, after = jnp.maximum(c - 1, 0), jnp.minimum(c + 1, N_CTX - 1)
    first = first_ref[c]
    low = moved_ref[0, c]
    prev_high = jnp.where(c > 0, moved_ref[1, before], 0)
    next_low = jnp.where(c < N_CTX - 1, moved_ref[0, after], 0)
    next_first = jnp.where(c < N_CTX - 1, first_ref[after], TOTAL)
    rank = iota(shape, dim)
    order = jnp.where(
        rank < prev_high,
        first - prev_high + rank,
        jnp.where(
            rank >= ROWS - next_low,
            next_first + rank - (ROWS - next_low),
            first + low + rank - prev_high,
        ),
    )
    return order - (ROWS * c - HALF)


def pool_kernel(
    c_ref, first_hbm, moved_hbm, place_hbm, bytes_hbm, grad_hbm, w_hbm, sent_ref, own_ref,
    first_ref, moved_ref, place_ref, bytes_ref, grad_ref, w_ref, sems,
):
    pairs = (
        (first_hbm, first_ref),
        (moved_hbm, moved_ref),
        (place_hbm, place_ref),
        (bytes_hbm, bytes_ref),
        (grad_hbm, grad_ref),
        (w_hbm, w_ref),
    )
    copies = [pltpu.make_async_copy(a, b, sems.at[i]) for i, (a, b) in enumerate(pairs)]
    for copy in copies:
        copy.start()
    for copy in copies[:5]:
        copy.wait()
    c = c_ref[0]
    offset = first_ref[c] - (ROWS * c - HALF)
    member = iota((WINDOW, bytes_ref.shape[0]), 0) == place_ref[...] + offset
    lengths = jnp.sum(member.astype(F32), axis=1, keepdims=True)
    pooled = dot(member.astype(F32).astype(BF), bytes_ref[...], ((1,), (0,)))
    pooled = (pooled / jnp.maximum(lengths, 1.0)).astype(BF)
    order = slot_order(c, first_ref, moved_ref, (WINDOW, ROWS), 1)
    slotted = (iota((WINDOW, ROWS), 0) == order).astype(F32).astype(BF)
    grads = dot(slotted, grad_ref[...], ((1,), (0,))).astype(BF)
    copies[5].wait()
    for at, value in (
        (0, dot(pooled, w_ref[0], ((1,), (0,))).astype(BF)),
        (1, grads),
        (2, dot(pooled, w_ref[1], ((1,), (0,))).astype(BF)),
        (3, dot(pooled, w_ref[2], ((1,), (0,))).astype(BF)),
    ):
        sent_ref[:, at * FEATS : (at + 1) * FEATS] = value[:ROWS]
        own_ref[:, at * FEATS : (at + 1) * FEATS] = value[ROWS:]


def columns(value, kind, head):
    at = kind * FEATS + head * HD
    return value[:, at : at + HD]


def spread_kernel(own_ref, got_ref, piece_ref):
    both = own_ref[...] + got_ref[...]
    for e in range(HEADS):
        q, g, k, v = (columns(both, kind, e) for kind in range(4))
        for a in range(PARTS_Q):
            asked = slice(a * ROWS_Q, (a + 1) * ROWS_Q)
            for b in range(PARTS_K):
                held = slice(b * ROWS_K, (b + 1) * ROWS_K)
                piece_ref[(a * HEADS + e) * PARTS_K + b] = jnp.concatenate(
                    [q[asked], g[asked], k[held], v[held]], axis=0
                )


def unpack(piece_ref):
    q = piece_ref[:, :ROWS_Q, :].reshape(TILE_Q, HD)
    g = piece_ref[:, ROWS_Q : 2 * ROWS_Q, :].reshape(TILE_Q, HD)
    k = piece_ref[:, 2 * ROWS_Q : 2 * ROWS_Q + ROWS_K, :].reshape(TILE_K, HD)
    v = piece_ref[:, 2 * ROWS_Q + ROWS_K :, :].reshape(TILE_K, HD)
    return q, g, k, v


def scores(c, q, k):
    row = iota((1, TILE_Q), 1)
    query = ROWS * (row // ROWS_Q) + ROWS_Q * (c // (HEADS * PARTS_K)) + row % ROWS_Q + HALF
    col = iota((TILE_K, 1), 0)
    key = ROWS * (col // ROWS_K) + ROWS_K * (c % PARTS_K) + col % ROWS_K + HALF
    allowed = (query & (TOTAL - 1)) >= (key & (TOTAL - 1))
    return jnp.where(allowed, dot(k, q, ((1,), (1,))) * (SCALE * LOG2E), NEG)


def forward_kernel(c_ref, piece_ref, stats_ref):
    q, g, k, v = unpack(piece_ref)
    score = scores(c_ref[0], q, k)
    top = jnp.maximum(jnp.max(score, axis=0, keepdims=True), FLOOR)
    weight = jnp.exp2(score - top)
    dprob = dot(v, g, ((1,), (1,)))
    rows = [
        top,
        jnp.sum(weight, axis=0, keepdims=True),
        jnp.sum(weight * dprob, axis=0, keepdims=True),
    ]
    rows = jnp.concatenate(rows + [top] * 5, axis=0)
    for i in range(PARTS_K):
        stats_ref[i] = rows


def backward_kernel(c_ref, piece_ref, stats_ref, term_ref):
    tops, sums, dots = (stats_ref[:, i, :] for i in range(3))
    peak = jnp.max(tops, axis=0, keepdims=True)
    each = jnp.exp2(tops - peak)
    norm = jnp.sum(each * sums, axis=0, keepdims=True)
    delta = jnp.sum(each * dots, axis=0, keepdims=True) / norm
    lse = peak + jnp.log(norm) * LOG2E
    q, g, k, v = unpack(piece_ref)
    prob = jnp.exp2(scores(c_ref[0], q, k) - lse)
    dprob = dot(v, g, ((1,), (1,)))
    dscore = (prob * (dprob - delta)).astype(BF)
    prob = prob.astype(BF)
    d_query = dot(dscore, k, ((0,), (0,))) * SCALE
    out = dot(prob, v, ((0,), (0,)))
    d_key = dot(dscore, q, ((1,), (0,))) * SCALE
    d_value = dot(prob, g, ((1,), (0,)))
    term_ref[:, :ROWS_Q, :] = d_query.reshape(N_CTX, ROWS_Q, HD).astype(BF)
    term_ref[:, ROWS_Q : 2 * ROWS_Q, :] = out.reshape(N_CTX, ROWS_Q, HD).astype(BF)
    term_ref[:, 2 * ROWS_Q : 2 * ROWS_Q + ROWS_K, :] = d_key.reshape(N_CTX, ROWS_K, HD).astype(BF)
    term_ref[:, 2 * ROWS_Q + ROWS_K :, :] = d_value.reshape(N_CTX, ROWS_K, HD).astype(BF)


def sum_kernel(term_ref, w_ref, piece_ref, out_ref):
    terms = term_ref[...].astype(F32).reshape(PARTS_Q, HEADS, PARTS_K, PIECE, HD)
    asked = jnp.sum(terms[:, :, :, : 2 * ROWS_Q], axis=2)
    held = jnp.sum(terms[:, :, :, 2 * ROWS_Q :], axis=0)

    def joined(values):
        return jnp.concatenate([v.reshape(ROWS, HD) for v in values], axis=1).astype(BF)

    d_query = joined([asked[:, e, :ROWS_Q] for e in range(HEADS)])
    out_ref[...] = joined([asked[:, e, ROWS_Q:] for e in range(HEADS)])
    d_key = joined([held[e, :, :ROWS_K] for e in range(HEADS)])
    d_value = joined([held[e, :, ROWS_K:] for e in range(HEADS)])
    part = dot(d_query, w_ref[0], ((1,), (1,)))
    part = part + dot(d_key, w_ref[1], ((1,), (1,)))
    part = (part + dot(d_value, w_ref[2], ((1,), (1,)))).astype(BF)
    for i in range(N_TP):
        piece_ref[i] = part[:, i * HD : (i + 1) * HD]


def head_sum_kernel(pieces_ref, sum_ref):
    sum_ref[...] = jnp.sum(pieces_ref[...].astype(F32), axis=0).astype(BF)


def slot_kernel(c_ref, first_ref, moved_ref, before_ref, own_ref, out_ref):
    order = slot_order(c_ref[0], first_ref, moved_ref, (ROWS, WINDOW), 0)
    picker = (iota((ROWS, WINDOW), 1) == order).astype(F32).astype(BF)
    window = jnp.concatenate([before_ref[...], own_ref[...]], axis=0)
    out_ref[...] = dot(picker, window, ((1,), (0,))).astype(BF)


def byte_kernel(c_ref, first_ref, place_ref, before_ref, own_ref, out_ref):
    c = c_ref[0]
    offset = first_ref[c] - (ROWS * c - HALF)
    member = (iota((place_ref.shape[0], WINDOW), 1) == place_ref[...] + offset).astype(F32)
    lengths = jnp.sum(member, axis=0, keepdims=True)
    own_length = jnp.sum(member * lengths, axis=1, keepdims=True)
    window = jnp.concatenate([before_ref[...], own_ref[...]], axis=0)
    out_ref[...] = (dot(member.astype(BF), window, ((1,), (0,))) / own_length).astype(BF)


def pool(c_ref, first, moved, place, byte_states, d_attn, w_qkv):
    hbm = pl.BlockSpec(memory_space=pltpu.HBM)
    vmem = pl.BlockSpec(memory_space=pltpu.VMEM)
    ins = (first, moved, place, byte_states, d_attn, w_qkv)
    spaces = (pltpu.SMEM, pltpu.SMEM) + (pltpu.VMEM,) * 4
    block = shaped((ROWS, 4 * FEATS), BF)
    return pl.pallas_call(
        pool_kernel,
        out_shape=(block, block),
        in_specs=[pl.BlockSpec(memory_space=pltpu.SMEM)] + [hbm] * len(ins),
        out_specs=(vmem, vmem),
        scratch_shapes=[space(x.shape, x.dtype) for space, x in zip(spaces, ins)]
        + [pltpu.SemaphoreType.DMA((len(ins),))],
        cost_estimate=pl.CostEstimate(flops=300_000_000, bytes_accessed=2_500_000, transcendentals=0),
        compiler_params=pltpu.CompilerParams(vmem_limit_bytes=60 * 1024 * 1024),
    )(c_ref, *ins)


def shards(byte_states, patch_of_byte, patch_first, moved, w_qkv, d_attn):
    c_ref = lax.axis_index(CTX).astype(I32).reshape(1)
    n_bytes = patch_of_byte.shape[0]
    stack = shaped((N_CTX, PIECE, HD), BF)

    sent, own = pool(
        c_ref, patch_first, moved, patch_of_byte.reshape(1, n_bytes), byte_states, d_attn, w_qkv
    )
    (pieces,) = call(spread_kernel, (own, shift(sent, CTX, N_CTX, -1)), (stack,), 1_000_000)
    pieces = swap(pieces, CTX)
    (stats,) = call(
        forward_kernel,
        (c_ref, pieces),
        (shaped((PARTS_K, 8, TILE_Q), F32),),
        300_000_000,
        1,
    )
    (terms,) = call(
        backward_kernel, (c_ref, pieces, swap(stats, "x")), (stack,), 900_000_000, 1
    )
    pieces, out = call(
        sum_kernel,
        (swap(terms, CTX), w_qkv),
        (shaped((N_TP, ROWS, HD), BF), shaped((ROWS, FEATS), BF)),
        100_000_000,
    )
    (d_pooled,) = call(head_sum_kernel, (swap(pieces, "tp"),), (shaped((ROWS, HD), BF),), 100_000)
    (attn_out,) = call(
        slot_kernel,
        (c_ref, patch_first, moved, shift(out, CTX, N_CTX, 1), out),
        (shaped((ROWS, FEATS), BF),),
        5_000_000,
        3,
    )
    (byte_grad,) = call(
        byte_kernel,
        (c_ref, patch_first, patch_of_byte.reshape(n_bytes, 1), shift(d_pooled, CTX, N_CTX, 1), d_pooled),
        (shaped((n_bytes, HD), BF),),
        10_000_000,
        2,
    )
    return attn_out, byte_grad


def solution(mesh):
    fine = Mesh(mesh.devices.reshape(SIZES), NAMES)
    placed = (P(CTX, None), P(CTX), P(), P(), P(None, None, "tp"), P(CTX, "tp"))
    return jax.shard_map(
        shards,
        mesh=fine,
        in_specs=placed,
        out_specs=(P(CTX, "tp"), P(CTX, "tp")),
        check_vma=False,
    )
```

time: 132 us -> 119 us (0.902)
  blocking collectives: 38.9 us -> 65.1 us
  waiting for transfers between devices: 35.6 us -> 13.4 us
  starting transfers between devices: 39.2 us -> 28.9 us
  local copies, waits for them, and re-layouts: 5.37 us -> 1.05 us
    all_to_all x3, blocking collectives: 38.9 us -> 65.1 us  [swap(): return lax.all_to_all(x, axis, split_axis=0, concat_axis=0, tiled=True)]
    all_to_all x3 -> x1, waiting for transfers between devices: 28.2 us -> 6.18 us  [swap(): return lax.all_to_all(x, axis, split_axis=0, concat_axis=0, tiled=True)]
    all_to_all x3 -> x1, starting transfers between devices: 20.5 us -> 9.83 us  [swap(): return lax.all_to_all(x, axis, split_axis=0, concat_axis=0, tiled=True)]
    unnamed x20 -> x10, local copies, waits for them, and re-layouts: 5.24 us -> 0.92 us
    pallas_call x9 -> x7, Pallas kernels: 10.9 us -> 7.09 us  [call(): pl.pallas_call(kernel, out_shape=tuple(outs), in_specs=[smem] * scalars +...]
    pallas_call x0 -> x1, Pallas kernels: none -> 2.77 us  [pool(): pl.pallas_call(pool_kernel, out_shape=(block, block), in_specs=[pl.BlockS...]
  transfers between devices with their start and end apart: 6 -> 4, of which waited for: 5 -> 3; matrix products, arithmetic and copies ran while one was open for 0% -> 0% of each run, Pallas kernels for 1% -> 1%
where the time goes in v3:
time: 119 us
  blocking collectives  65.1 us (55%)
  starting transfers between devices  28.9 us (24%)
  waiting for transfers between devices  13.4 us (11%)
  Pallas kernels  9.85 us (8%)
    all_to_all x3, blocking collectives, swap(): return lax.all_to_all(x, axis, split_axis=0, concat_axis=0, tiled=True)  65.1 us
    ppermute x3, starting transfers between devices, shift(): return lax.ppermute(x, axis, [(i, (i + by) % n) for i in range(n)])  19.1 us
    all_to_all x1, starting transfers between devices, swap(): return lax.all_to_all(x, axis, split_axis=0, concat_axis=0, tiled=True)  9.83 us
    ppermute x3, waiting for transfers between devices, shift(): return lax.ppermute(x, axis, [(i, (i + by) % n) for i in range(n)])  7.19 us
    pallas_call x7, Pallas kernels, call(): pl.pallas_call(kernel, out_shape=tuple(outs), in_specs=[smem] * scalars +...  7.09 us
    all_to_all x1, waiting for transfers between devices, swap(): return lax.all_to_all(x, axis, split_axis=0, concat_axis=0, tiled=True)  6.18 us
    pallas_call x1, Pallas kernels, pool(): pl.pallas_call(pool_kernel, out_shape=(block, block), in_specs=[pl.BlockS...  2.77 us
  transfers between devices with their start and end apart: 4, of which 3 were waited for; matrix products, arithmetic and copies ran while one was open for 0% of the time, Pallas kernels for 1%

profile of v3, /device:TPU:1, one launch (start us, length us, event | category | flops | bytes accessed | tf_op | source)
XLA Modules:
  0.0 119.0 jit_solution(15736710854918427813)
XLA Ops:
  0.6 2.8 %shard_map.77 = (bf16[64,1024]{1,0:T(8,128)(2,1)}, bf16[64,1024]{1,0:T(8,128)(2,1)}) custom-call(s32[1]{0:T(128)} %bitcast.c_ref, s32[64]{0:T(128)} %first_ref.3, s32[2,64]{1,0:T(2,128)} %moved_ref.1, s32[1,256]{1,0:T(1,128)} %bitcast.3, bf16[256,1024]{1,0:T(8,128)(2,1)} %bytes_hbm.1, bf16[64,256]{1,0:T(8,128)(2,1)} %grad_hbm.1, bf16[3,1024,256]{2,1,0:T(8,128)(2,1)} %w_ref.1), custom_call_target="tpu_custom_call" | custom-call | flops 300000000 | bytes 2500000 | tf_op jit(solution)/shard_map/pallas_call | solution.py:246
  3.4 14.7 %collective-permute-start = (bf16[64,1024]{1,0:T(8,128)(2,1)}, bf16[64,1024]{1,0:T(8,128)(2,1)S(1)}, u32[]{:S(2)}, u32[]{:S(2)}) collective-permute-start(bf16[64,1024]{1,0:T(8,128)(2,1)} %get-tuple-element.7), channel_id=1, source_target_pairs={{0,504},{8,0},{16,8},{24,16},{32,24},{40,32},{48,40},{56,48},{64,5... | collective-permute-start | bytes 393224 | tf_op jit(solution)/shard_map/ppermute | solution.py:41
  18.1 2.5 %collective-permute-done.got_ref = bf16[64,1024]{1,0:T(8,128)(2,1)S(1)} collective-permute-done((bf16[64,1024]{1,0:T(8,128)(2,1)}, bf16[64,1024]{1,0:T(8,128)(2,1)S(1)}, u32[]{:S(2)}, u32[]{:S(2)}) %collective-permute-start) | collective-permute-done | bytes 131104 | tf_op jit(solution)/shard_map/ppermute | solution.py:41
  20.6 0.0 copy-start.1
  20.6 0.9 copy-done.1
  21.5 0.1 shard_map.78
  21.6 30.0 %all_to_all.20.piece_ref = bf16[64,48,128]{2,1,0:T(8,128)(2,1)S(1)} all-to-all(bf16[64,48,128]{2,1,0:T(8,128)(2,1)S(1)} %shard_map.78), channel_id=1, replica_groups=mesh['z'=8,'yl'=2,'x'=4,'tp'=8] {'z','yl','x'}, dimensions={0} | all-to-all | bytes 1572864 | tf_op jit(solution)/shard_map/all_to_all | solution.py:45
  51.6 0.9 shard_map.79
  52.5 7.7 %all_to_all.21.stats_ref = f32[4,8,512]{2,1,0:T(8,128)S(1)} all-to-all(f32[4,8,512]{2,1,0:T(8,128)S(1)} %shard_map.79), channel_id=1, replica_groups=mesh['z'=8,'yl'=2,'x'=4,'tp'=8] {'x'}, dimensions={0} | all-to-all | bytes 131072 | tf_op jit(solution)/shard_map/all_to_all | solution.py:45
  60.2 2.1 %shard_map.80 = bf16[64,48,128]{2,1,0:T(8,128)(2,1)S(1)} custom-call(s32[1]{0:T(128)} %bitcast.c_ref, bf16[64,48,128]{2,1,0:T(8,128)(2,1)S(1)} %all_to_all.20.piece_ref, f32[4,8,512]{2,1,0:T(8,128)S(1)} %all_to_all.21.stats_ref), custom_call_target="tpu_custom_call" | custom-call | flops 900000000 | bytes 1638404 | tf_op jit(solution)/shard_map/pallas_call | solution.py:56
  62.3 0.0 copy-start
  62.3 27.4 %all_to_all.22.term_ref = bf16[64,48,128]{2,1,0:T(8,128)(2,1)S(1)} all-to-all(bf16[64,48,128]{2,1,0:T(8,128)(2,1)S(1)} %shard_map.80), channel_id=1, replica_groups=mesh['z'=8,'yl'=2,'x'=4,'tp'=8] {'z','yl','x'}, dimensions={0} | all-to-all | bytes 1572864 | tf_op jit(solution)/shard_map/all_to_all | solution.py:45
  89.7 0.0 copy-done
  89.7 0.0 copy-start.4
  89.7 0.0 copy-start.2
  89.7 0.0 copy-start.3
  89.7 1.2 %shard_map.81 = (bf16[8,64,128]{2,1,0:T(8,128)(2,1)}, bf16[64,256]{1,0:T(8,128)(2,1)S(1)}) custom-call(bf16[64,48,128]{2,1,0:T(8,128)(2,1)S(1)} %all_to_all.22.term_ref, bf16[3,1024,256]{2,1,0:T(8,128)(2,1)S(1)} %copy-done), custom_call_target="tpu_custom_call" | custom-call | flops 100000000 | bytes 2523136 | tf_op jit(solution)/shard_map/pallas_call | solution.py:56
  90.9 9.8 %all-to-all-start.3 = ((bf16[8,64,128]{2,1,0:T(8,128)(2,1)}), bf16[8,64,128]{2,1,0:T(8,128)(2,1)S(1)}, u32[]{:S(2)}, u32[]{:S(2)}) async-start(bf16[8,64,128]{2,1,0:T(8,128)(2,1)} %get-tuple-element.9), calls=%async_computation.3 | async-start | bytes 262144 | tf_op jit(solution)/shard_map/all_to_all | solution.py:45
  100.8 1.9 %collective-permute-start.1 = (bf16[64,256]{1,0:T(8,128)(2,1)S(1)}, bf16[64,256]{1,0:T(8,128)(2,1)S(1)}, u32[]{:S(2)}, u32[]{:S(2)}) collective-permute-start(bf16[64,256]{1,0:T(8,128)(2,1)S(1)} %get-tuple-element.8.own_ref), channel_id=1, source_target_pairs={{0,8},{8,16},{16,24},{24,32},{32,40},{40,48},{48,56},{56,64},{64,7... | collective-permute-start | bytes 98312 | tf_op jit(solution)/shard_map/ppermute | solution.py:41
  102.7 6.2 %all-to-all-done.3.pieces_ref = bf16[8,64,128]{2,1,0:T(8,128)(2,1)S(1)} async-done(((bf16[8,64,128]{2,1,0:T(8,128)(2,1)}), bf16[8,64,128]{2,1,0:T(8,128)(2,1)S(1)}, u32[]{:S(2)}, u32[]{:S(2)}) %all-to-all-start.3) | async-done | bytes 131104 | tf_op jit(solution)/shard_map/all_to_all | solution.py:45
  108.9 2.5 %collective-permute-start.2 = (bf16[64,128]{1,0:T(8,128)(2,1)S(1)}, bf16[64,128]{1,0:T(8,128)(2,1)S(1)}, u32[]{:S(2)}, u32[]{:S(2)}) collective-permute-start(bf16[64,128]{1,0:T(8,128)(2,1)S(1)} %shard_map.83.own_ref), channel_id=1, source_target_pairs={{0,8},{8,16},{16,24},{24,32},{32,40},{40,48},{48,56},{56,64},{64,7... | collective-permute-start | bytes 49160 | tf_op jit(solution)/shard_map/ppermute | solution.py:41
  111.4 0.0 copy-done.4
  111.4 0.1 copy.8.place_ref
  111.5 0.0 collective-permute-done.1.before_ref
  111.5 0.0 copy-done.2
  111.6 0.0 copy-done.3
  111.6 1.3 %shard_map.82 = bf16[64,256]{1,0:T(8,128)(2,1)} custom-call(s32[1]{0:T(128)} %bitcast.c_ref, s32[64]{0:T(128)S(1)} %copy-done.2, s32[2,64]{1,0:T(2,128)S(1)} %copy-done.3, bf16[64,256]{1,0:T(8,128)(2,1)S(1)} %collective-permute-done.1.before_ref, bf16[64,256]{1,0:T(8,128)(2,1)S(1)} %get-tuple-element.8.own_ref), custom_call_target="tpu_custom_call" | custom-call | flops 5000000 | bytes 99076 | tf_op jit(solution)/shard_map/pallas_call | solution.py:56
  112.9 4.7 %collective-permute-done.2.before_ref = bf16[64,128]{1,0:T(8,128)(2,1)S(1)} collective-permute-done((bf16[64,128]{1,0:T(8,128)(2,1)S(1)}, bf16[64,128]{1,0:T(8,128)(2,1)S(1)}, u32[]{:S(2)}, u32[]{:S(2)}) %collective-permute-start.2) | collective-permute-done | bytes 16416 | tf_op jit(solution)/shard_map/ppermute | solution.py:41
  117.6 1.4 %shard_map.84 = bf16[256,128]{1,0:T(8,128)(2,1)} custom-call(s32[1]{0:T(128)} %bitcast.c_ref, s32[64]{0:T(128)S(1)} %copy-done.2, s32[256,1]{1,0:T(8,128)S(1)} %copy.8.place_ref, bf16[64,128]{1,0:T(8,128)(2,1)S(1)} %collective-permute-done.2.before_ref, bf16[64,128]{1,0:T(8,128)(2,1)S(1)} %shard_map.83.own_ref), custom_call_target="tpu_custom_call" | custom-call | flops 10000000 | bytes 99588 | tf_op jit(solution)/shard_map/pallas_call | solution.py:56
  (1 shorter events, 0.0 us)
Async XLA Ops:
  3.4 17.2 %collective-permute-start = (bf16[64,1024]{1,0:T(8,128)(2,1)}, bf16[64,1024]{1,0:T(8,128)(2,1)S(1)}, u32[]{:S(2)}, u32[]{:S(2)}) collective-permute-start(bf16[64,1024]{1,0:T(8,128)(2,1)} %get-tuple-element.7), channel_id=1, source_target_pairs={{0,504},{8,0},{16,8},{24,16},{32,24},{40,32},{48,40},{56,48},{64,5... | collective-permute-start | bytes 393224 | tf_op jit(solution)/shard_map/ppermute | solution.py:41
  20.6 0.9 copy-start.1
  62.3 27.4 %copy-start = (bf16[3,1024,256]{2,1,0:T(8,128)(2,1)S(1)}, bf16[3,1024,256]{2,1,0:T(8,128)(2,1)}, u32[]{:S(2)}) copy-start(bf16[3,1024,256]{2,1,0:T(8,128)(2,1)} %w_ref.1) | copy-start | bytes 4718596
  89.7 21.7 %copy-start.4 = (s32[256]{0:T(256)S(1)}, s32[256]{0:T(256)}, u32[]{:S(2)}) copy-start(s32[256]{0:T(256)} %param.7) | copy-start | bytes 3076
  89.7 21.8 %copy-start.2 = (s32[64]{0:T(128)S(1)}, s32[64]{0:T(128)}, u32[]{:S(2)}) copy-start(s32[64]{0:T(128)} %first_ref.3) | copy-start | bytes 772
  89.7 21.9 %copy-start.3 = (s32[2,64]{1,0:T(2,128)S(1)}, s32[2,64]{1,0:T(2,128)}, u32[]{:S(2)}) copy-start(s32[2,64]{1,0:T(2,128)} %moved_ref.1) | copy-start | bytes 1540
  90.9 17.9 %all-to-all-start.3 = ((bf16[8,64,128]{2,1,0:T(8,128)(2,1)}), bf16[8,64,128]{2,1,0:T(8,128)(2,1)S(1)}, u32[]{:S(2)}, u32[]{:S(2)}) async-start(bf16[8,64,128]{2,1,0:T(8,128)(2,1)} %get-tuple-element.9), calls=%async_computation.3 | async-start | bytes 262144 | tf_op jit(solution)/shard_map/all_to_all | solution.py:45
  100.8 10.8 %collective-permute-start.1 = (bf16[64,256]{1,0:T(8,128)(2,1)S(1)}, bf16[64,256]{1,0:T(8,128)(2,1)S(1)}, u32[]{:S(2)}, u32[]{:S(2)}) collective-permute-start(bf16[64,256]{1,0:T(8,128)(2,1)S(1)} %get-tuple-element.8.own_ref), channel_id=1, source_target_pairs={{0,8},{8,16},{16,24},{24,32},{32,40},{40,48},{48,56},{56,64},{64,7... | collective-permute-start | bytes 98312 | tf_op jit(solution)/shard_map/ppermute | solution.py:41
  108.9 8.7 %collective-permute-start.2 = (bf16[64,128]{1,0:T(8,128)(2,1)S(1)}, bf16[64,128]{1,0:T(8,128)(2,1)S(1)}, u32[]{:S(2)}, u32[]{:S(2)}) collective-permute-start(bf16[64,128]{1,0:T(8,128)(2,1)S(1)} %shard_map.83.own_ref), channel_id=1, source_target_pairs={{0,8},{8,16},{16,24},{24,32},{32,40},{40,48},{48,56},{56,64},{64,7... | collective-permute-start | bytes 49160 | tf_op jit(solution)/shard_map/ppermute | solution.py:41

commit v4 on v3

--- a/solution.py
+++ b/solution.py
@@ -91,14 +91,13 @@
     c_ref, first_hbm, moved_hbm, place_hbm, bytes_hbm, grad_hbm, w_hbm, sent_ref, own_ref,
     first_ref, moved_ref, place_ref, bytes_ref, grad_ref, w_ref, sems,
 ):
-    pairs = (
+    pairs = [
         (first_hbm, first_ref),
         (moved_hbm, moved_ref),
         (place_hbm, place_ref),
         (bytes_hbm, bytes_ref),
         (grad_hbm, grad_ref),
-        (w_hbm, w_ref),
-    )
+    ] + [(w_hbm.at[i], w_ref.at[i]) for i in range(3)]
     copies = [pltpu.make_async_copy(a, b, sems.at[i]) for i, (a, b) in enumerate(pairs)]
     for copy in copies:
         copy.start()
@@ -113,13 +112,11 @@
     order = slot_order(c, first_ref, moved_ref, (WINDOW, ROWS), 1)
     slotted = (iota((WINDOW, ROWS), 0) == order).astype(F32).astype(BF)
     grads = dot(slotted, grad_ref[...], ((1,), (0,))).astype(BF)
-    copies[5].wait()
-    for at, value in (
-        (0, dot(pooled, w_ref[0], ((1,), (0,))).astype(BF)),
-        (1, grads),
-        (2, dot(pooled, w_ref[1], ((1,), (0,))).astype(BF)),
-        (3, dot(pooled, w_ref[2], ((1,), (0,))).astype(BF)),
-    ):
+    for at, value in ((0, None), (1, grads), (2, None), (3, None)):
+        if value is None:
+            part = max(at - 1, 0)
+            copies[5 + part].wait()
+            value = dot(pooled, w_ref[part], ((1,), (0,))).astype(BF)
         sent_ref[:, at * FEATS : (at + 1) * FEATS] = value[:ROWS]
         own_ref[:, at * FEATS : (at + 1) * FEATS] = value[ROWS:]
 
@@ -127,6 +124,10 @@
 def columns(value, kind, head):
     at = kind * FEATS + head * HD
     return value[:, at : at + HD]
+
+
+def hold_kernel(own_ref, held_ref):
+    held_ref[...] = own_ref[...]
 
 
 def spread_kernel(own_ref, got_ref, piece_ref):
@@ -216,25 +217,29 @@
         piece_ref[i] = part[:, i * HD : (i + 1) * HD]
 
 
-def head_sum_kernel(pieces_ref, sum_ref):
-    sum_ref[...] = jnp.sum(pieces_ref[...].astype(F32), axis=0).astype(BF)
-
-
-def slot_kernel(c_ref, first_ref, moved_ref, before_ref, own_ref, out_ref):
-    order = slot_order(c_ref[0], first_ref, moved_ref, (ROWS, WINDOW), 0)
-    picker = (iota((ROWS, WINDOW), 1) == order).astype(F32).astype(BF)
+def place_kernel(c_ref, first_ref, moved_ref, place_ref, picker_ref, member_ref, length_ref):
+    c = c_ref[0]
+    order = slot_order(c, first_ref, moved_ref, (ROWS, WINDOW), 0)
+    picker_ref[...] = (iota((ROWS, WINDOW), 1) == order).astype(F32).astype(BF)
+    offset = first_ref[c] - (ROWS * c - HALF)
+    member = (iota((WINDOW, place_ref.shape[1]), 0) == place_ref[...] + offset).astype(F32)
+    lengths = jnp.sum(member, axis=1, keepdims=True)
+    member = member.T
+    member_ref[...] = member.astype(BF)
+    spread = jnp.broadcast_to(lengths, (WINDOW, HD)).astype(BF)
+    length_ref[...] = dot(member.astype(BF), spread, ((1,), (0,)))
+
+
+def head_sum_kernel(pieces_ref, out_ref, both_ref):
+    both_ref[:, :HD] = jnp.sum(pieces_ref[...].astype(F32), axis=0).astype(BF)
+    both_ref[:, HD:] = out_ref[...]
+
+
+def last_kernel(before_ref, own_ref, picker_ref, member_ref, length_ref, out_ref, grad_ref):
     window = jnp.concatenate([before_ref[...], own_ref[...]], axis=0)
-    out_ref[...] = dot(picker, window, ((1,), (0,))).astype(BF)
-
-
-def byte_kernel(c_ref, first_ref, place_ref, before_ref, own_ref, out_ref):
-    c = c_ref[0]
-    offset = first_ref[c] - (ROWS * c - HALF)
-    member = (iota((place_ref.shape[0], WINDOW), 1) == place_ref[...] + offset).astype(F32)
-    lengths = jnp.sum(member, axis=0, keepdims=True)
-    own_length = jnp.sum(member * lengths, axis=1, keepdims=True)
-    window = jnp.concatenate([before_ref[...], own_ref[...]], axis=0)
-    out_ref[...] = (dot(member.astype(BF), window, ((1,), (0,))) / own_length).astype(BF)
+    out_ref[...] = dot(picker_ref[...], window[:, HD:], ((1,), (0,))).astype(BF)
+    spread = dot(member_ref[...], window[:, :HD], ((1,), (0,)))
+    grad_ref[...] = (spread / length_ref[...]).astype(BF)
 
 
 def pool(c_ref, first, moved, place, byte_states, d_attn, w_qkv):
@@ -249,7 +254,7 @@
         in_specs=[pl.BlockSpec(memory_space=pltpu.SMEM)] + [hbm] * len(ins),
         out_specs=(vmem, vmem),
         scratch_shapes=[space(x.shape, x.dtype) for space, x in zip(spaces, ins)]
-        + [pltpu.SemaphoreType.DMA((len(ins),))],
+        + [pltpu.SemaphoreType.DMA((len(ins) + 2,))],
         cost_estimate=pl.CostEstimate(flops=300_000_000, bytes_accessed=2_500_000, transcendentals=0),
         compiler_params=pltpu.CompilerParams(vmem_limit_bytes=60 * 1024 * 1024),
     )(c_ref, *ins)
@@ -259,10 +264,12 @@
     c_ref = lax.axis_index(CTX).astype(I32).reshape(1)
     n_bytes = patch_of_byte.shape[0]
     stack = shaped((N_CTX, PIECE, HD), BF)
+    place = patch_of_byte.reshape(1, n_bytes)
 
     sent, own = pool(
-        c_ref, patch_first, moved, patch_of_byte.reshape(1, n_bytes), byte_states, d_attn, w_qkv
-    )
+        c_ref, patch_first, moved, place, byte_states, d_attn, w_qkv
+    )
+    (own,) = call(hold_kernel, (own,), (shaped(own.shape, BF),), 100_000)
     (pieces,) = call(spread_kernel, (own, shift(sent, CTX, N_CTX, -1)), (stack,), 1_000_000)
     pieces = swap(pieces, CTX)
     (stats,) = call(
@@ -281,20 +288,25 @@
         (shaped((N_TP, ROWS, HD), BF), shaped((ROWS, FEATS), BF)),
         100_000_000,
     )
-    (d_pooled,) = call(head_sum_kernel, (swap(pieces, "tp"),), (shaped((ROWS, HD), BF),), 100_000)
-    (attn_out,) = call(
-        slot_kernel,
-        (c_ref, patch_first, moved, shift(out, CTX, N_CTX, 1), out),
-        (shaped((ROWS, FEATS), BF),),
-        5_000_000,
+    (both,) = call(
+        head_sum_kernel, (swap(pieces, "tp"), out), (shaped((ROWS, HD + FEATS), BF),), 100_000
+    )
+    picker, member, length = call(
+        place_kernel,
+        (c_ref, patch_first, moved, place),
+        (
+            shaped((ROWS, WINDOW), BF),
+            shaped((n_bytes, WINDOW), BF),
+            shaped((n_bytes, HD), F32),
+        ),
+        10_000_000,
         3,
     )
-    (byte_grad,) = call(
-        byte_kernel,
-        (c_ref, patch_first, patch_of_byte.reshape(n_bytes, 1), shift(d_pooled, CTX, N_CTX, 1), d_pooled),
-        (shaped((n_bytes, HD), BF),),
+    attn_out, byte_grad = call(
+        last_kernel,
+        (shift(both, CTX, N_CTX, 1), both, picker, member, length),
+        (shaped((ROWS, FEATS), BF), shaped((n_bytes, HD), BF)),
         10_000_000,
-        2,
     )
     return attn_out, byte_grad
 

time: 119 us -> 118 us (level)
  blocking collectives: 65.1 us -> 82.8 us
  starting transfers between devices: 28.9 us -> 17.2 us
  waiting for transfers between devices: 13.4 us -> 7.27 us
  Pallas kernels: 9.85 us -> 8.28 us
    all_to_all x3 -> x4, blocking collectives: 65.1 us -> 82.8 us  [swap(): return lax.all_to_all(x, axis, split_axis=0, concat_axis=0, tiled=True)]
    all_to_all x1 -> x0, starting transfers between devices: 9.83 us -> none  [swap(): return lax.all_to_all(x, axis, split_axis=0, concat_axis=0, tiled=True)]
    all_to_all x1 -> x0, waiting for transfers between devices: 6.18 us -> none  [swap(): return lax.all_to_all(x, axis, split_axis=0, concat_axis=0, tiled=True)]
    ppermute x3 -> x2, starting transfers between devices: 19.1 us -> 17.2 us  [shift(): return lax.ppermute(x, axis, [(i, (i + by) % n) for i in range(n)])]
    pallas_call x7 -> x8, Pallas kernels: 7.09 us -> 5.33 us  [call(): pl.pallas_call(kernel, out_shape=tuple(outs), in_specs=[smem] * scalars +...]
    ppermute x3 -> x2, waiting for transfers between devices: 7.19 us -> 7.27 us  [shift(): return lax.ppermute(x, axis, [(i, (i + by) % n) for i in range(n)])]
  transfers between devices with their start and end apart: 4 -> 2, of which waited for: 3 -> 2; matrix products, arithmetic and copies ran while one was open for 0% -> 0% of each run, Pallas kernels for 1% -> 1%
where the time goes in v4:
time: 118 us; the launch traced here: 117 us
  blocking collectives  82.8 us (70%)
  starting transfers between devices  17.2 us (15%)
  Pallas kernels  8.28 us (7%)
  waiting for transfers between devices  7.27 us (6%)
    all_to_all x4, blocking collectives, swap(): return lax.all_to_all(x, axis, split_axis=0, concat_axis=0, tiled=True)  82.8 us
    ppermute x2, starting transfers between devices, shift(): return lax.ppermute(x, axis, [(i, (i + by) % n) for i in range(n)])  17.2 us
    ppermute x2, waiting for transfers between devices, shift(): return lax.ppermute(x, axis, [(i, (i + by) % n) for i in range(n)])  7.27 us
    pallas_call x8, Pallas kernels, call(): pl.pallas_call(kernel, out_shape=tuple(outs), in_specs=[smem] * scalars +...  5.33 us
    pallas_call x1, Pallas kernels, pool(): pl.pallas_call(pool_kernel, out_shape=(block, block), in_specs=[pl.BlockS...  2.94 us
  transfers between devices with their start and end apart: 2, of which 2 were waited for; matrix products, arithmetic and copies ran while one was open for 0% of the time, Pallas kernels for 1%

profile of v4, /device:TPU:1, one launch (start us, length us, event | category | flops | bytes accessed | tf_op | source)
XLA Modules:
  0.0 117.2 jit_solution(16158390194115552089)
XLA Ops:
  0.6 2.9 %shard_map.77 = (bf16[64,1024]{1,0:T(8,128)(2,1)}, bf16[64,1024]{1,0:T(8,128)(2,1)}) custom-call(s32[1]{0:T(128)} %bitcast.c_ref, s32[64]{0:T(128)} %first_ref.1, s32[2,64]{1,0:T(2,128)} %moved_ref.1, s32[1,256]{1,0:T(1,128)} %bitcast.2, bf16[256,1024]{1,0:T(8,128)(2,1)} %bytes_hbm.1, bf16[64,256]{1,0:T(8,128)(2,1)} %grad_hbm.1, bf16[3,1024,256]{2,1,0:T(8,128)(2,1)} %w_ref.1), custom_call_target="tpu_custom_call" | custom-call | flops 300000000 | bytes 2500000 | tf_op jit(solution)/shard_map/pallas_call | solution.py:251
  3.6 14.7 %collective-permute-start = (bf16[64,1024]{1,0:T(8,128)(2,1)}, bf16[64,1024]{1,0:T(8,128)(2,1)S(1)}, u32[]{:S(2)}, u32[]{:S(2)}) collective-permute-start(bf16[64,1024]{1,0:T(8,128)(2,1)} %get-tuple-element.10), channel_id=1, source_target_pairs={{0,504},{8,0},{16,8},{24,16},{32,24},{40,32},{48,40},{56,48},{64,5... | collective-permute-start | bytes 393224 | tf_op jit(solution)/shard_map/ppermute | solution.py:41
  18.3 0.0 copy-start.1
  18.3 0.9 copy-done.1
  19.2 1.5 %collective-permute-done.got_ref = bf16[64,1024]{1,0:T(8,128)(2,1)S(1)} collective-permute-done((bf16[64,1024]{1,0:T(8,128)(2,1)}, bf16[64,1024]{1,0:T(8,128)(2,1)S(1)}, u32[]{:S(2)}, u32[]{:S(2)}) %collective-permute-start) | collective-permute-done | bytes 131104 | tf_op jit(solution)/shard_map/ppermute | solution.py:41
  20.8 0.1 shard_map.79
  20.9 30.0 %all_to_all.20.piece_ref = bf16[64,48,128]{2,1,0:T(8,128)(2,1)S(1)} all-to-all(bf16[64,48,128]{2,1,0:T(8,128)(2,1)S(1)} %shard_map.79), channel_id=1, replica_groups=mesh['z'=8,'yl'=2,'x'=4,'tp'=8] {'z','yl','x'}, dimensions={0} | all-to-all | bytes 1572864 | tf_op jit(solution)/shard_map/all_to_all | solution.py:45
  50.9 0.9 shard_map.80
  51.8 7.7 %all_to_all.21.stats_ref = f32[4,8,512]{2,1,0:T(8,128)S(1)} all-to-all(f32[4,8,512]{2,1,0:T(8,128)S(1)} %shard_map.80), channel_id=1, replica_groups=mesh['z'=8,'yl'=2,'x'=4,'tp'=8] {'x'}, dimensions={0} | all-to-all | bytes 131072 | tf_op jit(solution)/shard_map/all_to_all | solution.py:45
  59.5 2.0 %shard_map.81 = bf16[64,48,128]{2,1,0:T(8,128)(2,1)S(1)} custom-call(s32[1]{0:T(128)} %bitcast.c_ref, bf16[64,48,128]{2,1,0:T(8,128)(2,1)S(1)} %all_to_all.20.piece_ref, f32[4,8,512]{2,1,0:T(8,128)S(1)} %all_to_all.21.stats_ref), custom_call_target="tpu_custom_call" | custom-call | flops 900000000 | bytes 1638404 | tf_op jit(solution)/shard_map/pallas_call | solution.py:56
  61.5 0.0 copy-start
  61.5 27.4 %all_to_all.22.term_ref = bf16[64,48,128]{2,1,0:T(8,128)(2,1)S(1)} all-to-all(bf16[64,48,128]{2,1,0:T(8,128)(2,1)S(1)} %shard_map.81), channel_id=1, replica_groups=mesh['z'=8,'yl'=2,'x'=4,'tp'=8] {'z','yl','x'}, dimensions={0} | all-to-all | bytes 1572864 | tf_op jit(solution)/shard_map/all_to_all | solution.py:45
  89.0 0.0 copy-done
  89.0 0.0 copy-start.2
  89.0 0.0 copy-start.3
  89.0 0.0 copy-start.4
  89.0 0.6 shard_map.82
  89.6 17.7 %all_to_all.23.pieces_ref = bf16[8,64,128]{2,1,0:T(8,128)(2,1)S(1)} all-to-all(bf16[8,64,128]{2,1,0:T(8,128)(2,1)S(1)} %get-tuple-element.11), channel_id=1, replica_groups=mesh['z'=8,'yl'=2,'x'=4,'tp'=8] {'tp'}, dimensions={0} | all-to-all | bytes 262144 | tf_op jit(solution)/shard_map/all_to_all | solution.py:45
  107.3 2.5 %collective-permute-start.1 = (bf16[64,384]{1,0:T(8,128)(2,1)S(1)}, bf16[64,384]{1,0:T(8,128)(2,1)S(1)}, u32[]{:S(2)}, u32[]{:S(2)}) collective-permute-start(bf16[64,384]{1,0:T(8,128)(2,1)S(1)} %shard_map.83.own_ref), channel_id=1, source_target_pairs={{0,8},{8,16},{16,24},{24,32},{32,40},{40,48},{48,56},{56,64},{64,7... | collective-permute-start | bytes 147464 | tf_op jit(solution)/shard_map/ppermute | solution.py:41
  109.8 0.0 copy-done.2
  109.8 0.0 copy-done.3
  109.8 0.0 copy-done.4
  109.8 0.8 shard_map.84
  110.7 5.7 %collective-permute-done.1.before_ref = bf16[64,384]{1,0:T(8,128)(2,1)S(1)} collective-permute-done((bf16[64,384]{1,0:T(8,128)(2,1)S(1)}, bf16[64,384]{1,0:T(8,128)(2,1)S(1)}, u32[]{:S(2)}, u32[]{:S(2)}) %collective-permute-start.1) | collective-permute-done | bytes 49184 | tf_op jit(solution)/shard_map/ppermute | solution.py:41
  116.4 0.8 shard_map.85
  (2 shorter events, 0.0 us)
Async XLA Ops:
  3.6 17.2 %collective-permute-start = (bf16[64,1024]{1,0:T(8,128)(2,1)}, bf16[64,1024]{1,0:T(8,128)(2,1)S(1)}, u32[]{:S(2)}, u32[]{:S(2)}) collective-permute-start(bf16[64,1024]{1,0:T(8,128)(2,1)} %get-tuple-element.10), channel_id=1, source_target_pairs={{0,504},{8,0},{16,8},{24,16},{32,24},{40,32},{48,40},{56,48},{64,5... | collective-permute-start | bytes 393224 | tf_op jit(solution)/shard_map/ppermute | solution.py:41
  18.3 0.9 copy-start.1
  61.5 27.4 %copy-start = (bf16[3,1024,256]{2,1,0:T(8,128)(2,1)S(1)}, bf16[3,1024,256]{2,1,0:T(8,128)(2,1)}, u32[]{:S(2)}) copy-start(bf16[3,1024,256]{2,1,0:T(8,128)(2,1)} %w_ref.1) | copy-start | bytes 4718596
  89.0 20.9 %copy-start.2 = (s32[2,64]{1,0:T(2,128)S(1)}, s32[2,64]{1,0:T(2,128)}, u32[]{:S(2)}) copy-start(s32[2,64]{1,0:T(2,128)} %moved_ref.1) | copy-start | bytes 1540
  89.0 20.9 %copy-start.3 = (s32[256]{0:T(256)S(1)}, s32[256]{0:T(256)}, u32[]{:S(2)}) copy-start(s32[256]{0:T(256)} %param.7) | copy-start | bytes 3076
  89.0 20.9 %copy-start.4 = (s32[64]{0:T(128)S(1)}, s32[64]{0:T(128)}, u32[]{:S(2)}) copy-start(s32[64]{0:T(128)} %first_ref.1) | copy-start | bytes 772
  107.3 9.1 %collective-permute-start.1 = (bf16[64,384]{1,0:T(8,128)(2,1)S(1)}, bf16[64,384]{1,0:T(8,128)(2,1)S(1)}, u32[]{:S(2)}, u32[]{:S(2)}) collective-permute-start(bf16[64,384]{1,0:T(8,128)(2,1)S(1)} %shard_map.83.own_ref), channel_id=1, source_target_pairs={{0,8},{8,16},{16,24},{24,32},{32,40},{40,48},{48,56},{56,64},{64,7... | collective-permute-start | bytes 147464 | tf_op jit(solution)/shard_map/ppermute | solution.py:41

commit v5 on v4

--- a/solution.py
+++ b/solution.py
@@ -6,24 +6,24 @@
 from jax.sharding import Mesh, PartitionSpec as P
 
 HD = 128
-SIZES = (8, 2, 4, 8)
-NAMES = ("z", "yl", "x", "tp")
-CTX = ("z", "yl", "x")
+SIZES = (4, 2, 2, 2, 2, 8)
+NAMES = ("zh", "zl", "yl", "xh", "xl", "tp")
+CTX = ("zh", "zl", "yl", "xh", "xl")
+FAR = ("zh", "zl", "xh")
+NEAR = ("yl", "xl")
 N_CTX = 64
 N_TP = 8
+N_FAR = 16
+N_NEAR = 4
+N_ASK = 8
 ROWS = 64
 HEADS = 2
 FEATS = HEADS * HD
 TOTAL = N_CTX * ROWS
 WINDOW = 2 * ROWS
 HALF = ROWS // 2
-PARTS_Q = 8
-PARTS_K = 4
-ROWS_Q = ROWS // PARTS_Q
-ROWS_K = ROWS // PARTS_K
-TILE_Q = N_CTX * ROWS_Q
-TILE_K = N_CTX * ROWS_K
-PIECE = 2 * ROWS_Q + 2 * ROWS_K
+TILE_Q = N_ASK * ROWS
+TILE_K = N_FAR * ROWS
 SCALE = HD ** (-0.5)
 LOG2E = 1.4426950408889634
 NEG = -1e30
@@ -130,38 +130,39 @@
     held_ref[...] = own_ref[...]
 
 
-def spread_kernel(own_ref, got_ref, piece_ref):
+def spread_kernel(c_ref, own_ref, got_ref, keep_ref, give_ref, held_ref):
     both = own_ref[...] + got_ref[...]
+    asked, held = [], []
     for e in range(HEADS):
         q, g, k, v = (columns(both, kind, e) for kind in range(4))
-        for a in range(PARTS_Q):
-            asked = slice(a * ROWS_Q, (a + 1) * ROWS_Q)
-            for b in range(PARTS_K):
-                held = slice(b * ROWS_K, (b + 1) * ROWS_K)
-                piece_ref[(a * HEADS + e) * PARTS_K + b] = jnp.concatenate(
-                    [q[asked], g[asked], k[held], v[held]], axis=0
-                )
-
-
-def unpack(piece_ref):
-    q = piece_ref[:, :ROWS_Q, :].reshape(TILE_Q, HD)
-    g = piece_ref[:, ROWS_Q : 2 * ROWS_Q, :].reshape(TILE_Q, HD)
-    k = piece_ref[:, 2 * ROWS_Q : 2 * ROWS_Q + ROWS_K, :].reshape(TILE_K, HD)
-    v = piece_ref[:, 2 * ROWS_Q + ROWS_K :, :].reshape(TILE_K, HD)
-    return q, g, k, v
+        asked.append(jnp.concatenate([q, g], axis=1))
+        held.append(jnp.concatenate([k, v], axis=1))
+    second = ((c_ref[0] >> 3) & 1) == 1
+    keep_ref[...] = jnp.where(second, asked[1], asked[0])
+    give_ref[...] = jnp.where(second, asked[0], asked[1])
+    for i in range(N_FAR):
+        held_ref[i] = held[(i >> 1) & 1]
+
+
+def unpack(asked_ref, held_ref):
+    k = held_ref[:, :, :HD].reshape(TILE_K, HD)
+    v = held_ref[:, :, HD:].reshape(TILE_K, HD)
+    return asked_ref[:, :HD], asked_ref[:, HD:], k, v
 
 
 def scores(c, q, k):
     row = iota((1, TILE_Q), 1)
-    query = ROWS * (row // ROWS_Q) + ROWS_Q * (c // (HEADS * PARTS_K)) + row % ROWS_Q + HALF
+    block = ((row >> 6) & 1) * 8 + ((row >> 7) & 1) + ((row >> 8) & 1) * 4 + (c & 50)
+    query = ROWS * block + (row & 63) + HALF
     col = iota((TILE_K, 1), 0)
-    key = ROWS * (col // ROWS_K) + ROWS_K * (c % PARTS_K) + col % ROWS_K + HALF
+    block = (col >> 8) * 16 + ((col >> 7) & 1) * 8 + ((col >> 6) & 1) * 2 + (c & 5)
+    key = ROWS * block + (col & 63) + HALF
     allowed = (query & (TOTAL - 1)) >= (key & (TOTAL - 1))
     return jnp.where(allowed, dot(k, q, ((1,), (1,))) * (SCALE * LOG2E), NEG)
 
 
-def forward_kernel(c_ref, piece_ref, stats_ref):
-    q, g, k, v = unpack(piece_ref)
+def forward_kernel(c_ref, asked_ref, held_ref, stats_ref):
+    q, g, k, v = unpack(asked_ref, held_ref)
     score = scores(c_ref[0], q, k)
     top = jnp.maximum(jnp.max(score, axis=0, keepdims=True), FLOOR)
     weight = jnp.exp2(score - top)
@@ -172,44 +173,50 @@
         jnp.sum(weight * dprob, axis=0, keepdims=True),
     ]
     rows = jnp.concatenate(rows + [top] * 5, axis=0)
-    for i in range(PARTS_K):
+    for i in range(N_NEAR):
         stats_ref[i] = rows
 
 
-def backward_kernel(c_ref, piece_ref, stats_ref, term_ref):
+def backward_kernel(c_ref, asked_ref, held_ref, stats_ref, term_ref, keep_ref, give_ref):
     tops, sums, dots = (stats_ref[:, i, :] for i in range(3))
     peak = jnp.max(tops, axis=0, keepdims=True)
     each = jnp.exp2(tops - peak)
     norm = jnp.sum(each * sums, axis=0, keepdims=True)
     delta = jnp.sum(each * dots, axis=0, keepdims=True) / norm
     lse = peak + jnp.log(norm) * LOG2E
-    q, g, k, v = unpack(piece_ref)
+    q, g, k, v = unpack(asked_ref, held_ref)
     prob = jnp.exp2(scores(c_ref[0], q, k) - lse)
     dprob = dot(v, g, ((1,), (1,)))
     dscore = (prob * (dprob - delta)).astype(BF)
     prob = prob.astype(BF)
+    d_key = (dot(dscore, q, ((1,), (0,))) * SCALE).astype(BF)
+    d_value = dot(prob, g, ((1,), (0,))).astype(BF)
+    term_ref[:, :, :HD] = d_key.reshape(N_FAR, ROWS, HD)
+    term_ref[:, :, HD:] = d_value.reshape(N_FAR, ROWS, HD)
     d_query = dot(dscore, k, ((0,), (0,))) * SCALE
     out = dot(prob, v, ((0,), (0,)))
-    d_key = dot(dscore, q, ((1,), (0,))) * SCALE
-    d_value = dot(prob, g, ((1,), (0,)))
-    term_ref[:, :ROWS_Q, :] = d_query.reshape(N_CTX, ROWS_Q, HD).astype(BF)
-    term_ref[:, ROWS_Q : 2 * ROWS_Q, :] = out.reshape(N_CTX, ROWS_Q, HD).astype(BF)
-    term_ref[:, 2 * ROWS_Q : 2 * ROWS_Q + ROWS_K, :] = d_key.reshape(N_CTX, ROWS_K, HD).astype(BF)
-    term_ref[:, 2 * ROWS_Q + ROWS_K :, :] = d_value.reshape(N_CTX, ROWS_K, HD).astype(BF)
-
-
-def sum_kernel(term_ref, w_ref, piece_ref, out_ref):
-    terms = term_ref[...].astype(F32).reshape(PARTS_Q, HEADS, PARTS_K, PIECE, HD)
-    asked = jnp.sum(terms[:, :, :, : 2 * ROWS_Q], axis=2)
-    held = jnp.sum(terms[:, :, :, 2 * ROWS_Q :], axis=0)
-
-    def joined(values):
-        return jnp.concatenate([v.reshape(ROWS, HD) for v in values], axis=1).astype(BF)
-
-    d_query = joined([asked[:, e, :ROWS_Q] for e in range(HEADS)])
-    out_ref[...] = joined([asked[:, e, ROWS_Q:] for e in range(HEADS)])
-    d_key = joined([held[e, :, :ROWS_K] for e in range(HEADS)])
-    d_value = joined([held[e, :, ROWS_K:] for e in range(HEADS)])
+    second = ((c_ref[0] >> 2) & 1) == 1
+    half = TILE_Q // 2
+    for value, at in ((d_query, 0), (out, HD)):
+        keep_ref[:, at : at + HD] = jnp.where(second, value[half:], value[:half])
+        give_ref[:, at : at + HD] = jnp.where(second, value[:half], value[half:]).astype(BF)
+
+
+def sum_kernel(c_ref, term_ref, keep_ref, got_ref, w_ref, piece_ref, out_ref):
+    second = ((c_ref[0] >> 3) & 1) == 1
+    keep, got = keep_ref[...].astype(BF), got_ref[...]
+    asked = [jnp.where(second, got, keep), jnp.where(second, keep, got)]
+    d_query = jnp.concatenate([x[:, :HD] for x in asked], axis=1)
+    out_ref[...] = jnp.concatenate([x[:, HD:] for x in asked], axis=1)
+    held = []
+    for e in range(HEADS):
+        total = jnp.zeros((ROWS, 2 * HD), F32)
+        for i in range(N_FAR):
+            if (i >> 1) & 1 == e:
+                total = total + term_ref[i].astype(F32)
+        held.append(total.astype(BF))
+    d_key = jnp.concatenate([x[:, :HD] for x in held], axis=1)
+    d_value = jnp.concatenate([x[:, HD:] for x in held], axis=1)
     part = dot(d_query, w_ref[0], ((1,), (1,)))
     part = part + dot(d_key, w_ref[1], ((1,), (1,)))
     part = (part + dot(d_value, w_ref[2], ((1,), (1,)))).astype(BF)
@@ -260,33 +267,61 @@
     )(c_ref, *ins)
 
 
+def doubled(mine, axis):
+    got = shift(mine, axis, 2, 1)
+    second = lax.axis_index(axis) == 1
+    return jnp.concatenate([jnp.where(second, got, mine), jnp.where(second, mine, got)], axis=0)
+
+
+def halved(keep, got, axis):
+    total = keep + got.astype(F32)
+    half = total.shape[0] // 2
+    second = lax.axis_index(axis) == 1
+    keep = jnp.where(second, total[half:], total[:half])
+    return keep, jnp.where(second, total[:half], total[half:]).astype(BF)
+
+
 def shards(byte_states, patch_of_byte, patch_first, moved, w_qkv, d_attn):
     c_ref = lax.axis_index(CTX).astype(I32).reshape(1)
     n_bytes = patch_of_byte.shape[0]
-    stack = shaped((N_CTX, PIECE, HD), BF)
     place = patch_of_byte.reshape(1, n_bytes)
-
-    sent, own = pool(
-        c_ref, patch_first, moved, place, byte_states, d_attn, w_qkv
-    )
+    pair = shaped((ROWS, 2 * HD), BF)
+    stack = shaped((N_FAR, ROWS, 2 * HD), BF)
+
+    sent, own = pool(c_ref, patch_first, moved, place, byte_states, d_attn, w_qkv)
     (own,) = call(hold_kernel, (own,), (shaped(own.shape, BF),), 100_000)
-    (pieces,) = call(spread_kernel, (own, shift(sent, CTX, N_CTX, -1)), (stack,), 1_000_000)
-    pieces = swap(pieces, CTX)
+    keep, give, held = call(
+        spread_kernel, (c_ref, own, shift(sent, CTX, N_CTX, -1)), (pair, pair, stack), 1_000_000, 1
+    )
+    held = swap(held, FAR)
+    got = shift(give, "zl", 2, 1)
+    second = lax.axis_index("zl") == 1
+    asked = jnp.concatenate([jnp.where(second, got, keep), jnp.where(second, keep, got)], axis=0)
+    asked = doubled(doubled(asked, "xl"), "yl")
     (stats,) = call(
         forward_kernel,
-        (c_ref, pieces),
-        (shaped((PARTS_K, 8, TILE_Q), F32),),
+        (c_ref, asked, held),
+        (shaped((N_NEAR, 8, TILE_Q), F32),),
         300_000_000,
         1,
     )
-    (terms,) = call(
-        backward_kernel, (c_ref, pieces, swap(stats, "x")), (stack,), 900_000_000, 1
-    )
+    half = (TILE_Q // 2, 2 * HD)
+    terms, keep, give = call(
+        backward_kernel,
+        (c_ref, asked, held, swap(stats, NEAR)),
+        (stack, shaped(half, F32), shaped(half, BF)),
+        900_000_000,
+        1,
+    )
+    terms = swap(terms, FAR)
+    keep, give = halved(keep, shift(give, "yl", 2, 1), "xl")
+    keep, give = halved(keep, shift(give, "xl", 2, 1), "zl")
     pieces, out = call(
         sum_kernel,
-        (swap(terms, CTX), w_qkv),
+        (c_ref, terms, keep, shift(give, "zl", 2, 1), w_qkv),
         (shaped((N_TP, ROWS, HD), BF), shaped((ROWS, FEATS), BF)),
         100_000_000,
+        1,
     )
     (both,) = call(
         head_sum_kernel, (swap(pieces, "tp"), out), (shaped((ROWS, HD + FEATS), BF),), 100_000

time: 118 us -> 112 us (0.949)
  blocking collectives: 82.8 us -> 31.4 us
  starting transfers between devices: 17.2 us -> 47.7 us
  waiting for transfers between devices: 7.27 us -> 21.1 us
  Pallas kernels: 8.28 us -> 9.56 us
    all_to_all x4 -> x2, blocking collectives: 82.8 us -> 31.4 us  [swap(): return lax.all_to_all(x, axis, split_axis=0, concat_axis=0, tiled=True)]
    ppermute x2 -> x8, starting transfers between devices: 17.2 us -> 36.9 us  [shift(): return lax.ppermute(x, axis, [(i, (i + by) % n) for i in range(n)])]
    all_to_all x0 -> x2, starting transfers between devices: none -> 10.8 us  [swap(): return lax.all_to_all(x, axis, split_axis=0, concat_axis=0, tiled=True)]
    ppermute x2 -> x8, waiting for transfers between devices: 7.27 us -> 17.8 us  [shift(): return lax.ppermute(x, axis, [(i, (i + by) % n) for i in range(n)])]
    all_to_all x0 -> x2, waiting for transfers between devices: none -> 3.25 us  [swap(): return lax.all_to_all(x, axis, split_axis=0, concat_axis=0, tiled=True)]
    pallas_call x8, Pallas kernels: 5.33 us -> 6.61 us  [call(): pl.pallas_call(kernel, out_shape=tuple(outs), in_specs=[smem] * scalars +...]
  transfers between devices with their start and end apart: 2 -> 10, of which waited for: 2 -> 8; matrix products, arithmetic and copies ran while one was open for 0% -> 0% of each run, Pallas kernels for 1% -> 1%
where the time goes in v5:
time: 112 us
  starting transfers between devices  47.7 us (43%)
  blocking collectives  31.4 us (28%)
  waiting for transfers between devices  21.1 us (19%)
  Pallas kernels  9.56 us (9%)
    ppermute x8, starting transfers between devices, shift(): return lax.ppermute(x, axis, [(i, (i + by) % n) for i in range(n)])  36.9 us
    all_to_all x2, blocking collectives, swap(): return lax.all_to_all(x, axis, split_axis=0, concat_axis=0, tiled=True)  31.4 us
    ppermute x8, waiting for transfers between devices, shift(): return lax.ppermute(x, axis, [(i, (i + by) % n) for i in range(n)])  17.8 us
    all_to_all x2, starting transfers between devices, swap(): return lax.all_to_all(x, axis, split_axis=0, concat_axis=0, tiled=True)  10.8 us
    pallas_call x8, Pallas kernels, call(): pl.pallas_call(kernel, out_shape=tuple(outs), in_specs=[smem] * scalars +...  6.61 us
    all_to_all x2, waiting for transfers between devices, swap(): return lax.all_to_all(x, axis, split_axis=0, concat_axis=0, tiled=True)  3.25 us
    pallas_call x1, Pallas kernels, pool(): pl.pallas_call(pool_kernel, out_shape=(block, block), in_specs=[pl.BlockS...  2.96 us
  transfers between devices with their start and end apart: 10, of which 8 were waited for; matrix products, arithmetic and copies ran while one was open for 0% of the time, Pallas kernels for 1%

profile of v5, /device:TPU:1, one launch (start us, length us, event | category | flops | bytes accessed | tf_op | source)
XLA Modules:
  0.0 111.7 jit_solution(464708376805179937)
XLA Ops:
  0.7 3.0 %shard_map.77 = (bf16[64,1024]{1,0:T(8,128)(2,1)}, bf16[64,1024]{1,0:T(8,128)(2,1)}) custom-call(s32[1]{0:T(128)} %bitcast.c_ref, s32[64]{0:T(128)} %first_ref.1, s32[2,64]{1,0:T(2,128)} %moved_ref.1, s32[1,256]{1,0:T(1,128)} %bitcast.2, bf16[256,1024]{1,0:T(8,128)(2,1)} %bytes_hbm.1, bf16[64,256]{1,0:T(8,128)(2,1)} %grad_hbm.1, bf16[3,1024,256]{2,1,0:T(8,128)(2,1)} %w_ref.1), custom_call_target="tpu_custom_call" | custom-call | flops 300000000 | bytes 2500000 | tf_op jit(solution)/shard_map/pallas_call | solution.py:258
  3.6 14.7 %collective-permute-start = (bf16[64,1024]{1,0:T(8,128)(2,1)}, bf16[64,1024]{1,0:T(8,128)(2,1)S(1)}, u32[]{:S(2)}, u32[]{:S(2)}) collective-permute-start(bf16[64,1024]{1,0:T(8,128)(2,1)} %get-tuple-element.16), channel_id=1, source_target_pairs={{0,504},{8,0},{16,8},{24,16},{32,24},{40,32},{48,40},{56,48},{64,5... | collective-permute-start | bytes 393224 | tf_op jit(solution)/shard_map/ppermute | solution.py:41
  18.3 0.9 copy-done.1
  19.2 1.5 %collective-permute-done.got_ref = bf16[64,1024]{1,0:T(8,128)(2,1)S(1)} collective-permute-done((bf16[64,1024]{1,0:T(8,128)(2,1)}, bf16[64,1024]{1,0:T(8,128)(2,1)S(1)}, u32[]{:S(2)}, u32[]{:S(2)}) %collective-permute-start) | collective-permute-done | bytes 131104 | tf_op jit(solution)/shard_map/ppermute | solution.py:41
  20.8 0.9 shard_map.79
  21.7 1.9 %collective-permute-start.1 = (bf16[64,256]{1,0:T(8,128)(2,1)S(1)}, bf16[64,256]{1,0:T(8,128)(2,1)S(1)}, u32[]{:S(2)}, u32[]{:S(2)}) collective-permute-start(bf16[64,256]{1,0:T(8,128)(2,1)S(1)} %get-tuple-element.17), channel_id=1, source_target_pairs={{0,64},{64,0},{1,65},{65,1},{2,66},{66,2},{3,67},{67,3},{4,68},{68... | collective-permute-start | bytes 98312 | tf_op jit(solution)/shard_map/ppermute | solution.py:41
  23.6 3.9 %all-to-all-start = ((bf16[16,64,256]{2,1,0:T(8,128)(2,1)}), bf16[16,64,256]{2,1,0:T(8,128)(2,1)S(1)}, u32[]{:S(2)}, u32[]{:S(2)}) async-start(bf16[16,64,256]{2,1,0:T(8,128)(2,1)} %get-tuple-element.19), calls=%async_computation | async-start | bytes 1048576 | tf_op jit(solution)/shard_map/all_to_all | solution.py:45
  27.5 0.0 collective-permute-done.1
  27.5 4.3 %collective-permute-start.2 = (bf16[128,256]{1,0:T(8,128)(2,1)S(1)}, bf16[128,256]{1,0:T(8,128)(2,1)S(1)}, u32[]{:S(2)}, u32[]{:S(2)}) collective-permute-start(bf16[128,256]{1,0:T(8,128)(2,1)S(1)} %pad_maximum_fusion.2), channel_id=1, source_target_pairs={{0,8},{8,0},{1,9},{9,1},{2,10},{10,2},{3,11},{11,3},{4,12},{12,4},... | collective-permute-start | bytes 196616 | tf_op jit(solution)/shard_map/ppermute | solution.py:41
  31.9 2.2 %collective-permute-done.2 = bf16[128,256]{1,0:T(8,128)(2,1)S(1)} collective-permute-done((bf16[128,256]{1,0:T(8,128)(2,1)S(1)}, bf16[128,256]{1,0:T(8,128)(2,1)S(1)}, u32[]{:S(2)}, u32[]{:S(2)}) %collective-permute-start.2) | collective-permute-done | bytes 65568 | tf_op jit(solution)/shard_map/ppermute | solution.py:41
  34.2 5.3 %collective-permute-start.3 = (bf16[256,256]{1,0:T(8,128)(2,1)S(1)}, bf16[256,256]{1,0:T(8,128)(2,1)S(1)}, u32[]{:S(2)}, u32[]{:S(2)}) collective-permute-start(bf16[256,256]{1,0:T(8,128)(2,1)S(1)} %pad_maximum_fusion.1), channel_id=1, source_target_pairs={{0,32},{32,0},{1,33},{33,1},{2,34},{34,2},{3,35},{35,3},{4,36},{36... | collective-permute-start | bytes 393224 | tf_op jit(solution)/shard_map/ppermute | solution.py:41
  39.5 2.6 %collective-permute-done.3 = bf16[256,256]{1,0:T(8,128)(2,1)S(1)} collective-permute-done((bf16[256,256]{1,0:T(8,128)(2,1)S(1)}, bf16[256,256]{1,0:T(8,128)(2,1)S(1)}, u32[]{:S(2)}, u32[]{:S(2)}) %collective-permute-start.3) | collective-permute-done | bytes 131104 | tf_op jit(solution)/shard_map/ppermute | solution.py:41
  42.2 1.2 %all-to-all-done.held_ref = bf16[16,64,256]{2,1,0:T(8,128)(2,1)S(1)} async-done(((bf16[16,64,256]{2,1,0:T(8,128)(2,1)}), bf16[16,64,256]{2,1,0:T(8,128)(2,1)S(1)}, u32[]{:S(2)}, u32[]{:S(2)}) %all-to-all-start) | async-done | bytes 524320 | tf_op jit(solution)/shard_map/all_to_all | solution.py:45
  43.4 1.1 shard_map.80
  44.5 10.3 %all_to_all.20.stats_ref = f32[4,8,512]{2,1,0:T(8,128)S(1)} all-to-all(f32[4,8,512]{2,1,0:T(8,128)S(1)} %shard_map.80), channel_id=1, replica_groups=mesh['zh'=4,'zl'=2,'yl'=2,'xh'=2,'xl'=2,'tp'=8] {'yl','xl'}, dimensions={0} | all-to-all | bytes 131072 | tf_op jit(solution)/shard_map/all_to_all | solution.py:45
  54.8 2.4 %shard_map.81 = (bf16[16,64,256]{2,1,0:T(8,128)(2,1)}, f32[256,256]{1,0:T(8,128)S(1)}, bf16[256,256]{1,0:T(8,128)(2,1)S(1)}) custom-call(s32[1]{0:T(128)} %bitcast.c_ref, bf16[512,256]{1,0:T(8,128)(2,1)S(1)} %pad_maximum_fusion.asked_ref, bf16[16,64,256]{2,1,0:T(8,128)(2,1)S(1)} %all-to-all-done.held_ref, f32[4,8,512]{2,1,0:T(8,128)S(1)} %all_to_all.20.stats_ref), custom_call_target="tpu_custom_call" | custom-call | flops 900000000 | bytes 1769476 | tf_op jit(solution)/shard_map/pallas_call | solution.py:56
  57.2 2.5 %collective-permute-start.4 = (bf16[256,256]{1,0:T(8,128)(2,1)S(1)}, bf16[256,256]{1,0:T(8,128)(2,1)S(1)}, u32[]{:S(2)}, u32[]{:S(2)}) collective-permute-start(bf16[256,256]{1,0:T(8,128)(2,1)S(1)} %get-tuple-element.22), channel_id=1, source_target_pairs={{0,32},{32,0},{1,33},{33,1},{2,34},{34,2},{3,35},{35,3},{4,36},{36... | collective-permute-start | bytes 393224 | tf_op jit(solution)/shard_map/ppermute | solution.py:41
  59.7 6.9 %all-to-all-start.2 = ((bf16[16,64,256]{2,1,0:T(8,128)(2,1)}), bf16[16,64,256]{2,1,0:T(8,128)(2,1)S(1)}, u32[]{:S(2)}, u32[]{:S(2)}) async-start(bf16[16,64,256]{2,1,0:T(8,128)(2,1)} %get-tuple-element.20), calls=%async_computation.2 | async-start | bytes 1048576 | tf_op jit(solution)/shard_map/all_to_all | solution.py:45
  66.6 1.9 %collective-permute-start.5 = (bf16[128,256]{1,0:T(8,128)(2,1)S(1)}, bf16[128,256]{1,0:T(8,128)(2,1)S(1)}, u32[]{:S(2)}, u32[]{:S(2)}) collective-permute-start(bf16[128,256]{1,0:T(8,128)(2,1)S(1)} %select_convert_fusion), channel_id=1, source_target_pairs={{0,8},{8,0},{1,9},{9,1},{2,10},{10,2},{3,11},{11,3},{4,12},{12,4},... | collective-permute-start | bytes 196616 | tf_op jit(solution)/shard_map/ppermute | solution.py:41
  68.6 3.1 %collective-permute-done.5 = bf16[128,256]{1,0:T(8,128)(2,1)S(1)} collective-permute-done((bf16[128,256]{1,0:T(8,128)(2,1)S(1)}, bf16[128,256]{1,0:T(8,128)(2,1)S(1)}, u32[]{:S(2)}, u32[]{:S(2)}) %collective-permute-start.5) | collective-permute-done | bytes 65568 | tf_op jit(solution)/shard_map/ppermute | solution.py:41
  71.7 0.0 copy-start.2
  71.7 0.0 copy-start.3
  71.7 0.0 copy-start.4
  71.7 4.0 %collective-permute-start.6 = (bf16[64,256]{1,0:T(8,128)(2,1)S(1)}, bf16[64,256]{1,0:T(8,128)(2,1)S(1)}, u32[]{:S(2)}, u32[]{:S(2)}) collective-permute-start(bf16[64,256]{1,0:T(8,128)(2,1)S(1)} %select_convert_fusion.1), channel_id=1, source_target_pairs={{0,64},{64,0},{1,65},{65,1},{2,66},{66,2},{3,67},{67,3},{4,68},{68... | collective-permute-start | bytes 98312 | tf_op jit(solution)/shard_map/ppermute | solution.py:41
  75.7 2.4 %collective-permute-done.6.got_ref = bf16[64,256]{1,0:T(8,128)(2,1)S(1)} collective-permute-done((bf16[64,256]{1,0:T(8,128)(2,1)S(1)}, bf16[64,256]{1,0:T(8,128)(2,1)S(1)}, u32[]{:S(2)}, u32[]{:S(2)}) %collective-permute-start.6) | collective-permute-done | bytes 32800 | tf_op jit(solution)/shard_map/ppermute | solution.py:41
  78.1 2.1 %all-to-all-done.2.term_ref = bf16[16,64,256]{2,1,0:T(8,128)(2,1)S(1)} async-done(((bf16[16,64,256]{2,1,0:T(8,128)(2,1)}), bf16[16,64,256]{2,1,0:T(8,128)(2,1)S(1)}, u32[]{:S(2)}, u32[]{:S(2)}) %all-to-all-start.2) | async-done | bytes 524320 | tf_op jit(solution)/shard_map/all_to_all | solution.py:45
  80.2 0.6 shard_map.82
  80.8 21.1 %all_to_all.21.pieces_ref = bf16[8,64,128]{2,1,0:T(8,128)(2,1)S(1)} all-to-all(bf16[8,64,128]{2,1,0:T(8,128)(2,1)S(1)} %get-tuple-element.23), channel_id=1, replica_groups=mesh['zh'=4,'zl'=2,'yl'=2,'xh'=2,'xl'=2,'tp'=8] {'tp'}, dimensions={0} | all-to-all | bytes 262144 | tf_op jit(solution)/shard_map/all_to_all | solution.py:45
  101.9 2.3 %collective-permute-start.7 = (bf16[64,384]{1,0:T(8,128)(2,1)S(1)}, bf16[64,384]{1,0:T(8,128)(2,1)S(1)}, u32[]{:S(2)}, u32[]{:S(2)}) collective-permute-start(bf16[64,384]{1,0:T(8,128)(2,1)S(1)} %shard_map.83.own_ref), channel_id=1, source_target_pairs={{0,8},{8,16},{16,24},{24,32},{32,40},{40,48},{48,56},{56,64},{64,7... | collective-permute-start | bytes 147464 | tf_op jit(solution)/shard_map/ppermute | solution.py:41
  104.2 0.8 shard_map.84
  105.0 5.9 %collective-permute-done.7.before_ref = bf16[64,384]{1,0:T(8,128)(2,1)S(1)} collective-permute-done((bf16[64,384]{1,0:T(8,128)(2,1)S(1)}, bf16[64,384]{1,0:T(8,128)(2,1)S(1)}, u32[]{:S(2)}, u32[]{:S(2)}) %collective-permute-start.7) | collective-permute-done | bytes 49184 | tf_op jit(solution)/shard_map/ppermute | solution.py:41
  110.9 0.8 shard_map.85
  (20 shorter events, 0.2 us)
Async XLA Ops:
  3.6 17.2 %collective-permute-start = (bf16[64,1024]{1,0:T(8,128)(2,1)}, bf16[64,1024]{1,0:T(8,128)(2,1)S(1)}, u32[]{:S(2)}, u32[]{:S(2)}) collective-permute-start(bf16[64,1024]{1,0:T(8,128)(2,1)} %get-tuple-element.16), channel_id=1, source_target_pairs={{0,504},{8,0},{16,8},{24,16},{32,24},{40,32},{48,40},{56,48},{64,5... | collective-permute-start | bytes 393224 | tf_op jit(solution)/shard_map/ppermute | solution.py:41
  18.3 0.9 copy-start.1
  21.7 5.8 %collective-permute-start.1 = (bf16[64,256]{1,0:T(8,128)(2,1)S(1)}, bf16[64,256]{1,0:T(8,128)(2,1)S(1)}, u32[]{:S(2)}, u32[]{:S(2)}) collective-permute-start(bf16[64,256]{1,0:T(8,128)(2,1)S(1)} %get-tuple-element.17), channel_id=1, source_target_pairs={{0,64},{64,0},{1,65},{65,1},{2,66},{66,2},{3,67},{67,3},{4,68},{68... | collective-permute-start | bytes 98312 | tf_op jit(solution)/shard_map/ppermute | solution.py:41
  23.6 19.8 %all-to-all-start = ((bf16[16,64,256]{2,1,0:T(8,128)(2,1)}), bf16[16,64,256]{2,1,0:T(8,128)(2,1)S(1)}, u32[]{:S(2)}, u32[]{:S(2)}) async-start(bf16[16,64,256]{2,1,0:T(8,128)(2,1)} %get-tuple-element.19), calls=%async_computation | async-start | bytes 1048576 | tf_op jit(solution)/shard_map/all_to_all | solution.py:45
  27.5 6.6 %collective-permute-start.2 = (bf16[128,256]{1,0:T(8,128)(2,1)S(1)}, bf16[128,256]{1,0:T(8,128)(2,1)S(1)}, u32[]{:S(2)}, u32[]{:S(2)}) collective-permute-start(bf16[128,256]{1,0:T(8,128)(2,1)S(1)} %pad_maximum_fusion.2), channel_id=1, source_target_pairs={{0,8},{8,0},{1,9},{9,1},{2,10},{10,2},{3,11},{11,3},{4,12},{12,4},... | collective-permute-start | bytes 196616 | tf_op jit(solution)/shard_map/ppermute | solution.py:41
  34.2 8.0 %collective-permute-start.3 = (bf16[256,256]{1,0:T(8,128)(2,1)S(1)}, bf16[256,256]{1,0:T(8,128)(2,1)S(1)}, u32[]{:S(2)}, u32[]{:S(2)}) collective-permute-start(bf16[256,256]{1,0:T(8,128)(2,1)S(1)} %pad_maximum_fusion.1), channel_id=1, source_target_pairs={{0,32},{32,0},{1,33},{33,1},{2,34},{34,2},{3,35},{35,3},{4,36},{36... | collective-permute-start | bytes 393224 | tf_op jit(solution)/shard_map/ppermute | solution.py:41
  57.2 23.0 %copy-start = (bf16[3,1024,256]{2,1,0:T(8,128)(2,1)S(1)}, bf16[3,1024,256]{2,1,0:T(8,128)(2,1)}, u32[]{:S(2)}) copy-start(bf16[3,1024,256]{2,1,0:T(8,128)(2,1)} %w_ref.1) | copy-start | bytes 4718596
  57.2 9.4 %collective-permute-start.4 = (bf16[256,256]{1,0:T(8,128)(2,1)S(1)}, bf16[256,256]{1,0:T(8,128)(2,1)S(1)}, u32[]{:S(2)}, u32[]{:S(2)}) collective-permute-start(bf16[256,256]{1,0:T(8,128)(2,1)S(1)} %get-tuple-element.22), channel_id=1, source_target_pairs={{0,32},{32,0},{1,33},{33,1},{2,34},{34,2},{3,35},{35,3},{4,36},{36... | collective-permute-start | bytes 393224 | tf_op jit(solution)/shard_map/ppermute | solution.py:41
  59.7 20.5 %all-to-all-start.2 = ((bf16[16,64,256]{2,1,0:T(8,128)(2,1)}), bf16[16,64,256]{2,1,0:T(8,128)(2,1)S(1)}, u32[]{:S(2)}, u32[]{:S(2)}) async-start(bf16[16,64,256]{2,1,0:T(8,128)(2,1)} %get-tuple-element.20), calls=%async_computation.2 | async-start | bytes 1048576 | tf_op jit(solution)/shard_map/all_to_all | solution.py:45
  66.6 5.0 %collective-permute-start.5 = (bf16[128,256]{1,0:T(8,128)(2,1)S(1)}, bf16[128,256]{1,0:T(8,128)(2,1)S(1)}, u32[]{:S(2)}, u32[]{:S(2)}) collective-permute-start(bf16[128,256]{1,0:T(8,128)(2,1)S(1)} %select_convert_fusion), channel_id=1, source_target_pairs={{0,8},{8,0},{1,9},{9,1},{2,10},{10,2},{3,11},{11,3},{4,12},{12,4},... | collective-permute-start | bytes 196616 | tf_op jit(solution)/shard_map/ppermute | solution.py:41
  71.7 32.5 %copy-start.2 = (s32[2,64]{1,0:T(2,128)S(1)}, s32[2,64]{1,0:T(2,128)}, u32[]{:S(2)}) copy-start(s32[2,64]{1,0:T(2,128)} %moved_ref.1) | copy-start | bytes 1540
  71.7 32.5 %copy-start.3 = (s32[256]{0:T(256)S(1)}, s32[256]{0:T(256)}, u32[]{:S(2)}) copy-start(s32[256]{0:T(256)} %param.7) | copy-start | bytes 3076
  71.7 32.5 %copy-start.4 = (s32[64]{0:T(128)S(1)}, s32[64]{0:T(128)}, u32[]{:S(2)}) copy-start(s32[64]{0:T(128)} %first_ref.1) | copy-start | bytes 772
  71.7 6.4 %collective-permute-start.6 = (bf16[64,256]{1,0:T(8,128)(2,1)S(1)}, bf16[64,256]{1,0:T(8,128)(2,1)S(1)}, u32[]{:S(2)}, u32[]{:S(2)}) collective-permute-start(bf16[64,256]{1,0:T(8,128)(2,1)S(1)} %select_convert_fusion.1), channel_id=1, source_target_pairs={{0,64},{64,0},{1,65},{65,1},{2,66},{66,2},{3,67},{67,3},{4,68},{68... | collective-permute-start | bytes 98312 | tf_op jit(solution)/shard_map/ppermute | solution.py:41
  101.9 9.1 %collective-permute-start.7 = (bf16[64,384]{1,0:T(8,128)(2,1)S(1)}, bf16[64,384]{1,0:T(8,128)(2,1)S(1)}, u32[]{:S(2)}, u32[]{:S(2)}) collective-permute-start(bf16[64,384]{1,0:T(8,128)(2,1)S(1)} %shard_map.83.own_ref), channel_id=1, source_target_pairs={{0,8},{8,16},{16,24},{24,32},{32,40},{40,48},{48,56},{56,64},{64,7... | collective-permute-start | bytes 147464 | tf_op jit(solution)/shard_map/ppermute | solution.py:41

commit v6 on v5

--- a/solution.py
+++ b/solution.py
@@ -130,18 +130,23 @@
     held_ref[...] = own_ref[...]
 
 
-def spread_kernel(c_ref, own_ref, got_ref, keep_ref, give_ref, held_ref):
+def spread_kernel(own_ref, got_ref, asked_ref, held_ref):
     both = own_ref[...] + got_ref[...]
-    asked, held = [], []
+    held = []
     for e in range(HEADS):
         q, g, k, v = (columns(both, kind, e) for kind in range(4))
-        asked.append(jnp.concatenate([q, g], axis=1))
+        asked_ref[e] = jnp.concatenate([q, g], axis=1)
         held.append(jnp.concatenate([k, v], axis=1))
-    second = ((c_ref[0] >> 3) & 1) == 1
-    keep_ref[...] = jnp.where(second, asked[1], asked[0])
-    give_ref[...] = jnp.where(second, asked[0], asked[1])
     for i in range(N_FAR):
         held_ref[i] = held[(i >> 1) & 1]
+
+
+def near_index(c):
+    return ((c >> 2) & 1) * 2 + (c & 1)
+
+
+def quarter(at):
+    return pl.ds(pl.multiple_of(at * (TILE_Q // N_NEAR), TILE_Q // N_NEAR), TILE_Q // N_NEAR)
 
 
 def unpack(asked_ref, held_ref):
@@ -152,7 +157,7 @@
 
 def scores(c, q, k):
     row = iota((1, TILE_Q), 1)
-    block = ((row >> 6) & 1) * 8 + ((row >> 7) & 1) + ((row >> 8) & 1) * 4 + (c & 50)
+    block = ((row >> 6) & 1) * 8 + ((row >> 7) & 1) + (row >> 8) * 4 + (c & 50)
     query = ROWS * block + (row & 63) + HALF
     col = iota((TILE_K, 1), 0)
     block = (col >> 8) * 16 + ((col >> 7) & 1) * 8 + ((col >> 6) & 1) * 2 + (c & 5)
@@ -161,7 +166,10 @@
     return jnp.where(allowed, dot(k, q, ((1,), (1,))) * (SCALE * LOG2E), NEG)
 
 
-def forward_kernel(c_ref, asked_ref, held_ref, stats_ref):
+def forward_kernel(c_ref, mine_ref, one_ref, two_ref, three_ref, held_ref, stats_ref, asked_ref):
+    me = near_index(c_ref[0])
+    for k, ref in enumerate((mine_ref, one_ref, two_ref, three_ref)):
+        asked_ref[quarter(me ^ k), :] = ref[...]
     q, g, k, v = unpack(asked_ref, held_ref)
     score = scores(c_ref[0], q, k)
     top = jnp.maximum(jnp.max(score, axis=0, keepdims=True), FLOOR)
@@ -177,7 +185,7 @@
         stats_ref[i] = rows
 
 
-def backward_kernel(c_ref, asked_ref, held_ref, stats_ref, term_ref, keep_ref, give_ref):
+def backward_kernel(c_ref, asked_ref, held_ref, stats_ref, term_ref, grad_ref):
     tops, sums, dots = (stats_ref[:, i, :] for i in range(3))
     peak = jnp.max(tops, axis=0, keepdims=True)
     each = jnp.exp2(tops - peak)
@@ -193,18 +201,29 @@
     d_value = dot(prob, g, ((1,), (0,))).astype(BF)
     term_ref[:, :, :HD] = d_key.reshape(N_FAR, ROWS, HD)
     term_ref[:, :, HD:] = d_value.reshape(N_FAR, ROWS, HD)
-    d_query = dot(dscore, k, ((0,), (0,))) * SCALE
-    out = dot(prob, v, ((0,), (0,)))
-    second = ((c_ref[0] >> 2) & 1) == 1
-    half = TILE_Q // 2
-    for value, at in ((d_query, 0), (out, HD)):
-        keep_ref[:, at : at + HD] = jnp.where(second, value[half:], value[:half])
-        give_ref[:, at : at + HD] = jnp.where(second, value[:half], value[half:]).astype(BF)
+    grad_ref[:, :HD] = dot(dscore, k, ((0,), (0,))) * SCALE
+    grad_ref[:, HD:] = dot(prob, v, ((0,), (0,)))
+
+
+def part_kernel(c_ref, grad_ref, keep_ref, one_ref, two_ref, three_ref):
+    me = near_index(c_ref[0])
+    keep_ref[...] = grad_ref[quarter(me), :]
+    for k, ref in ((1, one_ref), (2, two_ref), (3, three_ref)):
+        ref[...] = grad_ref[quarter(me ^ k), :].astype(BF)
+
+
+def join_kernel(c_ref, keep_ref, one_ref, two_ref, three_ref, rest_ref, give_ref):
+    total = keep_ref[...]
+    for ref in (one_ref, two_ref, three_ref):
+        total = total + ref[...].astype(F32)
+    second = ((c_ref[0] >> 3) & 1) == 1
+    rest_ref[...] = jnp.where(second, total[ROWS:], total[:ROWS]).astype(BF)
+    give_ref[...] = jnp.where(second, total[:ROWS], total[ROWS:]).astype(BF)
 
 
 def sum_kernel(c_ref, term_ref, keep_ref, got_ref, w_ref, piece_ref, out_ref):
     second = ((c_ref[0] >> 3) & 1) == 1
-    keep, got = keep_ref[...].astype(BF), got_ref[...]
+    keep, got = keep_ref[...], got_ref[...]
     asked = [jnp.where(second, got, keep), jnp.where(second, keep, got)]
     d_query = jnp.concatenate([x[:, :HD] for x in asked], axis=1)
     out_ref[...] = jnp.concatenate([x[:, HD:] for x in asked], axis=1)
@@ -267,18 +286,8 @@
     )(c_ref, *ins)
 
 
-def doubled(mine, axis):
-    got = shift(mine, axis, 2, 1)
-    second = lax.axis_index(axis) == 1
-    return jnp.concatenate([jnp.where(second, got, mine), jnp.where(second, mine, got)], axis=0)
-
-
-def halved(keep, got, axis):
-    total = keep + got.astype(F32)
-    half = total.shape[0] // 2
-    second = lax.axis_index(axis) == 1
-    keep = jnp.where(second, total[half:], total[:half])
-    return keep, jnp.where(second, total[:half], total[half:]).astype(BF)
+def across(x, k):
+    return lax.ppermute(x, NEAR, [(i, i ^ k) for i in range(N_NEAR)])
 
 
 def shards(byte_states, patch_of_byte, patch_first, moved, w_qkv, d_attn):
@@ -290,32 +299,43 @@
 
     sent, own = pool(c_ref, patch_first, moved, place, byte_states, d_attn, w_qkv)
     (own,) = call(hold_kernel, (own,), (shaped(own.shape, BF),), 100_000)
-    keep, give, held = call(
-        spread_kernel, (c_ref, own, shift(sent, CTX, N_CTX, -1)), (pair, pair, stack), 1_000_000, 1
+    asked, held = call(
+        spread_kernel,
+        (own, shift(sent, CTX, N_CTX, -1)),
+        (shaped((HEADS, ROWS, 2 * HD), BF), stack),
+        1_000_000,
     )
     held = swap(held, FAR)
-    got = shift(give, "zl", 2, 1)
     second = lax.axis_index("zl") == 1
-    asked = jnp.concatenate([jnp.where(second, got, keep), jnp.where(second, keep, got)], axis=0)
-    asked = doubled(doubled(asked, "xl"), "yl")
-    (stats,) = call(
+    keep = jnp.where(second, asked[1], asked[0])
+    got = shift(jnp.where(second, asked[0], asked[1]), "zl", 2, 1)
+    mine = jnp.concatenate([jnp.where(second, got, keep), jnp.where(second, keep, got)], axis=0)
+    stats, asked = call(
         forward_kernel,
-        (c_ref, asked, held),
-        (shaped((N_NEAR, 8, TILE_Q), F32),),
+        (c_ref, mine, across(mine, 1), across(mine, 2), across(mine, 3), held),
+        (shaped((N_NEAR, 8, TILE_Q), F32), shaped((TILE_Q, 2 * HD), BF)),
         300_000_000,
         1,
     )
-    half = (TILE_Q // 2, 2 * HD)
-    terms, keep, give = call(
+    terms, grads = call(
         backward_kernel,
         (c_ref, asked, held, swap(stats, NEAR)),
-        (stack, shaped(half, F32), shaped(half, BF)),
+        (stack, shaped((TILE_Q, 2 * HD), F32)),
         900_000_000,
         1,
     )
     terms = swap(terms, FAR)
-    keep, give = halved(keep, shift(give, "yl", 2, 1), "xl")
-    keep, give = halved(keep, shift(give, "xl", 2, 1), "zl")
+    part = shaped((TILE_Q // N_NEAR, 2 * HD), BF)
+    keep, one, two, three = call(
+        part_kernel, (c_ref, grads), (shaped(part.shape, F32), part, part, part), 1_000_000, 1
+    )
+    keep, give = call(
+        join_kernel,
+        (c_ref, keep, across(one, 1), across(two, 2), across(three, 3)),
+        (pair, pair),
+        1_000_000,
+        1,
+    )
     pieces, out = call(
         sum_kernel,
         (c_ref, terms, keep, shift(give, "zl", 2, 1), w_qkv),

time: 112 us -> 120 us (1.071)
  starting transfers between devices: 47.7 us -> 56.8 us
  blocking collectives: 31.4 us -> 27.2 us
  waiting for transfers between devices: 21.1 us -> 24.3 us
    ppermute x0 -> x6, starting transfers between devices: none -> 19.2 us  [across(): return lax.ppermute(x, NEAR, [(i, i ^ k) for i in range(N_NEAR)])]
    ppermute x8 -> x4, starting transfers between devices: 36.9 us -> 24.8 us  [shift(): return lax.ppermute(x, axis, [(i, (i + by) % n) for i in range(n)])]
    ppermute x0 -> x6, waiting for transfers between devices: none -> 6.06 us  [across(): return lax.ppermute(x, NEAR, [(i, i ^ k) for i in range(N_NEAR)])]
    all_to_all x2, blocking collectives: 31.4 us -> 27.2 us  [swap(): return lax.all_to_all(x, axis, split_axis=0, concat_axis=0, tiled=True)]
    all_to_all x2, waiting for transfers between devices: 3.25 us -> 0.01 us  [swap(): return lax.all_to_all(x, axis, split_axis=0, concat_axis=0, tiled=True)]
    all_to_all x2, starting transfers between devices: 10.8 us -> 12.8 us  [swap(): return lax.all_to_all(x, axis, split_axis=0, concat_axis=0, tiled=True)]
    ppermute x8 -> x4, waiting for transfers between devices: 17.8 us -> 18.2 us  [shift(): return lax.ppermute(x, axis, [(i, (i + by) % n) for i in range(n)])]
    pallas_call x8 -> x10, Pallas kernels: 6.61 us -> 6.71 us  [call(): pl.pallas_call(kernel, out_shape=tuple(outs), in_specs=[smem] * scalars +...]
  transfers between devices with their start and end apart: 10 -> 12, of which waited for: 8 -> 6; matrix products, arithmetic and copies ran while one was open for 0% -> 0% of each run, Pallas kernels for 1% -> 1%
where the time goes in v6:
time: 120 us
  starting transfers between devices  56.8 us (47%)
  blocking collectives  27.2 us (23%)
  waiting for transfers between devices  24.3 us (20%)
  Pallas kernels  9.64 us (8%)
    all_to_all x2, blocking collectives, swap(): return lax.all_to_all(x, axis, split_axis=0, concat_axis=0, tiled=True)  27.2 us
    ppermute x4, starting transfers between devices, shift(): return lax.ppermute(x, axis, [(i, (i + by) % n) for i in range(n)])  24.8 us
    ppermute x6, starting transfers between devices, across(): return lax.ppermute(x, NEAR, [(i, i ^ k) for i in range(N_NEAR)])  19.2 us
    ppermute x4, waiting for transfers between devices, shift(): return lax.ppermute(x, axis, [(i, (i + by) % n) for i in range(n)])  18.2 us
    all_to_all x2, starting transfers between devices, swap(): return lax.all_to_all(x, axis, split_axis=0, concat_axis=0, tiled=True)  12.8 us
    pallas_call x10, Pallas kernels, call(): pl.pallas_call(kernel, out_shape=tuple(outs), in_specs=[smem] * scalars +...  6.71 us
    ppermute x6, waiting for transfers between devices, across(): return lax.ppermute(x, NEAR, [(i, i ^ k) for i in range(N_NEAR)])  6.06 us
    pallas_call x1, Pallas kernels, pool(): pl.pallas_call(pool_kernel, out_shape=(block, block), in_specs=[pl.BlockS...  2.94 us
  transfers between devices with their start and end apart: 12, of which 6 were waited for; matrix products, arithmetic and copies ran while one was open for 0% of the time, Pallas kernels for 1%

profile of v6, /device:TPU:1, one launch (start us, length us, event | category | flops | bytes accessed | tf_op | source)
XLA Modules:
  0.0 119.7 jit_solution(3702963312124779814)
XLA Ops:
  0.6 2.9 %shard_map.77 = (bf16[64,1024]{1,0:T(8,128)(2,1)}, bf16[64,1024]{1,0:T(8,128)(2,1)}) custom-call(s32[1]{0:T(128)} %bitcast.c_ref, s32[64]{0:T(128)} %first_ref.1, s32[2,64]{1,0:T(2,128)} %moved_ref.1, s32[1,256]{1,0:T(1,128)} %bitcast.7, bf16[256,1024]{1,0:T(8,128)(2,1)} %bytes_hbm.1, bf16[64,256]{1,0:T(8,128)(2,1)} %grad_hbm.1, bf16[3,1024,256]{2,1,0:T(8,128)(2,1)} %w_ref.1), custom_call_target="tpu_custom_call" | custom-call | flops 300000000 | bytes 2500000 | tf_op jit(solution)/shard_map/pallas_call | solution.py:277
  3.6 14.7 %collective-permute-start = (bf16[64,1024]{1,0:T(8,128)(2,1)}, bf16[64,1024]{1,0:T(8,128)(2,1)S(1)}, u32[]{:S(2)}, u32[]{:S(2)}) collective-permute-start(bf16[64,1024]{1,0:T(8,128)(2,1)} %get-tuple-element.22), channel_id=1, source_target_pairs={{0,504},{8,0},{16,8},{24,16},{32,24},{40,32},{48,40},{56,48},{64,5... | collective-permute-start | bytes 393224 | tf_op jit(solution)/shard_map/ppermute | solution.py:41
  18.3 0.9 copy-done.1
  19.2 1.5 %collective-permute-done.got_ref = bf16[64,1024]{1,0:T(8,128)(2,1)S(1)} collective-permute-done((bf16[64,1024]{1,0:T(8,128)(2,1)}, bf16[64,1024]{1,0:T(8,128)(2,1)S(1)}, u32[]{:S(2)}, u32[]{:S(2)}) %collective-permute-start) | collective-permute-done | bytes 131104 | tf_op jit(solution)/shard_map/ppermute | solution.py:41
  20.8 0.9 shard_map.79
  21.6 3.6 %all-to-all-start = ((bf16[16,64,256]{2,1,0:T(8,128)(2,1)}), bf16[16,64,256]{2,1,0:T(8,128)(2,1)S(1)}, u32[]{:S(2)}, u32[]{:S(2)}) async-start(bf16[16,64,256]{2,1,0:T(8,128)(2,1)} %get-tuple-element.24), calls=%async_computation | async-start | bytes 1048576 | tf_op jit(solution)/shard_map/all_to_all | solution.py:45
  25.2 3.2 %collective-permute-start.1 = (bf16[64,256]{1,0:T(8,128)(2,1)S(1)}, bf16[64,256]{1,0:T(8,128)(2,1)S(1)}, u32[]{:S(2)}, u32[]{:S(2)}) collective-permute-start(bf16[64,256]{1,0:T(8,128)(2,1)S(1)} %select_bitcast_fusion), channel_id=1, source_target_pairs={{0,64},{64,0},{1,65},{65,1},{2,66},{66,2},{3,67},{67,3},{4,68},{68... | collective-permute-start | bytes 98312 | tf_op jit(solution)/shard_map/ppermute | solution.py:41
  28.4 10.1 %collective-permute-done.1 = bf16[64,256]{1,0:T(8,128)(2,1)S(1)} collective-permute-done((bf16[64,256]{1,0:T(8,128)(2,1)S(1)}, bf16[64,256]{1,0:T(8,128)(2,1)S(1)}, u32[]{:S(2)}, u32[]{:S(2)}) %collective-permute-start.1) | collective-permute-done | bytes 32800 | tf_op jit(solution)/shard_map/ppermute | solution.py:41
  38.5 3.5 %collective-permute-start.2 = (bf16[128,256]{1,0:T(8,128)(2,1)S(1)}, bf16[128,256]{1,0:T(8,128)(2,1)S(1)}, u32[]{:S(2)}, u32[]{:S(2)}) collective-permute-start(bf16[128,256]{1,0:T(8,128)(2,1)S(1)} %pad_maximum_fusion.mine_ref), channel_id=1, source_target_pairs={{0,8},{8,0},{32,40},{40,32},{1,9},{9,1},{33,41},{41,33},{2,10},{10... | collective-permute-start | bytes 196616 | tf_op jit(solution)/shard_map/ppermute | solution.py:290
  42.0 5.3 %collective-permute-start.3 = (bf16[128,256]{1,0:T(8,128)(2,1)S(1)}, bf16[128,256]{1,0:T(8,128)(2,1)S(1)}, u32[]{:S(2)}, u32[]{:S(2)}) collective-permute-start(bf16[128,256]{1,0:T(8,128)(2,1)S(1)} %pad_maximum_fusion.mine_ref), channel_id=1, source_target_pairs={{0,32},{8,40},{32,0},{40,8},{1,33},{9,41},{33,1},{41,9},{2,34},{10... | collective-permute-start | bytes 196616 | tf_op jit(solution)/shard_map/ppermute | solution.py:290
  47.4 1.9 %collective-permute-start.4 = (bf16[128,256]{1,0:T(8,128)(2,1)S(1)}, bf16[128,256]{1,0:T(8,128)(2,1)S(1)}, u32[]{:S(2)}, u32[]{:S(2)}) collective-permute-start(bf16[128,256]{1,0:T(8,128)(2,1)S(1)} %pad_maximum_fusion.mine_ref), channel_id=1, source_target_pairs={{0,40},{8,32},{32,8},{40,0},{1,41},{9,33},{33,9},{41,1},{2,42},{10... | collective-permute-start | bytes 196616 | tf_op jit(solution)/shard_map/ppermute | solution.py:290
  49.3 0.0 collective-permute-done.2.one_ref
  49.3 4.0 %collective-permute-done.4.three_ref = bf16[128,256]{1,0:T(8,128)(2,1)S(1)} collective-permute-done((bf16[128,256]{1,0:T(8,128)(2,1)S(1)}, bf16[128,256]{1,0:T(8,128)(2,1)S(1)}, u32[]{:S(2)}, u32[]{:S(2)}) %collective-permute-start.4) | collective-permute-done | bytes 65568 | tf_op jit(solution)/shard_map/ppermute | solution.py:290
  53.3 1.1 shard_map.80
  54.4 6.1 %all_to_all.20.stats_ref = f32[4,8,512]{2,1,0:T(8,128)S(1)} all-to-all(f32[4,8,512]{2,1,0:T(8,128)S(1)} %get-tuple-element.26), channel_id=1, replica_groups=mesh['zh'=4,'zl'=2,'yl'=2,'xh'=2,'xl'=2,'tp'=8] {'yl','xl'}, dimensions={0} | all-to-all | bytes 131072 | tf_op jit(solution)/shard_map/all_to_all | solution.py:45
  60.4 2.4 %shard_map.81 = (bf16[16,64,256]{2,1,0:T(8,128)(2,1)}, f32[512,256]{1,0:T(8,128)S(1)}) custom-call(s32[1]{0:T(128)} %bitcast.c_ref, bf16[512,256]{1,0:T(8,128)(2,1)S(1)} %get-tuple-element.25.asked_ref, bf16[16,64,256]{2,1,0:T(8,128)(2,1)S(1)} %all-to-all-done.held_ref, f32[4,8,512]{2,1,0:T(8,128)S(1)} %all_to_all.20.stats_ref), custom_call_target="tpu_custom_call" | custom-call | flops 900000000 | bytes 1900548 | tf_op jit(solution)/shard_map/pallas_call | solution.py:56
  62.9 9.2 %all-to-all-start.2 = ((bf16[16,64,256]{2,1,0:T(8,128)(2,1)}), bf16[16,64,256]{2,1,0:T(8,128)(2,1)S(1)}, u32[]{:S(2)}, u32[]{:S(2)}) async-start(bf16[16,64,256]{2,1,0:T(8,128)(2,1)} %get-tuple-element.27), calls=%async_computation.2 | async-start | bytes 1048576 | tf_op jit(solution)/shard_map/all_to_all | solution.py:45
  72.1 0.0 copy-start.2
  72.2 0.0 copy-start.3
  72.2 0.0 copy-start.4
  72.2 2.1 %collective-permute-start.5 = (bf16[128,256]{1,0:T(8,128)(2,1)S(1)}, bf16[128,256]{1,0:T(8,128)(2,1)S(1)}, u32[]{:S(2)}, u32[]{:S(2)}) collective-permute-start(bf16[128,256]{1,0:T(8,128)(2,1)S(1)} %get-tuple-element.30), channel_id=1, source_target_pairs={{0,8},{8,0},{32,40},{40,32},{1,9},{9,1},{33,41},{41,33},{2,10},{10... | collective-permute-start | bytes 196616 | tf_op jit(solution)/shard_map/ppermute | solution.py:290
  74.2 2.4 %collective-permute-start.6 = (bf16[128,256]{1,0:T(8,128)(2,1)S(1)}, bf16[128,256]{1,0:T(8,128)(2,1)S(1)}, u32[]{:S(2)}, u32[]{:S(2)}) collective-permute-start(bf16[128,256]{1,0:T(8,128)(2,1)S(1)} %get-tuple-element.31), channel_id=1, source_target_pairs={{0,32},{8,40},{32,0},{40,8},{1,33},{9,41},{33,1},{41,9},{2,34},{10... | collective-permute-start | bytes 196616 | tf_op jit(solution)/shard_map/ppermute | solution.py:290
  76.6 4.1 %collective-permute-start.7 = (bf16[128,256]{1,0:T(8,128)(2,1)S(1)}, bf16[128,256]{1,0:T(8,128)(2,1)S(1)}, u32[]{:S(2)}, u32[]{:S(2)}) collective-permute-start(bf16[128,256]{1,0:T(8,128)(2,1)S(1)} %get-tuple-element.32), channel_id=1, source_target_pairs={{0,40},{8,32},{32,8},{40,0},{1,41},{9,33},{33,9},{41,1},{2,42},{10... | collective-permute-start | bytes 196616 | tf_op jit(solution)/shard_map/ppermute | solution.py:290
  80.7 2.1 %collective-permute-done.7.three_ref = bf16[128,256]{1,0:T(8,128)(2,1)S(1)} collective-permute-done((bf16[128,256]{1,0:T(8,128)(2,1)S(1)}, bf16[128,256]{1,0:T(8,128)(2,1)S(1)}, u32[]{:S(2)}, u32[]{:S(2)}) %collective-permute-start.7) | collective-permute-done | bytes 65568 | tf_op jit(solution)/shard_map/ppermute | solution.py:290
  82.9 3.2 %collective-permute-start.8 = (bf16[64,256]{1,0:T(8,128)(2,1)S(1)}, bf16[64,256]{1,0:T(8,128)(2,1)S(1)}, u32[]{:S(2)}, u32[]{:S(2)}) collective-permute-start(bf16[64,256]{1,0:T(8,128)(2,1)S(1)} %get-tuple-element.34), channel_id=1, source_target_pairs={{0,64},{64,0},{1,65},{65,1},{2,66},{66,2},{3,67},{67,3},{4,68},{68... | collective-permute-start | bytes 98312 | tf_op jit(solution)/shard_map/ppermute | solution.py:41
  86.1 1.7 %collective-permute-done.8.got_ref = bf16[64,256]{1,0:T(8,128)(2,1)S(1)} collective-permute-done((bf16[64,256]{1,0:T(8,128)(2,1)S(1)}, bf16[64,256]{1,0:T(8,128)(2,1)S(1)}, u32[]{:S(2)}, u32[]{:S(2)}) %collective-permute-start.8) | collective-permute-done | bytes 32800 | tf_op jit(solution)/shard_map/ppermute | solution.py:41
  87.8 0.6 shard_map.84
  88.4 21.2 %all_to_all.21.pieces_ref = bf16[8,64,128]{2,1,0:T(8,128)(2,1)S(1)} all-to-all(bf16[8,64,128]{2,1,0:T(8,128)(2,1)S(1)} %get-tuple-element.35), channel_id=1, replica_groups=mesh['zh'=4,'zl'=2,'yl'=2,'xh'=2,'xl'=2,'tp'=8] {'tp'}, dimensions={0} | all-to-all | bytes 262144 | tf_op jit(solution)/shard_map/all_to_all | solution.py:45
  109.6 3.6 %collective-permute-start.9 = (bf16[64,384]{1,0:T(8,128)(2,1)S(1)}, bf16[64,384]{1,0:T(8,128)(2,1)S(1)}, u32[]{:S(2)}, u32[]{:S(2)}) collective-permute-start(bf16[64,384]{1,0:T(8,128)(2,1)S(1)} %shard_map.85.own_ref), channel_id=1, source_target_pairs={{0,8},{8,16},{16,24},{24,32},{32,40},{40,48},{48,56},{56,64},{64,7... | collective-permute-start | bytes 147464 | tf_op jit(solution)/shard_map/ppermute | solution.py:41
  113.3 0.8 shard_map.86
  114.1 4.8 %collective-permute-done.9.before_ref = bf16[64,384]{1,0:T(8,128)(2,1)S(1)} collective-permute-done((bf16[64,384]{1,0:T(8,128)(2,1)S(1)}, bf16[64,384]{1,0:T(8,128)(2,1)S(1)}, u32[]{:S(2)}, u32[]{:S(2)}) %collective-permute-start.9) | collective-permute-done | bytes 49184 | tf_op jit(solution)/shard_map/ppermute | solution.py:41
  118.9 0.8 shard_map.87
  (18 shorter events, 0.2 us)
Async XLA Ops:
  3.6 17.2 %collective-permute-start = (bf16[64,1024]{1,0:T(8,128)(2,1)}, bf16[64,1024]{1,0:T(8,128)(2,1)S(1)}, u32[]{:S(2)}, u32[]{:S(2)}) collective-permute-start(bf16[64,1024]{1,0:T(8,128)(2,1)} %get-tuple-element.22), channel_id=1, source_target_pairs={{0,504},{8,0},{16,8},{24,16},{32,24},{40,32},{48,40},{56,48},{64,5... | collective-permute-start | bytes 393224 | tf_op jit(solution)/shard_map/ppermute | solution.py:41
  18.3 0.9 copy-start.1
  21.6 31.6 %all-to-all-start = ((bf16[16,64,256]{2,1,0:T(8,128)(2,1)}), bf16[16,64,256]{2,1,0:T(8,128)(2,1)S(1)}, u32[]{:S(2)}, u32[]{:S(2)}) async-start(bf16[16,64,256]{2,1,0:T(8,128)(2,1)} %get-tuple-element.24), calls=%async_computation | async-start | bytes 1048576 | tf_op jit(solution)/shard_map/all_to_all | solution.py:45
  25.2 13.3 %collective-permute-start.1 = (bf16[64,256]{1,0:T(8,128)(2,1)S(1)}, bf16[64,256]{1,0:T(8,128)(2,1)S(1)}, u32[]{:S(2)}, u32[]{:S(2)}) collective-permute-start(bf16[64,256]{1,0:T(8,128)(2,1)S(1)} %select_bitcast_fusion), channel_id=1, source_target_pairs={{0,64},{64,0},{1,65},{65,1},{2,66},{66,2},{3,67},{67,3},{4,68},{68... | collective-permute-start | bytes 98312 | tf_op jit(solution)/shard_map/ppermute | solution.py:41
  38.5 10.7 %collective-permute-start.2 = (bf16[128,256]{1,0:T(8,128)(2,1)S(1)}, bf16[128,256]{1,0:T(8,128)(2,1)S(1)}, u32[]{:S(2)}, u32[]{:S(2)}) collective-permute-start(bf16[128,256]{1,0:T(8,128)(2,1)S(1)} %pad_maximum_fusion.mine_ref), channel_id=1, source_target_pairs={{0,8},{8,0},{32,40},{40,32},{1,9},{9,1},{33,41},{41,33},{2,10},{10... | collective-permute-start | bytes 196616 | tf_op jit(solution)/shard_map/ppermute | solution.py:290
  42.0 7.3 %collective-permute-start.3 = (bf16[128,256]{1,0:T(8,128)(2,1)S(1)}, bf16[128,256]{1,0:T(8,128)(2,1)S(1)}, u32[]{:S(2)}, u32[]{:S(2)}) collective-permute-start(bf16[128,256]{1,0:T(8,128)(2,1)S(1)} %pad_maximum_fusion.mine_ref), channel_id=1, source_target_pairs={{0,32},{8,40},{32,0},{40,8},{1,33},{9,41},{33,1},{41,9},{2,34},{10... | collective-permute-start | bytes 196616 | tf_op jit(solution)/shard_map/ppermute | solution.py:290
  47.4 5.9 %collective-permute-start.4 = (bf16[128,256]{1,0:T(8,128)(2,1)S(1)}, bf16[128,256]{1,0:T(8,128)(2,1)S(1)}, u32[]{:S(2)}, u32[]{:S(2)}) collective-permute-start(bf16[128,256]{1,0:T(8,128)(2,1)S(1)} %pad_maximum_fusion.mine_ref), channel_id=1, source_target_pairs={{0,40},{8,32},{32,8},{40,0},{1,41},{9,33},{33,9},{41,1},{2,42},{10... | collective-permute-start | bytes 196616 | tf_op jit(solution)/shard_map/ppermute | solution.py:290
  62.9 25.0 %copy-start = (bf16[3,1024,256]{2,1,0:T(8,128)(2,1)S(1)}, bf16[3,1024,256]{2,1,0:T(8,128)(2,1)}, u32[]{:S(2)}) copy-start(bf16[3,1024,256]{2,1,0:T(8,128)(2,1)} %w_ref.1) | copy-start | bytes 4718596
  62.9 25.0 %all-to-all-start.2 = ((bf16[16,64,256]{2,1,0:T(8,128)(2,1)}), bf16[16,64,256]{2,1,0:T(8,128)(2,1)S(1)}, u32[]{:S(2)}, u32[]{:S(2)}) async-start(bf16[16,64,256]{2,1,0:T(8,128)(2,1)} %get-tuple-element.27), calls=%async_computation.2 | async-start | bytes 1048576 | tf_op jit(solution)/shard_map/all_to_all | solution.py:45
  72.1 41.1 %copy-start.2 = (s32[2,64]{1,0:T(2,128)S(1)}, s32[2,64]{1,0:T(2,128)}, u32[]{:S(2)}) copy-start(s32[2,64]{1,0:T(2,128)} %moved_ref.1) | copy-start | bytes 1540
  72.2 41.1 %copy-start.3 = (s32[256]{0:T(256)S(1)}, s32[256]{0:T(256)}, u32[]{:S(2)}) copy-start(s32[256]{0:T(256)} %param.7) | copy-start | bytes 3076
  72.2 41.1 %copy-start.4 = (s32[64]{0:T(128)S(1)}, s32[64]{0:T(128)}, u32[]{:S(2)}) copy-start(s32[64]{0:T(128)} %first_ref.1) | copy-start | bytes 772
  72.2 8.5 %collective-permute-start.5 = (bf16[128,256]{1,0:T(8,128)(2,1)S(1)}, bf16[128,256]{1,0:T(8,128)(2,1)S(1)}, u32[]{:S(2)}, u32[]{:S(2)}) collective-permute-start(bf16[128,256]{1,0:T(8,128)(2,1)S(1)} %get-tuple-element.30), channel_id=1, source_target_pairs={{0,8},{8,0},{32,40},{40,32},{1,9},{9,1},{33,41},{41,33},{2,10},{10... | collective-permute-start | bytes 196616 | tf_op jit(solution)/shard_map/ppermute | solution.py:290
  74.2 6.5 %collective-permute-start.6 = (bf16[128,256]{1,0:T(8,128)(2,1)S(1)}, bf16[128,256]{1,0:T(8,128)(2,1)S(1)}, u32[]{:S(2)}, u32[]{:S(2)}) collective-permute-start(bf16[128,256]{1,0:T(8,128)(2,1)S(1)} %get-tuple-element.31), channel_id=1, source_target_pairs={{0,32},{8,40},{32,0},{40,8},{1,33},{9,41},{33,1},{41,9},{2,34},{10... | collective-permute-start | bytes 196616 | tf_op jit(solution)/shard_map/ppermute | solution.py:290
  76.6 6.2 %collective-permute-start.7 = (bf16[128,256]{1,0:T(8,128)(2,1)S(1)}, bf16[128,256]{1,0:T(8,128)(2,1)S(1)}, u32[]{:S(2)}, u32[]{:S(2)}) collective-permute-start(bf16[128,256]{1,0:T(8,128)(2,1)S(1)} %get-tuple-element.32), channel_id=1, source_target_pairs={{0,40},{8,32},{32,8},{40,0},{1,41},{9,33},{33,9},{41,1},{2,42},{10... | collective-permute-start | bytes 196616 | tf_op jit(solution)/shard_map/ppermute | solution.py:290
  82.9 5.0 %collective-permute-start.8 = (bf16[64,256]{1,0:T(8,128)(2,1)S(1)}, bf16[64,256]{1,0:T(8,128)(2,1)S(1)}, u32[]{:S(2)}, u32[]{:S(2)}) collective-permute-start(bf16[64,256]{1,0:T(8,128)(2,1)S(1)} %get-tuple-element.34), channel_id=1, source_target_pairs={{0,64},{64,0},{1,65},{65,1},{2,66},{66,2},{3,67},{67,3},{4,68},{68... | collective-permute-start | bytes 98312 | tf_op jit(solution)/shard_map/ppermute | solution.py:41
  109.6 9.3 %collective-permute-start.9 = (bf16[64,384]{1,0:T(8,128)(2,1)S(1)}, bf16[64,384]{1,0:T(8,128)(2,1)S(1)}, u32[]{:S(2)}, u32[]{:S(2)}) collective-permute-start(bf16[64,384]{1,0:T(8,128)(2,1)S(1)} %shard_map.85.own_ref), channel_id=1, source_target_pairs={{0,8},{8,16},{16,24},{24,32},{32,40},{40,48},{48,56},{56,64},{64,7... | collective-permute-start | bytes 147464 | tf_op jit(solution)/shard_map/ppermute | solution.py:41

commit v7 on v5

--- a/solution.py
+++ b/solution.py
@@ -1,3 +1,5 @@
+import functools
+
 import jax
 import jax.numpy as jnp
 from jax import lax
@@ -28,6 +30,7 @@
 LOG2E = 1.4426950408889634
 NEG = -1e30
 FLOOR = -1e29
+HEAVY = 10_000_000_000
 BF = jnp.bfloat16
 F32 = jnp.float32
 I32 = jnp.int32
@@ -49,15 +52,17 @@
     return lax.broadcasted_iota(I32, shape, dim)
 
 
-def call(kernel, ins, outs, flops, scalars=0):
+def call(kernel, ins, outs, flops, scalars=0, passed=False):
     smem = pl.BlockSpec(memory_space=pltpu.SMEM)
     vmem = pl.BlockSpec(memory_space=pltpu.VMEM)
+    hbm = pl.BlockSpec(memory_space=pl.ANY)
     size = sum(x.size * x.dtype.itemsize for x in list(ins) + list(outs))
     return pl.pallas_call(
         kernel,
         out_shape=tuple(outs),
-        in_specs=[smem] * scalars + [vmem] * (len(ins) - scalars),
-        out_specs=tuple([vmem] * len(outs)),
+        in_specs=[smem] * scalars + [vmem] * (len(ins) - scalars - passed) + [hbm] * passed,
+        out_specs=tuple([vmem] * (len(outs) - passed) + [hbm] * passed),
+        input_output_aliases={len(ins) - 1: len(outs) - 1} if passed else {},
         cost_estimate=pl.CostEstimate(flops=flops, bytes_accessed=size, transcendentals=0),
         compiler_params=pltpu.CompilerParams(vmem_limit_bytes=40 * 1024 * 1024),
     )(*ins)
@@ -88,7 +93,7 @@
 
 
 def pool_kernel(
-    c_ref, first_hbm, moved_hbm, place_hbm, bytes_hbm, grad_hbm, w_hbm, sent_ref, own_ref,
+    c_ref, first_hbm, moved_hbm, place_hbm, bytes_hbm, grad_hbm, w_hbm, sent_ref, own_ref, swap_ref, both_ref,
     first_ref, moved_ref, place_ref, bytes_ref, grad_ref, w_ref, sems,
 ):
     pairs = [
@@ -112,36 +117,66 @@
     order = slot_order(c, first_ref, moved_ref, (WINDOW, ROWS), 1)
     slotted = (iota((WINDOW, ROWS), 0) == order).astype(F32).astype(BF)
     grads = dot(slotted, grad_ref[...], ((1,), (0,))).astype(BF)
-    for at, value in ((0, None), (1, grads), (2, None), (3, None)):
-        if value is None:
-            part = max(at - 1, 0)
-            copies[5 + part].wait()
-            value = dot(pooled, w_ref[part], ((1,), (0,))).astype(BF)
-        sent_ref[:, at * FEATS : (at + 1) * FEATS] = value[:ROWS]
-        own_ref[:, at * FEATS : (at + 1) * FEATS] = value[ROWS:]
-
-
-def columns(value, kind, head):
-    at = kind * FEATS + head * HD
-    return value[:, at : at + HD]
+    parts = []
+    for i in range(3):
+        copies[5 + i].wait()
+        parts.append(dot(pooled, w_ref[i], ((1,), (0,))).astype(BF))
+    query, key, value = parts
+
+    def asked(rows, second):
+        for ref, at in ((query, 0), (grads, HD)):
+            one, two = ref[rows, :HD], ref[rows, HD:]
+            yield slice(at, at + HD), jnp.where(second, two, one)
+
+    before, after = slice(0, ROWS), slice(ROWS, WINDOW)
+    mine = ((c >> 3) & 1) == 1
+    left = (((c + N_CTX - 1) >> 3) & 1) == 1
+    for ref, rows, second in (
+        (sent_ref, before, left),
+        (own_ref, after, mine),
+        (swap_ref, after, jnp.logical_not(mine)),
+        (both_ref, before, jnp.logical_not(left)),
+    ):
+        for at, part in asked(rows, second):
+            ref[:, at] = part
+    for ref, rows in ((sent_ref, before), (own_ref, after)):
+        for e in range(HEADS):
+            at = 2 * HD * (1 + e)
+            ref[:, at : at + HD] = key[rows, e * HD : (e + 1) * HD]
+            ref[:, at + HD : at + 2 * HD] = value[rows, e * HD : (e + 1) * HD]
 
 
 def hold_kernel(own_ref, held_ref):
     held_ref[...] = own_ref[...]
 
 
-def spread_kernel(c_ref, own_ref, got_ref, keep_ref, give_ref, held_ref):
-    both = own_ref[...] + got_ref[...]
-    asked, held = [], []
-    for e in range(HEADS):
-        q, g, k, v = (columns(both, kind, e) for kind in range(4))
-        asked.append(jnp.concatenate([q, g], axis=1))
-        held.append(jnp.concatenate([k, v], axis=1))
+def spread_kernel(c_ref, own_ref, got_ref, swap_ref, both_ref, asked_ref, held_ref):
+    mine = own_ref[...] + got_ref[...]
+    other = swap_ref[...] + both_ref[...]
     second = ((c_ref[0] >> 3) & 1) == 1
-    keep_ref[...] = jnp.where(second, asked[1], asked[0])
-    give_ref[...] = jnp.where(second, asked[0], asked[1])
+    here = mine[:, : 2 * HD]
+    asked_ref[:ROWS] = jnp.where(second, other, here)
+    asked_ref[ROWS:] = jnp.where(second, here, other)
     for i in range(N_FAR):
-        held_ref[i] = held[(i >> 1) & 1]
+        at = 2 * HD * (1 + ((i >> 1) & 1))
+        held_ref[i] = mine[:, at : at + 2 * HD]
+
+
+def join_kernel(bit, c_ref, mine_ref, got_ref, out_ref):
+    second = ((c_ref[0] >> bit) & 1) == 1
+    n = mine_ref.shape[0]
+    mine, got = mine_ref[...], got_ref[...]
+    out_ref[:n] = jnp.where(second, got, mine)
+    out_ref[n:] = jnp.where(second, mine, got)
+
+
+def halve_kernel(bit, c_ref, keep_ref, got_ref, *refs):
+    rest_ref, give_ref = refs[-3:-1] if len(refs) > 2 else refs
+    second = ((c_ref[0] >> bit) & 1) == 1
+    total = keep_ref[...] + got_ref[...].astype(F32)
+    half = total.shape[0] // 2
+    rest_ref[...] = jnp.where(second, total[half:], total[:half]).astype(rest_ref.dtype)
+    give_ref[...] = jnp.where(second, total[:half], total[half:]).astype(BF)
 
 
 def unpack(asked_ref, held_ref):
@@ -204,7 +239,7 @@
 
 def sum_kernel(c_ref, term_ref, keep_ref, got_ref, w_ref, piece_ref, out_ref):
     second = ((c_ref[0] >> 3) & 1) == 1
-    keep, got = keep_ref[...].astype(BF), got_ref[...]
+    keep, got = keep_ref[...], got_ref[...]
     asked = [jnp.where(second, got, keep), jnp.where(second, keep, got)]
     d_query = jnp.concatenate([x[:, :HD] for x in asked], axis=1)
     out_ref[...] = jnp.concatenate([x[:, HD:] for x in asked], axis=1)
@@ -254,12 +289,12 @@
     vmem = pl.BlockSpec(memory_space=pltpu.VMEM)
     ins = (first, moved, place, byte_states, d_attn, w_qkv)
     spaces = (pltpu.SMEM, pltpu.SMEM) + (pltpu.VMEM,) * 4
-    block = shaped((ROWS, 4 * FEATS), BF)
+    block, pair = shaped((ROWS, 3 * FEATS), BF), shaped((ROWS, FEATS), BF)
     return pl.pallas_call(
         pool_kernel,
-        out_shape=(block, block),
+        out_shape=(block, block, pair, pair),
         in_specs=[pl.BlockSpec(memory_space=pltpu.SMEM)] + [hbm] * len(ins),
-        out_specs=(vmem, vmem),
+        out_specs=(vmem,) * 4,
         scratch_shapes=[space(x.shape, x.dtype) for space, x in zip(spaces, ins)]
         + [pltpu.SemaphoreType.DMA((len(ins) + 2,))],
         cost_estimate=pl.CostEstimate(flops=300_000_000, bytes_accessed=2_500_000, transcendentals=0),
@@ -267,18 +302,10 @@
     )(c_ref, *ins)
 
 
-def doubled(mine, axis):
-    got = shift(mine, axis, 2, 1)
-    second = lax.axis_index(axis) == 1
-    return jnp.concatenate([jnp.where(second, got, mine), jnp.where(second, mine, got)], axis=0)
-
-
-def halved(keep, got, axis):
-    total = keep + got.astype(F32)
-    half = total.shape[0] // 2
-    second = lax.axis_index(axis) == 1
-    keep = jnp.where(second, total[half:], total[:half])
-    return keep, jnp.where(second, total[:half], total[half:]).astype(BF)
+def doubled(c_ref, mine, axis, bit, cost):
+    out = shaped((2 * mine.shape[0], mine.shape[1]), BF)
+    kernel = functools.partial(join_kernel, bit)
+    return call(kernel, (c_ref, mine, shift(mine, axis, 2, 1)), (out,), cost, 1)[0]
 
 
 def shards(byte_states, patch_of_byte, patch_first, moved, w_qkv, d_attn):
@@ -288,16 +315,23 @@
     pair = shaped((ROWS, 2 * HD), BF)
     stack = shaped((N_FAR, ROWS, 2 * HD), BF)
 
-    sent, own = pool(c_ref, patch_first, moved, place, byte_states, d_attn, w_qkv)
+    sent, own, swapped, crossed = pool(
+        c_ref, patch_first, moved, place, byte_states, d_attn, w_qkv
+    )
+    ring = [(i, (i - 1) % N_CTX) for i in range(N_CTX)]
+    sent = lax.ppermute(sent, CTX, ring)
+    swapped = lax.ppermute(swapped, CTX, [(i, i ^ 8) for i in range(N_CTX)])
+    crossed = lax.ppermute(crossed, CTX, [(i, j ^ 8) for i, j in ring])
     (own,) = call(hold_kernel, (own,), (shaped(own.shape, BF),), 100_000)
-    keep, give, held = call(
-        spread_kernel, (c_ref, own, shift(sent, CTX, N_CTX, -1)), (pair, pair, stack), 1_000_000, 1
+    asked, held = call(
+        spread_kernel,
+        (c_ref, own, sent, swapped, crossed),
+        (shaped((2 * ROWS, 2 * HD), BF), stack),
+        1_000_000,
+        1,
     )
     held = swap(held, FAR)
-    got = shift(give, "zl", 2, 1)
-    second = lax.axis_index("zl") == 1
-    asked = jnp.concatenate([jnp.where(second, got, keep), jnp.where(second, keep, got)], axis=0)
-    asked = doubled(doubled(asked, "xl"), "yl")
+    asked = doubled(c_ref, doubled(c_ref, asked, "xl", 0, HEAVY), "yl", 2, 1_000_000)
     (stats,) = call(
         forward_kernel,
         (c_ref, asked, held),
@@ -313,9 +347,23 @@
         900_000_000,
         1,
     )
+    quarter = (TILE_Q // 4, 2 * HD)
+    keep, give, terms = call(
+        functools.partial(halve_kernel, 0),
+        (c_ref, keep, shift(give, "yl", 2, 1), terms),
+        (shaped(quarter, F32), shaped(quarter, BF), stack),
+        HEAVY,
+        1,
+        True,
+    )
     terms = swap(terms, FAR)
-    keep, give = halved(keep, shift(give, "yl", 2, 1), "xl")
-    keep, give = halved(keep, shift(give, "xl", 2, 1), "zl")
+    keep, give = call(
+        functools.partial(halve_kernel, 3),
+        (c_ref, keep, shift(give, "xl", 2, 1)),
+        (pair, pair),
+        HEAVY,
+        1,
+    )
     pieces, out = call(
         sum_kernel,
         (c_ref, terms, keep, shift(give, "zl", 2, 1), w_qkv),

time: 112 us -> 120 us (1.071)
  waiting for transfers between devices: 21.1 us -> 29.3 us
    ppermute x0 -> x3, starting transfers between devices: none -> 20.3 us  [the longest x1 14.7 us: shards(): sent = lax.ppermute(sent, CTX, ring)]
    ppermute x8 -> x6, starting transfers between devices: 36.9 us -> 18.4 us  [shift(): return lax.ppermute(x, axis, [(i, (i + by) % n) for i in range(n)])]
    all_to_all x2, waiting for transfers between devices: 3.25 us -> 11.8 us  [swap(): return lax.all_to_all(x, axis, split_axis=0, concat_axis=0, tiled=True)]
    ppermute x8 -> x6, waiting for transfers between devices: 17.8 us -> 16.2 us  [shift(): return lax.ppermute(x, axis, [(i, (i + by) % n) for i in range(n)])]
    all_to_all x2, starting transfers between devices: 10.8 us -> 9.49 us  [swap(): return lax.all_to_all(x, axis, split_axis=0, concat_axis=0, tiled=True)]
    ppermute x0 -> x3, waiting for transfers between devices: none -> 1.23 us  [the longest x1 1.22 us: shards(): crossed = lax.ppermute(crossed, CTX, [(i, j ^ 8) for i, j in ring])]
    pallas_call x8 -> x12, Pallas kernels: 6.61 us -> 6.68 us  [call(): pl.pallas_call(kernel, out_shape=tuple(outs), in_specs=[smem] * scalars +...]
  transfers between devices with their start and end apart: 10 -> 11, of which waited for: 8 -> 7; matrix products, arithmetic and copies ran while one was open for 0% -> 0% of each run, Pallas kernels for 1% -> 1%
where the time goes in v7:
time: 120 us; the launch traced here: 119 us
  starting transfers between devices  48.2 us (40%)
  blocking collectives  30.5 us (25%)
  waiting for transfers between devices  29.3 us (24%)
  Pallas kernels  9.6 us (8%)
    all_to_all x2, blocking collectives, swap(): return lax.all_to_all(x, axis, split_axis=0, concat_axis=0, tiled=True)  30.5 us
    ppermute x6, starting transfers between devices, shift(): return lax.ppermute(x, axis, [(i, (i + by) % n) for i in range(n)])  18.4 us
    ppermute x6, waiting for transfers between devices, shift(): return lax.ppermute(x, axis, [(i, (i + by) % n) for i in range(n)])  16.2 us
    ppermute x1, starting transfers between devices, shards(): sent = lax.ppermute(sent, CTX, ring)  14.7 us
    all_to_all x2, waiting for transfers between devices, swap(): return lax.all_to_all(x, axis, split_axis=0, concat_axis=0, tiled=True)  11.8 us
    all_to_all x2, starting transfers between devices, swap(): return lax.all_to_all(x, axis, split_axis=0, concat_axis=0, tiled=True)  9.49 us
    pallas_call x12, Pallas kernels, call(): pl.pallas_call(kernel, out_shape=tuple(outs), in_specs=[smem] * scalars +...  6.68 us
    ppermute x1, starting transfers between devices, shards(): crossed = lax.ppermute(crossed, CTX, [(i, j ^ 8) for i, j in ring])  3.63 us
  transfers between devices with their start and end apart: 11, of which 7 were waited for; matrix products, arithmetic and copies ran while one was open for 0% of the time, Pallas kernels for 1%

profile of v7, /device:TPU:1, one launch (start us, length us, event | category | flops | bytes accessed | tf_op | source)
XLA Modules:
  0.0 119.3 jit_solution(5229832300240623731)
XLA Ops:
  0.6 2.9 %shard_map.77 = (bf16[64,768]{1,0:T(8,128)(2,1)}, bf16[64,768]{1,0:T(8,128)(2,1)}, bf16[64,256]{1,0:T(8,128)(2,1)}, bf16[64,256]{1,0:T(8,128)(2,1)}) custom-call(s32[1]{0:T(128)} %bitcast.c_ref, s32[64]{0:T(128)} %first_ref.1, s32[2,64]{1,0:T(2,128)} %moved_ref.1, s32[1,256]{1,0:T(1,128)} %bitcast.2, bf16[256,1024]{1,0:T(8,128)(2,1)} %bytes_hbm.1, ...), custom_call_target="tpu_custom_call" | custom-call | flops 300000000 | bytes 2500000 | tf_op jit(solution)/shard_map/pallas_call | solution.py:293
  3.6 14.7 %collective-permute-start = (bf16[64,768]{1,0:T(8,128)(2,1)}, bf16[64,768]{1,0:T(8,128)(2,1)S(1)}, u32[]{:S(2)}, u32[]{:S(2)}) collective-permute-start(bf16[64,768]{1,0:T(8,128)(2,1)} %get-tuple-element.22), channel_id=1, source_target_pairs={{0,504},{8,0},{16,8},{24,16},{32,24},{40,32},{48,40},{56,48},{64,5... | collective-permute-start | bytes 294920 | tf_op jit(solution)/shard_map/ppermute | solution.py:322
  18.3 1.9 %collective-permute-start.1 = (bf16[64,256]{1,0:T(8,128)(2,1)}, bf16[64,256]{1,0:T(8,128)(2,1)S(1)}, u32[]{:S(2)}, u32[]{:S(2)}) collective-permute-start(bf16[64,256]{1,0:T(8,128)(2,1)} %get-tuple-element.23), channel_id=1, source_target_pairs={{0,64},{8,72},{16,80},{24,88},{32,96},{40,104},{48,112},{56,120},{... | collective-permute-start | bytes 98312 | tf_op jit(solution)/shard_map/ppermute | solution.py:323
  20.2 3.6 %collective-permute-start.2 = (bf16[64,256]{1,0:T(8,128)(2,1)}, bf16[64,256]{1,0:T(8,128)(2,1)S(1)}, u32[]{:S(2)}, u32[]{:S(2)}) collective-permute-start(bf16[64,256]{1,0:T(8,128)(2,1)} %get-tuple-element.24), channel_id=1, source_target_pairs={{0,440},{8,64},{16,72},{24,80},{32,88},{40,96},{48,104},{56,112},{... | collective-permute-start | bytes 98312 | tf_op jit(solution)/shard_map/ppermute | solution.py:324
  23.9 0.9 copy-done.1
  24.8 1.2 %collective-permute-done.2.both_ref = bf16[64,256]{1,0:T(8,128)(2,1)S(1)} collective-permute-done((bf16[64,256]{1,0:T(8,128)(2,1)}, bf16[64,256]{1,0:T(8,128)(2,1)S(1)}, u32[]{:S(2)}, u32[]{:S(2)}) %collective-permute-start.2) | collective-permute-done | bytes 32800 | tf_op jit(solution)/shard_map/ppermute | solution.py:324
  26.0 0.9 shard_map.79
  26.8 2.0 %collective-permute-start.3 = (bf16[128,256]{1,0:T(8,128)(2,1)S(1)}, bf16[128,256]{1,0:T(8,128)(2,1)S(1)}, u32[]{:S(2)}, u32[]{:S(2)}) collective-permute-start(bf16[128,256]{1,0:T(8,128)(2,1)S(1)} %get-tuple-element.25.mine_ref), channel_id=1, source_target_pairs={{0,8},{8,0},{1,9},{9,1},{2,10},{10,2},{3,11},{11,3},{4,12},{12,4},... | collective-permute-start | bytes 196616 | tf_op jit(solution)/shard_map/ppermute | solution.py:44
  28.8 5.3 %all-to-all-start = ((bf16[16,64,256]{2,1,0:T(8,128)(2,1)}), bf16[16,64,256]{2,1,0:T(8,128)(2,1)S(1)}, u32[]{:S(2)}, u32[]{:S(2)}) async-start(bf16[16,64,256]{2,1,0:T(8,128)(2,1)} %get-tuple-element.26), calls=%async_computation | async-start | bytes 1048576 | tf_op jit(solution)/shard_map/all_to_all | solution.py:48
  34.2 5.3 %collective-permute-start.4 = (bf16[256,256]{1,0:T(8,128)(2,1)S(1)}, bf16[256,256]{1,0:T(8,128)(2,1)S(1)}, u32[]{:S(2)}, u32[]{:S(2)}) collective-permute-start(bf16[256,256]{1,0:T(8,128)(2,1)S(1)} %shard_map.80.mine_ref), channel_id=1, source_target_pairs={{0,32},{32,0},{1,33},{33,1},{2,34},{34,2},{3,35},{35,3},{4,36},{36... | collective-permute-start | bytes 393224 | tf_op jit(solution)/shard_map/ppermute | solution.py:44
  39.5 2.6 %collective-permute-done.4.got_ref = bf16[256,256]{1,0:T(8,128)(2,1)S(1)} collective-permute-done((bf16[256,256]{1,0:T(8,128)(2,1)S(1)}, bf16[256,256]{1,0:T(8,128)(2,1)S(1)}, u32[]{:S(2)}, u32[]{:S(2)}) %collective-permute-start.4) | collective-permute-done | bytes 131104 | tf_op jit(solution)/shard_map/ppermute | solution.py:44
  42.2 7.0 %all-to-all-done.held_ref = bf16[16,64,256]{2,1,0:T(8,128)(2,1)S(1)} async-done(((bf16[16,64,256]{2,1,0:T(8,128)(2,1)}), bf16[16,64,256]{2,1,0:T(8,128)(2,1)S(1)}, u32[]{:S(2)}, u32[]{:S(2)}) %all-to-all-start) | async-done | bytes 524320 | tf_op jit(solution)/shard_map/all_to_all | solution.py:48
  49.1 1.1 shard_map.82
  50.2 8.2 %all_to_all.20.stats_ref = f32[4,8,512]{2,1,0:T(8,128)S(1)} all-to-all(f32[4,8,512]{2,1,0:T(8,128)S(1)} %shard_map.82), channel_id=1, replica_groups=mesh['zh'=4,'zl'=2,'yl'=2,'xh'=2,'xl'=2,'tp'=8] {'yl','xl'}, dimensions={0} | all-to-all | bytes 131072 | tf_op jit(solution)/shard_map/all_to_all | solution.py:48
  58.4 2.4 %shard_map.83 = (bf16[16,64,256]{2,1,0:T(8,128)(2,1)}, f32[256,256]{1,0:T(8,128)S(1)}, bf16[256,256]{1,0:T(8,128)(2,1)S(1)}) custom-call(s32[1]{0:T(128)} %bitcast.c_ref, bf16[512,256]{1,0:T(8,128)(2,1)S(1)} %shard_map.81.asked_ref, bf16[16,64,256]{2,1,0:T(8,128)(2,1)S(1)} %all-to-all-done.held_ref, f32[4,8,512]{2,1,0:T(8,128)S(1)} %all_to_all.20.stats_ref), custom_call_target="tpu_custom_call" | custom-call | flops 900000000 | bytes 1769476 | tf_op jit(solution)/shard_map/pallas_call | solution.py:60
  60.8 2.4 %collective-permute-start.5 = (bf16[256,256]{1,0:T(8,128)(2,1)S(1)}, bf16[256,256]{1,0:T(8,128)(2,1)S(1)}, u32[]{:S(2)}, u32[]{:S(2)}) collective-permute-start(bf16[256,256]{1,0:T(8,128)(2,1)S(1)} %get-tuple-element.28), channel_id=1, source_target_pairs={{0,32},{32,0},{1,33},{33,1},{2,34},{34,2},{3,35},{35,3},{4,36},{36... | collective-permute-start | bytes 393224 | tf_op jit(solution)/shard_map/ppermute | solution.py:44
  63.2 3.3 %collective-permute-done.5.got_ref = bf16[256,256]{1,0:T(8,128)(2,1)S(1)} collective-permute-done((bf16[256,256]{1,0:T(8,128)(2,1)S(1)}, bf16[256,256]{1,0:T(8,128)(2,1)S(1)}, u32[]{:S(2)}, u32[]{:S(2)}) %collective-permute-start.5) | collective-permute-done | bytes 131104 | tf_op jit(solution)/shard_map/ppermute | solution.py:44
  66.5 2.4 %collective-permute-start.6 = (bf16[128,256]{1,0:T(8,128)(2,1)S(1)}, bf16[128,256]{1,0:T(8,128)(2,1)S(1)}, u32[]{:S(2)}, u32[]{:S(2)}) collective-permute-start(bf16[128,256]{1,0:T(8,128)(2,1)S(1)} %get-tuple-element.32), channel_id=1, source_target_pairs={{0,8},{8,0},{1,9},{9,1},{2,10},{10,2},{3,11},{11,3},{4,12},{12,4},... | collective-permute-start | bytes 196616 | tf_op jit(solution)/shard_map/ppermute | solution.py:44
  68.9 4.2 %all-to-all-start.2 = ((bf16[16,64,256]{2,1,0:T(8,128)(2,1)}), bf16[16,64,256]{2,1,0:T(8,128)(2,1)S(1)}, u32[]{:S(2)}, u32[]{:S(2)}) async-start(bf16[16,64,256]{2,1,0:T(8,128)(2,1)} %get-tuple-element.30), calls=%async_computation.2 | async-start | bytes 1048576 | tf_op jit(solution)/shard_map/all_to_all | solution.py:48
  73.1 0.0 copy-start
  73.2 0.0 copy-start.2
  73.2 0.0 copy-start.3
  73.2 0.0 copy-start.4
  73.2 3.4 %collective-permute-start.7 = (bf16[64,256]{1,0:T(8,128)(2,1)S(1)}, bf16[64,256]{1,0:T(8,128)(2,1)S(1)}, u32[]{:S(2)}, u32[]{:S(2)}) collective-permute-start(bf16[64,256]{1,0:T(8,128)(2,1)S(1)} %get-tuple-element.34), channel_id=1, source_target_pairs={{0,64},{64,0},{1,65},{65,1},{2,66},{66,2},{3,67},{67,3},{4,68},{68... | collective-permute-start | bytes 98312 | tf_op jit(solution)/shard_map/ppermute | solution.py:44
  76.6 5.0 %collective-permute-done.7.got_ref = bf16[64,256]{1,0:T(8,128)(2,1)S(1)} collective-permute-done((bf16[64,256]{1,0:T(8,128)(2,1)S(1)}, bf16[64,256]{1,0:T(8,128)(2,1)S(1)}, u32[]{:S(2)}, u32[]{:S(2)}) %collective-permute-start.7) | collective-permute-done | bytes 32800 | tf_op jit(solution)/shard_map/ppermute | solution.py:44
  81.7 4.9 %all-to-all-done.2.term_ref = bf16[16,64,256]{2,1,0:T(8,128)(2,1)S(1)} async-done(((bf16[16,64,256]{2,1,0:T(8,128)(2,1)}), bf16[16,64,256]{2,1,0:T(8,128)(2,1)S(1)}, u32[]{:S(2)}, u32[]{:S(2)}) %all-to-all-start.2) | async-done | bytes 524320 | tf_op jit(solution)/shard_map/all_to_all | solution.py:48
  86.5 0.6 shard_map.86
  87.1 22.3 %all_to_all.21.pieces_ref = bf16[8,64,128]{2,1,0:T(8,128)(2,1)S(1)} all-to-all(bf16[8,64,128]{2,1,0:T(8,128)(2,1)S(1)} %get-tuple-element.35), channel_id=1, replica_groups=mesh['zh'=4,'zl'=2,'yl'=2,'xh'=2,'xl'=2,'tp'=8] {'tp'}, dimensions={0} | all-to-all | bytes 262144 | tf_op jit(solution)/shard_map/all_to_all | solution.py:48
  109.4 3.0 %collective-permute-start.8 = (bf16[64,384]{1,0:T(8,128)(2,1)S(1)}, bf16[64,384]{1,0:T(8,128)(2,1)S(1)}, u32[]{:S(2)}, u32[]{:S(2)}) collective-permute-start(bf16[64,384]{1,0:T(8,128)(2,1)S(1)} %shard_map.87.own_ref), channel_id=1, source_target_pairs={{0,8},{8,16},{16,24},{24,32},{32,40},{40,48},{48,56},{56,64},{64,7... | collective-permute-start | bytes 147464 | tf_op jit(solution)/shard_map/ppermute | solution.py:44
  112.5 0.8 shard_map.88
  113.3 5.2 %collective-permute-done.8.before_ref = bf16[64,384]{1,0:T(8,128)(2,1)S(1)} collective-permute-done((bf16[64,384]{1,0:T(8,128)(2,1)S(1)}, bf16[64,384]{1,0:T(8,128)(2,1)S(1)}, u32[]{:S(2)}, u32[]{:S(2)}) %collective-permute-start.8) | collective-permute-done | bytes 49184 | tf_op jit(solution)/shard_map/ppermute | solution.py:44
  118.5 0.8 shard_map.89
  (15 shorter events, 0.1 us)
Async XLA Ops:
  3.6 22.4 %collective-permute-start = (bf16[64,768]{1,0:T(8,128)(2,1)}, bf16[64,768]{1,0:T(8,128)(2,1)S(1)}, u32[]{:S(2)}, u32[]{:S(2)}) collective-permute-start(bf16[64,768]{1,0:T(8,128)(2,1)} %get-tuple-element.22), channel_id=1, source_target_pairs={{0,504},{8,0},{16,8},{24,16},{32,24},{40,32},{48,40},{56,48},{64,5... | collective-permute-start | bytes 294920 | tf_op jit(solution)/shard_map/ppermute | solution.py:322
  18.3 6.5 %collective-permute-start.1 = (bf16[64,256]{1,0:T(8,128)(2,1)}, bf16[64,256]{1,0:T(8,128)(2,1)S(1)}, u32[]{:S(2)}, u32[]{:S(2)}) collective-permute-start(bf16[64,256]{1,0:T(8,128)(2,1)} %get-tuple-element.23), channel_id=1, source_target_pairs={{0,64},{8,72},{16,80},{24,88},{32,96},{40,104},{48,112},{56,120},{... | collective-permute-start | bytes 98312 | tf_op jit(solution)/shard_map/ppermute | solution.py:323
  20.2 5.8 %collective-permute-start.2 = (bf16[64,256]{1,0:T(8,128)(2,1)}, bf16[64,256]{1,0:T(8,128)(2,1)S(1)}, u32[]{:S(2)}, u32[]{:S(2)}) collective-permute-start(bf16[64,256]{1,0:T(8,128)(2,1)} %get-tuple-element.24), channel_id=1, source_target_pairs={{0,440},{8,64},{16,72},{24,80},{32,88},{40,96},{48,104},{56,112},{... | collective-permute-start | bytes 98312 | tf_op jit(solution)/shard_map/ppermute | solution.py:324
  23.8 0.9 copy-start.1
  26.8 7.3 %collective-permute-start.3 = (bf16[128,256]{1,0:T(8,128)(2,1)S(1)}, bf16[128,256]{1,0:T(8,128)(2,1)S(1)}, u32[]{:S(2)}, u32[]{:S(2)}) collective-permute-start(bf16[128,256]{1,0:T(8,128)(2,1)S(1)} %get-tuple-element.25.mine_ref), channel_id=1, source_target_pairs={{0,8},{8,0},{1,9},{9,1},{2,10},{10,2},{3,11},{11,3},{4,12},{12,4},... | collective-permute-start | bytes 196616 | tf_op jit(solution)/shard_map/ppermute | solution.py:44
  28.8 20.3 %all-to-all-start = ((bf16[16,64,256]{2,1,0:T(8,128)(2,1)}), bf16[16,64,256]{2,1,0:T(8,128)(2,1)S(1)}, u32[]{:S(2)}, u32[]{:S(2)}) async-start(bf16[16,64,256]{2,1,0:T(8,128)(2,1)} %get-tuple-element.26), calls=%async_computation | async-start | bytes 1048576 | tf_op jit(solution)/shard_map/all_to_all | solution.py:48
  34.2 8.0 %collective-permute-start.4 = (bf16[256,256]{1,0:T(8,128)(2,1)S(1)}, bf16[256,256]{1,0:T(8,128)(2,1)S(1)}, u32[]{:S(2)}, u32[]{:S(2)}) collective-permute-start(bf16[256,256]{1,0:T(8,128)(2,1)S(1)} %shard_map.80.mine_ref), channel_id=1, source_target_pairs={{0,32},{32,0},{1,33},{33,1},{2,34},{34,2},{3,35},{35,3},{4,36},{36... | collective-permute-start | bytes 393224 | tf_op jit(solution)/shard_map/ppermute | solution.py:44
  60.8 5.7 %collective-permute-start.5 = (bf16[256,256]{1,0:T(8,128)(2,1)S(1)}, bf16[256,256]{1,0:T(8,128)(2,1)S(1)}, u32[]{:S(2)}, u32[]{:S(2)}) collective-permute-start(bf16[256,256]{1,0:T(8,128)(2,1)S(1)} %get-tuple-element.28), channel_id=1, source_target_pairs={{0,32},{32,0},{1,33},{33,1},{2,34},{34,2},{3,35},{35,3},{4,36},{36... | collective-permute-start | bytes 393224 | tf_op jit(solution)/shard_map/ppermute | solution.py:44
  66.5 6.6 %collective-permute-start.6 = (bf16[128,256]{1,0:T(8,128)(2,1)S(1)}, bf16[128,256]{1,0:T(8,128)(2,1)S(1)}, u32[]{:S(2)}, u32[]{:S(2)}) collective-permute-start(bf16[128,256]{1,0:T(8,128)(2,1)S(1)} %get-tuple-element.32), channel_id=1, source_target_pairs={{0,8},{8,0},{1,9},{9,1},{2,10},{10,2},{3,11},{11,3},{4,12},{12,4},... | collective-permute-start | bytes 196616 | tf_op jit(solution)/shard_map/ppermute | solution.py:44
  68.9 17.6 %all-to-all-start.2 = ((bf16[16,64,256]{2,1,0:T(8,128)(2,1)}), bf16[16,64,256]{2,1,0:T(8,128)(2,1)S(1)}, u32[]{:S(2)}, u32[]{:S(2)}) async-start(bf16[16,64,256]{2,1,0:T(8,128)(2,1)} %get-tuple-element.30), calls=%async_computation.2 | async-start | bytes 1048576 | tf_op jit(solution)/shard_map/all_to_all | solution.py:48
  73.1 13.4 %copy-start = (bf16[3,1024,256]{2,1,0:T(8,128)(2,1)S(1)}, bf16[3,1024,256]{2,1,0:T(8,128)(2,1)}, u32[]{:S(2)}) copy-start(bf16[3,1024,256]{2,1,0:T(8,128)(2,1)} %w_ref.1) | copy-start | bytes 4718596
  73.2 39.3 %copy-start.2 = (s32[2,64]{1,0:T(2,128)S(1)}, s32[2,64]{1,0:T(2,128)}, u32[]{:S(2)}) copy-start(s32[2,64]{1,0:T(2,128)} %moved_ref.1) | copy-start | bytes 1540
  73.2 39.3 %copy-start.3 = (s32[256]{0:T(256)S(1)}, s32[256]{0:T(256)}, u32[]{:S(2)}) copy-start(s32[256]{0:T(256)} %param.7) | copy-start | bytes 3076
  73.2 39.3 %copy-start.4 = (s32[64]{0:T(128)S(1)}, s32[64]{0:T(128)}, u32[]{:S(2)}) copy-start(s32[64]{0:T(128)} %first_ref.1) | copy-start | bytes 772
  73.2 8.4 %collective-permute-start.7 = (bf16[64,256]{1,0:T(8,128)(2,1)S(1)}, bf16[64,256]{1,0:T(8,128)(2,1)S(1)}, u32[]{:S(2)}, u32[]{:S(2)}) collective-permute-start(bf16[64,256]{1,0:T(8,128)(2,1)S(1)} %get-tuple-element.34), channel_id=1, source_target_pairs={{0,64},{64,0},{1,65},{65,1},{2,66},{66,2},{3,67},{67,3},{4,68},{68... | collective-permute-start | bytes 98312 | tf_op jit(solution)/shard_map/ppermute | solution.py:44
  109.4 9.1 %collective-permute-start.8 = (bf16[64,384]{1,0:T(8,128)(2,1)S(1)}, bf16[64,384]{1,0:T(8,128)(2,1)S(1)}, u32[]{:S(2)}, u32[]{:S(2)}) collective-permute-start(bf16[64,384]{1,0:T(8,128)(2,1)S(1)} %shard_map.87.own_ref), channel_id=1, source_target_pairs={{0,8},{8,16},{16,24},{24,32},{32,40},{40,48},{48,56},{56,64},{64,7... | collective-permute-start | bytes 147464 | tf_op jit(solution)/shard_map/ppermute | solution.py:44

commit v8 on v5

--- a/solution.py
+++ b/solution.py
@@ -1,3 +1,5 @@
+import functools
+
 import jax
 import jax.numpy as jnp
 from jax import lax
@@ -9,8 +11,11 @@
 SIZES = (4, 2, 2, 2, 2, 8)
 NAMES = ("zh", "zl", "yl", "xh", "xl", "tp")
 CTX = ("zh", "zl", "yl", "xh", "xl")
-FAR = ("zh", "zl", "xh")
-NEAR = ("yl", "xl")
+BITS = {"zl": 3, "yl": 2, "xh": 1, "xl": 0}
+SPLIT, TWICE, AGAIN = "zl", "xl", "yl"
+NEAR = tuple(a for a in BITS if a in (TWICE, AGAIN))
+REST = tuple(a for a in BITS if a not in NEAR)
+FAR = ("zh",) + REST
 N_CTX = 64
 N_TP = 8
 N_FAR = 16
@@ -28,6 +33,8 @@
 LOG2E = 1.4426950408889634
 NEG = -1e30
 FLOOR = -1e29
+JOIN = 3_000_000_000
+HALVE = 5_000_000_000
 BF = jnp.bfloat16
 F32 = jnp.float32
 I32 = jnp.int32
@@ -49,14 +56,16 @@
     return lax.broadcasted_iota(I32, shape, dim)
 
 
-def call(kernel, ins, outs, flops, scalars=0):
+def call(kernel, ins, outs, flops, scalars=0, unread=0):
     smem = pl.BlockSpec(memory_space=pltpu.SMEM)
     vmem = pl.BlockSpec(memory_space=pltpu.VMEM)
     size = sum(x.size * x.dtype.itemsize for x in list(ins) + list(outs))
     return pl.pallas_call(
         kernel,
         out_shape=tuple(outs),
-        in_specs=[smem] * scalars + [vmem] * (len(ins) - scalars),
+        in_specs=[smem] * scalars
+        + [vmem] * (len(ins) - scalars - unread)
+        + [pl.BlockSpec(memory_space=pl.ANY)] * unread,
         out_specs=tuple([vmem] * len(outs)),
         cost_estimate=pl.CostEstimate(flops=flops, bytes_accessed=size, transcendentals=0),
         compiler_params=pltpu.CompilerParams(vmem_limit_bytes=40 * 1024 * 1024),
@@ -130,6 +139,10 @@
     held_ref[...] = own_ref[...]
 
 
+def bit(c, axis):
+    return (c >> BITS[axis]) & 1
+
+
 def spread_kernel(c_ref, own_ref, got_ref, keep_ref, give_ref, held_ref):
     both = own_ref[...] + got_ref[...]
     asked, held = [], []
@@ -137,11 +150,31 @@
         q, g, k, v = (columns(both, kind, e) for kind in range(4))
         asked.append(jnp.concatenate([q, g], axis=1))
         held.append(jnp.concatenate([k, v], axis=1))
-    second = ((c_ref[0] >> 3) & 1) == 1
+    second = bit(c_ref[0], SPLIT) == 1
     keep_ref[...] = jnp.where(second, asked[1], asked[0])
     give_ref[...] = jnp.where(second, asked[0], asked[1])
     for i in range(N_FAR):
-        held_ref[i] = held[(i >> 1) & 1]
+        held_ref[i] = held[head_of(i)]
+
+
+def head_of(i):
+    return (i >> (1 - REST.index(SPLIT))) & 1
+
+
+def join_kernel(axis, c_ref, mine_ref, got_ref, out_ref):
+    second = bit(c_ref[0], axis) == 1
+    n = mine_ref.shape[0]
+    mine, got = mine_ref[...], got_ref[...]
+    out_ref[:n] = jnp.where(second, got, mine)
+    out_ref[n:] = jnp.where(second, mine, got)
+
+
+def halve_kernel(axis, c_ref, keep_ref, got_ref, rest_ref, give_ref):
+    second = bit(c_ref[0], axis) == 1
+    total = keep_ref[...] + got_ref[...].astype(F32)
+    half = total.shape[0] // 2
+    rest_ref[...] = jnp.where(second, total[half:], total[:half]).astype(rest_ref.dtype)
+    give_ref[...] = jnp.where(second, total[:half], total[half:]).astype(BF)
 
 
 def unpack(asked_ref, held_ref):
@@ -150,12 +183,18 @@
     return asked_ref[:, :HD], asked_ref[:, HD:], k, v
 
 
+def moved_bits(index, axes, c):
+    block = sum(((index >> i) & 1) << BITS[axis] for i, axis in enumerate(axes))
+    fixed = sum(1 << BITS[axis] for axis in BITS if axis not in axes)
+    return block + (c & fixed)
+
+
 def scores(c, q, k):
     row = iota((1, TILE_Q), 1)
-    block = ((row >> 6) & 1) * 8 + ((row >> 7) & 1) + ((row >> 8) & 1) * 4 + (c & 50)
+    block = moved_bits(row >> 6, (SPLIT, TWICE, AGAIN), c) + (c & 48)
     query = ROWS * block + (row & 63) + HALF
     col = iota((TILE_K, 1), 0)
-    block = (col >> 8) * 16 + ((col >> 7) & 1) * 8 + ((col >> 6) & 1) * 2 + (c & 5)
+    block = moved_bits(col >> 6, REST[::-1], c) + (col >> 8) * 16
     key = ROWS * block + (col & 63) + HALF
     allowed = (query & (TOTAL - 1)) >= (key & (TOTAL - 1))
     return jnp.where(allowed, dot(k, q, ((1,), (1,))) * (SCALE * LOG2E), NEG)
@@ -195,16 +234,16 @@
     term_ref[:, :, HD:] = d_value.reshape(N_FAR, ROWS, HD)
     d_query = dot(dscore, k, ((0,), (0,))) * SCALE
     out = dot(prob, v, ((0,), (0,)))
-    second = ((c_ref[0] >> 2) & 1) == 1
+    second = bit(c_ref[0], AGAIN) == 1
     half = TILE_Q // 2
     for value, at in ((d_query, 0), (out, HD)):
         keep_ref[:, at : at + HD] = jnp.where(second, value[half:], value[:half])
         give_ref[:, at : at + HD] = jnp.where(second, value[:half], value[half:]).astype(BF)
 
 
-def sum_kernel(c_ref, term_ref, keep_ref, got_ref, w_ref, piece_ref, out_ref):
-    second = ((c_ref[0] >> 3) & 1) == 1
-    keep, got = keep_ref[...].astype(BF), got_ref[...]
+def sum_kernel(c_ref, term_ref, keep_ref, got_ref, w_ref, tables_any, piece_ref, out_ref):
+    second = bit(c_ref[0], SPLIT) == 1
+    keep, got = keep_ref[...], got_ref[...]
     asked = [jnp.where(second, got, keep), jnp.where(second, keep, got)]
     d_query = jnp.concatenate([x[:, :HD] for x in asked], axis=1)
     out_ref[...] = jnp.concatenate([x[:, HD:] for x in asked], axis=1)
@@ -212,7 +251,7 @@
     for e in range(HEADS):
         total = jnp.zeros((ROWS, 2 * HD), F32)
         for i in range(N_FAR):
-            if (i >> 1) & 1 == e:
+            if head_of(i) == e:
                 total = total + term_ref[i].astype(F32)
         held.append(total.astype(BF))
     d_key = jnp.concatenate([x[:, :HD] for x in held], axis=1)
@@ -267,37 +306,40 @@
     )(c_ref, *ins)
 
 
-def doubled(mine, axis):
-    got = shift(mine, axis, 2, 1)
-    second = lax.axis_index(axis) == 1
-    return jnp.concatenate([jnp.where(second, got, mine), jnp.where(second, mine, got)], axis=0)
-
-
-def halved(keep, got, axis):
-    total = keep + got.astype(F32)
-    half = total.shape[0] // 2
-    second = lax.axis_index(axis) == 1
-    keep = jnp.where(second, total[half:], total[:half])
-    return keep, jnp.where(second, total[:half], total[half:]).astype(BF)
+def pair(rows, dtype=BF):
+    return shaped((rows, 2 * HD), dtype)
+
+
+def joined(c_ref, mine, got, axis):
+    kernel = functools.partial(join_kernel, axis)
+    return call(kernel, (c_ref, mine, got), (pair(2 * mine.shape[0]),), JOIN, 1)[0]
+
+
+def halved(c_ref, keep, got, axis, dtype):
+    half = keep.shape[0] // 2
+    kernel = functools.partial(halve_kernel, axis)
+    return call(kernel, (c_ref, keep, got), (pair(half, dtype), pair(half)), HALVE, 1)
 
 
 def shards(byte_states, patch_of_byte, patch_first, moved, w_qkv, d_attn):
     c_ref = lax.axis_index(CTX).astype(I32).reshape(1)
     n_bytes = patch_of_byte.shape[0]
     place = patch_of_byte.reshape(1, n_bytes)
-    pair = shaped((ROWS, 2 * HD), BF)
     stack = shaped((N_FAR, ROWS, 2 * HD), BF)
 
     sent, own = pool(c_ref, patch_first, moved, place, byte_states, d_attn, w_qkv)
     (own,) = call(hold_kernel, (own,), (shaped(own.shape, BF),), 100_000)
     keep, give, held = call(
-        spread_kernel, (c_ref, own, shift(sent, CTX, N_CTX, -1)), (pair, pair, stack), 1_000_000, 1
+        spread_kernel,
+        (c_ref, own, shift(sent, CTX, N_CTX, -1)),
+        (pair(ROWS), pair(ROWS), stack),
+        1_000_000,
+        1,
     )
     held = swap(held, FAR)
-    got = shift(give, "zl", 2, 1)
-    second = lax.axis_index("zl") == 1
-    asked = jnp.concatenate([jnp.where(second, got, keep), jnp.where(second, keep, got)], axis=0)
-    asked = doubled(doubled(asked, "xl"), "yl")
+    asked = joined(c_ref, keep, shift(give, SPLIT, 2, 1), SPLIT)
+    for axis in (TWICE, AGAIN):
+        asked = joined(c_ref, asked, shift(asked, axis, 2, 1), axis)
     (stats,) = call(
         forward_kernel,
         (c_ref, asked, held),
@@ -305,27 +347,16 @@
         300_000_000,
         1,
     )
-    half = (TILE_Q // 2, 2 * HD)
     terms, keep, give = call(
         backward_kernel,
         (c_ref, asked, held, swap(stats, NEAR)),
-        (stack, shaped(half, F32), shaped(half, BF)),
+        (stack, pair(TILE_Q // 2, F32), pair(TILE_Q // 2)),
         900_000_000,
         1,
     )
     terms = swap(terms, FAR)
-    keep, give = halved(keep, shift(give, "yl", 2, 1), "xl")
-    keep, give = halved(keep, shift(give, "xl", 2, 1), "zl")
-    pieces, out = call(
-        sum_kernel,
-        (c_ref, terms, keep, shift(give, "zl", 2, 1), w_qkv),
-        (shaped((N_TP, ROWS, HD), BF), shaped((ROWS, FEATS), BF)),
-        100_000_000,
-        1,
-    )
-    (both,) = call(
-        head_sum_kernel, (swap(pieces, "tp"), out), (shaped((ROWS, HD + FEATS), BF),), 100_000
-    )
+    keep, give = halved(c_ref, keep, shift(give, AGAIN, 2, 1), TWICE, F32)
+    keep, give = halved(c_ref, keep, shift(give, TWICE, 2, 1), SPLIT, BF)
     picker, member, length = call(
         place_kernel,
         (c_ref, patch_first, moved, place),
@@ -337,6 +368,17 @@
         10_000_000,
         3,
     )
+    pieces, out = call(
+        sum_kernel,
+        (c_ref, terms, keep, shift(give, SPLIT, 2, 1), w_qkv, picker),
+        (shaped((N_TP, ROWS, HD), BF), shaped((ROWS, FEATS), BF)),
+        100_000_000,
+        1,
+        1,
+    )
+    (both,) = call(
+        head_sum_kernel, (swap(pieces, "tp"), out), (shaped((ROWS, HD + FEATS), BF),), 100_000
+    )
     attn_out, byte_grad = call(
         last_kernel,
         (shift(both, CTX, N_CTX, 1), both, picker, member, length),

time: 112 us -> 112 us (level)
    pallas_call x8 -> x13, Pallas kernels: 6.61 us -> 6.7 us  [call(): pl.pallas_call(kernel, out_shape=tuple(outs), in_specs=[smem] * scalars +...]
where the time goes in v8:
time: 112 us; the launch traced here: 111 us
  starting transfers between devices  47.5 us (42%)
  blocking collectives  31.4 us (28%)
  waiting for transfers between devices  21.2 us (19%)
  Pallas kernels  9.64 us (9%)
    ppermute x8, starting transfers between devices, shift(): return lax.ppermute(x, axis, [(i, (i + by) % n) for i in range(n)])  36.8 us
    all_to_all x2, blocking collectives, swap(): return lax.all_to_all(x, axis, split_axis=0, concat_axis=0, tiled=True)  31.4 us
    ppermute x8, waiting for transfers between devices, shift(): return lax.ppermute(x, axis, [(i, (i + by) % n) for i in range(n)])  17.8 us
    all_to_all x2, starting transfers between devices, swap(): return lax.all_to_all(x, axis, split_axis=0, concat_axis=0, tiled=True)  10.7 us
    pallas_call x13, Pallas kernels, call(): pl.pallas_call(kernel, out_shape=tuple(outs), in_specs=[smem] * scalars +...  6.7 us
    all_to_all x2, waiting for transfers between devices, swap(): return lax.all_to_all(x, axis, split_axis=0, concat_axis=0, tiled=True)  3.39 us
    pallas_call x1, Pallas kernels, pool(): pl.pallas_call(pool_kernel, out_shape=(block, block), in_specs=[pl.BlockS...  2.94 us
  transfers between devices with their start and end apart: 10, of which 8 were waited for; matrix products, arithmetic and copies ran while one was open for 0% of the time, Pallas kernels for 1%

profile of v8, /device:TPU:1, one launch (start us, length us, event | category | flops | bytes accessed | tf_op | source)
XLA Modules:
  0.0 111.5 jit_solution(14380439387805694608)
XLA Ops:
  0.6 2.9 %shard_map.77 = (bf16[64,1024]{1,0:T(8,128)(2,1)}, bf16[64,1024]{1,0:T(8,128)(2,1)}) custom-call(s32[1]{0:T(128)} %bitcast.c_ref, s32[64]{0:T(128)} %first_ref.1, s32[2,64]{1,0:T(2,128)} %moved_ref.1, s32[1,256]{1,0:T(1,128)} %bitcast.2, bf16[256,1024]{1,0:T(8,128)(2,1)} %bytes_hbm.1, bf16[64,256]{1,0:T(8,128)(2,1)} %grad_hbm.1, bf16[3,1024,256]{2,1,0:T(8,128)(2,1)} %w_ref.1), custom_call_target="tpu_custom_call" | custom-call | flops 300000000 | bytes 2500000 | tf_op jit(solution)/shard_map/pallas_call | solution.py:297
  3.6 14.7 %collective-permute-start = (bf16[64,1024]{1,0:T(8,128)(2,1)}, bf16[64,1024]{1,0:T(8,128)(2,1)S(1)}, u32[]{:S(2)}, u32[]{:S(2)}) collective-permute-start(bf16[64,1024]{1,0:T(8,128)(2,1)} %get-tuple-element.20), channel_id=1, source_target_pairs={{0,504},{8,0},{16,8},{24,16},{32,24},{40,32},{48,40},{56,48},{64,5... | collective-permute-start | bytes 393224 | tf_op jit(solution)/shard_map/ppermute | solution.py:48
  18.3 0.0 copy-start.1
  18.3 0.9 copy-done.1
  19.2 1.5 %collective-permute-done.got_ref = bf16[64,1024]{1,0:T(8,128)(2,1)S(1)} collective-permute-done((bf16[64,1024]{1,0:T(8,128)(2,1)}, bf16[64,1024]{1,0:T(8,128)(2,1)S(1)}, u32[]{:S(2)}, u32[]{:S(2)}) %collective-permute-start) | collective-permute-done | bytes 131104 | tf_op jit(solution)/shard_map/ppermute | solution.py:48
  20.8 0.9 shard_map.79
  21.6 1.9 %collective-permute-start.1 = (bf16[64,256]{1,0:T(8,128)(2,1)S(1)}, bf16[64,256]{1,0:T(8,128)(2,1)S(1)}, u32[]{:S(2)}, u32[]{:S(2)}) collective-permute-start(bf16[64,256]{1,0:T(8,128)(2,1)S(1)} %get-tuple-element.22), channel_id=1, source_target_pairs={{0,64},{64,0},{1,65},{65,1},{2,66},{66,2},{3,67},{67,3},{4,68},{68... | collective-permute-start | bytes 98312 | tf_op jit(solution)/shard_map/ppermute | solution.py:48
  23.5 3.9 %all-to-all-start = ((bf16[16,64,256]{2,1,0:T(8,128)(2,1)}), bf16[16,64,256]{2,1,0:T(8,128)(2,1)S(1)}, u32[]{:S(2)}, u32[]{:S(2)}) async-start(bf16[16,64,256]{2,1,0:T(8,128)(2,1)} %get-tuple-element.23), calls=%async_computation | async-start | bytes 1048576 | tf_op jit(solution)/shard_map/all_to_all | solution.py:52
  27.5 0.0 collective-permute-done.1.got_ref
  27.5 4.3 %collective-permute-start.2 = (bf16[128,256]{1,0:T(8,128)(2,1)S(1)}, bf16[128,256]{1,0:T(8,128)(2,1)S(1)}, u32[]{:S(2)}, u32[]{:S(2)}) collective-permute-start(bf16[128,256]{1,0:T(8,128)(2,1)S(1)} %shard_map.80.mine_ref), channel_id=1, source_target_pairs={{0,8},{8,0},{1,9},{9,1},{2,10},{10,2},{3,11},{11,3},{4,12},{12,4},... | collective-permute-start | bytes 196616 | tf_op jit(solution)/shard_map/ppermute | solution.py:48
  31.8 2.2 %collective-permute-done.2.got_ref = bf16[128,256]{1,0:T(8,128)(2,1)S(1)} collective-permute-done((bf16[128,256]{1,0:T(8,128)(2,1)S(1)}, bf16[128,256]{1,0:T(8,128)(2,1)S(1)}, u32[]{:S(2)}, u32[]{:S(2)}) %collective-permute-start.2) | collective-permute-done | bytes 65568 | tf_op jit(solution)/shard_map/ppermute | solution.py:48
  34.1 5.3 %collective-permute-start.3 = (bf16[256,256]{1,0:T(8,128)(2,1)S(1)}, bf16[256,256]{1,0:T(8,128)(2,1)S(1)}, u32[]{:S(2)}, u32[]{:S(2)}) collective-permute-start(bf16[256,256]{1,0:T(8,128)(2,1)S(1)} %shard_map.81.mine_ref), channel_id=1, source_target_pairs={{0,32},{32,0},{1,33},{33,1},{2,34},{34,2},{3,35},{35,3},{4,36},{36... | collective-permute-start | bytes 393224 | tf_op jit(solution)/shard_map/ppermute | solution.py:48
  39.4 2.6 %collective-permute-done.3.got_ref = bf16[256,256]{1,0:T(8,128)(2,1)S(1)} collective-permute-done((bf16[256,256]{1,0:T(8,128)(2,1)S(1)}, bf16[256,256]{1,0:T(8,128)(2,1)S(1)}, u32[]{:S(2)}, u32[]{:S(2)}) %collective-permute-start.3) | collective-permute-done | bytes 131104 | tf_op jit(solution)/shard_map/ppermute | solution.py:48
  42.0 1.3 %all-to-all-done.held_ref = bf16[16,64,256]{2,1,0:T(8,128)(2,1)S(1)} async-done(((bf16[16,64,256]{2,1,0:T(8,128)(2,1)}), bf16[16,64,256]{2,1,0:T(8,128)(2,1)S(1)}, u32[]{:S(2)}, u32[]{:S(2)}) %all-to-all-start) | async-done | bytes 524320 | tf_op jit(solution)/shard_map/all_to_all | solution.py:52
  43.3 1.1 shard_map.83
  44.4 10.3 %all_to_all.20.stats_ref = f32[4,8,512]{2,1,0:T(8,128)S(1)} all-to-all(f32[4,8,512]{2,1,0:T(8,128)S(1)} %shard_map.83), channel_id=1, replica_groups=mesh['zh'=4,'zl'=2,'yl'=2,'xh'=2,'xl'=2,'tp'=8] {'yl','xl'}, dimensions={0} | all-to-all | bytes 131072 | tf_op jit(solution)/shard_map/all_to_all | solution.py:52
  54.7 2.4 %shard_map.84 = (bf16[16,64,256]{2,1,0:T(8,128)(2,1)}, f32[256,256]{1,0:T(8,128)S(1)}, bf16[256,256]{1,0:T(8,128)(2,1)S(1)}) custom-call(s32[1]{0:T(128)} %bitcast.c_ref, bf16[512,256]{1,0:T(8,128)(2,1)S(1)} %shard_map.82.asked_ref, bf16[16,64,256]{2,1,0:T(8,128)(2,1)S(1)} %all-to-all-done.held_ref, f32[4,8,512]{2,1,0:T(8,128)S(1)} %all_to_all.20.stats_ref), custom_call_target="tpu_custom_call" | custom-call | flops 900000000 | bytes 1769476 | tf_op jit(solution)/shard_map/pallas_call | solution.py:63
  57.2 2.4 %collective-permute-start.4 = (bf16[256,256]{1,0:T(8,128)(2,1)S(1)}, bf16[256,256]{1,0:T(8,128)(2,1)S(1)}, u32[]{:S(2)}, u32[]{:S(2)}) collective-permute-start(bf16[256,256]{1,0:T(8,128)(2,1)S(1)} %get-tuple-element.26), channel_id=1, source_target_pairs={{0,32},{32,0},{1,33},{33,1},{2,34},{34,2},{3,35},{35,3},{4,36},{36... | collective-permute-start | bytes 393224 | tf_op jit(solution)/shard_map/ppermute | solution.py:48
  59.5 6.8 %all-to-all-start.2 = ((bf16[16,64,256]{2,1,0:T(8,128)(2,1)}), bf16[16,64,256]{2,1,0:T(8,128)(2,1)S(1)}, u32[]{:S(2)}, u32[]{:S(2)}) async-start(bf16[16,64,256]{2,1,0:T(8,128)(2,1)} %get-tuple-element.24), calls=%async_computation.2 | async-start | bytes 1048576 | tf_op jit(solution)/shard_map/all_to_all | solution.py:52
  66.3 0.0 collective-permute-done.4.got_ref
  66.4 1.9 %collective-permute-start.5 = (bf16[128,256]{1,0:T(8,128)(2,1)S(1)}, bf16[128,256]{1,0:T(8,128)(2,1)S(1)}, u32[]{:S(2)}, u32[]{:S(2)}) collective-permute-start(bf16[128,256]{1,0:T(8,128)(2,1)S(1)} %get-tuple-element.28), channel_id=1, source_target_pairs={{0,8},{8,0},{1,9},{9,1},{2,10},{10,2},{3,11},{11,3},{4,12},{12,4},... | collective-permute-start | bytes 196616 | tf_op jit(solution)/shard_map/ppermute | solution.py:48
  68.3 3.1 %collective-permute-done.5.got_ref = bf16[128,256]{1,0:T(8,128)(2,1)S(1)} collective-permute-done((bf16[128,256]{1,0:T(8,128)(2,1)S(1)}, bf16[128,256]{1,0:T(8,128)(2,1)S(1)}, u32[]{:S(2)}, u32[]{:S(2)}) %collective-permute-start.5) | collective-permute-done | bytes 65568 | tf_op jit(solution)/shard_map/ppermute | solution.py:48
  71.4 4.0 %collective-permute-start.6 = (bf16[64,256]{1,0:T(8,128)(2,1)S(1)}, bf16[64,256]{1,0:T(8,128)(2,1)S(1)}, u32[]{:S(2)}, u32[]{:S(2)}) collective-permute-start(bf16[64,256]{1,0:T(8,128)(2,1)S(1)} %get-tuple-element.30), channel_id=1, source_target_pairs={{0,64},{64,0},{1,65},{65,1},{2,66},{66,2},{3,67},{67,3},{4,68},{68... | collective-permute-start | bytes 98312 | tf_op jit(solution)/shard_map/ppermute | solution.py:48
  75.4 0.0 copy-done.2
  75.5 0.8 shard_map.87
  76.3 1.6 %collective-permute-done.6.got_ref = bf16[64,256]{1,0:T(8,128)(2,1)S(1)} collective-permute-done((bf16[64,256]{1,0:T(8,128)(2,1)S(1)}, bf16[64,256]{1,0:T(8,128)(2,1)S(1)}, u32[]{:S(2)}, u32[]{:S(2)}) %collective-permute-start.6) | collective-permute-done | bytes 32800 | tf_op jit(solution)/shard_map/ppermute | solution.py:48
  77.9 2.1 %all-to-all-done.2.term_ref = bf16[16,64,256]{2,1,0:T(8,128)(2,1)S(1)} async-done(((bf16[16,64,256]{2,1,0:T(8,128)(2,1)}), bf16[16,64,256]{2,1,0:T(8,128)(2,1)S(1)}, u32[]{:S(2)}, u32[]{:S(2)}) %all-to-all-start.2) | async-done | bytes 524320 | tf_op jit(solution)/shard_map/all_to_all | solution.py:52
  79.9 0.6 shard_map.88
  80.5 21.1 %all_to_all.21.pieces_ref = bf16[8,64,128]{2,1,0:T(8,128)(2,1)S(1)} all-to-all(bf16[8,64,128]{2,1,0:T(8,128)(2,1)S(1)} %get-tuple-element.32), channel_id=1, replica_groups=mesh['zh'=4,'zl'=2,'yl'=2,'xh'=2,'xl'=2,'tp'=8] {'tp'}, dimensions={0} | all-to-all | bytes 262144 | tf_op jit(solution)/shard_map/all_to_all | solution.py:52
  101.6 2.3 %collective-permute-start.7 = (bf16[64,384]{1,0:T(8,128)(2,1)S(1)}, bf16[64,384]{1,0:T(8,128)(2,1)S(1)}, u32[]{:S(2)}, u32[]{:S(2)}) collective-permute-start(bf16[64,384]{1,0:T(8,128)(2,1)S(1)} %shard_map.89.own_ref), channel_id=1, source_target_pairs={{0,8},{8,16},{16,24},{24,32},{32,40},{40,48},{48,56},{56,64},{64,7... | collective-permute-start | bytes 147464 | tf_op jit(solution)/shard_map/ppermute | solution.py:48
  103.9 6.8 %collective-permute-done.7.before_ref = bf16[64,384]{1,0:T(8,128)(2,1)S(1)} collective-permute-done((bf16[64,384]{1,0:T(8,128)(2,1)S(1)}, bf16[64,384]{1,0:T(8,128)(2,1)S(1)}, u32[]{:S(2)}, u32[]{:S(2)}) %collective-permute-start.7) | collective-permute-done | bytes 49184 | tf_op jit(solution)/shard_map/ppermute | solution.py:48
  110.7 0.8 shard_map.90
  (14 shorter events, 0.2 us)
Async XLA Ops:
  3.6 17.2 %collective-permute-start = (bf16[64,1024]{1,0:T(8,128)(2,1)}, bf16[64,1024]{1,0:T(8,128)(2,1)S(1)}, u32[]{:S(2)}, u32[]{:S(2)}) collective-permute-start(bf16[64,1024]{1,0:T(8,128)(2,1)} %get-tuple-element.20), channel_id=1, source_target_pairs={{0,504},{8,0},{16,8},{24,16},{32,24},{40,32},{48,40},{56,48},{64,5... | collective-permute-start | bytes 393224 | tf_op jit(solution)/shard_map/ppermute | solution.py:48
  18.3 0.9 copy-start.1
  21.6 5.8 %collective-permute-start.1 = (bf16[64,256]{1,0:T(8,128)(2,1)S(1)}, bf16[64,256]{1,0:T(8,128)(2,1)S(1)}, u32[]{:S(2)}, u32[]{:S(2)}) collective-permute-start(bf16[64,256]{1,0:T(8,128)(2,1)S(1)} %get-tuple-element.22), channel_id=1, source_target_pairs={{0,64},{64,0},{1,65},{65,1},{2,66},{66,2},{3,67},{67,3},{4,68},{68... | collective-permute-start | bytes 98312 | tf_op jit(solution)/shard_map/ppermute | solution.py:48
  23.5 19.8 %all-to-all-start = ((bf16[16,64,256]{2,1,0:T(8,128)(2,1)}), bf16[16,64,256]{2,1,0:T(8,128)(2,1)S(1)}, u32[]{:S(2)}, u32[]{:S(2)}) async-start(bf16[16,64,256]{2,1,0:T(8,128)(2,1)} %get-tuple-element.23), calls=%async_computation | async-start | bytes 1048576 | tf_op jit(solution)/shard_map/all_to_all | solution.py:52
  27.5 6.6 %collective-permute-start.2 = (bf16[128,256]{1,0:T(8,128)(2,1)S(1)}, bf16[128,256]{1,0:T(8,128)(2,1)S(1)}, u32[]{:S(2)}, u32[]{:S(2)}) collective-permute-start(bf16[128,256]{1,0:T(8,128)(2,1)S(1)} %shard_map.80.mine_ref), channel_id=1, source_target_pairs={{0,8},{8,0},{1,9},{9,1},{2,10},{10,2},{3,11},{11,3},{4,12},{12,4},... | collective-permute-start | bytes 196616 | tf_op jit(solution)/shard_map/ppermute | solution.py:48
  34.1 8.0 %collective-permute-start.3 = (bf16[256,256]{1,0:T(8,128)(2,1)S(1)}, bf16[256,256]{1,0:T(8,128)(2,1)S(1)}, u32[]{:S(2)}, u32[]{:S(2)}) collective-permute-start(bf16[256,256]{1,0:T(8,128)(2,1)S(1)} %shard_map.81.mine_ref), channel_id=1, source_target_pairs={{0,32},{32,0},{1,33},{33,1},{2,34},{34,2},{3,35},{35,3},{4,36},{36... | collective-permute-start | bytes 393224 | tf_op jit(solution)/shard_map/ppermute | solution.py:48
  57.2 9.2 %collective-permute-start.4 = (bf16[256,256]{1,0:T(8,128)(2,1)S(1)}, bf16[256,256]{1,0:T(8,128)(2,1)S(1)}, u32[]{:S(2)}, u32[]{:S(2)}) collective-permute-start(bf16[256,256]{1,0:T(8,128)(2,1)S(1)} %get-tuple-element.26), channel_id=1, source_target_pairs={{0,32},{32,0},{1,33},{33,1},{2,34},{34,2},{3,35},{35,3},{4,36},{36... | collective-permute-start | bytes 393224 | tf_op jit(solution)/shard_map/ppermute | solution.py:48
  59.5 20.4 %all-to-all-start.2 = ((bf16[16,64,256]{2,1,0:T(8,128)(2,1)}), bf16[16,64,256]{2,1,0:T(8,128)(2,1)S(1)}, u32[]{:S(2)}, u32[]{:S(2)}) async-start(bf16[16,64,256]{2,1,0:T(8,128)(2,1)} %get-tuple-element.24), calls=%async_computation.2 | async-start | bytes 1048576 | tf_op jit(solution)/shard_map/all_to_all | solution.py:52
  66.4 5.0 %collective-permute-start.5 = (bf16[128,256]{1,0:T(8,128)(2,1)S(1)}, bf16[128,256]{1,0:T(8,128)(2,1)S(1)}, u32[]{:S(2)}, u32[]{:S(2)}) collective-permute-start(bf16[128,256]{1,0:T(8,128)(2,1)S(1)} %get-tuple-element.28), channel_id=1, source_target_pairs={{0,8},{8,0},{1,9},{9,1},{2,10},{10,2},{3,11},{11,3},{4,12},{12,4},... | collective-permute-start | bytes 196616 | tf_op jit(solution)/shard_map/ppermute | solution.py:48
  71.4 4.1 %copy-start.2 = (s32[2,64]{1,0:T(2,128)S(1)}, s32[2,64]{1,0:T(2,128)}, u32[]{:S(2)}) copy-start(s32[2,64]{1,0:T(2,128)} %moved_ref.1) | copy-start | bytes 1540
  71.4 4.1 %copy-start.3 = (s32[256]{0:T(256)S(1)}, s32[256]{0:T(256)}, u32[]{:S(2)}) copy-start(s32[256]{0:T(256)} %param.7) | copy-start | bytes 3076
  71.4 4.1 %copy-start.4 = (s32[64]{0:T(128)S(1)}, s32[64]{0:T(128)}, u32[]{:S(2)}) copy-start(s32[64]{0:T(128)} %first_ref.1) | copy-start | bytes 772
  71.4 8.5 %copy-start = (bf16[3,1024,256]{2,1,0:T(8,128)(2,1)S(1)}, bf16[3,1024,256]{2,1,0:T(8,128)(2,1)}, u32[]{:S(2)}) copy-start(bf16[3,1024,256]{2,1,0:T(8,128)(2,1)} %w_ref.1) | copy-start | bytes 4718596
  71.4 6.4 %collective-permute-start.6 = (bf16[64,256]{1,0:T(8,128)(2,1)S(1)}, bf16[64,256]{1,0:T(8,128)(2,1)S(1)}, u32[]{:S(2)}, u32[]{:S(2)}) collective-permute-start(bf16[64,256]{1,0:T(8,128)(2,1)S(1)} %get-tuple-element.30), channel_id=1, source_target_pairs={{0,64},{64,0},{1,65},{65,1},{2,66},{66,2},{3,67},{67,3},{4,68},{68... | collective-permute-start | bytes 98312 | tf_op jit(solution)/shard_map/ppermute | solution.py:48
  101.6 9.1 %collective-permute-start.7 = (bf16[64,384]{1,0:T(8,128)(2,1)S(1)}, bf16[64,384]{1,0:T(8,128)(2,1)S(1)}, u32[]{:S(2)}, u32[]{:S(2)}) collective-permute-start(bf16[64,384]{1,0:T(8,128)(2,1)S(1)} %shard_map.89.own_ref), channel_id=1, source_target_pairs={{0,8},{8,16},{16,24},{24,32},{32,40},{40,48},{48,56},{56,64},{64,7... | collective-permute-start | bytes 147464 | tf_op jit(solution)/shard_map/ppermute | solution.py:48

commit v9 on v8

--- a/solution.py
+++ b/solution.py
@@ -12,7 +12,7 @@
 NAMES = ("zh", "zl", "yl", "xh", "xl", "tp")
 CTX = ("zh", "zl", "yl", "xh", "xl")
 BITS = {"zl": 3, "yl": 2, "xh": 1, "xl": 0}
-SPLIT, TWICE, AGAIN = "zl", "xl", "yl"
+SPLIT, TWICE, AGAIN = "xl", "yl", "zl"
 NEAR = tuple(a for a in BITS if a in (TWICE, AGAIN))
 REST = tuple(a for a in BITS if a not in NEAR)
 FAR = ("zh",) + REST

time: 112 us -> 111 us (level)
  starting transfers between devices: 47.5 us -> 45.6 us
    ppermute x8, waiting for transfers between devices: 17.8 us -> 20.4 us  [shift(): return lax.ppermute(x, axis, [(i, (i + by) % n) for i in range(n)])]
    all_to_all x2, waiting for transfers between devices: 3.39 us -> 1.19 us  [swap(): return lax.all_to_all(x, axis, split_axis=0, concat_axis=0, tiled=True)]
    ppermute x8, starting transfers between devices: 36.8 us -> 35.1 us  [shift(): return lax.ppermute(x, axis, [(i, (i + by) % n) for i in range(n)])]
  transfers between devices with their start and end apart: 10 -> 10, of which waited for: 8 -> 7; matrix products, arithmetic and copies ran while one was open for 0% -> 0% of each run, Pallas kernels for 1% -> 1%
where the time goes in v9:
time: 111 us; the launch traced here: 110 us
  starting transfers between devices  45.6 us (41%)
  blocking collectives  31.6 us (28%)
  waiting for transfers between devices  21.6 us (19%)
  Pallas kernels  9.63 us (9%)
    ppermute x8, starting transfers between devices, shift(): return lax.ppermute(x, axis, [(i, (i + by) % n) for i in range(n)])  35.1 us
    all_to_all x2, blocking collectives, swap(): return lax.all_to_all(x, axis, split_axis=0, concat_axis=0, tiled=True)  31.6 us
    ppermute x8, waiting for transfers between devices, shift(): return lax.ppermute(x, axis, [(i, (i + by) % n) for i in range(n)])  20.4 us
    all_to_all x2, starting transfers between devices, swap(): return lax.all_to_all(x, axis, split_axis=0, concat_axis=0, tiled=True)  10.5 us
    pallas_call x13, Pallas kernels, call(): pl.pallas_call(kernel, out_shape=tuple(outs), in_specs=[smem] * scalars +...  6.69 us
    pallas_call x1, Pallas kernels, pool(): pl.pallas_call(pool_kernel, out_shape=(block, block), in_specs=[pl.BlockS...  2.94 us
  transfers between devices with their start and end apart: 10, of which 7 were waited for; matrix products, arithmetic and copies ran while one was open for 0% of the time, Pallas kernels for 1%

profile of v9, /device:TPU:1, one launch (start us, length us, event | category | flops | bytes accessed | tf_op | source)
XLA Modules:
  0.0 110.2 jit_solution(4534663360687754890)
XLA Ops:
  0.6 2.9 %shard_map.77 = (bf16[64,1024]{1,0:T(8,128)(2,1)}, bf16[64,1024]{1,0:T(8,128)(2,1)}) custom-call(s32[1]{0:T(128)} %bitcast.c_ref, s32[64]{0:T(128)} %first_ref.1, s32[2,64]{1,0:T(2,128)} %moved_ref.1, s32[1,256]{1,0:T(1,128)} %bitcast.2, bf16[256,1024]{1,0:T(8,128)(2,1)} %bytes_hbm.1, bf16[64,256]{1,0:T(8,128)(2,1)} %grad_hbm.1, bf16[3,1024,256]{2,1,0:T(8,128)(2,1)} %w_ref.1), custom_call_target="tpu_custom_call" | custom-call | flops 300000000 | bytes 2500000 | tf_op jit(solution)/shard_map/pallas_call | solution.py:297
  3.6 14.7 %collective-permute-start = (bf16[64,1024]{1,0:T(8,128)(2,1)}, bf16[64,1024]{1,0:T(8,128)(2,1)S(1)}, u32[]{:S(2)}, u32[]{:S(2)}) collective-permute-start(bf16[64,1024]{1,0:T(8,128)(2,1)} %get-tuple-element.20), channel_id=1, source_target_pairs={{0,504},{8,0},{16,8},{24,16},{32,24},{40,32},{48,40},{56,48},{64,5... | collective-permute-start | bytes 393224 | tf_op jit(solution)/shard_map/ppermute | solution.py:48
  18.3 0.9 copy-done.1
  19.2 1.5 %collective-permute-done.got_ref = bf16[64,1024]{1,0:T(8,128)(2,1)S(1)} collective-permute-done((bf16[64,1024]{1,0:T(8,128)(2,1)}, bf16[64,1024]{1,0:T(8,128)(2,1)S(1)}, u32[]{:S(2)}, u32[]{:S(2)}) %collective-permute-start) | collective-permute-done | bytes 131104 | tf_op jit(solution)/shard_map/ppermute | solution.py:48
  20.8 0.9 shard_map.79
  21.6 1.9 %collective-permute-start.1 = (bf16[64,256]{1,0:T(8,128)(2,1)S(1)}, bf16[64,256]{1,0:T(8,128)(2,1)S(1)}, u32[]{:S(2)}, u32[]{:S(2)}) collective-permute-start(bf16[64,256]{1,0:T(8,128)(2,1)S(1)} %get-tuple-element.22), channel_id=1, source_target_pairs={{0,8},{8,0},{1,9},{9,1},{2,10},{10,2},{3,11},{11,3},{4,12},{12,4},... | collective-permute-start | bytes 98312 | tf_op jit(solution)/shard_map/ppermute | solution.py:48
  23.5 5.7 %all-to-all-start = ((bf16[16,64,256]{2,1,0:T(8,128)(2,1)}), bf16[16,64,256]{2,1,0:T(8,128)(2,1)S(1)}, u32[]{:S(2)}, u32[]{:S(2)}) async-start(bf16[16,64,256]{2,1,0:T(8,128)(2,1)} %get-tuple-element.23), calls=%async_computation | async-start | bytes 1048576 | tf_op jit(solution)/shard_map/all_to_all | solution.py:52
  29.3 0.0 collective-permute-done.1.got_ref
  29.3 4.1 %collective-permute-start.2 = (bf16[128,256]{1,0:T(8,128)(2,1)S(1)}, bf16[128,256]{1,0:T(8,128)(2,1)S(1)}, u32[]{:S(2)}, u32[]{:S(2)}) collective-permute-start(bf16[128,256]{1,0:T(8,128)(2,1)S(1)} %shard_map.80.mine_ref), channel_id=1, source_target_pairs={{0,32},{32,0},{1,33},{33,1},{2,34},{34,2},{3,35},{35,3},{4,36},{36... | collective-permute-start | bytes 196616 | tf_op jit(solution)/shard_map/ppermute | solution.py:48
  33.4 1.9 %collective-permute-done.2.got_ref = bf16[128,256]{1,0:T(8,128)(2,1)S(1)} collective-permute-done((bf16[128,256]{1,0:T(8,128)(2,1)S(1)}, bf16[128,256]{1,0:T(8,128)(2,1)S(1)}, u32[]{:S(2)}, u32[]{:S(2)}) %collective-permute-start.2) | collective-permute-done | bytes 65568 | tf_op jit(solution)/shard_map/ppermute | solution.py:48
  35.4 4.3 %collective-permute-start.3 = (bf16[256,256]{1,0:T(8,128)(2,1)S(1)}, bf16[256,256]{1,0:T(8,128)(2,1)S(1)}, u32[]{:S(2)}, u32[]{:S(2)}) collective-permute-start(bf16[256,256]{1,0:T(8,128)(2,1)S(1)} %shard_map.81.mine_ref), channel_id=1, source_target_pairs={{0,64},{64,0},{1,65},{65,1},{2,66},{66,2},{3,67},{67,3},{4,68},{68... | collective-permute-start | bytes 393224 | tf_op jit(solution)/shard_map/ppermute | solution.py:48
  39.7 5.8 %collective-permute-done.3.got_ref = bf16[256,256]{1,0:T(8,128)(2,1)S(1)} collective-permute-done((bf16[256,256]{1,0:T(8,128)(2,1)S(1)}, bf16[256,256]{1,0:T(8,128)(2,1)S(1)}, u32[]{:S(2)}, u32[]{:S(2)}) %collective-permute-start.3) | collective-permute-done | bytes 131104 | tf_op jit(solution)/shard_map/ppermute | solution.py:48
  45.5 0.0 all-to-all-done.held_ref
  45.5 1.1 shard_map.83
  46.6 10.1 %all_to_all.20.stats_ref = f32[4,8,512]{2,1,0:T(8,128)S(1)} all-to-all(f32[4,8,512]{2,1,0:T(8,128)S(1)} %shard_map.83), channel_id=1, replica_groups=mesh['zh'=4,'zl'=2,'yl'=2,'xh'=2,'xl'=2,'tp'=8] {'zl','yl'}, dimensions={0} | all-to-all | bytes 131072 | tf_op jit(solution)/shard_map/all_to_all | solution.py:52
  56.7 2.4 %shard_map.84 = (bf16[16,64,256]{2,1,0:T(8,128)(2,1)}, f32[256,256]{1,0:T(8,128)S(1)}, bf16[256,256]{1,0:T(8,128)(2,1)S(1)}) custom-call(s32[1]{0:T(128)} %bitcast.c_ref, bf16[512,256]{1,0:T(8,128)(2,1)S(1)} %shard_map.82.asked_ref, bf16[16,64,256]{2,1,0:T(8,128)(2,1)S(1)} %all-to-all-done.held_ref, f32[4,8,512]{2,1,0:T(8,128)S(1)} %all_to_all.20.stats_ref), custom_call_target="tpu_custom_call" | custom-call | flops 900000000 | bytes 1769476 | tf_op jit(solution)/shard_map/pallas_call | solution.py:63
  59.1 2.7 %collective-permute-start.4 = (bf16[256,256]{1,0:T(8,128)(2,1)S(1)}, bf16[256,256]{1,0:T(8,128)(2,1)S(1)}, u32[]{:S(2)}, u32[]{:S(2)}) collective-permute-start(bf16[256,256]{1,0:T(8,128)(2,1)S(1)} %get-tuple-element.26), channel_id=1, source_target_pairs={{0,64},{64,0},{1,65},{65,1},{2,66},{66,2},{3,67},{67,3},{4,68},{68... | collective-permute-start | bytes 393224 | tf_op jit(solution)/shard_map/ppermute | solution.py:48
  61.8 4.8 %all-to-all-start.2 = ((bf16[16,64,256]{2,1,0:T(8,128)(2,1)}), bf16[16,64,256]{2,1,0:T(8,128)(2,1)S(1)}, u32[]{:S(2)}, u32[]{:S(2)}) async-start(bf16[16,64,256]{2,1,0:T(8,128)(2,1)} %get-tuple-element.24), calls=%async_computation.2 | async-start | bytes 1048576 | tf_op jit(solution)/shard_map/all_to_all | solution.py:52
  66.6 0.0 collective-permute-done.4.got_ref
  66.6 2.1 %collective-permute-start.5 = (bf16[128,256]{1,0:T(8,128)(2,1)S(1)}, bf16[128,256]{1,0:T(8,128)(2,1)S(1)}, u32[]{:S(2)}, u32[]{:S(2)}) collective-permute-start(bf16[128,256]{1,0:T(8,128)(2,1)S(1)} %get-tuple-element.28), channel_id=1, source_target_pairs={{0,32},{32,0},{1,33},{33,1},{2,34},{34,2},{3,35},{35,3},{4,36},{36... | collective-permute-start | bytes 196616 | tf_op jit(solution)/shard_map/ppermute | solution.py:48
  68.7 2.9 %collective-permute-done.5.got_ref = bf16[128,256]{1,0:T(8,128)(2,1)S(1)} collective-permute-done((bf16[128,256]{1,0:T(8,128)(2,1)S(1)}, bf16[128,256]{1,0:T(8,128)(2,1)S(1)}, u32[]{:S(2)}, u32[]{:S(2)}) %collective-permute-start.5) | collective-permute-done | bytes 65568 | tf_op jit(solution)/shard_map/ppermute | solution.py:48
  71.7 3.4 %collective-permute-start.6 = (bf16[64,256]{1,0:T(8,128)(2,1)S(1)}, bf16[64,256]{1,0:T(8,128)(2,1)S(1)}, u32[]{:S(2)}, u32[]{:S(2)}) collective-permute-start(bf16[64,256]{1,0:T(8,128)(2,1)S(1)} %get-tuple-element.30), channel_id=1, source_target_pairs={{0,8},{8,0},{1,9},{9,1},{2,10},{10,2},{3,11},{11,3},{4,12},{12,4},... | collective-permute-start | bytes 98312 | tf_op jit(solution)/shard_map/ppermute | solution.py:48
  75.1 0.0 copy-done.2
  75.1 0.0 copy-done.3
  75.1 0.8 shard_map.87
  75.9 1.2 %collective-permute-done.6.got_ref = bf16[64,256]{1,0:T(8,128)(2,1)S(1)} collective-permute-done((bf16[64,256]{1,0:T(8,128)(2,1)S(1)}, bf16[64,256]{1,0:T(8,128)(2,1)S(1)}, u32[]{:S(2)}, u32[]{:S(2)}) %collective-permute-start.6) | collective-permute-done | bytes 32800 | tf_op jit(solution)/shard_map/ppermute | solution.py:48
  77.1 1.2 %all-to-all-done.2.term_ref = bf16[16,64,256]{2,1,0:T(8,128)(2,1)S(1)} async-done(((bf16[16,64,256]{2,1,0:T(8,128)(2,1)}), bf16[16,64,256]{2,1,0:T(8,128)(2,1)S(1)}, u32[]{:S(2)}, u32[]{:S(2)}) %all-to-all-start.2) | async-done | bytes 524320 | tf_op jit(solution)/shard_map/all_to_all | solution.py:52
  78.3 0.6 shard_map.88
  78.9 21.5 %all_to_all.21.pieces_ref = bf16[8,64,128]{2,1,0:T(8,128)(2,1)S(1)} all-to-all(bf16[8,64,128]{2,1,0:T(8,128)(2,1)S(1)} %get-tuple-element.32), channel_id=1, replica_groups=mesh['zh'=4,'zl'=2,'yl'=2,'xh'=2,'xl'=2,'tp'=8] {'tp'}, dimensions={0} | all-to-all | bytes 262144 | tf_op jit(solution)/shard_map/all_to_all | solution.py:52
  100.4 1.9 %collective-permute-start.7 = (bf16[64,384]{1,0:T(8,128)(2,1)S(1)}, bf16[64,384]{1,0:T(8,128)(2,1)S(1)}, u32[]{:S(2)}, u32[]{:S(2)}) collective-permute-start(bf16[64,384]{1,0:T(8,128)(2,1)S(1)} %shard_map.89.own_ref), channel_id=1, source_target_pairs={{0,8},{8,16},{16,24},{24,32},{32,40},{40,48},{48,56},{56,64},{64,7... | collective-permute-start | bytes 147464 | tf_op jit(solution)/shard_map/ppermute | solution.py:48
  102.3 7.1 %collective-permute-done.7.before_ref = bf16[64,384]{1,0:T(8,128)(2,1)S(1)} collective-permute-done((bf16[64,384]{1,0:T(8,128)(2,1)S(1)}, bf16[64,384]{1,0:T(8,128)(2,1)S(1)}, u32[]{:S(2)}, u32[]{:S(2)}) %collective-permute-start.7) | collective-permute-done | bytes 49184 | tf_op jit(solution)/shard_map/ppermute | solution.py:48
  109.4 0.8 shard_map.90
  (14 shorter events, 0.2 us)
Async XLA Ops:
  3.6 17.2 %collective-permute-start = (bf16[64,1024]{1,0:T(8,128)(2,1)}, bf16[64,1024]{1,0:T(8,128)(2,1)S(1)}, u32[]{:S(2)}, u32[]{:S(2)}) collective-permute-start(bf16[64,1024]{1,0:T(8,128)(2,1)} %get-tuple-element.20), channel_id=1, source_target_pairs={{0,504},{8,0},{16,8},{24,16},{32,24},{40,32},{48,40},{56,48},{64,5... | collective-permute-start | bytes 393224 | tf_op jit(solution)/shard_map/ppermute | solution.py:48
  18.3 0.9 copy-start.1
  21.6 7.7 %collective-permute-start.1 = (bf16[64,256]{1,0:T(8,128)(2,1)S(1)}, bf16[64,256]{1,0:T(8,128)(2,1)S(1)}, u32[]{:S(2)}, u32[]{:S(2)}) collective-permute-start(bf16[64,256]{1,0:T(8,128)(2,1)S(1)} %get-tuple-element.22), channel_id=1, source_target_pairs={{0,8},{8,0},{1,9},{9,1},{2,10},{10,2},{3,11},{11,3},{4,12},{12,4},... | collective-permute-start | bytes 98312 | tf_op jit(solution)/shard_map/ppermute | solution.py:48
  23.5 22.0 %all-to-all-start = ((bf16[16,64,256]{2,1,0:T(8,128)(2,1)}), bf16[16,64,256]{2,1,0:T(8,128)(2,1)S(1)}, u32[]{:S(2)}, u32[]{:S(2)}) async-start(bf16[16,64,256]{2,1,0:T(8,128)(2,1)} %get-tuple-element.23), calls=%async_computation | async-start | bytes 1048576 | tf_op jit(solution)/shard_map/all_to_all | solution.py:52
  29.3 6.0 %collective-permute-start.2 = (bf16[128,256]{1,0:T(8,128)(2,1)S(1)}, bf16[128,256]{1,0:T(8,128)(2,1)S(1)}, u32[]{:S(2)}, u32[]{:S(2)}) collective-permute-start(bf16[128,256]{1,0:T(8,128)(2,1)S(1)} %shard_map.80.mine_ref), channel_id=1, source_target_pairs={{0,32},{32,0},{1,33},{33,1},{2,34},{34,2},{3,35},{35,3},{4,36},{36... | collective-permute-start | bytes 196616 | tf_op jit(solution)/shard_map/ppermute | solution.py:48
  35.4 10.1 %collective-permute-start.3 = (bf16[256,256]{1,0:T(8,128)(2,1)S(1)}, bf16[256,256]{1,0:T(8,128)(2,1)S(1)}, u32[]{:S(2)}, u32[]{:S(2)}) collective-permute-start(bf16[256,256]{1,0:T(8,128)(2,1)S(1)} %shard_map.81.mine_ref), channel_id=1, source_target_pairs={{0,64},{64,0},{1,65},{65,1},{2,66},{66,2},{3,67},{67,3},{4,68},{68... | collective-permute-start | bytes 393224 | tf_op jit(solution)/shard_map/ppermute | solution.py:48
  59.1 7.4 %collective-permute-start.4 = (bf16[256,256]{1,0:T(8,128)(2,1)S(1)}, bf16[256,256]{1,0:T(8,128)(2,1)S(1)}, u32[]{:S(2)}, u32[]{:S(2)}) collective-permute-start(bf16[256,256]{1,0:T(8,128)(2,1)S(1)} %get-tuple-element.26), channel_id=1, source_target_pairs={{0,64},{64,0},{1,65},{65,1},{2,66},{66,2},{3,67},{67,3},{4,68},{68... | collective-permute-start | bytes 393224 | tf_op jit(solution)/shard_map/ppermute | solution.py:48
  61.8 16.5 %all-to-all-start.2 = ((bf16[16,64,256]{2,1,0:T(8,128)(2,1)}), bf16[16,64,256]{2,1,0:T(8,128)(2,1)S(1)}, u32[]{:S(2)}, u32[]{:S(2)}) async-start(bf16[16,64,256]{2,1,0:T(8,128)(2,1)} %get-tuple-element.24), calls=%async_computation.2 | async-start | bytes 1048576 | tf_op jit(solution)/shard_map/all_to_all | solution.py:52
  66.6 5.0 %collective-permute-start.5 = (bf16[128,256]{1,0:T(8,128)(2,1)S(1)}, bf16[128,256]{1,0:T(8,128)(2,1)S(1)}, u32[]{:S(2)}, u32[]{:S(2)}) collective-permute-start(bf16[128,256]{1,0:T(8,128)(2,1)S(1)} %get-tuple-element.28), channel_id=1, source_target_pairs={{0,32},{32,0},{1,33},{33,1},{2,34},{34,2},{3,35},{35,3},{4,36},{36... | collective-permute-start | bytes 196616 | tf_op jit(solution)/shard_map/ppermute | solution.py:48
  71.6 3.5 %copy-start.2 = (s32[2,64]{1,0:T(2,128)S(1)}, s32[2,64]{1,0:T(2,128)}, u32[]{:S(2)}) copy-start(s32[2,64]{1,0:T(2,128)} %moved_ref.1) | copy-start | bytes 1540
  71.6 3.5 %copy-start.3 = (s32[256]{0:T(256)S(1)}, s32[256]{0:T(256)}, u32[]{:S(2)}) copy-start(s32[256]{0:T(256)} %param.7) | copy-start | bytes 3076
  71.6 3.5 %copy-start.4 = (s32[64]{0:T(128)S(1)}, s32[64]{0:T(128)}, u32[]{:S(2)}) copy-start(s32[64]{0:T(128)} %first_ref.1) | copy-start | bytes 772
  71.6 6.6 %copy-start = (bf16[3,1024,256]{2,1,0:T(8,128)(2,1)S(1)}, bf16[3,1024,256]{2,1,0:T(8,128)(2,1)}, u32[]{:S(2)}) copy-start(bf16[3,1024,256]{2,1,0:T(8,128)(2,1)} %w_ref.1) | copy-start | bytes 4718596
  71.7 5.4 %collective-permute-start.6 = (bf16[64,256]{1,0:T(8,128)(2,1)S(1)}, bf16[64,256]{1,0:T(8,128)(2,1)S(1)}, u32[]{:S(2)}, u32[]{:S(2)}) collective-permute-start(bf16[64,256]{1,0:T(8,128)(2,1)S(1)} %get-tuple-element.30), channel_id=1, source_target_pairs={{0,8},{8,0},{1,9},{9,1},{2,10},{10,2},{3,11},{11,3},{4,12},{12,4},... | collective-permute-start | bytes 98312 | tf_op jit(solution)/shard_map/ppermute | solution.py:48
  100.4 9.1 %collective-permute-start.7 = (bf16[64,384]{1,0:T(8,128)(2,1)S(1)}, bf16[64,384]{1,0:T(8,128)(2,1)S(1)}, u32[]{:S(2)}, u32[]{:S(2)}) collective-permute-start(bf16[64,384]{1,0:T(8,128)(2,1)S(1)} %shard_map.89.own_ref), channel_id=1, source_target_pairs={{0,8},{8,16},{16,24},{24,32},{32,40},{40,48},{48,56},{56,64},{64,7... | collective-permute-start | bytes 147464 | tf_op jit(solution)/shard_map/ppermute | solution.py:48

commit v10 on v9

--- a/solution.py
+++ b/solution.py
@@ -200,12 +200,14 @@
     return jnp.where(allowed, dot(k, q, ((1,), (1,))) * (SCALE * LOG2E), NEG)
 
 
-def forward_kernel(c_ref, asked_ref, held_ref, stats_ref):
+def forward_kernel(c_ref, asked_ref, held_ref, stats_ref, weight_ref, dprob_ref):
     q, g, k, v = unpack(asked_ref, held_ref)
     score = scores(c_ref[0], q, k)
     top = jnp.maximum(jnp.max(score, axis=0, keepdims=True), FLOOR)
     weight = jnp.exp2(score - top)
     dprob = dot(v, g, ((1,), (1,)))
+    weight_ref[...] = weight
+    dprob_ref[...] = dprob
     rows = [
         top,
         jnp.sum(weight, axis=0, keepdims=True),
@@ -216,17 +218,18 @@
         stats_ref[i] = rows
 
 
-def backward_kernel(c_ref, asked_ref, held_ref, stats_ref, term_ref, keep_ref, give_ref):
+def backward_kernel(
+    c_ref, asked_ref, held_ref, own_ref, stats_ref, weight_ref, dprob_ref, term_ref, keep_ref, give_ref
+):
     tops, sums, dots = (stats_ref[:, i, :] for i in range(3))
     peak = jnp.max(tops, axis=0, keepdims=True)
     each = jnp.exp2(tops - peak)
     norm = jnp.sum(each * sums, axis=0, keepdims=True)
     delta = jnp.sum(each * dots, axis=0, keepdims=True) / norm
-    lse = peak + jnp.log(norm) * LOG2E
+    factor = jnp.exp2(own_ref[0, 0:1, :] - peak) / norm
     q, g, k, v = unpack(asked_ref, held_ref)
-    prob = jnp.exp2(scores(c_ref[0], q, k) - lse)
-    dprob = dot(v, g, ((1,), (1,)))
-    dscore = (prob * (dprob - delta)).astype(BF)
+    prob = weight_ref[...] * factor
+    dscore = (prob * (dprob_ref[...] - delta)).astype(BF)
     prob = prob.astype(BF)
     d_key = (dot(dscore, q, ((1,), (0,))) * SCALE).astype(BF)
     d_value = dot(prob, g, ((1,), (0,))).astype(BF)
@@ -340,16 +343,17 @@
     asked = joined(c_ref, keep, shift(give, SPLIT, 2, 1), SPLIT)
     for axis in (TWICE, AGAIN):
         asked = joined(c_ref, asked, shift(asked, axis, 2, 1), axis)
-    (stats,) = call(
+    tile = shaped((TILE_K, TILE_Q), F32)
+    stats, weight, dprob = call(
         forward_kernel,
         (c_ref, asked, held),
-        (shaped((N_NEAR, 8, TILE_Q), F32),),
+        (shaped((N_NEAR, 8, TILE_Q), F32), tile, tile),
         300_000_000,
         1,
     )
     terms, keep, give = call(
         backward_kernel,
-        (c_ref, asked, held, swap(stats, NEAR)),
+        (c_ref, asked, held, stats, swap(stats, NEAR), weight, dprob),
         (stack, pair(TILE_Q // 2, F32), pair(TILE_Q // 2)),
         900_000_000,
         1,

time: 111 us -> 110 us (level)
  no operation moved by 1% of the time
where the time goes in v10:
time: 110 us; the launch traced here: 109 us
  starting transfers between devices  45.6 us (41%)
  blocking collectives  31.6 us (29%)
  waiting for transfers between devices  21.6 us (20%)
  Pallas kernels  8.8 us (8%)
    ppermute x8, starting transfers between devices, shift(): return lax.ppermute(x, axis, [(i, (i + by) % n) for i in range(n)])  35.1 us
    all_to_all x2, blocking collectives, swap(): return lax.all_to_all(x, axis, split_axis=0, concat_axis=0, tiled=True)  31.6 us
    ppermute x8, waiting for transfers between devices, shift(): return lax.ppermute(x, axis, [(i, (i + by) % n) for i in range(n)])  20.4 us
    all_to_all x2, starting transfers between devices, swap(): return lax.all_to_all(x, axis, split_axis=0, concat_axis=0, tiled=True)  10.5 us
    pallas_call x13, Pallas kernels, call(): pl.pallas_call(kernel, out_shape=tuple(outs), in_specs=[smem] * scalars +...  5.85 us
    pallas_call x1, Pallas kernels, pool(): pl.pallas_call(pool_kernel, out_shape=(block, block), in_specs=[pl.BlockS...  2.96 us
  transfers between devices with their start and end apart: 10, of which 7 were waited for; matrix products, arithmetic and copies ran while one was open for 0% of the time, Pallas kernels for 1%

profile of v10, /device:TPU:1, one launch (start us, length us, event | category | flops | bytes accessed | tf_op | source)
XLA Modules:
  0.0 109.4 jit_solution(18153929295936602726)
XLA Ops:
  0.6 3.0 %shard_map.77 = (bf16[64,1024]{1,0:T(8,128)(2,1)}, bf16[64,1024]{1,0:T(8,128)(2,1)}) custom-call(s32[1]{0:T(128)} %bitcast.c_ref, s32[64]{0:T(128)} %first_ref.1, s32[2,64]{1,0:T(2,128)} %moved_ref.1, s32[1,256]{1,0:T(1,128)} %bitcast.2, bf16[256,1024]{1,0:T(8,128)(2,1)} %bytes_hbm.1, bf16[64,256]{1,0:T(8,128)(2,1)} %grad_hbm.1, bf16[3,1024,256]{2,1,0:T(8,128)(2,1)} %w_ref.1), custom_call_target="tpu_custom_call" | custom-call | flops 300000000 | bytes 2500000 | tf_op jit(solution)/shard_map/pallas_call | solution.py:300
  3.6 14.7 %collective-permute-start = (bf16[64,1024]{1,0:T(8,128)(2,1)}, bf16[64,1024]{1,0:T(8,128)(2,1)S(1)}, u32[]{:S(2)}, u32[]{:S(2)}) collective-permute-start(bf16[64,1024]{1,0:T(8,128)(2,1)} %get-tuple-element.23), channel_id=1, source_target_pairs={{0,504},{8,0},{16,8},{24,16},{32,24},{40,32},{48,40},{56,48},{64,5... | collective-permute-start | bytes 393224 | tf_op jit(solution)/shard_map/ppermute | solution.py:48
  18.3 0.0 copy-start.1
  18.3 0.9 copy-done.1
  19.2 1.5 %collective-permute-done.got_ref = bf16[64,1024]{1,0:T(8,128)(2,1)S(1)} collective-permute-done((bf16[64,1024]{1,0:T(8,128)(2,1)}, bf16[64,1024]{1,0:T(8,128)(2,1)S(1)}, u32[]{:S(2)}, u32[]{:S(2)}) %collective-permute-start) | collective-permute-done | bytes 131104 | tf_op jit(solution)/shard_map/ppermute | solution.py:48
  20.8 0.9 shard_map.79
  21.6 1.9 %collective-permute-start.1 = (bf16[64,256]{1,0:T(8,128)(2,1)S(1)}, bf16[64,256]{1,0:T(8,128)(2,1)S(1)}, u32[]{:S(2)}, u32[]{:S(2)}) collective-permute-start(bf16[64,256]{1,0:T(8,128)(2,1)S(1)} %get-tuple-element.25), channel_id=1, source_target_pairs={{0,8},{8,0},{1,9},{9,1},{2,10},{10,2},{3,11},{11,3},{4,12},{12,4},... | collective-permute-start | bytes 98312 | tf_op jit(solution)/shard_map/ppermute | solution.py:48
  23.6 5.7 %all-to-all-start = ((bf16[16,64,256]{2,1,0:T(8,128)(2,1)}), bf16[16,64,256]{2,1,0:T(8,128)(2,1)S(1)}, u32[]{:S(2)}, u32[]{:S(2)}) async-start(bf16[16,64,256]{2,1,0:T(8,128)(2,1)} %get-tuple-element.26), calls=%async_computation | async-start | bytes 1048576 | tf_op jit(solution)/shard_map/all_to_all | solution.py:52
  29.3 0.0 collective-permute-done.1.got_ref
  29.3 4.1 %collective-permute-start.2 = (bf16[128,256]{1,0:T(8,128)(2,1)S(1)}, bf16[128,256]{1,0:T(8,128)(2,1)S(1)}, u32[]{:S(2)}, u32[]{:S(2)}) collective-permute-start(bf16[128,256]{1,0:T(8,128)(2,1)S(1)} %shard_map.80.mine_ref), channel_id=1, source_target_pairs={{0,32},{32,0},{1,33},{33,1},{2,34},{34,2},{3,35},{35,3},{4,36},{36... | collective-permute-start | bytes 196616 | tf_op jit(solution)/shard_map/ppermute | solution.py:48
  33.5 1.9 %collective-permute-done.2.got_ref = bf16[128,256]{1,0:T(8,128)(2,1)S(1)} collective-permute-done((bf16[128,256]{1,0:T(8,128)(2,1)S(1)}, bf16[128,256]{1,0:T(8,128)(2,1)S(1)}, u32[]{:S(2)}, u32[]{:S(2)}) %collective-permute-start.2) | collective-permute-done | bytes 65568 | tf_op jit(solution)/shard_map/ppermute | solution.py:48
  35.4 4.3 %collective-permute-start.3 = (bf16[256,256]{1,0:T(8,128)(2,1)S(1)}, bf16[256,256]{1,0:T(8,128)(2,1)S(1)}, u32[]{:S(2)}, u32[]{:S(2)}) collective-permute-start(bf16[256,256]{1,0:T(8,128)(2,1)S(1)} %shard_map.81.mine_ref), channel_id=1, source_target_pairs={{0,64},{64,0},{1,65},{65,1},{2,66},{66,2},{3,67},{67,3},{4,68},{68... | collective-permute-start | bytes 393224 | tf_op jit(solution)/shard_map/ppermute | solution.py:48
  39.7 5.8 %collective-permute-done.3.got_ref = bf16[256,256]{1,0:T(8,128)(2,1)S(1)} collective-permute-done((bf16[256,256]{1,0:T(8,128)(2,1)S(1)}, bf16[256,256]{1,0:T(8,128)(2,1)S(1)}, u32[]{:S(2)}, u32[]{:S(2)}) %collective-permute-start.3) | collective-permute-done | bytes 131104 | tf_op jit(solution)/shard_map/ppermute | solution.py:48
  45.5 0.0 all-to-all-done.held_ref
  45.5 1.1 shard_map.83
  46.6 10.1 %all_to_all.20.stats_ref = f32[4,8,512]{2,1,0:T(8,128)S(1)} all-to-all(f32[4,8,512]{2,1,0:T(8,128)S(1)} %get-tuple-element.27.own_ref), channel_id=1, replica_groups=mesh['zh'=4,'zl'=2,'yl'=2,'xh'=2,'xl'=2,'tp'=8] {'zl','yl'}, dimensions={0} | all-to-all | bytes 131072 | tf_op jit(solution)/shard_map/all_to_all | solution.py:52
  56.8 1.5 %shard_map.84 = (bf16[16,64,256]{2,1,0:T(8,128)(2,1)}, f32[256,256]{1,0:T(8,128)S(1)}, bf16[256,256]{1,0:T(8,128)(2,1)S(1)}) custom-call(s32[1]{0:T(128)} %bitcast.c_ref, bf16[512,256]{1,0:T(8,128)(2,1)S(1)} %shard_map.82.asked_ref, bf16[16,64,256]{2,1,0:T(8,128)(2,1)S(1)} %all-to-all-done.held_ref, f32[4,8,512]{2,1,0:T(8,128)S(1)} %get-tuple-element.27.own_ref, ...), custom_call_target="tpu_custom_call" | custom-call | flops 900000000 | bytes 6029316 | tf_op jit(solution)/shard_map/pallas_call | solution.py:63
  58.3 2.7 %collective-permute-start.4 = (bf16[256,256]{1,0:T(8,128)(2,1)S(1)}, bf16[256,256]{1,0:T(8,128)(2,1)S(1)}, u32[]{:S(2)}, u32[]{:S(2)}) collective-permute-start(bf16[256,256]{1,0:T(8,128)(2,1)S(1)} %get-tuple-element.32), channel_id=1, source_target_pairs={{0,64},{64,0},{1,65},{65,1},{2,66},{66,2},{3,67},{67,3},{4,68},{68... | collective-permute-start | bytes 393224 | tf_op jit(solution)/shard_map/ppermute | solution.py:48
  61.0 4.8 %all-to-all-start.2 = ((bf16[16,64,256]{2,1,0:T(8,128)(2,1)}), bf16[16,64,256]{2,1,0:T(8,128)(2,1)S(1)}, u32[]{:S(2)}, u32[]{:S(2)}) async-start(bf16[16,64,256]{2,1,0:T(8,128)(2,1)} %get-tuple-element.30), calls=%async_computation.2 | async-start | bytes 1048576 | tf_op jit(solution)/shard_map/all_to_all | solution.py:52
  65.7 0.0 collective-permute-done.4.got_ref
  65.8 2.1 %collective-permute-start.5 = (bf16[128,256]{1,0:T(8,128)(2,1)S(1)}, bf16[128,256]{1,0:T(8,128)(2,1)S(1)}, u32[]{:S(2)}, u32[]{:S(2)}) collective-permute-start(bf16[128,256]{1,0:T(8,128)(2,1)S(1)} %get-tuple-element.34), channel_id=1, source_target_pairs={{0,32},{32,0},{1,33},{33,1},{2,34},{34,2},{3,35},{35,3},{4,36},{36... | collective-permute-start | bytes 196616 | tf_op jit(solution)/shard_map/ppermute | solution.py:48
  67.9 2.9 %collective-permute-done.5.got_ref = bf16[128,256]{1,0:T(8,128)(2,1)S(1)} collective-permute-done((bf16[128,256]{1,0:T(8,128)(2,1)S(1)}, bf16[128,256]{1,0:T(8,128)(2,1)S(1)}, u32[]{:S(2)}, u32[]{:S(2)}) %collective-permute-start.5) | collective-permute-done | bytes 65568 | tf_op jit(solution)/shard_map/ppermute | solution.py:48
  70.8 3.4 %collective-permute-start.6 = (bf16[64,256]{1,0:T(8,128)(2,1)S(1)}, bf16[64,256]{1,0:T(8,128)(2,1)S(1)}, u32[]{:S(2)}, u32[]{:S(2)}) collective-permute-start(bf16[64,256]{1,0:T(8,128)(2,1)S(1)} %get-tuple-element.36), channel_id=1, source_target_pairs={{0,8},{8,0},{1,9},{9,1},{2,10},{10,2},{3,11},{11,3},{4,12},{12,4},... | collective-permute-start | bytes 98312 | tf_op jit(solution)/shard_map/ppermute | solution.py:48
  74.3 0.0 copy-done.2
  74.3 0.8 shard_map.87
  75.1 1.2 %collective-permute-done.6.got_ref = bf16[64,256]{1,0:T(8,128)(2,1)S(1)} collective-permute-done((bf16[64,256]{1,0:T(8,128)(2,1)S(1)}, bf16[64,256]{1,0:T(8,128)(2,1)S(1)}, u32[]{:S(2)}, u32[]{:S(2)}) %collective-permute-start.6) | collective-permute-done | bytes 32800 | tf_op jit(solution)/shard_map/ppermute | solution.py:48
  76.3 1.2 %all-to-all-done.2.term_ref = bf16[16,64,256]{2,1,0:T(8,128)(2,1)S(1)} async-done(((bf16[16,64,256]{2,1,0:T(8,128)(2,1)}), bf16[16,64,256]{2,1,0:T(8,128)(2,1)S(1)}, u32[]{:S(2)}, u32[]{:S(2)}) %all-to-all-start.2) | async-done | bytes 524320 | tf_op jit(solution)/shard_map/all_to_all | solution.py:52
  77.4 0.6 shard_map.88
  78.0 21.5 %all_to_all.21.pieces_ref = bf16[8,64,128]{2,1,0:T(8,128)(2,1)S(1)} all-to-all(bf16[8,64,128]{2,1,0:T(8,128)(2,1)S(1)} %get-tuple-element.38), channel_id=1, replica_groups=mesh['zh'=4,'zl'=2,'yl'=2,'xh'=2,'xl'=2,'tp'=8] {'tp'}, dimensions={0} | all-to-all | bytes 262144 | tf_op jit(solution)/shard_map/all_to_all | solution.py:52
  99.6 2.0 %collective-permute-start.7 = (bf16[64,384]{1,0:T(8,128)(2,1)S(1)}, bf16[64,384]{1,0:T(8,128)(2,1)S(1)}, u32[]{:S(2)}, u32[]{:S(2)}) collective-permute-start(bf16[64,384]{1,0:T(8,128)(2,1)S(1)} %shard_map.89.own_ref), channel_id=1, source_target_pairs={{0,8},{8,16},{16,24},{24,32},{32,40},{40,48},{48,56},{56,64},{64,7... | collective-permute-start | bytes 147464 | tf_op jit(solution)/shard_map/ppermute | solution.py:48
  101.5 7.1 %collective-permute-done.7.before_ref = bf16[64,384]{1,0:T(8,128)(2,1)S(1)} collective-permute-done((bf16[64,384]{1,0:T(8,128)(2,1)S(1)}, bf16[64,384]{1,0:T(8,128)(2,1)S(1)}, u32[]{:S(2)}, u32[]{:S(2)}) %collective-permute-start.7) | collective-permute-done | bytes 49184 | tf_op jit(solution)/shard_map/ppermute | solution.py:48
  108.6 0.8 shard_map.90
  (14 shorter events, 0.2 us)
Async XLA Ops:
  3.6 17.2 %collective-permute-start = (bf16[64,1024]{1,0:T(8,128)(2,1)}, bf16[64,1024]{1,0:T(8,128)(2,1)S(1)}, u32[]{:S(2)}, u32[]{:S(2)}) collective-permute-start(bf16[64,1024]{1,0:T(8,128)(2,1)} %get-tuple-element.23), channel_id=1, source_target_pairs={{0,504},{8,0},{16,8},{24,16},{32,24},{40,32},{48,40},{56,48},{64,5... | collective-permute-start | bytes 393224 | tf_op jit(solution)/shard_map/ppermute | solution.py:48
  18.3 0.9 copy-start.1
  21.6 7.7 %collective-permute-start.1 = (bf16[64,256]{1,0:T(8,128)(2,1)S(1)}, bf16[64,256]{1,0:T(8,128)(2,1)S(1)}, u32[]{:S(2)}, u32[]{:S(2)}) collective-permute-start(bf16[64,256]{1,0:T(8,128)(2,1)S(1)} %get-tuple-element.25), channel_id=1, source_target_pairs={{0,8},{8,0},{1,9},{9,1},{2,10},{10,2},{3,11},{11,3},{4,12},{12,4},... | collective-permute-start | bytes 98312 | tf_op jit(solution)/shard_map/ppermute | solution.py:48
  23.6 22.0 %all-to-all-start = ((bf16[16,64,256]{2,1,0:T(8,128)(2,1)}), bf16[16,64,256]{2,1,0:T(8,128)(2,1)S(1)}, u32[]{:S(2)}, u32[]{:S(2)}) async-start(bf16[16,64,256]{2,1,0:T(8,128)(2,1)} %get-tuple-element.26), calls=%async_computation | async-start | bytes 1048576 | tf_op jit(solution)/shard_map/all_to_all | solution.py:52
  29.3 6.0 %collective-permute-start.2 = (bf16[128,256]{1,0:T(8,128)(2,1)S(1)}, bf16[128,256]{1,0:T(8,128)(2,1)S(1)}, u32[]{:S(2)}, u32[]{:S(2)}) collective-permute-start(bf16[128,256]{1,0:T(8,128)(2,1)S(1)} %shard_map.80.mine_ref), channel_id=1, source_target_pairs={{0,32},{32,0},{1,33},{33,1},{2,34},{34,2},{3,35},{35,3},{4,36},{36... | collective-permute-start | bytes 196616 | tf_op jit(solution)/shard_map/ppermute | solution.py:48
  35.4 10.1 %collective-permute-start.3 = (bf16[256,256]{1,0:T(8,128)(2,1)S(1)}, bf16[256,256]{1,0:T(8,128)(2,1)S(1)}, u32[]{:S(2)}, u32[]{:S(2)}) collective-permute-start(bf16[256,256]{1,0:T(8,128)(2,1)S(1)} %shard_map.81.mine_ref), channel_id=1, source_target_pairs={{0,64},{64,0},{1,65},{65,1},{2,66},{66,2},{3,67},{67,3},{4,68},{68... | collective-permute-start | bytes 393224 | tf_op jit(solution)/shard_map/ppermute | solution.py:48
  58.3 7.4 %collective-permute-start.4 = (bf16[256,256]{1,0:T(8,128)(2,1)S(1)}, bf16[256,256]{1,0:T(8,128)(2,1)S(1)}, u32[]{:S(2)}, u32[]{:S(2)}) collective-permute-start(bf16[256,256]{1,0:T(8,128)(2,1)S(1)} %get-tuple-element.32), channel_id=1, source_target_pairs={{0,64},{64,0},{1,65},{65,1},{2,66},{66,2},{3,67},{67,3},{4,68},{68... | collective-permute-start | bytes 393224 | tf_op jit(solution)/shard_map/ppermute | solution.py:48
  61.0 16.5 %all-to-all-start.2 = ((bf16[16,64,256]{2,1,0:T(8,128)(2,1)}), bf16[16,64,256]{2,1,0:T(8,128)(2,1)S(1)}, u32[]{:S(2)}, u32[]{:S(2)}) async-start(bf16[16,64,256]{2,1,0:T(8,128)(2,1)} %get-tuple-element.30), calls=%async_computation.2 | async-start | bytes 1048576 | tf_op jit(solution)/shard_map/all_to_all | solution.py:52
  65.8 5.0 %collective-permute-start.5 = (bf16[128,256]{1,0:T(8,128)(2,1)S(1)}, bf16[128,256]{1,0:T(8,128)(2,1)S(1)}, u32[]{:S(2)}, u32[]{:S(2)}) collective-permute-start(bf16[128,256]{1,0:T(8,128)(2,1)S(1)} %get-tuple-element.34), channel_id=1, source_target_pairs={{0,32},{32,0},{1,33},{33,1},{2,34},{34,2},{3,35},{35,3},{4,36},{36... | collective-permute-start | bytes 196616 | tf_op jit(solution)/shard_map/ppermute | solution.py:48
  70.8 3.5 %copy-start.2 = (s32[2,64]{1,0:T(2,128)S(1)}, s32[2,64]{1,0:T(2,128)}, u32[]{:S(2)}) copy-start(s32[2,64]{1,0:T(2,128)} %moved_ref.1) | copy-start | bytes 1540
  70.8 3.5 %copy-start.3 = (s32[256]{0:T(256)S(1)}, s32[256]{0:T(256)}, u32[]{:S(2)}) copy-start(s32[256]{0:T(256)} %param.7) | copy-start | bytes 3076
  70.8 3.5 %copy-start.4 = (s32[64]{0:T(128)S(1)}, s32[64]{0:T(128)}, u32[]{:S(2)}) copy-start(s32[64]{0:T(128)} %first_ref.1) | copy-start | bytes 772
  70.8 6.6 %copy-start = (bf16[3,1024,256]{2,1,0:T(8,128)(2,1)S(1)}, bf16[3,1024,256]{2,1,0:T(8,128)(2,1)}, u32[]{:S(2)}) copy-start(bf16[3,1024,256]{2,1,0:T(8,128)(2,1)} %w_ref.1) | copy-start | bytes 4718596
  70.8 5.4 %collective-permute-start.6 = (bf16[64,256]{1,0:T(8,128)(2,1)S(1)}, bf16[64,256]{1,0:T(8,128)(2,1)S(1)}, u32[]{:S(2)}, u32[]{:S(2)}) collective-permute-start(bf16[64,256]{1,0:T(8,128)(2,1)S(1)} %get-tuple-element.36), channel_id=1, source_target_pairs={{0,8},{8,0},{1,9},{9,1},{2,10},{10,2},{3,11},{11,3},{4,12},{12,4},... | collective-permute-start | bytes 98312 | tf_op jit(solution)/shard_map/ppermute | solution.py:48
  99.6 9.1 %collective-permute-start.7 = (bf16[64,384]{1,0:T(8,128)(2,1)S(1)}, bf16[64,384]{1,0:T(8,128)(2,1)S(1)}, u32[]{:S(2)}, u32[]{:S(2)}) collective-permute-start(bf16[64,384]{1,0:T(8,128)(2,1)S(1)} %shard_map.89.own_ref), channel_id=1, source_target_pairs={{0,8},{8,16},{16,24},{24,32},{32,40},{40,48},{48,56},{56,64},{64,7... | collective-permute-start | bytes 147464 | tf_op jit(solution)/shard_map/ppermute | solution.py:48

commit v11 on v10

--- a/solution.py
+++ b/solution.py
@@ -33,7 +33,7 @@
 LOG2E = 1.4426950408889634
 NEG = -1e30
 FLOOR = -1e29
-JOIN = 3_000_000_000
+JOIN = 5_000_000_000
 HALVE = 5_000_000_000
 BF = jnp.bfloat16
 F32 = jnp.float32
@@ -200,7 +200,10 @@
     return jnp.where(allowed, dot(k, q, ((1,), (1,))) * (SCALE * LOG2E), NEG)
 
 
-def forward_kernel(c_ref, asked_ref, held_ref, stats_ref, weight_ref, dprob_ref):
+def forward_kernel(
+    c_ref, mine_ref, got_ref, held_ref, stats_ref, weight_ref, dprob_ref, asked_ref
+):
+    join_kernel(AGAIN, c_ref, mine_ref, got_ref, asked_ref)
     q, g, k, v = unpack(asked_ref, held_ref)
     score = scores(c_ref[0], q, k)
     top = jnp.maximum(jnp.max(score, axis=0, keepdims=True), FLOOR)
@@ -341,13 +344,12 @@
     )
     held = swap(held, FAR)
     asked = joined(c_ref, keep, shift(give, SPLIT, 2, 1), SPLIT)
-    for axis in (TWICE, AGAIN):
-        asked = joined(c_ref, asked, shift(asked, axis, 2, 1), axis)
+    mine = joined(c_ref, asked, shift(asked, TWICE, 2, 1), TWICE)
     tile = shaped((TILE_K, TILE_Q), F32)
-    stats, weight, dprob = call(
+    stats, weight, dprob, asked = call(
         forward_kernel,
-        (c_ref, asked, held),
-        (shaped((N_NEAR, 8, TILE_Q), F32), tile, tile),
+        (c_ref, mine, shift(mine, AGAIN, 2, 1), held),
+        (shaped((N_NEAR, 8, TILE_Q), F32), tile, tile, pair(TILE_Q)),
         300_000_000,
         1,
     )

time: 110 us -> 110 us (level)
    pallas_call x13 -> x12, Pallas kernels: 5.85 us -> 5.83 us  [call(): pl.pallas_call(kernel, out_shape=tuple(outs), in_specs=[smem] * scalars +...]
where the time goes in v11:
time: 110 us; the launch traced here: 109 us
  starting transfers between devices  45.6 us (41%)
  blocking collectives  31.6 us (29%)
  waiting for transfers between devices  21.6 us (20%)
  Pallas kernels  8.79 us (8%)
    ppermute x8, starting transfers between devices, shift(): return lax.ppermute(x, axis, [(i, (i + by) % n) for i in range(n)])  35.1 us
    all_to_all x2, blocking collectives, swap(): return lax.all_to_all(x, axis, split_axis=0, concat_axis=0, tiled=True)  31.6 us
    ppermute x8, waiting for transfers between devices, shift(): return lax.ppermute(x, axis, [(i, (i + by) % n) for i in range(n)])  20.4 us
    all_to_all x2, starting transfers between devices, swap(): return lax.all_to_all(x, axis, split_axis=0, concat_axis=0, tiled=True)  10.5 us
    pallas_call x12, Pallas kernels, call(): pl.pallas_call(kernel, out_shape=tuple(outs), in_specs=[smem] * scalars +...  5.83 us
    pallas_call x1, Pallas kernels, pool(): pl.pallas_call(pool_kernel, out_shape=(block, block), in_specs=[pl.BlockS...  2.96 us
  transfers between devices with their start and end apart: 10, of which 7 were waited for; matrix products, arithmetic and copies ran while one was open for 0% of the time, Pallas kernels for 1%

profile of v11, /device:TPU:1, one launch (start us, length us, event | category | flops | bytes accessed | tf_op | source)
XLA Modules:
  0.0 109.4 jit_solution(3032215426718715256)
XLA Ops:
  0.6 3.0 %shard_map.77 = (bf16[64,1024]{1,0:T(8,128)(2,1)}, bf16[64,1024]{1,0:T(8,128)(2,1)}) custom-call(s32[1]{0:T(128)} %bitcast.c_ref, s32[64]{0:T(128)} %first_ref.1, s32[2,64]{1,0:T(2,128)} %moved_ref.1, s32[1,256]{1,0:T(1,128)} %bitcast.2, bf16[256,1024]{1,0:T(8,128)(2,1)} %bytes_hbm.1, bf16[64,256]{1,0:T(8,128)(2,1)} %grad_hbm.1, bf16[3,1024,256]{2,1,0:T(8,128)(2,1)} %w_ref.1), custom_call_target="tpu_custom_call" | custom-call | flops 300000000 | bytes 2500000 | tf_op jit(solution)/shard_map/pallas_call | solution.py:303
  3.6 14.7 %collective-permute-start = (bf16[64,1024]{1,0:T(8,128)(2,1)}, bf16[64,1024]{1,0:T(8,128)(2,1)S(1)}, u32[]{:S(2)}, u32[]{:S(2)}) collective-permute-start(bf16[64,1024]{1,0:T(8,128)(2,1)} %get-tuple-element.24), channel_id=1, source_target_pairs={{0,504},{8,0},{16,8},{24,16},{32,24},{40,32},{48,40},{56,48},{64,5... | collective-permute-start | bytes 393224 | tf_op jit(solution)/shard_map/ppermute | solution.py:48
  18.3 0.9 copy-done.1
  19.2 1.5 %collective-permute-done.got_ref = bf16[64,1024]{1,0:T(8,128)(2,1)S(1)} collective-permute-done((bf16[64,1024]{1,0:T(8,128)(2,1)}, bf16[64,1024]{1,0:T(8,128)(2,1)S(1)}, u32[]{:S(2)}, u32[]{:S(2)}) %collective-permute-start) | collective-permute-done | bytes 131104 | tf_op jit(solution)/shard_map/ppermute | solution.py:48
  20.8 0.9 shard_map.79
  21.6 1.9 %collective-permute-start.1 = (bf16[64,256]{1,0:T(8,128)(2,1)S(1)}, bf16[64,256]{1,0:T(8,128)(2,1)S(1)}, u32[]{:S(2)}, u32[]{:S(2)}) collective-permute-start(bf16[64,256]{1,0:T(8,128)(2,1)S(1)} %get-tuple-element.26), channel_id=1, source_target_pairs={{0,8},{8,0},{1,9},{9,1},{2,10},{10,2},{3,11},{11,3},{4,12},{12,4},... | collective-permute-start | bytes 98312 | tf_op jit(solution)/shard_map/ppermute | solution.py:48
  23.6 5.7 %all-to-all-start = ((bf16[16,64,256]{2,1,0:T(8,128)(2,1)}), bf16[16,64,256]{2,1,0:T(8,128)(2,1)S(1)}, u32[]{:S(2)}, u32[]{:S(2)}) async-start(bf16[16,64,256]{2,1,0:T(8,128)(2,1)} %get-tuple-element.27), calls=%async_computation | async-start | bytes 1048576 | tf_op jit(solution)/shard_map/all_to_all | solution.py:52
  29.3 0.0 collective-permute-done.1.got_ref
  29.3 4.1 %collective-permute-start.2 = (bf16[128,256]{1,0:T(8,128)(2,1)S(1)}, bf16[128,256]{1,0:T(8,128)(2,1)S(1)}, u32[]{:S(2)}, u32[]{:S(2)}) collective-permute-start(bf16[128,256]{1,0:T(8,128)(2,1)S(1)} %shard_map.80.mine_ref), channel_id=1, source_target_pairs={{0,32},{32,0},{1,33},{33,1},{2,34},{34,2},{3,35},{35,3},{4,36},{36... | collective-permute-start | bytes 196616 | tf_op jit(solution)/shard_map/ppermute | solution.py:48
  33.5 1.9 %collective-permute-done.2.got_ref = bf16[128,256]{1,0:T(8,128)(2,1)S(1)} collective-permute-done((bf16[128,256]{1,0:T(8,128)(2,1)S(1)}, bf16[128,256]{1,0:T(8,128)(2,1)S(1)}, u32[]{:S(2)}, u32[]{:S(2)}) %collective-permute-start.2) | collective-permute-done | bytes 65568 | tf_op jit(solution)/shard_map/ppermute | solution.py:48
  35.4 4.3 %collective-permute-start.3 = (bf16[256,256]{1,0:T(8,128)(2,1)S(1)}, bf16[256,256]{1,0:T(8,128)(2,1)S(1)}, u32[]{:S(2)}, u32[]{:S(2)}) collective-permute-start(bf16[256,256]{1,0:T(8,128)(2,1)S(1)} %shard_map.81.mine_ref), channel_id=1, source_target_pairs={{0,64},{64,0},{1,65},{65,1},{2,66},{66,2},{3,67},{67,3},{4,68},{68... | collective-permute-start | bytes 393224 | tf_op jit(solution)/shard_map/ppermute | solution.py:48
  39.7 5.8 %collective-permute-done.3.got_ref = bf16[256,256]{1,0:T(8,128)(2,1)S(1)} collective-permute-done((bf16[256,256]{1,0:T(8,128)(2,1)S(1)}, bf16[256,256]{1,0:T(8,128)(2,1)S(1)}, u32[]{:S(2)}, u32[]{:S(2)}) %collective-permute-start.3) | collective-permute-done | bytes 131104 | tf_op jit(solution)/shard_map/ppermute | solution.py:48
  45.5 0.0 all-to-all-done.held_ref
  45.5 1.1 %shard_map.82 = (f32[4,8,512]{2,1,0:T(8,128)S(1)}, f32[1024,512]{1,0:T(8,128)S(1)}, f32[1024,512]{1,0:T(8,128)S(1)}, bf16[512,256]{1,0:T(8,128)(2,1)S(1)}) custom-call(s32[1]{0:T(128)} %bitcast.c_ref, bf16[256,256]{1,0:T(8,128)(2,1)S(1)} %shard_map.81.mine_ref, bf16[256,256]{1,0:T(8,128)(2,1)S(1)} %collective-permute-done.3.got_ref, ...), custom_call_target="tpu_custom_call" | custom-call | flops 300000000 | bytes 5308420 | tf_op jit(solution)/shard_map/pallas_call | solution.py:63
  46.6 10.1 %all_to_all.20.stats_ref = f32[4,8,512]{2,1,0:T(8,128)S(1)} all-to-all(f32[4,8,512]{2,1,0:T(8,128)S(1)} %get-tuple-element.29.own_ref), channel_id=1, replica_groups=mesh['zh'=4,'zl'=2,'yl'=2,'xh'=2,'xl'=2,'tp'=8] {'zl','yl'}, dimensions={0} | all-to-all | bytes 131072 | tf_op jit(solution)/shard_map/all_to_all | solution.py:52
  56.8 1.5 %shard_map.83 = (bf16[16,64,256]{2,1,0:T(8,128)(2,1)}, f32[256,256]{1,0:T(8,128)S(1)}, bf16[256,256]{1,0:T(8,128)(2,1)S(1)}) custom-call(s32[1]{0:T(128)} %bitcast.c_ref, bf16[512,256]{1,0:T(8,128)(2,1)S(1)} %get-tuple-element.28.asked_ref, bf16[16,64,256]{2,1,0:T(8,128)(2,1)S(1)} %all-to-all-done.held_ref, f32[4,8,512]{2,1,0:T(8,128)S(1)} %get-tuple-element.29.own_ref, ...), custom_call_target="tpu_custom_call" | custom-call | flops 900000000 | bytes 6029316 | tf_op jit(solution)/shard_map/pallas_call | solution.py:63
  58.3 2.6 %collective-permute-start.4 = (bf16[256,256]{1,0:T(8,128)(2,1)S(1)}, bf16[256,256]{1,0:T(8,128)(2,1)S(1)}, u32[]{:S(2)}, u32[]{:S(2)}) collective-permute-start(bf16[256,256]{1,0:T(8,128)(2,1)S(1)} %get-tuple-element.34), channel_id=1, source_target_pairs={{0,64},{64,0},{1,65},{65,1},{2,66},{66,2},{3,67},{67,3},{4,68},{68... | collective-permute-start | bytes 393224 | tf_op jit(solution)/shard_map/ppermute | solution.py:48
  61.0 4.7 %all-to-all-start.2 = ((bf16[16,64,256]{2,1,0:T(8,128)(2,1)}), bf16[16,64,256]{2,1,0:T(8,128)(2,1)S(1)}, u32[]{:S(2)}, u32[]{:S(2)}) async-start(bf16[16,64,256]{2,1,0:T(8,128)(2,1)} %get-tuple-element.32), calls=%async_computation.2 | async-start | bytes 1048576 | tf_op jit(solution)/shard_map/all_to_all | solution.py:52
  65.7 0.0 collective-permute-done.4.got_ref
  65.8 2.1 %collective-permute-start.5 = (bf16[128,256]{1,0:T(8,128)(2,1)S(1)}, bf16[128,256]{1,0:T(8,128)(2,1)S(1)}, u32[]{:S(2)}, u32[]{:S(2)}) collective-permute-start(bf16[128,256]{1,0:T(8,128)(2,1)S(1)} %get-tuple-element.36), channel_id=1, source_target_pairs={{0,32},{32,0},{1,33},{33,1},{2,34},{34,2},{3,35},{35,3},{4,36},{36... | collective-permute-start | bytes 196616 | tf_op jit(solution)/shard_map/ppermute | solution.py:48
  67.9 2.9 %collective-permute-done.5.got_ref = bf16[128,256]{1,0:T(8,128)(2,1)S(1)} collective-permute-done((bf16[128,256]{1,0:T(8,128)(2,1)S(1)}, bf16[128,256]{1,0:T(8,128)(2,1)S(1)}, u32[]{:S(2)}, u32[]{:S(2)}) %collective-permute-start.5) | collective-permute-done | bytes 65568 | tf_op jit(solution)/shard_map/ppermute | solution.py:48
  70.8 3.4 %collective-permute-start.6 = (bf16[64,256]{1,0:T(8,128)(2,1)S(1)}, bf16[64,256]{1,0:T(8,128)(2,1)S(1)}, u32[]{:S(2)}, u32[]{:S(2)}) collective-permute-start(bf16[64,256]{1,0:T(8,128)(2,1)S(1)} %get-tuple-element.38), channel_id=1, source_target_pairs={{0,8},{8,0},{1,9},{9,1},{2,10},{10,2},{3,11},{11,3},{4,12},{12,4},... | collective-permute-start | bytes 98312 | tf_op jit(solution)/shard_map/ppermute | solution.py:48
  74.2 0.0 copy-done.2
  74.2 0.0 copy-done.3
  74.3 0.8 shard_map.86
  75.1 1.2 %collective-permute-done.6.got_ref = bf16[64,256]{1,0:T(8,128)(2,1)S(1)} collective-permute-done((bf16[64,256]{1,0:T(8,128)(2,1)S(1)}, bf16[64,256]{1,0:T(8,128)(2,1)S(1)}, u32[]{:S(2)}, u32[]{:S(2)}) %collective-permute-start.6) | collective-permute-done | bytes 32800 | tf_op jit(solution)/shard_map/ppermute | solution.py:48
  76.2 1.2 %all-to-all-done.2.term_ref = bf16[16,64,256]{2,1,0:T(8,128)(2,1)S(1)} async-done(((bf16[16,64,256]{2,1,0:T(8,128)(2,1)}), bf16[16,64,256]{2,1,0:T(8,128)(2,1)S(1)}, u32[]{:S(2)}, u32[]{:S(2)}) %all-to-all-start.2) | async-done | bytes 524320 | tf_op jit(solution)/shard_map/all_to_all | solution.py:52
  77.4 0.6 shard_map.87
  78.0 21.5 %all_to_all.21.pieces_ref = bf16[8,64,128]{2,1,0:T(8,128)(2,1)S(1)} all-to-all(bf16[8,64,128]{2,1,0:T(8,128)(2,1)S(1)} %get-tuple-element.40), channel_id=1, replica_groups=mesh['zh'=4,'zl'=2,'yl'=2,'xh'=2,'xl'=2,'tp'=8] {'tp'}, dimensions={0} | all-to-all | bytes 262144 | tf_op jit(solution)/shard_map/all_to_all | solution.py:52
  99.5 2.0 %collective-permute-start.7 = (bf16[64,384]{1,0:T(8,128)(2,1)S(1)}, bf16[64,384]{1,0:T(8,128)(2,1)S(1)}, u32[]{:S(2)}, u32[]{:S(2)}) collective-permute-start(bf16[64,384]{1,0:T(8,128)(2,1)S(1)} %shard_map.88.own_ref), channel_id=1, source_target_pairs={{0,8},{8,16},{16,24},{24,32},{32,40},{40,48},{48,56},{56,64},{64,7... | collective-permute-start | bytes 147464 | tf_op jit(solution)/shard_map/ppermute | solution.py:48
  101.5 7.1 %collective-permute-done.7.before_ref = bf16[64,384]{1,0:T(8,128)(2,1)S(1)} collective-permute-done((bf16[64,384]{1,0:T(8,128)(2,1)S(1)}, bf16[64,384]{1,0:T(8,128)(2,1)S(1)}, u32[]{:S(2)}, u32[]{:S(2)}) %collective-permute-start.7) | collective-permute-done | bytes 49184 | tf_op jit(solution)/shard_map/ppermute | solution.py:48
  108.6 0.8 shard_map.89
  (13 shorter events, 0.1 us)
Async XLA Ops:
  3.6 17.2 %collective-permute-start = (bf16[64,1024]{1,0:T(8,128)(2,1)}, bf16[64,1024]{1,0:T(8,128)(2,1)S(1)}, u32[]{:S(2)}, u32[]{:S(2)}) collective-permute-start(bf16[64,1024]{1,0:T(8,128)(2,1)} %get-tuple-element.24), channel_id=1, source_target_pairs={{0,504},{8,0},{16,8},{24,16},{32,24},{40,32},{48,40},{56,48},{64,5... | collective-permute-start | bytes 393224 | tf_op jit(solution)/shard_map/ppermute | solution.py:48
  18.3 0.9 copy-start.1
  21.6 7.7 %collective-permute-start.1 = (bf16[64,256]{1,0:T(8,128)(2,1)S(1)}, bf16[64,256]{1,0:T(8,128)(2,1)S(1)}, u32[]{:S(2)}, u32[]{:S(2)}) collective-permute-start(bf16[64,256]{1,0:T(8,128)(2,1)S(1)} %get-tuple-element.26), channel_id=1, source_target_pairs={{0,8},{8,0},{1,9},{9,1},{2,10},{10,2},{3,11},{11,3},{4,12},{12,4},... | collective-permute-start | bytes 98312 | tf_op jit(solution)/shard_map/ppermute | solution.py:48
  23.6 22.0 %all-to-all-start = ((bf16[16,64,256]{2,1,0:T(8,128)(2,1)}), bf16[16,64,256]{2,1,0:T(8,128)(2,1)S(1)}, u32[]{:S(2)}, u32[]{:S(2)}) async-start(bf16[16,64,256]{2,1,0:T(8,128)(2,1)} %get-tuple-element.27), calls=%async_computation | async-start | bytes 1048576 | tf_op jit(solution)/shard_map/all_to_all | solution.py:52
  29.3 6.0 %collective-permute-start.2 = (bf16[128,256]{1,0:T(8,128)(2,1)S(1)}, bf16[128,256]{1,0:T(8,128)(2,1)S(1)}, u32[]{:S(2)}, u32[]{:S(2)}) collective-permute-start(bf16[128,256]{1,0:T(8,128)(2,1)S(1)} %shard_map.80.mine_ref), channel_id=1, source_target_pairs={{0,32},{32,0},{1,33},{33,1},{2,34},{34,2},{3,35},{35,3},{4,36},{36... | collective-permute-start | bytes 196616 | tf_op jit(solution)/shard_map/ppermute | solution.py:48
  35.4 10.1 %collective-permute-start.3 = (bf16[256,256]{1,0:T(8,128)(2,1)S(1)}, bf16[256,256]{1,0:T(8,128)(2,1)S(1)}, u32[]{:S(2)}, u32[]{:S(2)}) collective-permute-start(bf16[256,256]{1,0:T(8,128)(2,1)S(1)} %shard_map.81.mine_ref), channel_id=1, source_target_pairs={{0,64},{64,0},{1,65},{65,1},{2,66},{66,2},{3,67},{67,3},{4,68},{68... | collective-permute-start | bytes 393224 | tf_op jit(solution)/shard_map/ppermute | solution.py:48
  58.3 7.4 %collective-permute-start.4 = (bf16[256,256]{1,0:T(8,128)(2,1)S(1)}, bf16[256,256]{1,0:T(8,128)(2,1)S(1)}, u32[]{:S(2)}, u32[]{:S(2)}) collective-permute-start(bf16[256,256]{1,0:T(8,128)(2,1)S(1)} %get-tuple-element.34), channel_id=1, source_target_pairs={{0,64},{64,0},{1,65},{65,1},{2,66},{66,2},{3,67},{67,3},{4,68},{68... | collective-permute-start | bytes 393224 | tf_op jit(solution)/shard_map/ppermute | solution.py:48
  61.0 16.5 %all-to-all-start.2 = ((bf16[16,64,256]{2,1,0:T(8,128)(2,1)}), bf16[16,64,256]{2,1,0:T(8,128)(2,1)S(1)}, u32[]{:S(2)}, u32[]{:S(2)}) async-start(bf16[16,64,256]{2,1,0:T(8,128)(2,1)} %get-tuple-element.32), calls=%async_computation.2 | async-start | bytes 1048576 | tf_op jit(solution)/shard_map/all_to_all | solution.py:52
  65.8 5.0 %collective-permute-start.5 = (bf16[128,256]{1,0:T(8,128)(2,1)S(1)}, bf16[128,256]{1,0:T(8,128)(2,1)S(1)}, u32[]{:S(2)}, u32[]{:S(2)}) collective-permute-start(bf16[128,256]{1,0:T(8,128)(2,1)S(1)} %get-tuple-element.36), channel_id=1, source_target_pairs={{0,32},{32,0},{1,33},{33,1},{2,34},{34,2},{3,35},{35,3},{4,36},{36... | collective-permute-start | bytes 196616 | tf_op jit(solution)/shard_map/ppermute | solution.py:48
  70.8 3.5 %copy-start.2 = (s32[2,64]{1,0:T(2,128)S(1)}, s32[2,64]{1,0:T(2,128)}, u32[]{:S(2)}) copy-start(s32[2,64]{1,0:T(2,128)} %moved_ref.1) | copy-start | bytes 1540
  70.8 3.5 %copy-start.3 = (s32[256]{0:T(256)S(1)}, s32[256]{0:T(256)}, u32[]{:S(2)}) copy-start(s32[256]{0:T(256)} %param.7) | copy-start | bytes 3076
  70.8 3.5 %copy-start.4 = (s32[64]{0:T(128)S(1)}, s32[64]{0:T(128)}, u32[]{:S(2)}) copy-start(s32[64]{0:T(128)} %first_ref.1) | copy-start | bytes 772
  70.8 6.6 %copy-start = (bf16[3,1024,256]{2,1,0:T(8,128)(2,1)S(1)}, bf16[3,1024,256]{2,1,0:T(8,128)(2,1)}, u32[]{:S(2)}) copy-start(bf16[3,1024,256]{2,1,0:T(8,128)(2,1)} %w_ref.1) | copy-start | bytes 4718596
  70.8 5.4 %collective-permute-start.6 = (bf16[64,256]{1,0:T(8,128)(2,1)S(1)}, bf16[64,256]{1,0:T(8,128)(2,1)S(1)}, u32[]{:S(2)}, u32[]{:S(2)}) collective-permute-start(bf16[64,256]{1,0:T(8,128)(2,1)S(1)} %get-tuple-element.38), channel_id=1, source_target_pairs={{0,8},{8,0},{1,9},{9,1},{2,10},{10,2},{3,11},{11,3},{4,12},{12,4},... | collective-permute-start | bytes 98312 | tf_op jit(solution)/shard_map/ppermute | solution.py:48
  99.5 9.1 %collective-permute-start.7 = (bf16[64,384]{1,0:T(8,128)(2,1)S(1)}, bf16[64,384]{1,0:T(8,128)(2,1)S(1)}, u32[]{:S(2)}, u32[]{:S(2)}) collective-permute-start(bf16[64,384]{1,0:T(8,128)(2,1)S(1)} %shard_map.88.own_ref), channel_id=1, source_target_pairs={{0,8},{8,16},{16,24},{24,32},{32,40},{40,48},{48,56},{56,64},{64,7... | collective-permute-start | bytes 147464 | tf_op jit(solution)/shard_map/ppermute | solution.py:48

commit v12 on v11

--- a/solution.py
+++ b/solution.py
@@ -97,8 +97,8 @@
 
 
 def pool_kernel(
-    c_ref, first_hbm, moved_hbm, place_hbm, bytes_hbm, grad_hbm, w_hbm, sent_ref, own_ref,
-    first_ref, moved_ref, place_ref, bytes_ref, grad_ref, w_ref, sems,
+    c_ref, first_hbm, moved_hbm, place_hbm, bytes_hbm, grad_hbm, w_hbm, sent_hbm, own_hbm,
+    first_ref, moved_ref, place_ref, bytes_ref, grad_ref, w_ref, sems, sent_ref, own_ref, outs,
 ):
     pairs = [
         (first_hbm, first_ref),
@@ -121,13 +121,21 @@
     order = slot_order(c, first_ref, moved_ref, (WINDOW, ROWS), 1)
     slotted = (iota((WINDOW, ROWS), 0) == order).astype(F32).astype(BF)
     grads = dot(slotted, grad_ref[...], ((1,), (0,))).astype(BF)
-    for at, value in ((0, None), (1, grads), (2, None), (3, None)):
+    leaving = []
+    for at, value in ((1, grads), (0, None), (2, None), (3, None)):
         if value is None:
             part = max(at - 1, 0)
             copies[5 + part].wait()
             value = dot(pooled, w_ref[part], ((1,), (0,))).astype(BF)
-        sent_ref[:, at * FEATS : (at + 1) * FEATS] = value[:ROWS]
-        own_ref[:, at * FEATS : (at + 1) * FEATS] = value[ROWS:]
+        place = slice(at * FEATS, (at + 1) * FEATS)
+        sent_ref[:, place] = value[:ROWS]
+        own_ref[:, place] = value[ROWS:]
+        for i, (a, b) in enumerate(((sent_ref, sent_hbm), (own_ref, own_hbm))):
+            copy = pltpu.make_async_copy(a.at[:, place], b.at[:, place], outs.at[2 * at + i])
+            copy.start()
+            leaving.append(copy)
+    for copy in leaving:
+        copy.wait()
 
 
 def columns(value, kind, head):
@@ -296,7 +304,6 @@
 
 def pool(c_ref, first, moved, place, byte_states, d_attn, w_qkv):
     hbm = pl.BlockSpec(memory_space=pltpu.HBM)
-    vmem = pl.BlockSpec(memory_space=pltpu.VMEM)
     ins = (first, moved, place, byte_states, d_attn, w_qkv)
     spaces = (pltpu.SMEM, pltpu.SMEM) + (pltpu.VMEM,) * 4
     block = shaped((ROWS, 4 * FEATS), BF)
@@ -304,9 +311,14 @@
         pool_kernel,
         out_shape=(block, block),
         in_specs=[pl.BlockSpec(memory_space=pltpu.SMEM)] + [hbm] * len(ins),
-        out_specs=(vmem, vmem),
+        out_specs=(hbm, hbm),
         scratch_shapes=[space(x.shape, x.dtype) for space, x in zip(spaces, ins)]
-        + [pltpu.SemaphoreType.DMA((len(ins) + 2,))],
+        + [
+            pltpu.SemaphoreType.DMA((len(ins) + 2,)),
+            pltpu.VMEM(block.shape, BF),
+            pltpu.VMEM(block.shape, BF),
+            pltpu.SemaphoreType.DMA((8,)),
+        ],
         cost_estimate=pl.CostEstimate(flops=300_000_000, bytes_accessed=2_500_000, transcendentals=0),
         compiler_params=pltpu.CompilerParams(vmem_limit_bytes=60 * 1024 * 1024),
     )(c_ref, *ins)

time: 110 us -> 110 us (level)
  no operation moved by 1% of the time
where the time goes in v12:
time: 110 us; the launch traced here: 109 us
  starting transfers between devices  45.6 us (41%)
  blocking collectives  31.6 us (29%)
  waiting for transfers between devices  21.6 us (20%)
  Pallas kernels  8.8 us (8%)
    ppermute x8, starting transfers between devices, shift(): return lax.ppermute(x, axis, [(i, (i + by) % n) for i in range(n)])  35.1 us
    all_to_all x2, blocking collectives, swap(): return lax.all_to_all(x, axis, split_axis=0, concat_axis=0, tiled=True)  31.6 us
    ppermute x8, waiting for transfers between devices, shift(): return lax.ppermute(x, axis, [(i, (i + by) % n) for i in range(n)])  20.4 us
    all_to_all x2, starting transfers between devices, swap(): return lax.all_to_all(x, axis, split_axis=0, concat_axis=0, tiled=True)  10.5 us
    pallas_call x12, Pallas kernels, call(): pl.pallas_call(kernel, out_shape=tuple(outs), in_specs=[smem] * scalars +...  5.84 us
    pallas_call x1, Pallas kernels, pool(): pl.pallas_call(pool_kernel, out_shape=(block, block), in_specs=[pl.BlockS...  2.96 us
  transfers between devices with their start and end apart: 10, of which 7 were waited for; matrix products, arithmetic and copies ran while one was open for 0% of the time, Pallas kernels for 1%

profile of v12, /device:TPU:1, one launch (start us, length us, event | category | flops | bytes accessed | tf_op | source)
XLA Modules:
  0.0 109.4 jit_solution(15697540672399910181)
XLA Ops:
  0.6 3.0 %shard_map.77 = (bf16[64,1024]{1,0:T(8,128)(2,1)}, bf16[64,1024]{1,0:T(8,128)(2,1)}) custom-call(s32[1]{0:T(128)} %bitcast.c_ref, s32[64]{0:T(128)} %first_ref.1, s32[2,64]{1,0:T(2,128)} %moved_ref.1, s32[1,256]{1,0:T(1,128)} %bitcast.2, bf16[256,1024]{1,0:T(8,128)(2,1)} %bytes_hbm.1, bf16[64,256]{1,0:T(8,128)(2,1)} %grad_hbm.1, bf16[3,1024,256]{2,1,0:T(8,128)(2,1)} %w_ref.1), custom_call_target="tpu_custom_call" | custom-call | flops 300000000 | bytes 2500000 | tf_op jit(solution)/shard_map/pallas_call | solution.py:310
  3.6 14.7 %collective-permute-start = (bf16[64,1024]{1,0:T(8,128)(2,1)}, bf16[64,1024]{1,0:T(8,128)(2,1)S(1)}, u32[]{:S(2)}, u32[]{:S(2)}) collective-permute-start(bf16[64,1024]{1,0:T(8,128)(2,1)} %get-tuple-element.24), channel_id=1, source_target_pairs={{0,504},{8,0},{16,8},{24,16},{32,24},{40,32},{48,40},{56,48},{64,5... | collective-permute-start | bytes 393224 | tf_op jit(solution)/shard_map/ppermute | solution.py:48
  18.3 0.0 copy-start.1
  18.3 0.9 copy-done.1
  19.2 1.5 %collective-permute-done.got_ref = bf16[64,1024]{1,0:T(8,128)(2,1)S(1)} collective-permute-done((bf16[64,1024]{1,0:T(8,128)(2,1)}, bf16[64,1024]{1,0:T(8,128)(2,1)S(1)}, u32[]{:S(2)}, u32[]{:S(2)}) %collective-permute-start) | collective-permute-done | bytes 131104 | tf_op jit(solution)/shard_map/ppermute | solution.py:48
  20.8 0.9 shard_map.79
  21.7 1.9 %collective-permute-start.1 = (bf16[64,256]{1,0:T(8,128)(2,1)S(1)}, bf16[64,256]{1,0:T(8,128)(2,1)S(1)}, u32[]{:S(2)}, u32[]{:S(2)}) collective-permute-start(bf16[64,256]{1,0:T(8,128)(2,1)S(1)} %get-tuple-element.26), channel_id=1, source_target_pairs={{0,8},{8,0},{1,9},{9,1},{2,10},{10,2},{3,11},{11,3},{4,12},{12,4},... | collective-permute-start | bytes 98312 | tf_op jit(solution)/shard_map/ppermute | solution.py:48
  23.6 5.7 %all-to-all-start = ((bf16[16,64,256]{2,1,0:T(8,128)(2,1)}), bf16[16,64,256]{2,1,0:T(8,128)(2,1)S(1)}, u32[]{:S(2)}, u32[]{:S(2)}) async-start(bf16[16,64,256]{2,1,0:T(8,128)(2,1)} %get-tuple-element.27), calls=%async_computation | async-start | bytes 1048576 | tf_op jit(solution)/shard_map/all_to_all | solution.py:52
  29.3 0.0 collective-permute-done.1.got_ref
  29.3 4.1 %collective-permute-start.2 = (bf16[128,256]{1,0:T(8,128)(2,1)S(1)}, bf16[128,256]{1,0:T(8,128)(2,1)S(1)}, u32[]{:S(2)}, u32[]{:S(2)}) collective-permute-start(bf16[128,256]{1,0:T(8,128)(2,1)S(1)} %shard_map.80.mine_ref), channel_id=1, source_target_pairs={{0,32},{32,0},{1,33},{33,1},{2,34},{34,2},{3,35},{35,3},{4,36},{36... | collective-permute-start | bytes 196616 | tf_op jit(solution)/shard_map/ppermute | solution.py:48
  33.5 1.9 %collective-permute-done.2.got_ref = bf16[128,256]{1,0:T(8,128)(2,1)S(1)} collective-permute-done((bf16[128,256]{1,0:T(8,128)(2,1)S(1)}, bf16[128,256]{1,0:T(8,128)(2,1)S(1)}, u32[]{:S(2)}, u32[]{:S(2)}) %collective-permute-start.2) | collective-permute-done | bytes 65568 | tf_op jit(solution)/shard_map/ppermute | solution.py:48
  35.4 4.3 %collective-permute-start.3 = (bf16[256,256]{1,0:T(8,128)(2,1)S(1)}, bf16[256,256]{1,0:T(8,128)(2,1)S(1)}, u32[]{:S(2)}, u32[]{:S(2)}) collective-permute-start(bf16[256,256]{1,0:T(8,128)(2,1)S(1)} %shard_map.81.mine_ref), channel_id=1, source_target_pairs={{0,64},{64,0},{1,65},{65,1},{2,66},{66,2},{3,67},{67,3},{4,68},{68... | collective-permute-start | bytes 393224 | tf_op jit(solution)/shard_map/ppermute | solution.py:48
  39.7 5.8 %collective-permute-done.3.got_ref = bf16[256,256]{1,0:T(8,128)(2,1)S(1)} collective-permute-done((bf16[256,256]{1,0:T(8,128)(2,1)S(1)}, bf16[256,256]{1,0:T(8,128)(2,1)S(1)}, u32[]{:S(2)}, u32[]{:S(2)}) %collective-permute-start.3) | collective-permute-done | bytes 131104 | tf_op jit(solution)/shard_map/ppermute | solution.py:48
  45.5 0.0 all-to-all-done.held_ref
  45.5 1.1 %shard_map.82 = (f32[4,8,512]{2,1,0:T(8,128)S(1)}, f32[1024,512]{1,0:T(8,128)S(1)}, f32[1024,512]{1,0:T(8,128)S(1)}, bf16[512,256]{1,0:T(8,128)(2,1)S(1)}) custom-call(s32[1]{0:T(128)} %bitcast.c_ref, bf16[256,256]{1,0:T(8,128)(2,1)S(1)} %shard_map.81.mine_ref, bf16[256,256]{1,0:T(8,128)(2,1)S(1)} %collective-permute-done.3.got_ref, ...), custom_call_target="tpu_custom_call" | custom-call | flops 300000000 | bytes 5308420 | tf_op jit(solution)/shard_map/pallas_call | solution.py:63
  46.6 10.1 %all_to_all.20.stats_ref = f32[4,8,512]{2,1,0:T(8,128)S(1)} all-to-all(f32[4,8,512]{2,1,0:T(8,128)S(1)} %get-tuple-element.29.own_ref), channel_id=1, replica_groups=mesh['zh'=4,'zl'=2,'yl'=2,'xh'=2,'xl'=2,'tp'=8] {'zl','yl'}, dimensions={0} | all-to-all | bytes 131072 | tf_op jit(solution)/shard_map/all_to_all | solution.py:52
  56.8 1.5 %shard_map.83 = (bf16[16,64,256]{2,1,0:T(8,128)(2,1)}, f32[256,256]{1,0:T(8,128)S(1)}, bf16[256,256]{1,0:T(8,128)(2,1)S(1)}) custom-call(s32[1]{0:T(128)} %bitcast.c_ref, bf16[512,256]{1,0:T(8,128)(2,1)S(1)} %get-tuple-element.28.asked_ref, bf16[16,64,256]{2,1,0:T(8,128)(2,1)S(1)} %all-to-all-done.held_ref, f32[4,8,512]{2,1,0:T(8,128)S(1)} %get-tuple-element.29.own_ref, ...), custom_call_target="tpu_custom_call" | custom-call | flops 900000000 | bytes 6029316 | tf_op jit(solution)/shard_map/pallas_call | solution.py:63
  58.3 2.6 %collective-permute-start.4 = (bf16[256,256]{1,0:T(8,128)(2,1)S(1)}, bf16[256,256]{1,0:T(8,128)(2,1)S(1)}, u32[]{:S(2)}, u32[]{:S(2)}) collective-permute-start(bf16[256,256]{1,0:T(8,128)(2,1)S(1)} %get-tuple-element.34), channel_id=1, source_target_pairs={{0,64},{64,0},{1,65},{65,1},{2,66},{66,2},{3,67},{67,3},{4,68},{68... | collective-permute-start | bytes 393224 | tf_op jit(solution)/shard_map/ppermute | solution.py:48
  61.0 4.7 %all-to-all-start.2 = ((bf16[16,64,256]{2,1,0:T(8,128)(2,1)}), bf16[16,64,256]{2,1,0:T(8,128)(2,1)S(1)}, u32[]{:S(2)}, u32[]{:S(2)}) async-start(bf16[16,64,256]{2,1,0:T(8,128)(2,1)} %get-tuple-element.32), calls=%async_computation.2 | async-start | bytes 1048576 | tf_op jit(solution)/shard_map/all_to_all | solution.py:52
  65.7 0.0 collective-permute-done.4.got_ref
  65.8 2.1 %collective-permute-start.5 = (bf16[128,256]{1,0:T(8,128)(2,1)S(1)}, bf16[128,256]{1,0:T(8,128)(2,1)S(1)}, u32[]{:S(2)}, u32[]{:S(2)}) collective-permute-start(bf16[128,256]{1,0:T(8,128)(2,1)S(1)} %get-tuple-element.36), channel_id=1, source_target_pairs={{0,32},{32,0},{1,33},{33,1},{2,34},{34,2},{3,35},{35,3},{4,36},{36... | collective-permute-start | bytes 196616 | tf_op jit(solution)/shard_map/ppermute | solution.py:48
  67.9 2.9 %collective-permute-done.5.got_ref = bf16[128,256]{1,0:T(8,128)(2,1)S(1)} collective-permute-done((bf16[128,256]{1,0:T(8,128)(2,1)S(1)}, bf16[128,256]{1,0:T(8,128)(2,1)S(1)}, u32[]{:S(2)}, u32[]{:S(2)}) %collective-permute-start.5) | collective-permute-done | bytes 65568 | tf_op jit(solution)/shard_map/ppermute | solution.py:48
  70.8 3.4 %collective-permute-start.6 = (bf16[64,256]{1,0:T(8,128)(2,1)S(1)}, bf16[64,256]{1,0:T(8,128)(2,1)S(1)}, u32[]{:S(2)}, u32[]{:S(2)}) collective-permute-start(bf16[64,256]{1,0:T(8,128)(2,1)S(1)} %get-tuple-element.38), channel_id=1, source_target_pairs={{0,8},{8,0},{1,9},{9,1},{2,10},{10,2},{3,11},{11,3},{4,12},{12,4},... | collective-permute-start | bytes 98312 | tf_op jit(solution)/shard_map/ppermute | solution.py:48
  74.2 0.0 copy-done.2
  74.3 0.8 shard_map.86
  75.1 1.2 %collective-permute-done.6.got_ref = bf16[64,256]{1,0:T(8,128)(2,1)S(1)} collective-permute-done((bf16[64,256]{1,0:T(8,128)(2,1)S(1)}, bf16[64,256]{1,0:T(8,128)(2,1)S(1)}, u32[]{:S(2)}, u32[]{:S(2)}) %collective-permute-start.6) | collective-permute-done | bytes 32800 | tf_op jit(solution)/shard_map/ppermute | solution.py:48
  76.2 1.2 %all-to-all-done.2.term_ref = bf16[16,64,256]{2,1,0:T(8,128)(2,1)S(1)} async-done(((bf16[16,64,256]{2,1,0:T(8,128)(2,1)}), bf16[16,64,256]{2,1,0:T(8,128)(2,1)S(1)}, u32[]{:S(2)}, u32[]{:S(2)}) %all-to-all-start.2) | async-done | bytes 524320 | tf_op jit(solution)/shard_map/all_to_all | solution.py:52
  77.4 0.6 shard_map.87
  78.0 21.5 %all_to_all.21.pieces_ref = bf16[8,64,128]{2,1,0:T(8,128)(2,1)S(1)} all-to-all(bf16[8,64,128]{2,1,0:T(8,128)(2,1)S(1)} %get-tuple-element.40), channel_id=1, replica_groups=mesh['zh'=4,'zl'=2,'yl'=2,'xh'=2,'xl'=2,'tp'=8] {'tp'}, dimensions={0} | all-to-all | bytes 262144 | tf_op jit(solution)/shard_map/all_to_all | solution.py:52
  99.5 1.9 %collective-permute-start.7 = (bf16[64,384]{1,0:T(8,128)(2,1)S(1)}, bf16[64,384]{1,0:T(8,128)(2,1)S(1)}, u32[]{:S(2)}, u32[]{:S(2)}) collective-permute-start(bf16[64,384]{1,0:T(8,128)(2,1)S(1)} %shard_map.88.own_ref), channel_id=1, source_target_pairs={{0,8},{8,16},{16,24},{24,32},{32,40},{40,48},{48,56},{56,64},{64,7... | collective-permute-start | bytes 147464 | tf_op jit(solution)/shard_map/ppermute | solution.py:48
  101.5 7.1 %collective-permute-done.7.before_ref = bf16[64,384]{1,0:T(8,128)(2,1)S(1)} collective-permute-done((bf16[64,384]{1,0:T(8,128)(2,1)S(1)}, bf16[64,384]{1,0:T(8,128)(2,1)S(1)}, u32[]{:S(2)}, u32[]{:S(2)}) %collective-permute-start.7) | collective-permute-done | bytes 49184 | tf_op jit(solution)/shard_map/ppermute | solution.py:48
  108.6 0.8 shard_map.89
  (13 shorter events, 0.1 us)
Async XLA Ops:
  3.6 17.2 %collective-permute-start = (bf16[64,1024]{1,0:T(8,128)(2,1)}, bf16[64,1024]{1,0:T(8,128)(2,1)S(1)}, u32[]{:S(2)}, u32[]{:S(2)}) collective-permute-start(bf16[64,1024]{1,0:T(8,128)(2,1)} %get-tuple-element.24), channel_id=1, source_target_pairs={{0,504},{8,0},{16,8},{24,16},{32,24},{40,32},{48,40},{56,48},{64,5... | collective-permute-start | bytes 393224 | tf_op jit(solution)/shard_map/ppermute | solution.py:48
  18.3 0.9 copy-start.1
  21.7 7.7 %collective-permute-start.1 = (bf16[64,256]{1,0:T(8,128)(2,1)S(1)}, bf16[64,256]{1,0:T(8,128)(2,1)S(1)}, u32[]{:S(2)}, u32[]{:S(2)}) collective-permute-start(bf16[64,256]{1,0:T(8,128)(2,1)S(1)} %get-tuple-element.26), channel_id=1, source_target_pairs={{0,8},{8,0},{1,9},{9,1},{2,10},{10,2},{3,11},{11,3},{4,12},{12,4},... | collective-permute-start | bytes 98312 | tf_op jit(solution)/shard_map/ppermute | solution.py:48
  23.6 22.0 %all-to-all-start = ((bf16[16,64,256]{2,1,0:T(8,128)(2,1)}), bf16[16,64,256]{2,1,0:T(8,128)(2,1)S(1)}, u32[]{:S(2)}, u32[]{:S(2)}) async-start(bf16[16,64,256]{2,1,0:T(8,128)(2,1)} %get-tuple-element.27), calls=%async_computation | async-start | bytes 1048576 | tf_op jit(solution)/shard_map/all_to_all | solution.py:52
  29.3 6.0 %collective-permute-start.2 = (bf16[128,256]{1,0:T(8,128)(2,1)S(1)}, bf16[128,256]{1,0:T(8,128)(2,1)S(1)}, u32[]{:S(2)}, u32[]{:S(2)}) collective-permute-start(bf16[128,256]{1,0:T(8,128)(2,1)S(1)} %shard_map.80.mine_ref), channel_id=1, source_target_pairs={{0,32},{32,0},{1,33},{33,1},{2,34},{34,2},{3,35},{35,3},{4,36},{36... | collective-permute-start | bytes 196616 | tf_op jit(solution)/shard_map/ppermute | solution.py:48
  35.4 10.1 %collective-permute-start.3 = (bf16[256,256]{1,0:T(8,128)(2,1)S(1)}, bf16[256,256]{1,0:T(8,128)(2,1)S(1)}, u32[]{:S(2)}, u32[]{:S(2)}) collective-permute-start(bf16[256,256]{1,0:T(8,128)(2,1)S(1)} %shard_map.81.mine_ref), channel_id=1, source_target_pairs={{0,64},{64,0},{1,65},{65,1},{2,66},{66,2},{3,67},{67,3},{4,68},{68... | collective-permute-start | bytes 393224 | tf_op jit(solution)/shard_map/ppermute | solution.py:48
  58.3 7.4 %collective-permute-start.4 = (bf16[256,256]{1,0:T(8,128)(2,1)S(1)}, bf16[256,256]{1,0:T(8,128)(2,1)S(1)}, u32[]{:S(2)}, u32[]{:S(2)}) collective-permute-start(bf16[256,256]{1,0:T(8,128)(2,1)S(1)} %get-tuple-element.34), channel_id=1, source_target_pairs={{0,64},{64,0},{1,65},{65,1},{2,66},{66,2},{3,67},{67,3},{4,68},{68... | collective-permute-start | bytes 393224 | tf_op jit(solution)/shard_map/ppermute | solution.py:48
  61.0 16.5 %all-to-all-start.2 = ((bf16[16,64,256]{2,1,0:T(8,128)(2,1)}), bf16[16,64,256]{2,1,0:T(8,128)(2,1)S(1)}, u32[]{:S(2)}, u32[]{:S(2)}) async-start(bf16[16,64,256]{2,1,0:T(8,128)(2,1)} %get-tuple-element.32), calls=%async_computation.2 | async-start | bytes 1048576 | tf_op jit(solution)/shard_map/all_to_all | solution.py:52
  65.8 5.0 %collective-permute-start.5 = (bf16[128,256]{1,0:T(8,128)(2,1)S(1)}, bf16[128,256]{1,0:T(8,128)(2,1)S(1)}, u32[]{:S(2)}, u32[]{:S(2)}) collective-permute-start(bf16[128,256]{1,0:T(8,128)(2,1)S(1)} %get-tuple-element.36), channel_id=1, source_target_pairs={{0,32},{32,0},{1,33},{33,1},{2,34},{34,2},{3,35},{35,3},{4,36},{36... | collective-permute-start | bytes 196616 | tf_op jit(solution)/shard_map/ppermute | solution.py:48
  70.8 3.5 %copy-start.2 = (s32[2,64]{1,0:T(2,128)S(1)}, s32[2,64]{1,0:T(2,128)}, u32[]{:S(2)}) copy-start(s32[2,64]{1,0:T(2,128)} %moved_ref.1) | copy-start | bytes 1540
  70.8 3.5 %copy-start.3 = (s32[256]{0:T(256)S(1)}, s32[256]{0:T(256)}, u32[]{:S(2)}) copy-start(s32[256]{0:T(256)} %param.7) | copy-start | bytes 3076
  70.8 3.5 %copy-start.4 = (s32[64]{0:T(128)S(1)}, s32[64]{0:T(128)}, u32[]{:S(2)}) copy-start(s32[64]{0:T(128)} %first_ref.1) | copy-start | bytes 772
  70.8 6.6 %copy-start = (bf16[3,1024,256]{2,1,0:T(8,128)(2,1)S(1)}, bf16[3,1024,256]{2,1,0:T(8,128)(2,1)}, u32[]{:S(2)}) copy-start(bf16[3,1024,256]{2,1,0:T(8,128)(2,1)} %w_ref.1) | copy-start | bytes 4718596
  70.8 5.4 %collective-permute-start.6 = (bf16[64,256]{1,0:T(8,128)(2,1)S(1)}, bf16[64,256]{1,0:T(8,128)(2,1)S(1)}, u32[]{:S(2)}, u32[]{:S(2)}) collective-permute-start(bf16[64,256]{1,0:T(8,128)(2,1)S(1)} %get-tuple-element.38), channel_id=1, source_target_pairs={{0,8},{8,0},{1,9},{9,1},{2,10},{10,2},{3,11},{11,3},{4,12},{12,4},... | collective-permute-start | bytes 98312 | tf_op jit(solution)/shard_map/ppermute | solution.py:48
  99.5 9.1 %collective-permute-start.7 = (bf16[64,384]{1,0:T(8,128)(2,1)S(1)}, bf16[64,384]{1,0:T(8,128)(2,1)S(1)}, u32[]{:S(2)}, u32[]{:S(2)}) collective-permute-start(bf16[64,384]{1,0:T(8,128)(2,1)S(1)} %shard_map.88.own_ref), channel_id=1, source_target_pairs={{0,8},{8,16},{16,24},{24,32},{32,40},{40,48},{48,56},{56,64},{64,7... | collective-permute-start | bytes 147464 | tf_op jit(solution)/shard_map/ppermute | solution.py:48

commit v13 on v11

--- a/solution.py
+++ b/solution.py
@@ -108,8 +108,8 @@
         (grad_hbm, grad_ref),
     ] + [(w_hbm.at[i], w_ref.at[i]) for i in range(3)]
     copies = [pltpu.make_async_copy(a, b, sems.at[i]) for i, (a, b) in enumerate(pairs)]
-    for copy in copies:
-        copy.start()
+    for i in (3, 2, 5, 6, 7, 0, 1, 4):
+        copies[i].start()
     for copy in copies[:5]:
         copy.wait()
     c = c_ref[0]

time: 110 us -> 110 us (level)
  no operation moved by 1% of the time
where the time goes in v13:
time: 110 us
  starting transfers between devices  45.6 us (41%)
  blocking collectives  31.6 us (29%)
  waiting for transfers between devices  21.6 us (20%)
  Pallas kernels  9.13 us (8%)
    ppermute x8, starting transfers between devices, shift(): return lax.ppermute(x, axis, [(i, (i + by) % n) for i in range(n)])  35.1 us
    all_to_all x2, blocking collectives, swap(): return lax.all_to_all(x, axis, split_axis=0, concat_axis=0, tiled=True)  31.6 us
    ppermute x8, waiting for transfers between devices, shift(): return lax.ppermute(x, axis, [(i, (i + by) % n) for i in range(n)])  20.4 us
    all_to_all x2, starting transfers between devices, swap(): return lax.all_to_all(x, axis, split_axis=0, concat_axis=0, tiled=True)  10.5 us
    pallas_call x12, Pallas kernels, call(): pl.pallas_call(kernel, out_shape=tuple(outs), in_specs=[smem] * scalars +...  5.83 us
    pallas_call x1, Pallas kernels, pool(): pl.pallas_call(pool_kernel, out_shape=(block, block), in_specs=[pl.BlockS...  3.3 us
  transfers between devices with their start and end apart: 10, of which 7 were waited for; matrix products, arithmetic and copies ran while one was open for 0% of the time, Pallas kernels for 1%

profile of v13, /device:TPU:1, one launch (start us, length us, event | category | flops | bytes accessed | tf_op | source)
XLA Modules:
  0.0 109.7 jit_solution(3414949578468221151)
XLA Ops:
  0.6 3.3 %shard_map.77 = (bf16[64,1024]{1,0:T(8,128)(2,1)}, bf16[64,1024]{1,0:T(8,128)(2,1)}) custom-call(s32[1]{0:T(128)} %bitcast.c_ref, s32[64]{0:T(128)} %first_ref.1, s32[2,64]{1,0:T(2,128)} %moved_ref.1, s32[1,256]{1,0:T(1,128)} %bitcast.2, bf16[256,1024]{1,0:T(8,128)(2,1)} %bytes_hbm.1, bf16[64,256]{1,0:T(8,128)(2,1)} %grad_hbm.1, bf16[3,1024,256]{2,1,0:T(8,128)(2,1)} %w_ref.1), custom_call_target="tpu_custom_call" | custom-call | flops 300000000 | bytes 2500000 | tf_op jit(solution)/shard_map/pallas_call | solution.py:303
  3.9 14.7 %collective-permute-start = (bf16[64,1024]{1,0:T(8,128)(2,1)}, bf16[64,1024]{1,0:T(8,128)(2,1)S(1)}, u32[]{:S(2)}, u32[]{:S(2)}) collective-permute-start(bf16[64,1024]{1,0:T(8,128)(2,1)} %get-tuple-element.24), channel_id=1, source_target_pairs={{0,504},{8,0},{16,8},{24,16},{32,24},{40,32},{48,40},{56,48},{64,5... | collective-permute-start | bytes 393224 | tf_op jit(solution)/shard_map/ppermute | solution.py:48
  18.7 0.0 copy-start.1
  18.7 0.9 copy-done.1
  19.6 1.5 %collective-permute-done.got_ref = bf16[64,1024]{1,0:T(8,128)(2,1)S(1)} collective-permute-done((bf16[64,1024]{1,0:T(8,128)(2,1)}, bf16[64,1024]{1,0:T(8,128)(2,1)S(1)}, u32[]{:S(2)}, u32[]{:S(2)}) %collective-permute-start) | collective-permute-done | bytes 131104 | tf_op jit(solution)/shard_map/ppermute | solution.py:48
  21.1 0.9 shard_map.79
  22.0 1.9 %collective-permute-start.1 = (bf16[64,256]{1,0:T(8,128)(2,1)S(1)}, bf16[64,256]{1,0:T(8,128)(2,1)S(1)}, u32[]{:S(2)}, u32[]{:S(2)}) collective-permute-start(bf16[64,256]{1,0:T(8,128)(2,1)S(1)} %get-tuple-element.26), channel_id=1, source_target_pairs={{0,8},{8,0},{1,9},{9,1},{2,10},{10,2},{3,11},{11,3},{4,12},{12,4},... | collective-permute-start | bytes 98312 | tf_op jit(solution)/shard_map/ppermute | solution.py:48
  23.9 5.7 %all-to-all-start = ((bf16[16,64,256]{2,1,0:T(8,128)(2,1)}), bf16[16,64,256]{2,1,0:T(8,128)(2,1)S(1)}, u32[]{:S(2)}, u32[]{:S(2)}) async-start(bf16[16,64,256]{2,1,0:T(8,128)(2,1)} %get-tuple-element.27), calls=%async_computation | async-start | bytes 1048576 | tf_op jit(solution)/shard_map/all_to_all | solution.py:52
  29.7 0.0 collective-permute-done.1.got_ref
  29.7 4.1 %collective-permute-start.2 = (bf16[128,256]{1,0:T(8,128)(2,1)S(1)}, bf16[128,256]{1,0:T(8,128)(2,1)S(1)}, u32[]{:S(2)}, u32[]{:S(2)}) collective-permute-start(bf16[128,256]{1,0:T(8,128)(2,1)S(1)} %shard_map.80.mine_ref), channel_id=1, source_target_pairs={{0,32},{32,0},{1,33},{33,1},{2,34},{34,2},{3,35},{35,3},{4,36},{36... | collective-permute-start | bytes 196616 | tf_op jit(solution)/shard_map/ppermute | solution.py:48
  33.8 1.9 %collective-permute-done.2.got_ref = bf16[128,256]{1,0:T(8,128)(2,1)S(1)} collective-permute-done((bf16[128,256]{1,0:T(8,128)(2,1)S(1)}, bf16[128,256]{1,0:T(8,128)(2,1)S(1)}, u32[]{:S(2)}, u32[]{:S(2)}) %collective-permute-start.2) | collective-permute-done | bytes 65568 | tf_op jit(solution)/shard_map/ppermute | solution.py:48
  35.7 4.3 %collective-permute-start.3 = (bf16[256,256]{1,0:T(8,128)(2,1)S(1)}, bf16[256,256]{1,0:T(8,128)(2,1)S(1)}, u32[]{:S(2)}, u32[]{:S(2)}) collective-permute-start(bf16[256,256]{1,0:T(8,128)(2,1)S(1)} %shard_map.81.mine_ref), channel_id=1, source_target_pairs={{0,64},{64,0},{1,65},{65,1},{2,66},{66,2},{3,67},{67,3},{4,68},{68... | collective-permute-start | bytes 393224 | tf_op jit(solution)/shard_map/ppermute | solution.py:48
  40.1 5.8 %collective-permute-done.3.got_ref = bf16[256,256]{1,0:T(8,128)(2,1)S(1)} collective-permute-done((bf16[256,256]{1,0:T(8,128)(2,1)S(1)}, bf16[256,256]{1,0:T(8,128)(2,1)S(1)}, u32[]{:S(2)}, u32[]{:S(2)}) %collective-permute-start.3) | collective-permute-done | bytes 131104 | tf_op jit(solution)/shard_map/ppermute | solution.py:48
  45.8 0.0 all-to-all-done.held_ref
  45.8 1.1 %shard_map.82 = (f32[4,8,512]{2,1,0:T(8,128)S(1)}, f32[1024,512]{1,0:T(8,128)S(1)}, f32[1024,512]{1,0:T(8,128)S(1)}, bf16[512,256]{1,0:T(8,128)(2,1)S(1)}) custom-call(s32[1]{0:T(128)} %bitcast.c_ref, bf16[256,256]{1,0:T(8,128)(2,1)S(1)} %shard_map.81.mine_ref, bf16[256,256]{1,0:T(8,128)(2,1)S(1)} %collective-permute-done.3.got_ref, ...), custom_call_target="tpu_custom_call" | custom-call | flops 300000000 | bytes 5308420 | tf_op jit(solution)/shard_map/pallas_call | solution.py:63
  47.0 10.1 %all_to_all.20.stats_ref = f32[4,8,512]{2,1,0:T(8,128)S(1)} all-to-all(f32[4,8,512]{2,1,0:T(8,128)S(1)} %get-tuple-element.29.own_ref), channel_id=1, replica_groups=mesh['zh'=4,'zl'=2,'yl'=2,'xh'=2,'xl'=2,'tp'=8] {'zl','yl'}, dimensions={0} | all-to-all | bytes 131072 | tf_op jit(solution)/shard_map/all_to_all | solution.py:52
  57.1 1.5 %shard_map.83 = (bf16[16,64,256]{2,1,0:T(8,128)(2,1)}, f32[256,256]{1,0:T(8,128)S(1)}, bf16[256,256]{1,0:T(8,128)(2,1)S(1)}) custom-call(s32[1]{0:T(128)} %bitcast.c_ref, bf16[512,256]{1,0:T(8,128)(2,1)S(1)} %get-tuple-element.28.asked_ref, bf16[16,64,256]{2,1,0:T(8,128)(2,1)S(1)} %all-to-all-done.held_ref, f32[4,8,512]{2,1,0:T(8,128)S(1)} %get-tuple-element.29.own_ref, ...), custom_call_target="tpu_custom_call" | custom-call | flops 900000000 | bytes 6029316 | tf_op jit(solution)/shard_map/pallas_call | solution.py:63
  58.6 2.6 %collective-permute-start.4 = (bf16[256,256]{1,0:T(8,128)(2,1)S(1)}, bf16[256,256]{1,0:T(8,128)(2,1)S(1)}, u32[]{:S(2)}, u32[]{:S(2)}) collective-permute-start(bf16[256,256]{1,0:T(8,128)(2,1)S(1)} %get-tuple-element.34), channel_id=1, source_target_pairs={{0,64},{64,0},{1,65},{65,1},{2,66},{66,2},{3,67},{67,3},{4,68},{68... | collective-permute-start | bytes 393224 | tf_op jit(solution)/shard_map/ppermute | solution.py:48
  61.3 4.7 %all-to-all-start.2 = ((bf16[16,64,256]{2,1,0:T(8,128)(2,1)}), bf16[16,64,256]{2,1,0:T(8,128)(2,1)S(1)}, u32[]{:S(2)}, u32[]{:S(2)}) async-start(bf16[16,64,256]{2,1,0:T(8,128)(2,1)} %get-tuple-element.32), calls=%async_computation.2 | async-start | bytes 1048576 | tf_op jit(solution)/shard_map/all_to_all | solution.py:52
  66.1 0.0 collective-permute-done.4.got_ref
  66.1 2.1 %collective-permute-start.5 = (bf16[128,256]{1,0:T(8,128)(2,1)S(1)}, bf16[128,256]{1,0:T(8,128)(2,1)S(1)}, u32[]{:S(2)}, u32[]{:S(2)}) collective-permute-start(bf16[128,256]{1,0:T(8,128)(2,1)S(1)} %get-tuple-element.36), channel_id=1, source_target_pairs={{0,32},{32,0},{1,33},{33,1},{2,34},{34,2},{3,35},{35,3},{4,36},{36... | collective-permute-start | bytes 196616 | tf_op jit(solution)/shard_map/ppermute | solution.py:48
  68.2 2.9 %collective-permute-done.5.got_ref = bf16[128,256]{1,0:T(8,128)(2,1)S(1)} collective-permute-done((bf16[128,256]{1,0:T(8,128)(2,1)S(1)}, bf16[128,256]{1,0:T(8,128)(2,1)S(1)}, u32[]{:S(2)}, u32[]{:S(2)}) %collective-permute-start.5) | collective-permute-done | bytes 65568 | tf_op jit(solution)/shard_map/ppermute | solution.py:48
  71.2 3.4 %collective-permute-start.6 = (bf16[64,256]{1,0:T(8,128)(2,1)S(1)}, bf16[64,256]{1,0:T(8,128)(2,1)S(1)}, u32[]{:S(2)}, u32[]{:S(2)}) collective-permute-start(bf16[64,256]{1,0:T(8,128)(2,1)S(1)} %get-tuple-element.38), channel_id=1, source_target_pairs={{0,8},{8,0},{1,9},{9,1},{2,10},{10,2},{3,11},{11,3},{4,12},{12,4},... | collective-permute-start | bytes 98312 | tf_op jit(solution)/shard_map/ppermute | solution.py:48
  74.6 0.8 shard_map.86
  75.4 1.2 %collective-permute-done.6.got_ref = bf16[64,256]{1,0:T(8,128)(2,1)S(1)} collective-permute-done((bf16[64,256]{1,0:T(8,128)(2,1)S(1)}, bf16[64,256]{1,0:T(8,128)(2,1)S(1)}, u32[]{:S(2)}, u32[]{:S(2)}) %collective-permute-start.6) | collective-permute-done | bytes 32800 | tf_op jit(solution)/shard_map/ppermute | solution.py:48
  76.6 1.2 %all-to-all-done.2.term_ref = bf16[16,64,256]{2,1,0:T(8,128)(2,1)S(1)} async-done(((bf16[16,64,256]{2,1,0:T(8,128)(2,1)}), bf16[16,64,256]{2,1,0:T(8,128)(2,1)S(1)}, u32[]{:S(2)}, u32[]{:S(2)}) %all-to-all-start.2) | async-done | bytes 524320 | tf_op jit(solution)/shard_map/all_to_all | solution.py:52
  77.8 0.0 copy-done
  77.8 0.6 shard_map.87
  78.4 21.5 %all_to_all.21.pieces_ref = bf16[8,64,128]{2,1,0:T(8,128)(2,1)S(1)} all-to-all(bf16[8,64,128]{2,1,0:T(8,128)(2,1)S(1)} %get-tuple-element.40), channel_id=1, replica_groups=mesh['zh'=4,'zl'=2,'yl'=2,'xh'=2,'xl'=2,'tp'=8] {'tp'}, dimensions={0} | all-to-all | bytes 262144 | tf_op jit(solution)/shard_map/all_to_all | solution.py:52
  99.9 2.0 %collective-permute-start.7 = (bf16[64,384]{1,0:T(8,128)(2,1)S(1)}, bf16[64,384]{1,0:T(8,128)(2,1)S(1)}, u32[]{:S(2)}, u32[]{:S(2)}) collective-permute-start(bf16[64,384]{1,0:T(8,128)(2,1)S(1)} %shard_map.88.own_ref), channel_id=1, source_target_pairs={{0,8},{8,16},{16,24},{24,32},{32,40},{40,48},{48,56},{56,64},{64,7... | collective-permute-start | bytes 147464 | tf_op jit(solution)/shard_map/ppermute | solution.py:48
  101.8 7.1 %collective-permute-done.7.before_ref = bf16[64,384]{1,0:T(8,128)(2,1)S(1)} collective-permute-done((bf16[64,384]{1,0:T(8,128)(2,1)S(1)}, bf16[64,384]{1,0:T(8,128)(2,1)S(1)}, u32[]{:S(2)}, u32[]{:S(2)}) %collective-permute-start.7) | collective-permute-done | bytes 49184 | tf_op jit(solution)/shard_map/ppermute | solution.py:48
  108.9 0.8 shard_map.89
  (13 shorter events, 0.1 us)
Async XLA Ops:
  3.9 17.2 %collective-permute-start = (bf16[64,1024]{1,0:T(8,128)(2,1)}, bf16[64,1024]{1,0:T(8,128)(2,1)S(1)}, u32[]{:S(2)}, u32[]{:S(2)}) collective-permute-start(bf16[64,1024]{1,0:T(8,128)(2,1)} %get-tuple-element.24), channel_id=1, source_target_pairs={{0,504},{8,0},{16,8},{24,16},{32,24},{40,32},{48,40},{56,48},{64,5... | collective-permute-start | bytes 393224 | tf_op jit(solution)/shard_map/ppermute | solution.py:48
  18.7 0.9 copy-start.1
  22.0 7.7 %collective-permute-start.1 = (bf16[64,256]{1,0:T(8,128)(2,1)S(1)}, bf16[64,256]{1,0:T(8,128)(2,1)S(1)}, u32[]{:S(2)}, u32[]{:S(2)}) collective-permute-start(bf16[64,256]{1,0:T(8,128)(2,1)S(1)} %get-tuple-element.26), channel_id=1, source_target_pairs={{0,8},{8,0},{1,9},{9,1},{2,10},{10,2},{3,11},{11,3},{4,12},{12,4},... | collective-permute-start | bytes 98312 | tf_op jit(solution)/shard_map/ppermute | solution.py:48
  23.9 21.9 %all-to-all-start = ((bf16[16,64,256]{2,1,0:T(8,128)(2,1)}), bf16[16,64,256]{2,1,0:T(8,128)(2,1)S(1)}, u32[]{:S(2)}, u32[]{:S(2)}) async-start(bf16[16,64,256]{2,1,0:T(8,128)(2,1)} %get-tuple-element.27), calls=%async_computation | async-start | bytes 1048576 | tf_op jit(solution)/shard_map/all_to_all | solution.py:52
  29.7 6.0 %collective-permute-start.2 = (bf16[128,256]{1,0:T(8,128)(2,1)S(1)}, bf16[128,256]{1,0:T(8,128)(2,1)S(1)}, u32[]{:S(2)}, u32[]{:S(2)}) collective-permute-start(bf16[128,256]{1,0:T(8,128)(2,1)S(1)} %shard_map.80.mine_ref), channel_id=1, source_target_pairs={{0,32},{32,0},{1,33},{33,1},{2,34},{34,2},{3,35},{35,3},{4,36},{36... | collective-permute-start | bytes 196616 | tf_op jit(solution)/shard_map/ppermute | solution.py:48
  35.7 10.1 %collective-permute-start.3 = (bf16[256,256]{1,0:T(8,128)(2,1)S(1)}, bf16[256,256]{1,0:T(8,128)(2,1)S(1)}, u32[]{:S(2)}, u32[]{:S(2)}) collective-permute-start(bf16[256,256]{1,0:T(8,128)(2,1)S(1)} %shard_map.81.mine_ref), channel_id=1, source_target_pairs={{0,64},{64,0},{1,65},{65,1},{2,66},{66,2},{3,67},{67,3},{4,68},{68... | collective-permute-start | bytes 393224 | tf_op jit(solution)/shard_map/ppermute | solution.py:48
  58.6 7.4 %collective-permute-start.4 = (bf16[256,256]{1,0:T(8,128)(2,1)S(1)}, bf16[256,256]{1,0:T(8,128)(2,1)S(1)}, u32[]{:S(2)}, u32[]{:S(2)}) collective-permute-start(bf16[256,256]{1,0:T(8,128)(2,1)S(1)} %get-tuple-element.34), channel_id=1, source_target_pairs={{0,64},{64,0},{1,65},{65,1},{2,66},{66,2},{3,67},{67,3},{4,68},{68... | collective-permute-start | bytes 393224 | tf_op jit(solution)/shard_map/ppermute | solution.py:48
  61.3 16.5 %all-to-all-start.2 = ((bf16[16,64,256]{2,1,0:T(8,128)(2,1)}), bf16[16,64,256]{2,1,0:T(8,128)(2,1)S(1)}, u32[]{:S(2)}, u32[]{:S(2)}) async-start(bf16[16,64,256]{2,1,0:T(8,128)(2,1)} %get-tuple-element.32), calls=%async_computation.2 | async-start | bytes 1048576 | tf_op jit(solution)/shard_map/all_to_all | solution.py:52
  66.1 5.0 %collective-permute-start.5 = (bf16[128,256]{1,0:T(8,128)(2,1)S(1)}, bf16[128,256]{1,0:T(8,128)(2,1)S(1)}, u32[]{:S(2)}, u32[]{:S(2)}) collective-permute-start(bf16[128,256]{1,0:T(8,128)(2,1)S(1)} %get-tuple-element.36), channel_id=1, source_target_pairs={{0,32},{32,0},{1,33},{33,1},{2,34},{34,2},{3,35},{35,3},{4,36},{36... | collective-permute-start | bytes 196616 | tf_op jit(solution)/shard_map/ppermute | solution.py:48
  71.1 3.5 %copy-start.2 = (s32[2,64]{1,0:T(2,128)S(1)}, s32[2,64]{1,0:T(2,128)}, u32[]{:S(2)}) copy-start(s32[2,64]{1,0:T(2,128)} %moved_ref.1) | copy-start | bytes 1540
  71.1 3.5 %copy-start.3 = (s32[256]{0:T(256)S(1)}, s32[256]{0:T(256)}, u32[]{:S(2)}) copy-start(s32[256]{0:T(256)} %param.7) | copy-start | bytes 3076
  71.1 3.5 %copy-start.4 = (s32[64]{0:T(128)S(1)}, s32[64]{0:T(128)}, u32[]{:S(2)}) copy-start(s32[64]{0:T(128)} %first_ref.1) | copy-start | bytes 772
  71.1 6.6 %copy-start = (bf16[3,1024,256]{2,1,0:T(8,128)(2,1)S(1)}, bf16[3,1024,256]{2,1,0:T(8,128)(2,1)}, u32[]{:S(2)}) copy-start(bf16[3,1024,256]{2,1,0:T(8,128)(2,1)} %w_ref.1) | copy-start | bytes 4718596
  71.2 5.4 %collective-permute-start.6 = (bf16[64,256]{1,0:T(8,128)(2,1)S(1)}, bf16[64,256]{1,0:T(8,128)(2,1)S(1)}, u32[]{:S(2)}, u32[]{:S(2)}) collective-permute-start(bf16[64,256]{1,0:T(8,128)(2,1)S(1)} %get-tuple-element.38), channel_id=1, source_target_pairs={{0,8},{8,0},{1,9},{9,1},{2,10},{10,2},{3,11},{11,3},{4,12},{12,4},... | collective-permute-start | bytes 98312 | tf_op jit(solution)/shard_map/ppermute | solution.py:48
  99.9 9.1 %collective-permute-start.7 = (bf16[64,384]{1,0:T(8,128)(2,1)S(1)}, bf16[64,384]{1,0:T(8,128)(2,1)S(1)}, u32[]{:S(2)}, u32[]{:S(2)}) collective-permute-start(bf16[64,384]{1,0:T(8,128)(2,1)S(1)} %shard_map.88.own_ref), channel_id=1, source_target_pairs={{0,8},{8,16},{16,24},{24,32},{32,40},{40,48},{48,56},{56,64},{64,7... | collective-permute-start | bytes 147464 | tf_op jit(solution)/shard_map/ppermute | solution.py:48
